TPU v7x, 32 devices: a whole 2x2x4 slice. The times are simulated.
32 devices in a mesh: seq: 8 (over z, y), head: 4 (over x, core).
Axes of the slice: x: 2, y: 2, z: 4, core: 2. Of those that a mesh axis runs over, the one named last changes fastest.
Arguments:
- queries: bfloat16 [4096, 4096], P('seq', 'head'), may hold values from -6 to 6
- keys: bfloat16 [4096, 4096], P('seq', 'head'), may hold values from -6 to 6
- values: bfloat16 [4096, 4096], P('seq', 'head'), may hold values from -6 to 6
- out_grad: bfloat16 [4096, 4096], P('seq', 'head'), may hold values from -6 to 6
- gain: float32 [4096], P('head'), may hold values from 0.3 to 3
Outputs:
- query_grad: bfloat16 [4096, 4096], P('seq', 'head')
- key_grad: bfloat16 [4096, 4096], P('seq', 'head')
- value_grad: bfloat16 [4096, 4096], P('seq', 'head')
All inputs are finite; a program needn't handle non-finite values.
Results may differ from a plain program's by a relative error of at most 0.0058.
Values may be sent and summed in bfloat16 or wider, within the bound.
No kernel may reach another device: no remote copies, remote signals or barrier semaphores. Data moves between devices by JAX's collectives and lax.ppermute only.
A program may use at most 128 MiB of HBM per device.

v0:
```python
import jax
import jax.numpy as jnp
from jax import lax
from jax.sharding import PartitionSpec as P

HEAD_DIM = 128
D = 4096


def entering(part, axis, combine, identity, reverse):
    count = lax.axis_size(axis)
    place = lax.axis_index(axis)
    ahead = count - 1 - place if reverse else place
    gathered = lax.all_gather(part, axis)
    state = jnp.zeros_like(part) + jnp.asarray(identity, part.dtype)

    def one(lap, state):
        source = count - 1 - lap if reverse else lap
        return combine(state, lax.dynamic_index_in_dim(gathered, source, 0, False))

    return lax.fori_loop(0, ahead, one, state)


def add_states(earlier, later):
    return earlier + later


def shards(queries, keys, values, out_grad, gain):
    rows_local, width = queries.shape
    heads_local = width // HEAD_DIM
    shape = (rows_local, heads_local, HEAD_DIM)
    query_heads = queries.reshape(shape)
    key_heads = keys.reshape(shape)
    value_heads = values.reshape(shape)
    rows_index = lax.broadcasted_iota(jnp.int32, (rows_local, rows_local), 0)
    cols_index = lax.broadcasted_iota(jnp.int32, (rows_local, rows_local), 1)
    causal = (rows_index >= cols_index)[None]
    own_kv = jnp.einsum("thd,the->hde", key_heads, value_heads, preferred_element_type=jnp.float32)
    kv_state = entering(own_kv, "seq", add_states, jnp.zeros_like(own_kv), False)
    kv_low = kv_state.astype(jnp.bfloat16)
    scores = jnp.einsum("thd,shd->hts", query_heads, key_heads, preferred_element_type=jnp.float32)
    weights = jnp.where(causal, scores, 0.0).astype(jnp.bfloat16)
    attended = jnp.einsum("hts,she->the", weights, value_heads, preferred_element_type=jnp.float32)
    attended = attended + jnp.einsum(
        "thd,hde->the", query_heads, kv_low, preferred_element_type=jnp.float32
    )
    attended = attended.reshape(rows_local, width)
    scaled = gain[None, :] * out_grad.astype(jnp.float32)
    square_sum, cross_sum = lax.psum(
        (jnp.sum(attended * attended, axis=1), jnp.sum(scaled * attended, axis=1)), "head"
    )
    rms_rows = jnp.sqrt(square_sum / D + 1e-06)
    dout = scaled / rms_rows[:, None] - attended * (cross_sum / (D * rms_rows**3))[:, None]
    dout_heads = dout.astype(jnp.bfloat16).reshape(shape)
    own_grad = jnp.einsum(
        "thd,the->hde", query_heads, dout_heads, preferred_element_type=jnp.float32
    )
    grad_state = entering(own_grad, "seq", add_states, jnp.zeros_like(own_grad), True)
    grad_low = grad_state.astype(jnp.bfloat16)
    dscore = jnp.einsum("the,she->hts", dout_heads, value_heads, preferred_element_type=jnp.float32)
    dscore = jnp.where(causal, dscore, 0.0).astype(jnp.bfloat16)
    query_grad = jnp.einsum("hts,shd->thd", dscore, key_heads, preferred_element_type=jnp.float32)
    query_grad = query_grad + jnp.einsum(
        "the,hde->thd", dout_heads, kv_low, preferred_element_type=jnp.float32
    )
    key_grad = jnp.einsum("hts,thd->shd", dscore, query_heads, preferred_element_type=jnp.float32)
    key_grad = key_grad + jnp.einsum(
        "she,hde->shd", value_heads, grad_low, preferred_element_type=jnp.float32
    )
    value_grad = jnp.einsum("hts,the->she", weights, dout_heads, preferred_element_type=jnp.float32)
    value_grad = value_grad + jnp.einsum(
        "shd,hde->she", key_heads, grad_low, preferred_element_type=jnp.float32
    )
    return (
        query_grad.reshape(rows_local, width).astype(jnp.bfloat16),
        key_grad.reshape(rows_local, width).astype(jnp.bfloat16),
        value_grad.reshape(rows_local, width).astype(jnp.bfloat16),
    )


def solution(mesh):
    return jax.shard_map(
        shards,
        mesh=mesh,
        in_specs=(
            P("seq", "head"),
            P("seq", "head"),
            P("seq", "head"),
            P("seq", "head"),
            P("head"),
        ),
        out_specs=(P("seq", "head"), P("seq", "head"), P("seq", "head")),
        check_vma=False,
    )
```

profile of v0, /device:TPU:0, one launch (start us, length us, event | category | flops | bytes accessed | tf_op | source)
XLA Modules:
  0.0 217.7 jit_solution(11028200902330610181)
XLA Ops:
  7.2 2.6 %copy.62 = bf16[64,8,8,128]{3,2,1,0:T(8,128)(2,1)} copy(bf16[64,8,8,128]{3,1,2,0:T(8,128)(2,1)} %bitcast.111) | data formatting | bytes 2097152
  9.8 1.6 copy.35
  12.9 2.5 %select_convert_fusion.1 = bf16[8,512,512]{2,1,0:T(8,128)(2,1)S(1)} fusion(pred[512,512]{1,0:T(8,128)(4,1)S(1)} %iota_compare_fusion, bf16[512,1024]{1,0:T(8,128)(2,1)} %param.10, bf16[512,1024]{1,0:T(8,128)(2,1)S(1)} %copy-done), kind=kOutput, calls=%fused_computation.3 | convolution fusion | flops 541065216 | bytes 6553600 | tf_op jit(solution)/shard_map/thd,shd->hts/dot_general | solution.py:41
  15.5 2.0 copy-done.1
  17.4 2.9 %fusion.2 = f32[8,512,128]{1,2,0:T(8,128)} fusion(bf16[8,512,512]{2,1,0:T(8,128)(2,1)S(1)} %select_convert_fusion.1, bf16[512,1024]{1,0:T(8,128)(2,1)S(1)} %copy-done.3), kind=kOutput, calls=%fused_computation.15 | convolution fusion | flops 536870912 | bytes 7340032 | tf_op jit(solution)/shard_map/hts,she->the/dot_general | solution.py:43
  20.3 68.7 %all-gather.5.cloned.1.call-done = f32[64,128,128]{2,1,0:T(8,128)} async-done(((f32[8,128,128]{2,1,0:T(8,128)}), f32[64,128,128]{2,1,0:T(8,128)}) %all-gather.5.cloned.1.call-update) | async-done | bytes 4194320 | tf_op jit(solution)/shard_map/all_gather | solution.py:14
  89.1 3.5 %multiply_reduce_fusion.1 = (f32[512]{0:T(512)S(1)}, f32[512,8,128]{0,2,1:T(8,128)}) fusion(f32[8,128,128]{2,1,0:T(8,128)S(1)} %get-tuple-element.82, f32[8,512,128]{1,2,0:T(8,128)} %fusion.2, bf16[512,1024]{1,0:T(8,128)(2,1)S(1)} %copy-done), kind=kOutput, calls=%fused_computation.12 | convolution fusion | flops 135921152 | bytes 5769216 | tf_op jit(solution)/shard_map/thd,hde->the/dot_general | solution.py:44
  92.6 3.0 %copy.40 = f32[512,1024]{1,0:T(8,128)} copy(f32[512,1024]{0,1:T(8,128)} %bitcast.109) | data formatting | bytes 4194304 | tf_op jit(solution)/shard_map/reshape | solution.py:47
  95.6 1.9 multiply_reduce_fusion
  97.5 5.7 %all-reduce = (f32[512]{0:T(512)S(1)}, f32[512]{0:T(512)S(1)}) all-reduce(f32[512]{0:T(512)S(1)} %multiply_reduce_fusion, f32[512]{0:T(512)S(1)} %get-tuple-element.114), channel_id=1, replica_groups=mesh['seq'=8,'head'=4] {'head'}, use_global_device_ids=true, to_apply=%region_5.6 | all-reduce | flops 1024 | bytes 8192 | tf_op jit(solution)/shard_map/psum | solution.py:49
  103.2 3.0 %subtract_convert_fusion = bf16[512,1024]{1,0:T(8,128)(2,1)} fusion(f32[512,1024]{1,0:T(8,128)} %copy.40, bf16[512,1024]{1,0:T(8,128)(2,1)S(1)} %copy-done.9, f32[512]{0:T(512)S(1)} %get-tuple-element.113, f32[512]{0:T(512)S(1)} %get-tuple-element.112, f32[1024]{0:T(1024)S(1)} %copy-done.11), kind=kLoop, calls=%fused_computation.10 | loop fusion | flops 3145728 | bytes 4202496 | tf_op jit(solution)/shard_map/convert_element_type | solution.py:54
  106.2 1.5 copy.58
  109.2 2.7 %select_convert_fusion = bf16[8,512,512]{2,1,0:T(8,128)(2,1)S(1)} fusion(pred[512,512]{1,0:T(8,128)(4,1)S(1)} %iota_compare_fusion, bf16[512,8,128]{0,2,1:T(8,128)(2,1)S(1)} %bitcast.106, bf16[512,1024]{1,0:T(8,128)(2,1)} %param.11), kind=kOutput, calls=%fused_computation.2 | convolution fusion | flops 541065216 | bytes 6553600 | tf_op jit(solution)/shard_map/the,she->hts/dot_general | solution.py:60
  111.9 1.5 fusion.31
  113.9 1.4 fusion.1
  115.3 2.3 %copy.53 = bf16[512,1024]{1,0:T(8,128)(2,1)} copy(bf16[512,1024]{0,1:T(8,128)(2,1)} %bitcast.112) | data formatting | bytes 2097152
  117.6 4.2 %fusion.32 = f32[8,128,512]{2,1,0:T(8,128)} fusion(bf16[512,8,128]{0,2,1:T(8,128)(2,1)S(1)} %bitcast.108, bf16[8,512,512]{2,1,0:T(8,128)(2,1)} %copy-done.1), kind=kOutput, calls=%fused_computation.48 | convolution fusion | flops 536870912 | bytes 7340032 | tf_op jit(solution)/shard_map/hts,the->she/dot_general | solution.py:70
  121.8 67.8 %all-gather.7.cloned.1.call-done = f32[64,128,128]{2,1,0:T(8,128)} async-done(((f32[8,128,128]{2,1,0:T(8,128)}), f32[64,128,128]{2,1,0:T(8,128)}) %all-gather.7.cloned.1.call-update) | async-done | bytes 4194320 | tf_op jit(solution)/shard_map/all_gather | solution.py:14
  189.6 8.4 %while.23 = (s32[]{:T(128)}, f32[8,128,128]{2,1,0:T(8,128)S(1)}, s32[]{:T(128)}, f32[8,8,128,128]{3,2,1,0:T(8,128)}, s32[]{:T(128)}, /*index=5*/s32[]{:T(128)}, s32[]{:T(128)}, s32[]{:T(128)}) while((s32[]{:T(128)}, f32[8,128,128]{2,1,0:T(8,128)S(1)}, s32[]{:T(128)}, f32[8,8,128,128]{3,2,1,0:T(8,128)}, s32[]{:T(128)}, /*index=5*/s32[]{:T(128)}, ...), condition=%wide.region_7.8_spmd, body=%wide.region_6.7_spmd.sunk | while | flops 131078 | bytes 1573007 | solution.py:21
  198.1 1.8 fusion.4
  200.7 1.5 add_convert_fusion
  202.2 2.4 %copy.55 = bf16[512,1024]{1,0:T(8,128)(2,1)} copy(bf16[512,1024]{0,1:T(8,128)(2,1)} %bitcast.113) | data formatting | bytes 2097152
  204.6 4.0 %fusion = bf16[512,8,128]{0,2,1:T(8,128)(2,1)} fusion(f32[8,128,512]{2,1,0:T(8,128)S(1)} %copy-done.8, bf16[8,512,512]{2,1,0:T(8,128)(2,1)} %copy-done.2, bf16[512,1024]{1,0:T(8,128)(2,1)S(1)} %copy-done), kind=kOutput, calls=%fused_computation.5 | convolution fusion | flops 537919488 | bytes 8388608 | tf_op jit(solution)/shard_map/hts,thd->shd/dot_general | solution.py:66
  208.6 2.3 %copy.54 = bf16[512,1024]{1,0:T(8,128)(2,1)} copy(bf16[512,1024]{0,1:T(8,128)(2,1)} %bitcast.114) | data formatting | bytes 2097152
  (42 shorter events, 12.6 us)
Async XLA Ops:
  7.2 5.8 %copy-start = (bf16[512,1024]{1,0:T(8,128)(2,1)S(1)}, bf16[512,1024]{1,0:T(8,128)(2,1)}, u32[]{:S(2)}) copy-start(bf16[512,1024]{1,0:T(8,128)(2,1)} %param.9) | copy-start | bytes 3145732
  7.2 81.9 %all-gather.5.cloned.1.call-start = ((), (), s32[]{:S(2)}) async-start(), calls=%async_computation | async-start | bytes 4718592 | tf_op jit(solution)/shard_map/all_gather | solution.py:14
  7.2 4.3 %copy-start.3 = (bf16[512,1024]{1,0:T(8,128)(2,1)S(1)}, bf16[512,1024]{1,0:T(8,128)(2,1)}, u32[]{:S(2)}) copy-start(bf16[512,1024]{1,0:T(8,128)(2,1)} %param.11) | copy-start | bytes 3145732
  11.5 4.0 %copy-start.5 = (bf16[512,8,128]{0,2,1:T(8,128)(2,1)}, bf16[512,8,128]{0,2,1:T(8,128)(2,1)S(1)}, u32[]{:S(2)}) copy-start(bf16[512,8,128]{0,2,1:T(8,128)(2,1)S(1)} %copy.35) | copy-start | bytes 3145732
  12.8 176.8 %all-gather.7.cloned.1.call-start = ((), (), s32[]{:S(2)}) async-start(), calls=%async_computation.1 | async-start | bytes 4718592 | tf_op jit(solution)/shard_map/all_gather | solution.py:14
  15.5 2.0 copy-start.1
  92.6 3.0 %copy-start.9 = (bf16[512,1024]{1,0:T(8,128)(2,1)S(1)}, bf16[512,1024]{1,0:T(8,128)(2,1)}, u32[]{:S(2)}) copy-start(bf16[512,1024]{1,0:T(8,128)(2,1)} %param.12) | copy-start | bytes 3145732
  92.6 3.0 %copy-start.11 = (f32[1024]{0:T(1024)S(1)}, f32[1024]{0:T(1024)}, u32[]{:S(2)}) copy-start(f32[1024]{0:T(1024)} %param.13) | copy-start | bytes 12292
  109.2 2.7 %copy-start.6 = (bf16[512,8,128]{0,2,1:T(8,128)(2,1)S(1)}, bf16[512,8,128]{0,2,1:T(8,128)(2,1)}, u32[]{:S(2)}) copy-start(bf16[512,8,128]{0,2,1:T(8,128)(2,1)} %copy-done.5) | copy-start | bytes 3145732
  111.9 1.9 copy-start.2
  189.6 8.5 %copy-start.4 = (bf16[512,1024]{1,0:T(8,128)(2,1)S(1)}, bf16[512,1024]{1,0:T(8,128)(2,1)}, u32[]{:S(2)}) copy-start(bf16[512,1024]{1,0:T(8,128)(2,1)} %param.11) | copy-start | bytes 3145732
  198.1 1.9 copy-start.7
  198.1 2.6 %copy-start.10 = (bf16[512,1024]{1,0:T(8,128)(2,1)S(1)}, bf16[512,1024]{1,0:T(8,128)(2,1)}, u32[]{:S(2)}) copy-start(bf16[512,1024]{1,0:T(8,128)(2,1)} %param.10) | copy-start | bytes 3145732
  202.2 2.4 %copy-start.8 = (f32[8,128,512]{2,1,0:T(8,128)S(1)}, f32[8,128,512]{2,1,0:T(8,128)}, u32[]{:S(2)}) copy-start(f32[8,128,512]{2,1,0:T(8,128)} %fusion.4) | copy-start | bytes 6291460
Sparse Core Ops, SparseCore 0:
  12.9 76.0 all-gather.4
  109.3 80.2 all-gather.6
where the time goes:
time: 218 us
  waiting for transfers between devices  137 us (63%)
  matrix products  27.6 us (13%)
  local copies, waits for them, and re-layouts  20 us (9%)
  between operations  14.2 us (7%)
  other arithmetic  13.3 us (6%)
  blocking collectives  5.66 us (3%)
    all_gather x2, waiting for transfers between devices, entering(): gathered = lax.all_gather(part, axis)  137 us
    unnamed x28, local copies, waits for them, and re-layouts  12.8 us
    add x7, other arithmetic, add_states(): return earlier + later  8.26 us
    psum x1, blocking collectives, shards(): lax.psum((jnp.sum(attended * attended, axis=1), jnp.sum(scaled * attended...  5.66 us
  transfers between devices with their start and end apart: 2, of which 2 were waited for; matrix products, arithmetic and copies ran while one was open for 8% of the time, Pallas kernels for 0%

commit v1 on v0

--- a/solution.py
+++ b/solution.py
@@ -7,22 +7,16 @@
 D = 4096
 
 
-def entering(part, axis, combine, identity, reverse):
+def entering(part, axis, reverse):
     count = lax.axis_size(axis)
-    place = lax.axis_index(axis)
-    ahead = count - 1 - place if reverse else place
-    gathered = lax.all_gather(part, axis)
-    state = jnp.zeros_like(part) + jnp.asarray(identity, part.dtype)
-
-    def one(lap, state):
-        source = count - 1 - lap if reverse else lap
-        return combine(state, lax.dynamic_index_in_dim(gathered, source, 0, False))
-
-    return lax.fori_loop(0, ahead, one, state)
-
-
-def add_states(earlier, later):
-    return earlier + later
+    heads, rows, cols = part.shape
+    pieces = part.astype(jnp.bfloat16).reshape(count, heads * rows // count, cols)
+    blocks = lax.all_to_all(pieces, axis, 0, 0).astype(jnp.float32)
+    own = lax.broadcasted_iota(jnp.int32, (count, count), 0)
+    other = lax.broadcasted_iota(jnp.int32, (count, count), 1)
+    taken = other > own if reverse else other < own
+    states = jnp.sum(jnp.where(taken[:, :, None, None], blocks[None], 0.0), axis=1)
+    return lax.all_to_all(states.astype(jnp.bfloat16), axis, 0, 0).reshape(part.shape)
 
 
 def shards(queries, keys, values, out_grad, gain):
@@ -36,8 +30,7 @@
     cols_index = lax.broadcasted_iota(jnp.int32, (rows_local, rows_local), 1)
     causal = (rows_index >= cols_index)[None]
     own_kv = jnp.einsum("thd,the->hde", key_heads, value_heads, preferred_element_type=jnp.float32)
-    kv_state = entering(own_kv, "seq", add_states, jnp.zeros_like(own_kv), False)
-    kv_low = kv_state.astype(jnp.bfloat16)
+    kv_low = entering(own_kv, "seq", False)
     scores = jnp.einsum("thd,shd->hts", query_heads, key_heads, preferred_element_type=jnp.float32)
     weights = jnp.where(causal, scores, 0.0).astype(jnp.bfloat16)
     attended = jnp.einsum("hts,she->the", weights, value_heads, preferred_element_type=jnp.float32)
@@ -55,8 +48,7 @@
     own_grad = jnp.einsum(
         "thd,the->hde", query_heads, dout_heads, preferred_element_type=jnp.float32
     )
-    grad_state = entering(own_grad, "seq", add_states, jnp.zeros_like(own_grad), True)
-    grad_low = grad_state.astype(jnp.bfloat16)
+    grad_low = entering(own_grad, "seq", True)
     dscore = jnp.einsum("the,she->hts", dout_heads, value_heads, preferred_element_type=jnp.float32)
     dscore = jnp.where(causal, dscore, 0.0).astype(jnp.bfloat16)
     query_grad = jnp.einsum("hts,shd->thd", dscore, key_heads, preferred_element_type=jnp.float32)

time: 218 us -> 92.9 us (0.43)
  waiting for transfers between devices: 137 us -> 12.1 us
  starting transfers between devices: 0.08 us -> 19.1 us
  between operations: 14.2 us -> 0.8 us
  other arithmetic: 13.3 us -> 6.1 us
  matrix products: 27.6 us -> 32 us
  local copies, waits for them, and re-layouts: 20 us -> 16.2 us
    all_gather x2 -> x0, waiting for transfers between devices: 137 us -> none  [entering(): gathered = lax.all_gather(part, axis)]
    all_to_all x0 -> x4, starting transfers between devices: none -> 19.1 us  [the longest x2 11.3 us: entering(): blocks = lax.all_to_all(pieces, axis, 0, 0).astype(jnp.float32)]
    all_to_all x0 -> x4, waiting for transfers between devices: none -> 12.1 us  [the longest x2 6.8 us: entering(): blocks = lax.all_to_all(pieces, axis, 0, 0).astype(jnp.float32)]
    add x7 -> x0, other arithmetic: 8.26 us -> none  [add_states(): return earlier + later]
    unnamed x28 -> x24, local copies, waits for them, and re-layouts: 12.8 us -> 9.31 us
  transfers between devices with their start and end apart: 2 -> 4, of which waited for: 2 -> 4; matrix products, arithmetic and copies ran while one was open for 8% -> 22% of each run, Pallas kernels for 0% -> 0%
where the time goes in v1:
time: 92.9 us; the launch traced here: 92 us
  matrix products  32 us (34%)
  starting transfers between devices  19.1 us (21%)
  local copies, waits for them, and re-layouts  16.2 us (17%)
  waiting for transfers between devices  12.1 us (13%)
  other arithmetic  6.1 us (7%)
  blocking collectives  5.66 us (6%)
    all_to_all x2, starting transfers between devices, entering(): blocks = lax.all_to_all(pieces, axis, 0, 0).astype(jnp.float32)  11.3 us
    unnamed x24, local copies, waits for them, and re-layouts  9.31 us
    all_to_all x2, starting transfers between devices, entering(): lax.all_to_all(states.astype(jnp.bfloat16), axis, 0, 0).reshape(part.shape)  7.81 us
    all_to_all x2, waiting for transfers between devices, entering(): blocks = lax.all_to_all(pieces, axis, 0, 0).astype(jnp.float32)  6.8 us
    psum x1, blocking collectives, shards(): lax.psum((jnp.sum(attended * attended, axis=1), jnp.sum(scaled * attended...  5.66 us
    all_to_all x2, waiting for transfers between devices, entering(): lax.all_to_all(states.astype(jnp.bfloat16), axis, 0, 0).reshape(part.shape)  5.31 us
    dot_general x1, matrix products, shards(): jnp.einsum('hts,the->she', weights, dout_heads, preferred_element_type=jn...  4.35 us
    dot_general x1, matrix products, shards(): jnp.einsum('hts,she->the', weights, value_heads, preferred_element_type=j...  3.98 us
  transfers between devices with their start and end apart: 4, of which 4 were waited for; matrix products, arithmetic and copies ran while one was open for 22% of the time, Pallas kernels for 0%

profile of v1, /device:TPU:0, one launch (start us, length us, event | category | flops | bytes accessed | tf_op | source)
XLA Modules:
  0.0 92.0 jit_solution(10335640397028548605)
XLA Ops:
  0.7 1.6 %copy.63 = bf16[64,8,8,128]{3,2,1,0:T(8,128)(2,1)S(1)} copy(bf16[64,8,8,128]{3,1,2,0:T(8,128)(2,1)} %bitcast.104) | data formatting | bytes 2097152
  3.8 2.5 %convolution_convert_fusion.1 = bf16[8,128,128]{2,1,0:T(8,128)(2,1)} fusion(bf16[512,8,128]{0,2,1:T(8,128)(2,1)} %copy.35, bf16[512,1024]{1,0:T(8,128)(2,1)S(1)} %copy-done.4), kind=kOutput, calls=%fused_computation.15 | convolution fusion | flops 134348800 | bytes 2359296 | tf_op jit(solution)/shard_map/thd,the->hde/dot_general | solution.py:32
  6.2 7.3 %all-to-all-start = ((bf16[8,128,128]{2,1,0:T(8,128)(2,1)}), bf16[8,128,128]{2,1,0:T(8,128)(2,1)S(1)}, u32[]{:S(2)}, u32[]{:S(2)}) async-start(bf16[8,128,128]{2,1,0:T(8,128)(2,1)} %convolution_convert_fusion.1), calls=%async_computation | async-start | bytes 524288 | tf_op jit(solution)/shard_map/all_to_all | solution.py:14
  14.3 3.3 %select_convert_fusion.1 = bf16[8,512,512]{2,1,0:T(8,128)(2,1)} fusion(pred[512,512]{1,0:T(8,128)(4,1)S(1)} %iota_compare_fusion, bf16[512,1024]{1,0:T(8,128)(2,1)S(1)} %copy-done.2, bf16[512,1024]{1,0:T(8,128)(2,1)S(1)} %copy-done), kind=kOutput, calls=%fused_computation.1 | convolution fusion | flops 541065216 | bytes 6553600 | tf_op jit(solution)/shard_map/thd,shd->hts/dot_general | solution.py:34
  17.6 4.9 %all-to-all-done = bf16[8,128,128]{2,1,0:T(8,128)(2,1)S(1)} async-done(((bf16[8,128,128]{2,1,0:T(8,128)(2,1)}), bf16[8,128,128]{2,1,0:T(8,128)(2,1)S(1)}, u32[]{:S(2)}, u32[]{:S(2)}) %all-to-all-start) | async-done | bytes 262176 | tf_op jit(solution)/shard_map/all_to_all | solution.py:14
  23.9 3.6 %all-to-all-start.1 = ((bf16[8,128,128]{1,2,0:T(8,128)(2,1)}), bf16[8,128,128]{1,2,0:T(8,128)(2,1)S(1)}, u32[]{:S(2)}, u32[]{:S(2)}) async-start(bf16[8,128,128]{1,2,0:T(8,128)(2,1)} %copy.37), calls=%async_computation.1 | async-start | bytes 524288 | tf_op jit(solution)/shard_map/all_to_all | solution.py:19
  27.5 4.0 %fusion.3 = f32[8,512,128]{1,2,0:T(8,128)S(1)} fusion(bf16[8,512,512]{2,1,0:T(8,128)(2,1)} %select_convert_fusion.1, bf16[512,1024]{1,0:T(8,128)(2,1)} %param.7), kind=kOutput, calls=%fused_computation.17 | convolution fusion | flops 536870912 | bytes 7340032 | tf_op jit(solution)/shard_map/hts,she->the/dot_general | solution.py:36
  31.4 4.6 %all-to-all-done.1 = bf16[8,128,128]{1,2,0:T(8,128)(2,1)S(1)} async-done(((bf16[8,128,128]{1,2,0:T(8,128)(2,1)}), bf16[8,128,128]{1,2,0:T(8,128)(2,1)S(1)}, u32[]{:S(2)}, u32[]{:S(2)}) %all-to-all-start.1) | async-done | bytes 262176 | tf_op jit(solution)/shard_map/all_to_all | solution.py:19
  36.0 1.8 %multiply_reduce_fusion.1 = (f32[512]{0:T(512)S(1)}, f32[512,8,128]{0,2,1:T(8,128)}) fusion(bf16[8,128,128]{1,2,0:T(8,128)(2,1)S(1)} %all-to-all-done.1, f32[8,512,128]{1,2,0:T(8,128)S(1)} %fusion.3, bf16[512,1024]{1,0:T(8,128)(2,1)S(1)} %copy-done), kind=kOutput, calls=%fused_computation.12 | convolution fusion | flops 135790080 | bytes 5507072 | tf_op jit(solution)/shard_map/thd,hde->the/dot_general | solution.py:37
  37.8 1.9 %copy.40 = f32[512,1024]{1,0:T(8,128)S(1)} copy(f32[512,1024]{0,1:T(8,128)} %bitcast.103) | data formatting | bytes 4194304 | tf_op jit(solution)/shard_map/reshape | solution.py:40
  41.3 5.7 %all-reduce = (f32[512]{0:T(512)S(1)}, f32[512]{0:T(512)S(1)}) all-reduce(f32[512]{0:T(512)S(1)} %multiply_reduce_fusion, f32[512]{0:T(512)S(1)} %get-tuple-element.13), channel_id=1, replica_groups=mesh['seq'=8,'head'=4] {'head'}, use_global_device_ids=true, to_apply=%region_4.5 | all-reduce | flops 1024 | bytes 8192 | tf_op jit(solution)/shard_map/psum | solution.py:42
  47.0 2.6 %subtract_convert_fusion = bf16[512,1024]{1,0:T(8,128)(2,1)} fusion(f32[512,1024]{1,0:T(8,128)S(1)} %copy.40, bf16[512,1024]{1,0:T(8,128)(2,1)} %param.8, f32[512]{0:T(512)S(1)} %get-tuple-element.12, f32[512]{0:T(512)S(1)} %get-tuple-element.11, f32[1024]{0:T(1024)S(1)} %copy-done.9), kind=kLoop, calls=%fused_computation.10 | loop fusion | flops 3145728 | bytes 4202496 | tf_op jit(solution)/shard_map/convert_element_type | solution.py:47
  49.6 1.6 %copy.59 = bf16[512,1024]{0,1:T(8,128)(2,1)S(1)} copy(bf16[512,1024]{1,0:T(8,128)(2,1)} %subtract_convert_fusion) | data formatting | bytes 2097152 | tf_op jit(solution)/shard_map/reshape | solution.py:47
  52.4 4.0 %all-to-all-start.2 = ((bf16[8,128,128]{1,2,0:T(8,128)(2,1)}), bf16[8,128,128]{1,2,0:T(8,128)(2,1)}, u32[]{:S(2)}, u32[]{:S(2)}) async-start(bf16[8,128,128]{1,2,0:T(8,128)(2,1)} %fusion.2), calls=%async_computation.2 | async-start | bytes 524288 | tf_op jit(solution)/shard_map/all_to_all | solution.py:14
  56.4 2.4 %select_convert_fusion = bf16[8,512,512]{2,1,0:T(8,128)(2,1)S(1)} fusion(pred[512,512]{1,0:T(8,128)(4,1)} %copy-done.8, bf16[512,8,128]{0,2,1:T(8,128)(2,1)S(1)} %bitcast.100, bf16[512,1024]{1,0:T(8,128)(2,1)S(1)} %copy-done.5), kind=kOutput, calls=%fused_computation | convolution fusion | flops 541065216 | bytes 6553600 | tf_op jit(solution)/shard_map/the,she->hts/dot_general | solution.py:52
  58.9 2.0 %copy-done.1 = bf16[8,512,512]{2,1,0:T(8,128)(2,1)} copy-done((bf16[8,512,512]{2,1,0:T(8,128)(2,1)}, bf16[8,512,512]{2,1,0:T(8,128)(2,1)S(1)}, u32[]{:S(2)}) %copy-start.1) | copy-done | bytes 4194328
  60.9 2.8 %fusion.27 = f32[8,512,128]{1,2,0:T(8,128)} fusion(bf16[8,512,512]{2,1,0:T(8,128)(2,1)S(1)} %select_convert_fusion, bf16[512,8,128]{0,2,1:T(8,128)(2,1)S(1)} %copy-done.7), kind=kOutput, calls=%fused_computation.46 | convolution fusion | flops 536870912 | bytes 7340032 | tf_op jit(solution)/shard_map/hts,shd->thd/dot_general | solution.py:54
  63.7 1.9 %all-to-all-done.2 = bf16[8,128,128]{1,2,0:T(8,128)(2,1)} async-done(((bf16[8,128,128]{1,2,0:T(8,128)(2,1)}), bf16[8,128,128]{1,2,0:T(8,128)(2,1)}, u32[]{:S(2)}, u32[]{:S(2)}) %all-to-all-start.2) | async-done | bytes 262176 | tf_op jit(solution)/shard_map/all_to_all | solution.py:14
  68.0 4.2 %all-to-all-start.3 = ((bf16[8,128,128]{2,1,0:T(8,128)(2,1)}), bf16[8,128,128]{2,1,0:T(8,128)(2,1)}, u32[]{:S(2)}, u32[]{:S(2)}) async-start(bf16[8,128,128]{2,1,0:T(8,128)(2,1)} %select_reduce_fusion), calls=%async_computation.3 | async-start | bytes 524288 | tf_op jit(solution)/shard_map/all_to_all | solution.py:19
  72.2 2.1 %fusion.1 = bf16[512,8,128]{0,2,1:T(8,128)(2,1)S(1)} fusion(f32[8,512,128]{1,2,0:T(8,128)} %fusion.27, bf16[8,128,128]{1,2,0:T(8,128)(2,1)S(1)} %all-to-all-done.1, bf16[512,8,128]{0,2,1:T(8,128)(2,1)S(1)} %bitcast.101), kind=kOutput, calls=%fused_computation.7 | convolution fusion | flops 135266304 | bytes 4456448 | tf_op jit(solution)/shard_map/the,hde->thd/dot_general | solution.py:55
  75.6 4.3 %fusion.28 = f32[8,128,512]{2,1,0:T(8,128)} fusion(bf16[512,8,128]{0,2,1:T(8,128)(2,1)S(1)} %bitcast.102, bf16[8,512,512]{2,1,0:T(8,128)(2,1)} %select_convert_fusion.1), kind=kOutput, calls=%fused_computation.47 | convolution fusion | flops 536870912 | bytes 7340032 | tf_op jit(solution)/shard_map/hts,the->she/dot_general | solution.py:62
  80.7 3.2 %add_convert_fusion = bf16[8,128,512]{2,1,0:T(8,128)(2,1)} fusion(f32[8,128,512]{2,1,0:T(8,128)} %fusion.28, bf16[8,128,128]{2,1,0:T(8,128)(2,1)} %all-to-all-done.3, bf16[512,1024]{1,0:T(8,128)(2,1)S(1)} %copy-done.3), kind=kOutput, calls=%fused_computation.9 | convolution fusion | flops 135266304 | bytes 4456448 | tf_op jit(solution)/shard_map/shd,hde->she/dot_general | solution.py:63
  83.9 2.4 %copy.56 = bf16[512,1024]{1,0:T(8,128)(2,1)} copy(bf16[512,1024]{0,1:T(8,128)(2,1)} %bitcast.106) | data formatting | bytes 2097152
  87.6 3.1 %fusion = bf16[512,8,128]{0,2,1:T(8,128)(2,1)S(1)} fusion(f32[8,128,512]{2,1,0:T(8,128)S(1)} %fusion.5, bf16[8,512,512]{2,1,0:T(8,128)(2,1)} %copy-done.1, bf16[512,1024]{1,0:T(8,128)(2,1)S(1)} %copy-done), kind=kOutput, calls=%fused_computation.5 | convolution fusion | flops 537919488 | bytes 8388608 | tf_op jit(solution)/shard_map/hts,thd->shd/dot_general | solution.py:58
  (35 shorter events, 13.5 us)
Async XLA Ops:
  0.6 13.7 %copy-start = (bf16[512,1024]{1,0:T(8,128)(2,1)S(1)}, bf16[512,1024]{1,0:T(8,128)(2,1)}, u32[]{:S(2)}) copy-start(bf16[512,1024]{1,0:T(8,128)(2,1)} %param.5) | copy-start | bytes 3145732
  0.6 3.1 %copy-start.4 = (bf16[512,1024]{1,0:T(8,128)(2,1)S(1)}, bf16[512,1024]{1,0:T(8,128)(2,1)}, u32[]{:S(2)}) copy-start(bf16[512,1024]{1,0:T(8,128)(2,1)} %param.7) | copy-start | bytes 3145732
  3.8 10.5 %copy-start.2 = (bf16[512,1024]{1,0:T(8,128)(2,1)S(1)}, bf16[512,1024]{1,0:T(8,128)(2,1)}, u32[]{:S(2)}) copy-start(bf16[512,1024]{1,0:T(8,128)(2,1)} %param.6) | copy-start | bytes 3145732
  6.2 16.2 %all-to-all-start = ((bf16[8,128,128]{2,1,0:T(8,128)(2,1)}), bf16[8,128,128]{2,1,0:T(8,128)(2,1)S(1)}, u32[]{:S(2)}, u32[]{:S(2)}) async-start(bf16[8,128,128]{2,1,0:T(8,128)(2,1)} %convolution_convert_fusion.1), calls=%async_computation | async-start | bytes 524288 | tf_op jit(solution)/shard_map/all_to_all | solution.py:14
  13.6 0.7 copy-start.8
  23.9 12.2 %all-to-all-start.1 = ((bf16[8,128,128]{1,2,0:T(8,128)(2,1)}), bf16[8,128,128]{1,2,0:T(8,128)(2,1)S(1)}, u32[]{:S(2)}, u32[]{:S(2)}) async-start(bf16[8,128,128]{1,2,0:T(8,128)(2,1)} %copy.37), calls=%async_computation.1 | async-start | bytes 524288 | tf_op jit(solution)/shard_map/all_to_all | solution.py:19
  37.8 1.9 %copy-start.9 = (f32[1024]{0:T(1024)S(1)}, f32[1024]{0:T(1024)}, u32[]{:S(2)}) copy-start(f32[1024]{0:T(1024)} %param.9) | copy-start | bytes 12292
  49.6 6.8 %copy-start.5 = (bf16[512,1024]{1,0:T(8,128)(2,1)S(1)}, bf16[512,1024]{1,0:T(8,128)(2,1)}, u32[]{:S(2)}) copy-start(bf16[512,1024]{1,0:T(8,128)(2,1)} %param.7) | copy-start | bytes 3145732
  52.4 13.3 %all-to-all-start.2 = ((bf16[8,128,128]{1,2,0:T(8,128)(2,1)}), bf16[8,128,128]{1,2,0:T(8,128)(2,1)}, u32[]{:S(2)}, u32[]{:S(2)}) async-start(bf16[8,128,128]{1,2,0:T(8,128)(2,1)} %fusion.2), calls=%async_computation.2 | async-start | bytes 524288 | tf_op jit(solution)/shard_map/all_to_all | solution.py:14
  56.4 4.4 %copy-start.7 = (bf16[512,8,128]{0,2,1:T(8,128)(2,1)S(1)}, bf16[512,8,128]{0,2,1:T(8,128)(2,1)}, u32[]{:S(2)}) copy-start(bf16[512,8,128]{0,2,1:T(8,128)(2,1)} %copy.35) | copy-start | bytes 3145732
  58.9 2.0 %copy-start.1 = (bf16[8,512,512]{2,1,0:T(8,128)(2,1)}, bf16[8,512,512]{2,1,0:T(8,128)(2,1)S(1)}, u32[]{:S(2)}) copy-start(bf16[8,512,512]{2,1,0:T(8,128)(2,1)S(1)} %select_convert_fusion) | copy-start | bytes 12582916
  68.0 12.7 %all-to-all-start.3 = ((bf16[8,128,128]{2,1,0:T(8,128)(2,1)}), bf16[8,128,128]{2,1,0:T(8,128)(2,1)}, u32[]{:S(2)}, u32[]{:S(2)}) async-start(bf16[8,128,128]{2,1,0:T(8,128)(2,1)} %select_reduce_fusion), calls=%async_computation.3 | async-start | bytes 524288 | tf_op jit(solution)/shard_map/all_to_all | solution.py:19
  75.6 5.1 %copy-start.3 = (bf16[512,1024]{1,0:T(8,128)(2,1)S(1)}, bf16[512,1024]{1,0:T(8,128)(2,1)}, u32[]{:S(2)}) copy-start(bf16[512,1024]{1,0:T(8,128)(2,1)} %param.6) | copy-start | bytes 3145732
  83.9 2.4 %copy-start.6 = (bf16[512,1024]{1,0:T(8,128)(2,1)S(1)}, bf16[512,1024]{1,0:T(8,128)(2,1)}, u32[]{:S(2)}) copy-start(bf16[512,1024]{1,0:T(8,128)(2,1)} %param.7) | copy-start | bytes 3145732

commit v2 on v1

--- a/solution.py
+++ b/solution.py
@@ -7,16 +7,37 @@
 D = 4096
 
 
+def exchange(pieces, axis):
+    count = lax.axis_size(axis)
+    if count > 8:
+        return lax.all_to_all(pieces, axis, 0, 0)
+    got = [pieces[0]]
+    for shift in range(1, count):
+        pairs = [(place, (place + shift) % count) for place in range(count)]
+        got.append(lax.ppermute(pieces[shift], axis, pairs))
+    return jnp.stack(got)
+
+
 def entering(part, axis, reverse):
     count = lax.axis_size(axis)
+    place = lax.axis_index(axis)
     heads, rows, cols = part.shape
     pieces = part.astype(jnp.bfloat16).reshape(count, heads * rows // count, cols)
-    blocks = lax.all_to_all(pieces, axis, 0, 0).astype(jnp.float32)
-    own = lax.broadcasted_iota(jnp.int32, (count, count), 0)
+    lane = lax.broadcasted_iota(jnp.int32, (count, count), 0)
     other = lax.broadcasted_iota(jnp.int32, (count, count), 1)
-    taken = other > own if reverse else other < own
+    direct = count > 8
+    if not direct:
+        pieces = lax.dynamic_slice_in_dim(jnp.concatenate([pieces, pieces]), place, count, 0)
+        lane = (place + lane) % count
+        other = (place - other) % count
+    blocks = exchange(pieces, axis).astype(jnp.float32)
+    taken = other > lane if reverse else other < lane
     states = jnp.sum(jnp.where(taken[:, :, None, None], blocks[None], 0.0), axis=1)
-    return lax.all_to_all(states.astype(jnp.bfloat16), axis, 0, 0).reshape(part.shape)
+    states = exchange(states.astype(jnp.bfloat16), axis)
+    if not direct:
+        states = jnp.flip(states, 0)
+        states = lax.dynamic_slice_in_dim(jnp.concatenate([states, states]), count - 1 - place, count, 0)
+    return states.reshape(part.shape)
 
 
 def shards(queries, keys, values, out_grad, gain):

time: 92.9 us -> 151 us (1.63)
  waiting for transfers between devices: 12.1 us -> 46.4 us
  starting transfers between devices: 19.1 us -> 33.7 us
  local copies, waits for them, and re-layouts: 16.2 us -> 26.5 us
    ppermute x0 -> x28, waiting for transfers between devices: none -> 46.4 us  [exchange(): got.append(lax.ppermute(pieces[shift], axis, pairs))]
    ppermute x0 -> x28, starting transfers between devices: none -> 33.7 us  [exchange(): got.append(lax.ppermute(pieces[shift], axis, pairs))]
    all_to_all x4 -> x0, starting transfers between devices: 19.1 us -> none  [the longest x2 11.3 us: entering(): blocks = lax.all_to_all(pieces, axis, 0, 0).astype(jnp.float32)]
    all_to_all x4 -> x0, waiting for transfers between devices: 12.1 us -> none  [the longest x2 6.8 us: entering(): blocks = lax.all_to_all(pieces, axis, 0, 0).astype(jnp.float32)]
    unnamed x24 -> x56, local copies, waits for them, and re-layouts: 9.31 us -> 16.8 us
    rev x0 -> x2, local copies, waits for them, and re-layouts: none -> 1.93 us  [entering(): states = jnp.flip(states, 0)]
    dot_general x1, matrix products: 1.39 us -> 3.16 us  [shards(): jnp.einsum('she,hde->shd', value_heads, grad_low, preferred_element_type=...]
    dot_general x1, matrix products: 3.16 us -> 1.53 us  [shards(): jnp.einsum('shd,hde->she', key_heads, grad_low, preferred_element_type=jn...]
  transfers between devices with their start and end apart: 4 -> 28, of which waited for: 4 -> 10; matrix products, arithmetic and copies ran while one was open for 22% -> 15% of each run, Pallas kernels for 0% -> 0%
where the time goes in v2:
time: 151 us; the launch traced here: 150 us
  waiting for transfers between devices  46.4 us (31%)
  starting transfers between devices  33.7 us (22%)
  matrix products  30.8 us (20%)
  local copies, waits for them, and re-layouts  26.5 us (18%)
  other arithmetic  5.71 us (4%)
  blocking collectives  5.66 us (4%)
    ppermute x28, waiting for transfers between devices, exchange(): got.append(lax.ppermute(pieces[shift], axis, pairs))  46.4 us
    ppermute x28, starting transfers between devices, exchange(): got.append(lax.ppermute(pieces[shift], axis, pairs))  33.7 us
    unnamed x56, local copies, waits for them, and re-layouts  16.8 us
    psum x1, blocking collectives, shards(): lax.psum((jnp.sum(attended * attended, axis=1), jnp.sum(scaled * attended...  5.66 us
    dot_general x1, matrix products, shards(): jnp.einsum('hts,the->she', weights, dout_heads, preferred_element_type=jn...  4.28 us
    dot_general x1, matrix products, shards(): jnp.einsum('hts,thd->shd', dscore, query_heads, preferred_element_type=jn...  4.02 us
    dot_general x1, matrix products, shards(): jnp.einsum('hts,she->the', weights, value_heads, preferred_element_type=j...  3.99 us
    dot_general x1, matrix products, shards(): jnp.einsum('thd,shd->hts', query_heads, key_heads, preferred_element_type...  3.29 us
  transfers between devices with their start and end apart: 28, of which 10 were waited for; matrix products, arithmetic and copies ran while one was open for 15% of the time, Pallas kernels for 0%

profile of v2, /device:TPU:0, one launch (start us, length us, event | category | flops | bytes accessed | tf_op | source)
XLA Modules:
  0.0 149.9 jit_solution(9401383055774803603)
XLA Ops:
  5.7 6.1 %collective-permute-start.6 = (bf16[128,128]{1,0:T(8,128)(2,1)S(1)}, bf16[128,128]{1,0:T(8,128)(2,1)S(1)}, u32[]{:S(2)}, u32[]{:S(2)}) collective-permute-start(bf16[128,128]{1,0:T(8,128)(2,1)S(1)} %get-tuple-element.35), channel_id=1, source_target_pairs={{0,28},{4,0},{8,4},{12,8},{16,12},{20,16},{24,20},{28,24},{1,29},{... | collective-permute-start | bytes 98312 | tf_op jit(solution)/shard_map/ppermute | solution.py:17
  12.2 3.0 %collective-permute-start.3 = (bf16[128,128]{1,0:T(8,128)(2,1)S(1)}, bf16[128,128]{1,0:T(8,128)(2,1)S(1)}, u32[]{:S(2)}, u32[]{:S(2)}) collective-permute-start(bf16[128,128]{1,0:T(8,128)(2,1)S(1)} %get-tuple-element.38), channel_id=1, source_target_pairs={{0,16},{4,20},{8,24},{12,28},{16,0},{20,4},{24,8},{28,12},{1,17},{... | collective-permute-start | bytes 98312 | tf_op jit(solution)/shard_map/ppermute | solution.py:17
  16.9 3.3 %select_convert_fusion.1 = bf16[8,512,512]{2,1,0:T(8,128)(2,1)} fusion(pred[512,512]{1,0:T(8,128)(4,1)S(1)} %iota_compare_fusion, bf16[512,1024]{1,0:T(8,128)(2,1)S(1)} %copy-done.6, bf16[512,1024]{1,0:T(8,128)(2,1)S(1)} %copy-done), kind=kOutput, calls=%fused_computation.1 | convolution fusion | flops 541065216 | bytes 6553600 | tf_op jit(solution)/shard_map/thd,shd->hts/dot_general | solution.py:55
  21.8 5.8 %collective-permute-done.1 = bf16[128,128]{1,0:T(8,128)(2,1)S(1)} collective-permute-done((bf16[128,128]{1,0:T(8,128)(2,1)S(1)}, bf16[128,128]{1,0:T(8,128)(2,1)S(1)}, u32[]{:S(2)}, u32[]{:S(2)}) %collective-permute-start.1) | collective-permute-done | bytes 32800 | tf_op jit(solution)/shard_map/ppermute | solution.py:17
  27.7 5.7 %collective-permute-done.2 = bf16[128,128]{1,0:T(8,128)(2,1)S(1)} collective-permute-done((bf16[128,128]{1,0:T(8,128)(2,1)S(1)}, bf16[128,128]{1,0:T(8,128)(2,1)S(1)}, u32[]{:S(2)}, u32[]{:S(2)}) %collective-permute-start.2) | collective-permute-done | bytes 32800 | tf_op jit(solution)/shard_map/ppermute | solution.py:17
  34.9 4.0 %fusion.3 = f32[8,512,128]{1,2,0:T(8,128)S(1)} fusion(bf16[8,512,512]{2,1,0:T(8,128)(2,1)} %select_convert_fusion.1, bf16[512,1024]{1,0:T(8,128)(2,1)} %param.7), kind=kOutput, calls=%fused_computation.17 | convolution fusion | flops 536870912 | bytes 7340032 | tf_op jit(solution)/shard_map/hts,she->the/dot_general | solution.py:57
  38.9 4.8 %collective-permute-start.13 = (bf16[128,128]{0,1:T(8,128)(2,1)S(1)}, bf16[128,128]{0,1:T(8,128)(2,1)S(1)}, u32[]{:S(2)}, u32[]{:S(2)}) collective-permute-start(bf16[128,128]{0,1:T(8,128)(2,1)S(1)} %get-tuple-element.27), channel_id=1, source_target_pairs={{0,28},{4,0},{8,4},{12,8},{16,12},{20,16},{24,20},{28,24},{1,29},{... | collective-permute-start | bytes 98312 | tf_op jit(solution)/shard_map/ppermute | solution.py:17
  43.7 3.0 %collective-permute-start.10 = (bf16[128,128]{0,1:T(8,128)(2,1)S(1)}, bf16[128,128]{0,1:T(8,128)(2,1)S(1)}, u32[]{:S(2)}, u32[]{:S(2)}) collective-permute-start(bf16[128,128]{0,1:T(8,128)(2,1)S(1)} %get-tuple-element.30), channel_id=1, source_target_pairs={{0,16},{4,20},{8,24},{12,28},{16,0},{20,4},{24,8},{28,12},{1,17},{... | collective-permute-start | bytes 98312 | tf_op jit(solution)/shard_map/ppermute | solution.py:17
  47.3 5.1 %collective-permute-done.8 = bf16[128,128]{0,1:T(8,128)(2,1)S(1)} collective-permute-done((bf16[128,128]{0,1:T(8,128)(2,1)S(1)}, bf16[128,128]{0,1:T(8,128)(2,1)S(1)}, u32[]{:S(2)}, u32[]{:S(2)}) %collective-permute-start.8) | collective-permute-done | bytes 32800 | tf_op jit(solution)/shard_map/ppermute | solution.py:17
  53.0 5.1 %collective-permute-done.9 = bf16[128,128]{0,1:T(8,128)(2,1)S(1)} collective-permute-done((bf16[128,128]{0,1:T(8,128)(2,1)S(1)}, bf16[128,128]{0,1:T(8,128)(2,1)S(1)}, u32[]{:S(2)}, u32[]{:S(2)}) %collective-permute-start.9) | collective-permute-done | bytes 32800 | tf_op jit(solution)/shard_map/ppermute | solution.py:17
  67.6 5.7 %all-reduce = (f32[512]{0:T(512)S(1)}, f32[512]{0:T(512)S(1)}) all-reduce(f32[512]{0:T(512)S(1)} %multiply_reduce_fusion, f32[512]{0:T(512)S(1)} %get-tuple-element.47), channel_id=1, replica_groups=mesh['seq'=8,'head'=4] {'head'}, use_global_device_ids=true, to_apply=%region_4.5 | all-reduce | flops 1024 | bytes 8192 | tf_op jit(solution)/shard_map/psum | solution.py:63
  73.3 2.6 %subtract_convert_fusion = bf16[512,1024]{1,0:T(8,128)(2,1)} fusion(f32[512,1024]{1,0:T(8,128)S(1)} %copy.40, bf16[512,1024]{1,0:T(8,128)(2,1)} %param.8, f32[512]{0:T(512)S(1)} %get-tuple-element.46, f32[512]{0:T(512)S(1)} %get-tuple-element.45, f32[1024]{0:T(1024)S(1)} %copy-done.13), kind=kLoop, calls=%fused_computation.10 | loop fusion | flops 3145728 | bytes 4202496 | tf_op jit(solution)/shard_map/convert_element_type | solution.py:68
  77.4 4.3 %fusion.38 = f32[8,128,512]{2,1,0:T(8,128)} fusion(bf16[512,8,128]{0,2,1:T(8,128)(2,1)S(1)} %bitcast.207, bf16[8,512,512]{2,1,0:T(8,128)(2,1)} %select_convert_fusion.1), kind=kOutput, calls=%fused_computation.129 | convolution fusion | flops 536870912 | bytes 7340032 | tf_op jit(solution)/shard_map/hts,the->she/dot_general | solution.py:83
  86.6 3.8 %collective-permute-start.17 = (bf16[128,128]{0,1:T(8,128)(2,1)S(1)}, bf16[128,128]{0,1:T(8,128)(2,1)S(1)}, u32[]{:S(2)}, u32[]{:S(2)}) collective-permute-start(bf16[128,128]{0,1:T(8,128)(2,1)S(1)} %get-tuple-element.22), channel_id=1, source_target_pairs={{0,16},{4,20},{8,24},{12,28},{16,0},{20,4},{24,8},{28,12},{1,17},{... | collective-permute-start | bytes 98312 | tf_op jit(solution)/shard_map/ppermute | solution.py:17
  91.9 2.9 %fusion.37 = f32[8,512,128]{1,2,0:T(8,128)} fusion(bf16[8,512,512]{2,1,0:T(8,128)(2,1)S(1)} %select_convert_fusion, bf16[512,8,128]{0,2,1:T(8,128)(2,1)S(1)} %copy-done.8), kind=kOutput, calls=%fused_computation.128 | convolution fusion | flops 536870912 | bytes 7340032 | tf_op jit(solution)/shard_map/hts,shd->thd/dot_general | solution.py:75
  97.0 5.7 %collective-permute-done.15 = bf16[128,128]{0,1:T(8,128)(2,1)S(1)} collective-permute-done((bf16[128,128]{0,1:T(8,128)(2,1)S(1)}, bf16[128,128]{0,1:T(8,128)(2,1)S(1)}, u32[]{:S(2)}, u32[]{:S(2)}) %collective-permute-start.15) | collective-permute-done | bytes 32800 | tf_op jit(solution)/shard_map/ppermute | solution.py:17
  102.8 5.7 %collective-permute-done.16 = bf16[128,128]{0,1:T(8,128)(2,1)S(1)} collective-permute-done((bf16[128,128]{0,1:T(8,128)(2,1)S(1)}, bf16[128,128]{0,1:T(8,128)(2,1)S(1)}, u32[]{:S(2)}, u32[]{:S(2)}) %collective-permute-start.16) | collective-permute-done | bytes 32800 | tf_op jit(solution)/shard_map/ppermute | solution.py:17
  113.5 4.6 %collective-permute-start.27 = (bf16[128,128]{1,0:T(8,128)(2,1)S(1)}, bf16[128,128]{1,0:T(8,128)(2,1)S(1)}, u32[]{:S(2)}, u32[]{:S(2)}) collective-permute-start(bf16[128,128]{1,0:T(8,128)(2,1)S(1)} %get-tuple-element.11), channel_id=1, source_target_pairs={{0,28},{4,0},{8,4},{12,8},{16,12},{20,16},{24,20},{28,24},{1,29},{... | collective-permute-start | bytes 98312 | tf_op jit(solution)/shard_map/ppermute | solution.py:17
  118.1 2.9 %collective-permute-start.24 = (bf16[128,128]{1,0:T(8,128)(2,1)S(1)}, bf16[128,128]{1,0:T(8,128)(2,1)S(1)}, u32[]{:S(2)}, u32[]{:S(2)}) collective-permute-start(bf16[128,128]{1,0:T(8,128)(2,1)S(1)} %get-tuple-element.14), channel_id=1, source_target_pairs={{0,16},{4,20},{8,24},{12,28},{16,0},{20,4},{24,8},{28,12},{1,17},{... | collective-permute-start | bytes 98312 | tf_op jit(solution)/shard_map/ppermute | solution.py:17
  122.4 4.3 %collective-permute-done.22 = bf16[128,128]{1,0:T(8,128)(2,1)S(1)} collective-permute-done((bf16[128,128]{1,0:T(8,128)(2,1)S(1)}, bf16[128,128]{1,0:T(8,128)(2,1)S(1)}, u32[]{:S(2)}, u32[]{:S(2)}) %collective-permute-start.22) | collective-permute-done | bytes 32800 | tf_op jit(solution)/shard_map/ppermute | solution.py:17
  127.3 5.1 %collective-permute-done.23 = bf16[128,128]{1,0:T(8,128)(2,1)S(1)} collective-permute-done((bf16[128,128]{1,0:T(8,128)(2,1)S(1)}, bf16[128,128]{1,0:T(8,128)(2,1)S(1)}, u32[]{:S(2)}, u32[]{:S(2)}) %collective-permute-start.23) | collective-permute-done | bytes 32800 | tf_op jit(solution)/shard_map/ppermute | solution.py:17
  136.5 3.2 %fusion.5 = f32[8,128,512]{2,1,0:T(8,128)} fusion(s32[]{:T(128)S(6)} %select_n.56, bf16[8,128,128]{2,1,0:T(8,128)(2,1)S(1)} %rev.8, bf16[512,1024]{1,0:T(8,128)(2,1)} %param.7), kind=kOutput, calls=%fused_computation.19 | convolution fusion | flops 134348800 | bytes 3407876 | tf_op jit(solution)/shard_map/she,hde->shd/dot_general | solution.py:80
  141.2 2.4 %copy.56 = bf16[512,1024]{1,0:T(8,128)(2,1)} copy(bf16[512,1024]{0,1:T(8,128)(2,1)} %bitcast.214) | data formatting | bytes 2097152
  143.6 4.0 %fusion = bf16[512,8,128]{0,2,1:T(8,128)(2,1)} fusion(f32[8,128,512]{2,1,0:T(8,128)S(1)} %copy-done.3, bf16[8,512,512]{2,1,0:T(8,128)(2,1)} %copy-done.1, bf16[512,1024]{1,0:T(8,128)(2,1)S(1)} %copy-done), kind=kOutput, calls=%fused_computation.5 | convolution fusion | flops 537919488 | bytes 8388608 | tf_op jit(solution)/shard_map/hts,thd->shd/dot_general | solution.py:79
  (129 shorter events, 45.9 us)
Async XLA Ops:
  5.7 27.8 %collective-permute-start.6 = (bf16[128,128]{1,0:T(8,128)(2,1)S(1)}, bf16[128,128]{1,0:T(8,128)(2,1)S(1)}, u32[]{:S(2)}, u32[]{:S(2)}) collective-permute-start(bf16[128,128]{1,0:T(8,128)(2,1)S(1)} %get-tuple-element.35), channel_id=1, source_target_pairs={{0,28},{4,0},{8,4},{12,8},{16,12},{20,16},{24,20},{28,24},{1,29},{... | collective-permute-start | bytes 98312 | tf_op jit(solution)/shard_map/ppermute | solution.py:17
  11.7 21.7 %collective-permute-start.5 = (bf16[128,128]{1,0:T(8,128)(2,1)S(1)}, bf16[128,128]{1,0:T(8,128)(2,1)S(1)}, u32[]{:S(2)}, u32[]{:S(2)}) collective-permute-start(bf16[128,128]{1,0:T(8,128)(2,1)S(1)} %get-tuple-element.36), channel_id=1, source_target_pairs={{0,24},{4,28},{8,0},{12,4},{16,8},{20,12},{24,16},{28,20},{1,25},{... | collective-permute-start | bytes 98312 | tf_op jit(solution)/shard_map/ppermute | solution.py:17
  12.2 21.2 %collective-permute-start.4 = (bf16[128,128]{1,0:T(8,128)(2,1)S(1)}, bf16[128,128]{1,0:T(8,128)(2,1)S(1)}, u32[]{:S(2)}, u32[]{:S(2)}) collective-permute-start(bf16[128,128]{1,0:T(8,128)(2,1)S(1)} %get-tuple-element.37), channel_id=1, source_target_pairs={{0,20},{4,24},{8,28},{12,0},{16,4},{20,8},{24,12},{28,16},{1,21},{... | collective-permute-start | bytes 98312 | tf_op jit(solution)/shard_map/ppermute | solution.py:17
  12.2 21.2 %collective-permute-start.3 = (bf16[128,128]{1,0:T(8,128)(2,1)S(1)}, bf16[128,128]{1,0:T(8,128)(2,1)S(1)}, u32[]{:S(2)}, u32[]{:S(2)}) collective-permute-start(bf16[128,128]{1,0:T(8,128)(2,1)S(1)} %get-tuple-element.38), channel_id=1, source_target_pairs={{0,16},{4,20},{8,24},{12,28},{16,0},{20,4},{24,8},{28,12},{1,17},{... | collective-permute-start | bytes 98312 | tf_op jit(solution)/shard_map/ppermute | solution.py:17
  15.2 6.6 %collective-permute-start = (bf16[128,128]{1,0:T(8,128)(2,1)S(1)}, bf16[128,128]{1,0:T(8,128)(2,1)S(1)}, u32[]{:S(2)}, u32[]{:S(2)}) collective-permute-start(bf16[128,128]{1,0:T(8,128)(2,1)S(1)} %get-tuple-element.41), channel_id=1, source_target_pairs={{0,4},{4,8},{8,12},{12,16},{16,20},{20,24},{24,28},{28,0},{1,5},{5... | collective-permute-start | bytes 98312 | tf_op jit(solution)/shard_map/ppermute | solution.py:17
  21.8 5.9 %collective-permute-start.1 = (bf16[128,128]{1,0:T(8,128)(2,1)S(1)}, bf16[128,128]{1,0:T(8,128)(2,1)S(1)}, u32[]{:S(2)}, u32[]{:S(2)}) collective-permute-start(bf16[128,128]{1,0:T(8,128)(2,1)S(1)} %get-tuple-element.40), channel_id=1, source_target_pairs={{0,8},{4,12},{8,16},{12,20},{16,24},{20,28},{24,0},{28,4},{1,9},{5... | collective-permute-start | bytes 98312 | tf_op jit(solution)/shard_map/ppermute | solution.py:17
  34.9 11.8 %collective-permute-start.7 = (bf16[128,128]{0,1:T(8,128)(2,1)S(1)}, bf16[128,128]{0,1:T(8,128)(2,1)S(1)}, u32[]{:S(2)}, u32[]{:S(2)}) collective-permute-start(bf16[128,128]{0,1:T(8,128)(2,1)S(1)} %get-tuple-element.33), channel_id=1, source_target_pairs={{0,4},{4,8},{8,12},{12,16},{16,20},{20,24},{24,28},{28,0},{1,5},{5... | collective-permute-start | bytes 98312 | tf_op jit(solution)/shard_map/ppermute | solution.py:17
  38.9 21.7 %collective-permute-start.13 = (bf16[128,128]{0,1:T(8,128)(2,1)S(1)}, bf16[128,128]{0,1:T(8,128)(2,1)S(1)}, u32[]{:S(2)}, u32[]{:S(2)}) collective-permute-start(bf16[128,128]{0,1:T(8,128)(2,1)S(1)} %get-tuple-element.27), channel_id=1, source_target_pairs={{0,28},{4,0},{8,4},{12,8},{16,12},{20,16},{24,20},{28,24},{1,29},{... | collective-permute-start | bytes 98312 | tf_op jit(solution)/shard_map/ppermute | solution.py:17
  43.6 16.3 %collective-permute-start.12 = (bf16[128,128]{0,1:T(8,128)(2,1)S(1)}, bf16[128,128]{0,1:T(8,128)(2,1)S(1)}, u32[]{:S(2)}, u32[]{:S(2)}) collective-permute-start(bf16[128,128]{0,1:T(8,128)(2,1)S(1)} %get-tuple-element.28), channel_id=1, source_target_pairs={{0,24},{4,28},{8,0},{12,4},{16,8},{20,12},{24,16},{28,20},{1,25},{... | collective-permute-start | bytes 98312 | tf_op jit(solution)/shard_map/ppermute | solution.py:17
  43.6 15.7 %collective-permute-start.11 = (bf16[128,128]{0,1:T(8,128)(2,1)S(1)}, bf16[128,128]{0,1:T(8,128)(2,1)S(1)}, u32[]{:S(2)}, u32[]{:S(2)}) collective-permute-start(bf16[128,128]{0,1:T(8,128)(2,1)S(1)} %get-tuple-element.29), channel_id=1, source_target_pairs={{0,20},{4,24},{8,28},{12,0},{16,4},{20,8},{24,12},{28,16},{1,21},{... | collective-permute-start | bytes 98312 | tf_op jit(solution)/shard_map/ppermute | solution.py:17
  43.7 15.0 %collective-permute-start.10 = (bf16[128,128]{0,1:T(8,128)(2,1)S(1)}, bf16[128,128]{0,1:T(8,128)(2,1)S(1)}, u32[]{:S(2)}, u32[]{:S(2)}) collective-permute-start(bf16[128,128]{0,1:T(8,128)(2,1)S(1)} %get-tuple-element.30), channel_id=1, source_target_pairs={{0,16},{4,20},{8,24},{12,28},{16,0},{20,4},{24,8},{28,12},{1,17},{... | collective-permute-start | bytes 98312 | tf_op jit(solution)/shard_map/ppermute | solution.py:17
  46.6 5.7 %collective-permute-start.8 = (bf16[128,128]{0,1:T(8,128)(2,1)S(1)}, bf16[128,128]{0,1:T(8,128)(2,1)S(1)}, u32[]{:S(2)}, u32[]{:S(2)}) collective-permute-start(bf16[128,128]{0,1:T(8,128)(2,1)S(1)} %get-tuple-element.32), channel_id=1, source_target_pairs={{0,8},{4,12},{8,16},{12,20},{16,24},{20,28},{24,0},{28,4},{1,9},{5... | collective-permute-start | bytes 98312 | tf_op jit(solution)/shard_map/ppermute | solution.py:17
  84.6 24.0 %collective-permute-start.20 = (bf16[128,128]{0,1:T(8,128)(2,1)S(1)}, bf16[128,128]{0,1:T(8,128)(2,1)S(1)}, u32[]{:S(2)}, u32[]{:S(2)}) collective-permute-start(bf16[128,128]{0,1:T(8,128)(2,1)S(1)} %get-tuple-element.19), channel_id=1, source_target_pairs={{0,28},{4,0},{8,4},{12,8},{16,12},{20,16},{24,20},{28,24},{1,29},{... | collective-permute-start | bytes 98312 | tf_op jit(solution)/shard_map/ppermute | solution.py:17
  84.8 23.7 %collective-permute-start.19 = (bf16[128,128]{0,1:T(8,128)(2,1)S(1)}, bf16[128,128]{0,1:T(8,128)(2,1)S(1)}, u32[]{:S(2)}, u32[]{:S(2)}) collective-permute-start(bf16[128,128]{0,1:T(8,128)(2,1)S(1)} %get-tuple-element.20), channel_id=1, source_target_pairs={{0,24},{4,28},{8,0},{12,4},{16,8},{20,12},{24,16},{28,20},{1,25},{... | collective-permute-start | bytes 98312 | tf_op jit(solution)/shard_map/ppermute | solution.py:17
  85.8 22.7 %collective-permute-start.18 = (bf16[128,128]{0,1:T(8,128)(2,1)S(1)}, bf16[128,128]{0,1:T(8,128)(2,1)S(1)}, u32[]{:S(2)}, u32[]{:S(2)}) collective-permute-start(bf16[128,128]{0,1:T(8,128)(2,1)S(1)} %get-tuple-element.21), channel_id=1, source_target_pairs={{0,20},{4,24},{8,28},{12,0},{16,4},{20,8},{24,12},{28,16},{1,21},{... | collective-permute-start | bytes 98312 | tf_op jit(solution)/shard_map/ppermute | solution.py:17
  86.6 21.9 %collective-permute-start.17 = (bf16[128,128]{0,1:T(8,128)(2,1)S(1)}, bf16[128,128]{0,1:T(8,128)(2,1)S(1)}, u32[]{:S(2)}, u32[]{:S(2)}) collective-permute-start(bf16[128,128]{0,1:T(8,128)(2,1)S(1)} %get-tuple-element.22), channel_id=1, source_target_pairs={{0,16},{4,20},{8,24},{12,28},{16,0},{20,4},{24,8},{28,12},{1,17},{... | collective-permute-start | bytes 98312 | tf_op jit(solution)/shard_map/ppermute | solution.py:17
  90.4 6.6 %collective-permute-start.14 = (bf16[128,128]{0,1:T(8,128)(2,1)S(1)}, bf16[128,128]{0,1:T(8,128)(2,1)S(1)}, u32[]{:S(2)}, u32[]{:S(2)}) collective-permute-start(bf16[128,128]{0,1:T(8,128)(2,1)S(1)} %get-tuple-element.25), channel_id=1, source_target_pairs={{0,4},{4,8},{8,12},{12,16},{16,20},{20,24},{24,28},{28,0},{1,5},{5... | collective-permute-start | bytes 98312 | tf_op jit(solution)/shard_map/ppermute | solution.py:17
  102.7 5.7 %collective-permute-start.16 = (bf16[128,128]{0,1:T(8,128)(2,1)S(1)}, bf16[128,128]{0,1:T(8,128)(2,1)S(1)}, u32[]{:S(2)}, u32[]{:S(2)}) collective-permute-start(bf16[128,128]{0,1:T(8,128)(2,1)S(1)} %get-tuple-element.23), channel_id=1, source_target_pairs={{0,12},{4,16},{8,20},{12,24},{16,28},{20,0},{24,4},{28,8},{1,13},{... | collective-permute-start | bytes 98312 | tf_op jit(solution)/shard_map/ppermute | solution.py:17
  109.9 11.1 %collective-permute-start.21 = (bf16[128,128]{1,0:T(8,128)(2,1)}, bf16[128,128]{1,0:T(8,128)(2,1)}, u32[]{:S(2)}, u32[]{:S(2)}) collective-permute-start(bf16[128,128]{1,0:T(8,128)(2,1)} %get-tuple-element.17), channel_id=1, source_target_pairs={{0,4},{4,8},{8,12},{12,16},{16,20},{20,24},{24,28},{28,0},{1,5},{5... | collective-permute-start | bytes 98312 | tf_op jit(solution)/shard_map/ppermute | solution.py:17
  113.5 21.4 %collective-permute-start.27 = (bf16[128,128]{1,0:T(8,128)(2,1)S(1)}, bf16[128,128]{1,0:T(8,128)(2,1)S(1)}, u32[]{:S(2)}, u32[]{:S(2)}) collective-permute-start(bf16[128,128]{1,0:T(8,128)(2,1)S(1)} %get-tuple-element.11), channel_id=1, source_target_pairs={{0,28},{4,0},{8,4},{12,8},{16,12},{20,16},{24,20},{28,24},{1,29},{... | collective-permute-start | bytes 98312 | tf_op jit(solution)/shard_map/ppermute | solution.py:17
  118.0 16.2 %collective-permute-start.26 = (bf16[128,128]{1,0:T(8,128)(2,1)S(1)}, bf16[128,128]{1,0:T(8,128)(2,1)S(1)}, u32[]{:S(2)}, u32[]{:S(2)}) collective-permute-start(bf16[128,128]{1,0:T(8,128)(2,1)S(1)} %get-tuple-element.12), channel_id=1, source_target_pairs={{0,24},{4,28},{8,0},{12,4},{16,8},{20,12},{24,16},{28,20},{1,25},{... | collective-permute-start | bytes 98312 | tf_op jit(solution)/shard_map/ppermute | solution.py:17
  118.1 15.6 %collective-permute-start.25 = (bf16[128,128]{1,0:T(8,128)(2,1)S(1)}, bf16[128,128]{1,0:T(8,128)(2,1)S(1)}, u32[]{:S(2)}, u32[]{:S(2)}) collective-permute-start(bf16[128,128]{1,0:T(8,128)(2,1)S(1)} %get-tuple-element.13), channel_id=1, source_target_pairs={{0,20},{4,24},{8,28},{12,0},{16,4},{20,8},{24,12},{28,16},{1,21},{... | collective-permute-start | bytes 98312 | tf_op jit(solution)/shard_map/ppermute | solution.py:17
  118.1 15.0 %collective-permute-start.24 = (bf16[128,128]{1,0:T(8,128)(2,1)S(1)}, bf16[128,128]{1,0:T(8,128)(2,1)S(1)}, u32[]{:S(2)}, u32[]{:S(2)}) collective-permute-start(bf16[128,128]{1,0:T(8,128)(2,1)S(1)} %get-tuple-element.14), channel_id=1, source_target_pairs={{0,16},{4,20},{8,24},{12,28},{16,0},{20,4},{24,8},{28,12},{1,17},{... | collective-permute-start | bytes 98312 | tf_op jit(solution)/shard_map/ppermute | solution.py:17
  121.0 5.7 %collective-permute-start.22 = (bf16[128,128]{1,0:T(8,128)(2,1)S(1)}, bf16[128,128]{1,0:T(8,128)(2,1)S(1)}, u32[]{:S(2)}, u32[]{:S(2)}) collective-permute-start(bf16[128,128]{1,0:T(8,128)(2,1)S(1)} %copy-done.12), channel_id=1, source_target_pairs={{0,8},{4,12},{8,16},{12,20},{16,24},{20,28},{24,0},{28,4},{1,9},{5... | collective-permute-start | bytes 98312 | tf_op jit(solution)/shard_map/ppermute | solution.py:17
  (18 other events, 117.9 us)

commit v3 on v1

v3 whole, which is shorter than its diff:
```python
import functools

import jax
import jax.numpy as jnp
from jax import lax
from jax.experimental import pallas as pl
from jax.experimental.pallas import tpu as pltpu
from jax.sharding import PartitionSpec as P

HEAD_DIM = 128
BLOCK = 256
EPSILON = 1e-06
MIB = 1 << 20


def mm(a, b):
    return lax.dot_general(a, b, (((1,), (0,)), ((), ())), preferred_element_type=jnp.float32)


def mm_nt(a, b):
    return lax.dot_general(a, b, (((1,), (1,)), ((), ())), preferred_element_type=jnp.float32)


def mm_tn(a, b):
    return lax.dot_general(a, b, (((0,), (0,)), ((), ())), preferred_element_type=jnp.float32)


def head_columns(ref):
    return [slice(at, at + HEAD_DIM) for at in range(0, ref.shape[1], HEAD_DIM)]


def masked(scores, row_start, col_start, rows_first):
    rows = row_start + lax.broadcasted_iota(jnp.int32, scores.shape, 0)
    cols = col_start + lax.broadcasted_iota(jnp.int32, scores.shape, 1)
    keep = rows >= cols if rows_first else cols >= rows
    return jnp.where(keep, scores, 0.0).astype(jnp.bfloat16)


def states_body(key_ref, value_ref, state_ref):
    for cols in head_columns(key_ref):
        state_ref[cols, :] = mm_tn(key_ref[:, cols], value_ref[:, cols]).astype(jnp.bfloat16)


def local_body(query_ref, key_ref, value_ref, local_ref):
    rows = query_ref.shape[0]
    for cols in head_columns(query_ref):
        for start in range(0, rows, BLOCK):
            end = start + BLOCK
            scores = mm_nt(query_ref[start:end, cols], key_ref[:end, cols])
            weights = masked(scores, start, 0, True)
            local_ref[start:end, cols] = mm(weights, value_ref[:end, cols])


def scan_body(reverse, block_ref, state_ref):
    count = block_ref.shape[0]
    total = jnp.zeros(block_ref.shape[1:], jnp.float32)
    order = range(count - 1, -1, -1) if reverse else range(count)
    for place in order:
        state_ref[place] = total.astype(jnp.bfloat16)
        total = total + block_ref[place].astype(jnp.float32)


def sums_body(query_ref, grad_ref, gain_ref, local_ref, state_ref, sums_ref, square, cross):
    step = pl.program_id(0)

    @pl.when(step == 0)
    def _():
        square[...] = jnp.zeros_like(square)
        cross[...] = jnp.zeros_like(cross)

    for cols in head_columns(query_ref):
        attended = local_ref[:, cols] + mm(query_ref[:, cols], state_ref[cols, :])
        scaled = gain_ref[:, cols] * grad_ref[:, cols].astype(jnp.float32)
        square[...] += attended * attended
        cross[...] += scaled * attended

    @pl.when(step == pl.num_programs(0) - 1)
    def _():
        sums_ref[0:1, :] = jnp.sum(square[...].T, axis=0, keepdims=True)
        sums_ref[1:2, :] = jnp.sum(cross[...].T, axis=0, keepdims=True)


def dout_body(width, query_ref, grad_ref, gain_ref, local_ref, state_ref, sums_ref, dout_ref, own_ref, factors):
    @pl.when(pl.program_id(0) == 0)
    def _():
        inverse = 1.0 / jnp.sqrt(sums_ref[0:1, :] / width + EPSILON)
        drop = sums_ref[1:2, :] * (inverse * inverse * inverse) / width
        both = jnp.concatenate([inverse, drop] + [jnp.zeros_like(drop)] * 6, axis=0)
        factors[...] = both.T

    inverse = factors[:, 0:1]
    drop = factors[:, 1:2]
    for cols in head_columns(query_ref):
        query = query_ref[:, cols]
        attended = local_ref[:, cols] + mm(query, state_ref[cols, :])
        scaled = gain_ref[:, cols] * grad_ref[:, cols].astype(jnp.float32)
        dout = (scaled * inverse - attended * drop).astype(jnp.bfloat16)
        dout_ref[:, cols] = dout
        own_ref[cols, :] = mm_tn(query, dout).astype(jnp.bfloat16)


def query_body(key_ref, value_ref, dout_ref, state_ref, out_ref):
    rows = dout_ref.shape[0]
    for cols in head_columns(dout_ref):
        for start in range(0, rows, BLOCK):
            end = start + BLOCK
            dout = dout_ref[start:end, cols]
            dscore = masked(mm_nt(dout, value_ref[:end, cols]), start, 0, True)
            grad = mm(dscore, key_ref[:end, cols]) + mm_nt(dout, state_ref[cols, :])
            out_ref[start:end, cols] = grad.astype(jnp.bfloat16)


def inner_body(query_ref, key_ref, value_ref, dout_ref, key_out, value_out):
    rows = dout_ref.shape[0]
    for cols in head_columns(dout_ref):
        for start in range(0, rows, BLOCK):
            end = start + BLOCK
            query = query_ref[start:, cols]
            dout = dout_ref[start:, cols]
            dscore = masked(mm_nt(value_ref[start:end, cols], dout), 0, 0, False)
            key_out[start:end, cols] = mm(dscore, query)
            weights = masked(mm_nt(key_ref[start:end, cols], query), 0, 0, False)
            value_out[start:end, cols] = mm(weights, dout)


def final_body(key_ref, value_ref, key_part, value_part, state_ref, key_out, value_out):
    for cols in head_columns(key_ref):
        state = state_ref[cols, :]
        key_grad = key_part[:, cols] + mm_nt(value_ref[:, cols], state)
        key_out[:, cols] = key_grad.astype(jnp.bfloat16)
        value_grad = value_part[:, cols] + mm(key_ref[:, cols], state)
        value_out[:, cols] = value_grad.astype(jnp.bfloat16)


def by_heads(body, args, kinds, outs, heads_step, flops, scratch=()):
    rows, width = args[0].shape
    step_cols = heads_step * HEAD_DIM
    specs = {
        "tokens": pl.BlockSpec((rows, step_cols), lambda step: (0, step)),
        "gain": pl.BlockSpec((1, step_cols), lambda step: (0, step)),
        "state": pl.BlockSpec((step_cols, HEAD_DIM), lambda step: (step, 0)),
        "sums": pl.BlockSpec((2, rows), lambda step: (0, 0)),
    }
    shapes = {"tokens": (rows, width), "state": (width, HEAD_DIM), "sums": (2, rows)}
    out_shape = [jax.ShapeDtypeStruct(shapes[kind], dtype) for kind, dtype in outs]
    moved = sum(a.size * a.dtype.itemsize for a in args)
    moved += sum(o.size * o.dtype.itemsize for o in out_shape)
    result = pl.pallas_call(
        body,
        grid=(width // step_cols,),
        in_specs=[specs[kind] for kind in kinds],
        out_specs=[specs[kind] for kind, _ in outs],
        out_shape=out_shape,
        scratch_shapes=scratch,
        compiler_params=pltpu.CompilerParams(vmem_limit_bytes=24 * MIB),
        cost_estimate=pl.CostEstimate(flops=flops, bytes_accessed=moved, transcendentals=0),
    )(*args)
    return result


def scan_blocks(blocks, reverse):
    return pl.pallas_call(
        functools.partial(scan_body, reverse),
        out_shape=jax.ShapeDtypeStruct(blocks.shape, blocks.dtype),
        compiler_params=pltpu.CompilerParams(vmem_limit_bytes=8 * MIB),
        cost_estimate=pl.CostEstimate(
            flops=blocks.size, bytes_accessed=4 * blocks.size, transcendentals=0
        ),
    )(blocks)


def entering(state, axis, reverse):
    count = lax.axis_size(axis)
    rows, cols = state.shape
    pieces = state.reshape(count, rows // count, cols)
    blocks = lax.all_to_all(pieces, axis, 0, 0)
    states = scan_blocks(blocks, reverse)
    return lax.all_to_all(states, axis, 0, 0).reshape(rows, cols)


def shards(queries, keys, values, out_grad, gain):
    rows, width = queries.shape
    total_width = width * lax.axis_size("head")
    bf16, f32 = jnp.bfloat16, jnp.float32
    small = 2 * rows * width * HEAD_DIM
    large = 2 * rows * rows * width * 3 // 4
    gain_row = gain.reshape(1, width)

    (own_kv,) = by_heads(states_body, (keys, values), ("tokens",) * 2, [("state", bf16)], 2, small)
    kv_low = entering(own_kv, "seq", False)
    (local,) = by_heads(
        local_body, (queries, keys, values), ("tokens",) * 3, [("tokens", f32)], 2, 2 * large
    )
    shared = (queries, out_grad, gain_row, local, kv_low)
    shared_kinds = ("tokens", "tokens", "gain", "tokens", "state")
    (sums,) = by_heads(
        sums_body,
        shared,
        shared_kinds,
        [("sums", f32)],
        2,
        small,
        [pltpu.VMEM((rows, HEAD_DIM), f32)] * 2,
    )
    sums = lax.psum(sums, "head")
    dout, own_grad = by_heads(
        functools.partial(dout_body, total_width),
        shared + (sums,),
        shared_kinds + ("sums",),
        [("tokens", bf16), ("state", bf16)],
        2,
        2 * small,
        [pltpu.VMEM((rows, 8), f32)],
    )
    grad_low = entering(own_grad, "seq", True)
    (query_grad,) = by_heads(
        query_body,
        (keys, values, dout, kv_low),
        ("tokens",) * 3 + ("state",),
        [("tokens", bf16)],
        2,
        2 * large + small,
    )
    key_part, value_part = by_heads(
        inner_body,
        (queries, keys, values, dout),
        ("tokens",) * 4,
        [("tokens", f32)] * 2,
        2,
        4 * large,
    )
    key_grad, value_grad = by_heads(
        final_body,
        (keys, values, key_part, value_part, grad_low),
        ("tokens",) * 4 + ("state",),
        [("tokens", bf16)] * 2,
        2,
        2 * small,
    )
    return query_grad, key_grad, value_grad


def solution(mesh):
    return jax.shard_map(
        shards,
        mesh=mesh,
        in_specs=(
            P("seq", "head"),
            P("seq", "head"),
            P("seq", "head"),
            P("seq", "head"),
            P("head"),
        ),
        out_specs=(P("seq", "head"), P("seq", "head"), P("seq", "head")),
        check_vma=False,
    )
```

time: 92.9 us -> 90.1 us (0.970)
  matrix products: 32 us -> 0 us
  blocking collectives: 5.66 us -> 34.6 us
  Pallas kernels: 0 us -> 26.4 us
  starting transfers between devices: 19.1 us -> 7.63 us
  waiting for transfers between devices: 12.1 us -> 1.93 us
  other arithmetic: 6.1 us -> 0 us
  local copies, waits for them, and re-layouts: 16.2 us -> 17.8 us
    dot_general x12 -> x0, matrix products: 32 us -> none  [the longest x1 4.35 us: shards(): jnp.einsum('hts,the->she', weights, dout_heads, preferred_element_type=jn...]
    all_to_all x0 -> x2, blocking collectives: none -> 29 us  [entering(): blocks = lax.all_to_all(pieces, axis, 0, 0)]
    pallas_call x0 -> x9, Pallas kernels: none -> 26.4 us  [the longest x7 24.9 us: by_heads(): pl.pallas_call(body, grid=(width // step_cols,), in_specs=[specs[kind] fo...]
    all_to_all x4 -> x2, starting transfers between devices: 19.1 us -> 7.63 us  [entering(): return lax.all_to_all(states, axis, 0, 0).reshape(rows, cols)]
    all_to_all x4 -> x2, waiting for transfers between devices: 12.1 us -> 1.93 us  [entering(): return lax.all_to_all(states, axis, 0, 0).reshape(rows, cols)]
    unnamed x24 -> x38, local copies, waits for them, and re-layouts: 9.31 us -> 17.8 us
    reshape x3 -> x0, local copies, waits for them, and re-layouts: 4.97 us -> none  [the longest x1 1.93 us: shards(): attended = attended.reshape(rows_local, width)]
    reduce_sum x3 -> x0, other arithmetic: 3.34 us -> none  [the longest x2 1.76 us: entering(): jnp.sum(jnp.where(taken[:, :, None, None], blocks[None], 0.0), axis=1)]
  transfers between devices with their start and end apart: 4 -> 2, of which waited for: 4 -> 1; matrix products, arithmetic and copies ran while one was open for 22% -> 0% of each run, Pallas kernels for 0% -> 17%
where the time goes in v3:
time: 90.1 us; the launch traced here: 89.1 us
  blocking collectives  34.6 us (38%)
  Pallas kernels  26.4 us (29%)
  local copies, waits for them, and re-layouts  17.8 us (20%)
  starting transfers between devices  7.63 us (8%)
  waiting for transfers between devices  1.93 us (2%)
    all_to_all x2, blocking collectives, entering(): blocks = lax.all_to_all(pieces, axis, 0, 0)  29 us
    pallas_call x7, Pallas kernels, by_heads(): pl.pallas_call(body, grid=(width // step_cols,), in_specs=[specs[kind] fo...  24.9 us
    unnamed x38, local copies, waits for them, and re-layouts  17.8 us
    all_to_all x2, starting transfers between devices, entering(): return lax.all_to_all(states, axis, 0, 0).reshape(rows, cols)  7.63 us
    psum x1, blocking collectives, shards(): sums = lax.psum(sums, 'head')  5.67 us
    all_to_all x2, waiting for transfers between devices, entering(): return lax.all_to_all(states, axis, 0, 0).reshape(rows, cols)  1.93 us
  transfers between devices with their start and end apart: 2, of which 1 were waited for; matrix products, arithmetic and copies ran while one was open for 0% of the time, Pallas kernels for 17%

profile of v3, /device:TPU:0, one launch (start us, length us, event | category | flops | bytes accessed | tf_op | source)
XLA Modules:
  0.0 89.1 jit_solution(15110726191043978637)
XLA Ops:
  1.9 1.2 %copy-done.2 = bf16[512,1024]{1,0:T(8,128)(2,1)S(1)} copy-done((bf16[512,1024]{1,0:T(8,128)(2,1)S(1)}, bf16[512,1024]{1,0:T(8,128)(2,1)}, u32[]{:S(2)}) %copy-start.2) | copy-done | bytes 1048600
  3.1 1.4 %shard_map.77 = bf16[1024,128]{1,0:T(8,128)(2,1)S(1)} custom-call(bf16[512,1024]{1,0:T(8,128)(2,1)S(1)} %copy-done, bf16[512,1024]{1,0:T(8,128)(2,1)S(1)} %copy-done.2), custom_call_target="tpu_custom_call" | custom-call | flops 134217728 | bytes 2359296 | tf_op jit(solution)/shard_map/pallas_call | solution.py:148
  4.5 16.0 %all_to_all.20.block_ref = bf16[8,128,128]{2,1,0:T(8,128)(2,1)S(1)} all-to-all(bf16[8,128,128]{2,1,0:T(8,128)(2,1)S(1)} %bitcast.8), channel_id=1, replica_groups=mesh['seq'=8,'head'=4] {'seq'}, dimensions={0} | all-to-all | bytes 524288 | tf_op jit(solution)/shard_map/all_to_all | solution.py:176
  21.3 3.6 %all-to-all-start.1 = ((bf16[8,128,128]{2,1,0:T(8,128)(2,1)}), bf16[8,128,128]{2,1,0:T(8,128)(2,1)S(1)}, u32[]{:S(2)}, u32[]{:S(2)}) async-start(bf16[8,128,128]{2,1,0:T(8,128)(2,1)} %shard_map.78), calls=%async_computation.1 | async-start | bytes 524288 | tf_op jit(solution)/shard_map/all_to_all | solution.py:178
  24.9 1.2 %copy-done.3 = bf16[512,1024]{1,0:T(8,128)(2,1)S(1)} copy-done((bf16[512,1024]{1,0:T(8,128)(2,1)S(1)}, bf16[512,1024]{1,0:T(8,128)(2,1)}, u32[]{:S(2)}) %copy-start.3) | copy-done | bytes 1048600
  26.1 1.2 %copy-done.5 = bf16[512,1024]{1,0:T(8,128)(2,1)S(1)} copy-done((bf16[512,1024]{1,0:T(8,128)(2,1)S(1)}, bf16[512,1024]{1,0:T(8,128)(2,1)}, u32[]{:S(2)}) %copy-start.5) | copy-done | bytes 1048600
  27.3 4.2 %shard_map.76.local_ref = f32[512,1024]{1,0:T(8,128)S(1)} custom-call(bf16[512,1024]{1,0:T(8,128)(2,1)S(1)} %copy-done.5, bf16[512,1024]{1,0:T(8,128)(2,1)S(1)} %copy-done.1, bf16[512,1024]{1,0:T(8,128)(2,1)S(1)} %copy-done.3), custom_call_target="tpu_custom_call" | custom-call | flops 805306368 | bytes 5242880 | tf_op jit(solution)/shard_map/pallas_call | solution.py:148
  31.5 1.9 %all-to-all-done.1 = bf16[8,128,128]{2,1,0:T(8,128)(2,1)S(1)} async-done(((bf16[8,128,128]{2,1,0:T(8,128)(2,1)}), bf16[8,128,128]{2,1,0:T(8,128)(2,1)S(1)}, u32[]{:S(2)}, u32[]{:S(2)}) %all-to-all-start.1) | async-done | bytes 262176 | tf_op jit(solution)/shard_map/all_to_all | solution.py:178
  33.4 1.2 %copy-done.6 = bf16[512,1024]{1,0:T(8,128)(2,1)S(1)} copy-done((bf16[512,1024]{1,0:T(8,128)(2,1)S(1)}, bf16[512,1024]{1,0:T(8,128)(2,1)}, u32[]{:S(2)}) %copy-start.6) | copy-done | bytes 1048600
  34.7 1.2 %copy-done.9 = bf16[512,1024]{1,0:T(8,128)(2,1)S(1)} copy-done((bf16[512,1024]{1,0:T(8,128)(2,1)S(1)}, bf16[512,1024]{1,0:T(8,128)(2,1)}, u32[]{:S(2)}) %copy-start.9) | copy-done | bytes 1048600
  35.9 1.7 %shard_map.79 = f32[2,512]{1,0:T(2,128)S(1)} custom-call(bf16[512,1024]{1,0:T(8,128)(2,1)S(1)} %copy-done.6, bf16[512,1024]{1,0:T(8,128)(2,1)S(1)} %copy-done.9, f32[1,1024]{1,0:T(1,128)S(1)} %bitcast.10, f32[512,1024]{1,0:T(8,128)S(1)} %shard_map.76.local_ref, bf16[1024,128]{1,0:T(8,128)(2,1)S(1)} %bitcast.5), custom_call_target="tpu_custom_call" | custom-call | flops 134217728 | bytes 4464640 | tf_op jit(solution)/shard_map/pallas_call | solution.py:148
  37.6 5.7 %psum.7.sums_ref = f32[2,512]{1,0:T(2,128)S(1)} all-reduce(f32[2,512]{1,0:T(2,128)S(1)} %shard_map.79), channel_id=1, replica_groups=mesh['seq'=8,'head'=4] {'head'}, use_global_device_ids=true, to_apply=%region_0.0 | all-reduce | flops 1024 | bytes 8192 | tf_op jit(solution)/shard_map/psum | solution.py:205
  43.3 1.2 %copy-done.7 = bf16[512,1024]{1,0:T(8,128)(2,1)S(1)} copy-done((bf16[512,1024]{1,0:T(8,128)(2,1)S(1)}, bf16[512,1024]{1,0:T(8,128)(2,1)}, u32[]{:S(2)}) %copy-start.7) | copy-done | bytes 1048600
  44.5 1.2 %copy-done.10 = bf16[512,1024]{1,0:T(8,128)(2,1)S(1)} copy-done((bf16[512,1024]{1,0:T(8,128)(2,1)S(1)}, bf16[512,1024]{1,0:T(8,128)(2,1)}, u32[]{:S(2)}) %copy-start.10) | copy-done | bytes 1048600
  45.7 2.7 %shard_map.80 = (bf16[512,1024]{1,0:T(8,128)(2,1)S(1)}, bf16[1024,128]{1,0:T(8,128)(2,1)S(1)}) custom-call(bf16[512,1024]{1,0:T(8,128)(2,1)S(1)} %copy-done.7, bf16[512,1024]{1,0:T(8,128)(2,1)S(1)} %copy-done.10, f32[1,1024]{1,0:T(1,128)S(1)} %bitcast.11, f32[512,1024]{1,0:T(8,128)S(1)} %shard_map.76.local_ref, bf16[1024,128]{1,0:T(8,128)(2,1)S(1)} %bitcast.6, ...), custom_call_target="tpu_custom_call" | custom-call | flops 268435456 | bytes 5775360 | tf_op jit(solution)/shard_map/pallas_call | solution.py:148
  49.4 13.0 %all_to_all.21.block_ref = bf16[8,128,128]{2,1,0:T(8,128)(2,1)S(1)} all-to-all(bf16[8,128,128]{2,1,0:T(8,128)(2,1)S(1)} %bitcast.9), channel_id=1, replica_groups=mesh['seq'=8,'head'=4] {'seq'}, dimensions={0} | all-to-all | bytes 524288 | tf_op jit(solution)/shard_map/all_to_all | solution.py:176
  63.1 4.0 %all-to-all-start.3 = ((bf16[8,128,128]{2,1,0:T(8,128)(2,1)}), bf16[8,128,128]{2,1,0:T(8,128)(2,1)}, u32[]{:S(2)}, u32[]{:S(2)}) async-start(bf16[8,128,128]{2,1,0:T(8,128)(2,1)} %shard_map.83), calls=%async_computation.3 | async-start | bytes 524288 | tf_op jit(solution)/shard_map/all_to_all | solution.py:178
  68.4 4.5 %shard_map.81 = bf16[512,1024]{1,0:T(8,128)(2,1)} custom-call(bf16[512,1024]{1,0:T(8,128)(2,1)S(1)} %copy-done.1, bf16[512,1024]{1,0:T(8,128)(2,1)S(1)} %copy-done.4, bf16[512,1024]{1,0:T(8,128)(2,1)S(1)} %copy-done.16, bf16[1024,128]{1,0:T(8,128)(2,1)S(1)} %bitcast.7), custom_call_target="tpu_custom_call" | custom-call | flops 939524096 | bytes 4456448 | tf_op jit(solution)/shard_map/pallas_call | solution.py:148
  73.0 6.2 %shard_map.82 = (f32[512,1024]{1,0:T(8,128)S(1)}, f32[512,1024]{1,0:T(8,128)S(1)}) custom-call(bf16[512,1024]{1,0:T(8,128)(2,1)S(1)} %copy-done.8, bf16[512,1024]{1,0:T(8,128)(2,1)S(1)} %copy-done.1, bf16[512,1024]{1,0:T(8,128)(2,1)S(1)} %copy-done.4, bf16[512,1024]{1,0:T(8,128)(2,1)S(1)} %copy-done.17), custom_call_target="tpu_custom_call" | custom-call | flops 1610612736 | bytes 8388608 | tf_op jit(solution)/shard_map/pallas_call | solution.py:148
  79.2 1.3 %copy-done.11 = f32[512,1024]{1,0:T(8,128)} copy-done((f32[512,1024]{1,0:T(8,128)}, f32[512,1024]{1,0:T(8,128)S(1)}, u32[]{:S(2)}) %copy-start.11) | copy-done | bytes 2097176
  80.5 1.3 %copy-done.13 = f32[512,1024]{1,0:T(8,128)} copy-done((f32[512,1024]{1,0:T(8,128)}, f32[512,1024]{1,0:T(8,128)S(1)}, u32[]{:S(2)}) %copy-start.13) | copy-done | bytes 2097176
  81.8 1.6 %copy-done.12 = f32[512,1024]{1,0:T(8,128)S(1)} copy-done((f32[512,1024]{1,0:T(8,128)S(1)}, f32[512,1024]{1,0:T(8,128)}, u32[]{:S(2)}) %copy-start.12) | copy-done | bytes 2097176
  83.4 1.6 %copy-done.14 = f32[512,1024]{1,0:T(8,128)S(1)} copy-done((f32[512,1024]{1,0:T(8,128)S(1)}, f32[512,1024]{1,0:T(8,128)}, u32[]{:S(2)}) %copy-start.14) | copy-done | bytes 2097176
  85.0 4.1 %shard_map.84 = (bf16[512,1024]{1,0:T(8,128)(2,1)}, bf16[512,1024]{1,0:T(8,128)(2,1)}) custom-call(bf16[512,1024]{1,0:T(8,128)(2,1)S(1)} %copy-done.1, bf16[512,1024]{1,0:T(8,128)(2,1)S(1)} %copy-done.4, f32[512,1024]{1,0:T(8,128)S(1)} %copy-done.12, f32[512,1024]{1,0:T(8,128)S(1)} %copy-done.14, bf16[1024,128]{1,0:T(8,128)(2,1)} %bitcast.4.state_ref), custom_call_target="tpu_custom_call" | custom-call | flops 268435456 | bytes 8650752 | tf_op jit(solution)/shard_map/pallas_call | solution.py:148
  (30 shorter events, 4.9 us)
Async XLA Ops:
  0.6 1.2 %copy-start = (bf16[512,1024]{1,0:T(8,128)(2,1)S(1)}, bf16[512,1024]{1,0:T(8,128)(2,1)}, u32[]{:S(2)}) copy-start(bf16[512,1024]{1,0:T(8,128)(2,1)} %key_ref.9) | copy-start | bytes 3145732
  1.9 1.2 %copy-start.2 = (bf16[512,1024]{1,0:T(8,128)(2,1)S(1)}, bf16[512,1024]{1,0:T(8,128)(2,1)}, u32[]{:S(2)}) copy-start(bf16[512,1024]{1,0:T(8,128)(2,1)} %value_ref.9) | copy-start | bytes 3145732
  3.1 21.8 %copy-start.1 = (bf16[512,1024]{1,0:T(8,128)(2,1)S(1)}, bf16[512,1024]{1,0:T(8,128)(2,1)}, u32[]{:S(2)}) copy-start(bf16[512,1024]{1,0:T(8,128)(2,1)} %key_ref.9) | copy-start | bytes 3145732
  21.3 12.2 %all-to-all-start.1 = ((bf16[8,128,128]{2,1,0:T(8,128)(2,1)}), bf16[8,128,128]{2,1,0:T(8,128)(2,1)S(1)}, u32[]{:S(2)}, u32[]{:S(2)}) async-start(bf16[8,128,128]{2,1,0:T(8,128)(2,1)} %shard_map.78), calls=%async_computation.1 | async-start | bytes 524288 | tf_op jit(solution)/shard_map/all_to_all | solution.py:178
  24.9 1.2 %copy-start.3 = (bf16[512,1024]{1,0:T(8,128)(2,1)S(1)}, bf16[512,1024]{1,0:T(8,128)(2,1)}, u32[]{:S(2)}) copy-start(bf16[512,1024]{1,0:T(8,128)(2,1)} %value_ref.9) | copy-start | bytes 3145732
  26.1 1.2 %copy-start.5 = (bf16[512,1024]{1,0:T(8,128)(2,1)S(1)}, bf16[512,1024]{1,0:T(8,128)(2,1)}, u32[]{:S(2)}) copy-start(bf16[512,1024]{1,0:T(8,128)(2,1)} %query_ref.7) | copy-start | bytes 3145732
  27.3 6.1 %copy-start.18 = (f32[1024]{0:T(1024)S(1)}, f32[1024]{0:T(1024)}, u32[]{:S(2)}) copy-start(f32[1024]{0:T(1024)} %param.9) | copy-start | bytes 12292
  33.4 1.2 %copy-start.6 = (bf16[512,1024]{1,0:T(8,128)(2,1)S(1)}, bf16[512,1024]{1,0:T(8,128)(2,1)}, u32[]{:S(2)}) copy-start(bf16[512,1024]{1,0:T(8,128)(2,1)} %query_ref.7) | copy-start | bytes 3145732
  34.6 1.2 %copy-start.9 = (bf16[512,1024]{1,0:T(8,128)(2,1)S(1)}, bf16[512,1024]{1,0:T(8,128)(2,1)}, u32[]{:S(2)}) copy-start(bf16[512,1024]{1,0:T(8,128)(2,1)} %grad_ref.3) | copy-start | bytes 3145732
  43.3 1.2 %copy-start.7 = (bf16[512,1024]{1,0:T(8,128)(2,1)S(1)}, bf16[512,1024]{1,0:T(8,128)(2,1)}, u32[]{:S(2)}) copy-start(bf16[512,1024]{1,0:T(8,128)(2,1)} %query_ref.7) | copy-start | bytes 3145732
  44.5 1.2 %copy-start.10 = (bf16[512,1024]{1,0:T(8,128)(2,1)S(1)}, bf16[512,1024]{1,0:T(8,128)(2,1)}, u32[]{:S(2)}) copy-start(bf16[512,1024]{1,0:T(8,128)(2,1)} %grad_ref.3) | copy-start | bytes 3145732
  48.5 1.0 %copy-start.15 = (bf16[512,1024]{1,0:T(8,128)(2,1)}, bf16[512,1024]{1,0:T(8,128)(2,1)S(1)}, u32[]{:S(2)}) copy-start(bf16[512,1024]{1,0:T(8,128)(2,1)S(1)} %get-tuple-element.9.dout_ref) | copy-start | bytes 3145732
  49.4 17.8 %copy-start.4 = (bf16[512,1024]{1,0:T(8,128)(2,1)S(1)}, bf16[512,1024]{1,0:T(8,128)(2,1)}, u32[]{:S(2)}) copy-start(bf16[512,1024]{1,0:T(8,128)(2,1)} %value_ref.9) | copy-start | bytes 3145732
  63.1 18.7 %all-to-all-start.3 = ((bf16[8,128,128]{2,1,0:T(8,128)(2,1)}), bf16[8,128,128]{2,1,0:T(8,128)(2,1)}, u32[]{:S(2)}, u32[]{:S(2)}) async-start(bf16[8,128,128]{2,1,0:T(8,128)(2,1)} %shard_map.83), calls=%async_computation.3 | async-start | bytes 524288 | tf_op jit(solution)/shard_map/all_to_all | solution.py:178
  67.2 1.2 %copy-start.16 = (bf16[512,1024]{1,0:T(8,128)(2,1)S(1)}, bf16[512,1024]{1,0:T(8,128)(2,1)}, u32[]{:S(2)}) copy-start(bf16[512,1024]{1,0:T(8,128)(2,1)} %copy-done.15) | copy-start | bytes 3145732
  68.4 4.5 %copy-start.8 = (bf16[512,1024]{1,0:T(8,128)(2,1)S(1)}, bf16[512,1024]{1,0:T(8,128)(2,1)}, u32[]{:S(2)}) copy-start(bf16[512,1024]{1,0:T(8,128)(2,1)} %query_ref.7) | copy-start | bytes 3145732
  68.4 4.5 %copy-start.17 = (bf16[512,1024]{1,0:T(8,128)(2,1)S(1)}, bf16[512,1024]{1,0:T(8,128)(2,1)}, u32[]{:S(2)}) copy-start(bf16[512,1024]{1,0:T(8,128)(2,1)} %copy-done.15) | copy-start | bytes 3145732
  79.2 1.3 %copy-start.11 = (f32[512,1024]{1,0:T(8,128)}, f32[512,1024]{1,0:T(8,128)S(1)}, u32[]{:S(2)}) copy-start(f32[512,1024]{1,0:T(8,128)S(1)} %get-tuple-element.10.key_part) | copy-start | bytes 6291460
  80.5 1.3 %copy-start.13 = (f32[512,1024]{1,0:T(8,128)}, f32[512,1024]{1,0:T(8,128)S(1)}, u32[]{:S(2)}) copy-start(f32[512,1024]{1,0:T(8,128)S(1)} %get-tuple-element.11.value_part) | copy-start | bytes 6291460
  81.8 1.6 %copy-start.12 = (f32[512,1024]{1,0:T(8,128)S(1)}, f32[512,1024]{1,0:T(8,128)}, u32[]{:S(2)}) copy-start(f32[512,1024]{1,0:T(8,128)} %copy-done.11) | copy-start | bytes 6291460
  83.4 1.6 %copy-start.14 = (f32[512,1024]{1,0:T(8,128)S(1)}, f32[512,1024]{1,0:T(8,128)}, u32[]{:S(2)}) copy-start(f32[512,1024]{1,0:T(8,128)} %copy-done.13) | copy-start | bytes 6291460

commit v4 on v3

--- a/solution.py
+++ b/solution.py
@@ -118,17 +118,17 @@
             query = query_ref[start:, cols]
             dout = dout_ref[start:, cols]
             dscore = masked(mm_nt(value_ref[start:end, cols], dout), 0, 0, False)
-            key_out[start:end, cols] = mm(dscore, query)
+            key_out[start:end, cols] = mm(dscore, query).astype(jnp.bfloat16)
             weights = masked(mm_nt(key_ref[start:end, cols], query), 0, 0, False)
-            value_out[start:end, cols] = mm(weights, dout)
+            value_out[start:end, cols] = mm(weights, dout).astype(jnp.bfloat16)
 
 
 def final_body(key_ref, value_ref, key_part, value_part, state_ref, key_out, value_out):
     for cols in head_columns(key_ref):
         state = state_ref[cols, :]
-        key_grad = key_part[:, cols] + mm_nt(value_ref[:, cols], state)
+        key_grad = key_part[:, cols].astype(jnp.float32) + mm_nt(value_ref[:, cols], state)
         key_out[:, cols] = key_grad.astype(jnp.bfloat16)
-        value_grad = value_part[:, cols] + mm(key_ref[:, cols], state)
+        value_grad = value_part[:, cols].astype(jnp.float32) + mm(key_ref[:, cols], state)
         value_out[:, cols] = value_grad.astype(jnp.bfloat16)
 
 
@@ -152,7 +152,7 @@
         out_specs=[specs[kind] for kind, _ in outs],
         out_shape=out_shape,
         scratch_shapes=scratch,
-        compiler_params=pltpu.CompilerParams(vmem_limit_bytes=24 * MIB),
+        compiler_params=pltpu.CompilerParams(vmem_limit_bytes=60 * MIB),
         cost_estimate=pl.CostEstimate(flops=flops, bytes_accessed=moved, transcendentals=0),
     )(*args)
     return result
@@ -162,20 +162,21 @@
     return pl.pallas_call(
         functools.partial(scan_body, reverse),
         out_shape=jax.ShapeDtypeStruct(blocks.shape, blocks.dtype),
-        compiler_params=pltpu.CompilerParams(vmem_limit_bytes=8 * MIB),
+        compiler_params=pltpu.CompilerParams(vmem_limit_bytes=60 * MIB),
         cost_estimate=pl.CostEstimate(
             flops=blocks.size, bytes_accessed=4 * blocks.size, transcendentals=0
         ),
     )(blocks)
 
 
-def entering(state, axis, reverse):
+def exchange(pieces, axis):
+    return lax.all_to_all(pieces, axis, 0, 0)
+
+
+def in_pieces(state, axis):
     count = lax.axis_size(axis)
     rows, cols = state.shape
-    pieces = state.reshape(count, rows // count, cols)
-    blocks = lax.all_to_all(pieces, axis, 0, 0)
-    states = scan_blocks(blocks, reverse)
-    return lax.all_to_all(states, axis, 0, 0).reshape(rows, cols)
+    return state.reshape(count, rows // count, cols)
 
 
 def shards(queries, keys, values, out_grad, gain):
@@ -187,7 +188,8 @@
     gain_row = gain.reshape(1, width)
 
     (own_kv,) = by_heads(states_body, (keys, values), ("tokens",) * 2, [("state", bf16)], 2, small)
-    kv_low = entering(own_kv, "seq", False)
+    kv_blocks = exchange(in_pieces(own_kv, "seq"), "seq")
+    kv_low = exchange(scan_blocks(kv_blocks, False), "seq").reshape(own_kv.shape)
     (local,) = by_heads(
         local_body, (queries, keys, values), ("tokens",) * 3, [("tokens", f32)], 2, 2 * large
     )
@@ -212,7 +214,7 @@
         2 * small,
         [pltpu.VMEM((rows, 8), f32)],
     )
-    grad_low = entering(own_grad, "seq", True)
+    grad_blocks = exchange(in_pieces(own_grad, "seq"), "seq")
     (query_grad,) = by_heads(
         query_body,
         (keys, values, dout, kv_low),
@@ -221,11 +223,13 @@
         2,
         2 * large + small,
     )
+    grad_blocks, query_grad = lax.optimization_barrier((grad_blocks, query_grad))
+    grad_low = exchange(scan_blocks(grad_blocks, True), "seq").reshape(own_grad.shape)
     key_part, value_part = by_heads(
         inner_body,
         (queries, keys, values, dout),
         ("tokens",) * 4,
-        [("tokens", f32)] * 2,
+        [("tokens", bf16)] * 2,
         2,
         4 * large,
     )

time: 90.1 us -> 84.4 us (0.937)
  local copies, waits for them, and re-layouts: 17.8 us -> 2.1 us
  Pallas kernels: 26.4 us -> 40.4 us
  blocking collectives: 34.6 us -> 22.6 us
  waiting for transfers between devices: 1.93 us -> 6.38 us
  starting transfers between devices: 7.63 us -> 11.2 us
    unnamed x38 -> x6, local copies, waits for them, and re-layouts: 17.8 us -> 2.1 us
    all_to_all x2 -> x1, blocking collectives: 29 us -> 16.3 us  [exchange(): return lax.all_to_all(pieces, axis, 0, 0)]
    pallas_call x7, Pallas kernels: 24.9 us -> 37 us  [by_heads(): pl.pallas_call(body, grid=(width // step_cols,), in_specs=[specs[kind] fo...]
    all_to_all x2 -> x3, waiting for transfers between devices: 1.93 us -> 6.38 us  [exchange(): return lax.all_to_all(pieces, axis, 0, 0)]
    all_to_all x2 -> x3, starting transfers between devices: 7.63 us -> 11.2 us  [exchange(): return lax.all_to_all(pieces, axis, 0, 0)]
    pallas_call x2, Pallas kernels: 1.49 us -> 3.38 us  [scan_blocks(): pl.pallas_call(functools.partial(scan_body, reverse), out_shape=jax.Shape...]
  transfers between devices with their start and end apart: 2 -> 3, of which waited for: 1 -> 3; matrix products, arithmetic and copies ran while one was open for 0% -> 0% of each run, Pallas kernels for 17% -> 23%
where the time goes in v4:
time: 84.4 us; the launch traced here: 83.3 us
  Pallas kernels  40.4 us (48%)
  blocking collectives  22.6 us (27%)
  starting transfers between devices  11.2 us (13%)
  waiting for transfers between devices  6.38 us (8%)
  local copies, waits for them, and re-layouts  2.1 us (2%)
    pallas_call x7, Pallas kernels, by_heads(): pl.pallas_call(body, grid=(width // step_cols,), in_specs=[specs[kind] fo...  37 us
    all_to_all x1, blocking collectives, exchange(): return lax.all_to_all(pieces, axis, 0, 0)  16.3 us
    all_to_all x3, starting transfers between devices, exchange(): return lax.all_to_all(pieces, axis, 0, 0)  11.2 us
    all_to_all x3, waiting for transfers between devices, exchange(): return lax.all_to_all(pieces, axis, 0, 0)  6.38 us
    psum x1, blocking collectives, shards(): sums = lax.psum(sums, 'head')  6.35 us
    pallas_call x2, Pallas kernels, scan_blocks(): pl.pallas_call(functools.partial(scan_body, reverse), out_shape=jax.Shape...  3.38 us
    unnamed x6, local copies, waits for them, and re-layouts  2.1 us
  transfers between devices with their start and end apart: 3, of which 3 were waited for; matrix products, arithmetic and copies ran while one was open for 0% of the time, Pallas kernels for 23%

profile of v4, /device:TPU:0, one launch (start us, length us, event | category | flops | bytes accessed | tf_op | source)
XLA Modules:
  0.0 83.3 jit_solution(10005270297813141667)
XLA Ops:
  0.6 3.9 %shard_map.77 = bf16[1024,128]{1,0:T(8,128)(2,1)} custom-call(bf16[512,1024]{1,0:T(8,128)(2,1)} %key_ref.9, bf16[512,1024]{1,0:T(8,128)(2,1)} %value_ref.9), custom_call_target="tpu_custom_call" | custom-call | flops 134217728 | bytes 2359296 | tf_op jit(solution)/shard_map/pallas_call | solution.py:148
  4.6 16.3 %all_to_all.20.block_ref = bf16[8,128,128]{2,1,0:T(8,128)(2,1)} all-to-all(bf16[8,128,128]{2,1,0:T(8,128)(2,1)} %bitcast.9), channel_id=1, replica_groups=mesh['seq'=8,'head'=4] {'seq'}, dimensions={0} | all-to-all | bytes 524288 | tf_op jit(solution)/shard_map/all_to_all | solution.py:173
  20.9 1.7 %shard_map.78 = bf16[8,128,128]{2,1,0:T(8,128)(2,1)} custom-call(bf16[8,128,128]{2,1,0:T(8,128)(2,1)} %all_to_all.20.block_ref), custom_call_target="tpu_custom_call" | custom-call | flops 131072 | bytes 524288 | tf_op jit(solution)/shard_map/pallas_call | solution.py:162
  22.5 3.6 %all-to-all-start.1 = ((bf16[8,128,128]{2,1,0:T(8,128)(2,1)}), bf16[8,128,128]{2,1,0:T(8,128)(2,1)S(1)}, u32[]{:S(2)}, u32[]{:S(2)}) async-start(bf16[8,128,128]{2,1,0:T(8,128)(2,1)} %shard_map.78), calls=%async_computation.1 | async-start | bytes 524288 | tf_op jit(solution)/shard_map/all_to_all | solution.py:173
  26.1 6.1 %shard_map.76.local_ref = f32[512,1024]{1,0:T(8,128)} custom-call(bf16[512,1024]{1,0:T(8,128)(2,1)} %query_ref.7, bf16[512,1024]{1,0:T(8,128)(2,1)} %key_ref.9, bf16[512,1024]{1,0:T(8,128)(2,1)} %value_ref.9), custom_call_target="tpu_custom_call" | custom-call | flops 805306368 | bytes 5242880 | tf_op jit(solution)/shard_map/pallas_call | solution.py:148
  32.3 2.4 %all-to-all-done.1 = bf16[8,128,128]{2,1,0:T(8,128)(2,1)S(1)} async-done(((bf16[8,128,128]{2,1,0:T(8,128)(2,1)}), bf16[8,128,128]{2,1,0:T(8,128)(2,1)S(1)}, u32[]{:S(2)}, u32[]{:S(2)}) %all-to-all-start.1) | async-done | bytes 262176 | tf_op jit(solution)/shard_map/all_to_all | solution.py:173
  34.7 0.0 copy-start
  34.7 0.7 copy-done
  35.4 4.2 %shard_map.79 = f32[2,512]{1,0:T(2,128)} custom-call(bf16[512,1024]{1,0:T(8,128)(2,1)} %query_ref.7, bf16[512,1024]{1,0:T(8,128)(2,1)} %grad_ref.3, f32[1,1024]{1,0:T(1,128)} %bitcast.11, f32[512,1024]{1,0:T(8,128)} %shard_map.76.local_ref, bf16[1024,128]{1,0:T(8,128)(2,1)} %bitcast.5), custom_call_target="tpu_custom_call" | custom-call | flops 134217728 | bytes 4464640 | tf_op jit(solution)/shard_map/pallas_call | solution.py:148
  39.6 6.3 %psum.7.sums_ref = f32[2,512]{1,0:T(2,128)} all-reduce(f32[2,512]{1,0:T(2,128)} %shard_map.79), channel_id=1, replica_groups=mesh['seq'=8,'head'=4] {'head'}, use_global_device_ids=true, to_apply=%region_0.0 | all-reduce | flops 1024 | bytes 8192 | tf_op jit(solution)/shard_map/psum | solution.py:207
  45.9 5.0 %shard_map.80 = (bf16[512,1024]{1,0:T(8,128)(2,1)}, bf16[1024,128]{1,0:T(8,128)(2,1)}) custom-call(bf16[512,1024]{1,0:T(8,128)(2,1)} %query_ref.7, bf16[512,1024]{1,0:T(8,128)(2,1)} %grad_ref.3, f32[1,1024]{1,0:T(1,128)} %bitcast.12, f32[512,1024]{1,0:T(8,128)} %shard_map.76.local_ref, bf16[1024,128]{1,0:T(8,128)(2,1)} %bitcast.6, f32[2,512]{1,0:T(2,128)} %psum.7.sums_ref), custom_call_target="tpu_custom_call" | custom-call | flops 268435456 | bytes 5775360 | tf_op jit(solution)/shard_map/pallas_call | solution.py:148
  50.9 4.0 %all-to-all-start.2 = ((bf16[8,128,128]{2,1,0:T(8,128)(2,1)}), bf16[8,128,128]{2,1,0:T(8,128)(2,1)S(1)}, u32[]{:S(2)}, u32[]{:S(2)}) async-start(bf16[8,128,128]{2,1,0:T(8,128)(2,1)} %bitcast.10), calls=%async_computation.2 | async-start | bytes 524288 | tf_op jit(solution)/shard_map/all_to_all | solution.py:173
  54.9 5.7 %shard_map.81 = bf16[512,1024]{1,0:T(8,128)(2,1)} custom-call(bf16[512,1024]{1,0:T(8,128)(2,1)} %key_ref.9, bf16[512,1024]{1,0:T(8,128)(2,1)} %value_ref.9, bf16[512,1024]{1,0:T(8,128)(2,1)} %get-tuple-element.12.dout_ref, bf16[1024,128]{1,0:T(8,128)(2,1)} %bitcast.7), custom_call_target="tpu_custom_call" | custom-call | flops 939524096 | bytes 4456448 | tf_op jit(solution)/shard_map/pallas_call | solution.py:148
  60.6 2.9 %all-to-all-done.2.block_ref = bf16[8,128,128]{2,1,0:T(8,128)(2,1)S(1)} async-done(((bf16[8,128,128]{2,1,0:T(8,128)(2,1)}), bf16[8,128,128]{2,1,0:T(8,128)(2,1)S(1)}, u32[]{:S(2)}, u32[]{:S(2)}) %all-to-all-start.2) | async-done | bytes 262176 | tf_op jit(solution)/shard_map/all_to_all | solution.py:173
  63.5 0.0 copy-start.2
  63.5 0.7 copy-done.2
  64.2 1.7 %shard_map.83 = bf16[8,128,128]{2,1,0:T(8,128)(2,1)} custom-call(bf16[8,128,128]{2,1,0:T(8,128)(2,1)} %copy-done.2), custom_call_target="tpu_custom_call" | custom-call | flops 131072 | bytes 524288 | tf_op jit(solution)/shard_map/pallas_call | solution.py:162
  65.9 3.6 %all-to-all-start.3 = ((bf16[8,128,128]{2,1,0:T(8,128)(2,1)}), bf16[8,128,128]{2,1,0:T(8,128)(2,1)S(1)}, u32[]{:S(2)}, u32[]{:S(2)}) async-start(bf16[8,128,128]{2,1,0:T(8,128)(2,1)} %shard_map.83), calls=%async_computation.3 | async-start | bytes 524288 | tf_op jit(solution)/shard_map/all_to_all | solution.py:173
  69.4 7.5 %shard_map.82 = (bf16[512,1024]{1,0:T(8,128)(2,1)}, bf16[512,1024]{1,0:T(8,128)(2,1)}) custom-call(bf16[512,1024]{1,0:T(8,128)(2,1)} %query_ref.7, bf16[512,1024]{1,0:T(8,128)(2,1)} %key_ref.9, bf16[512,1024]{1,0:T(8,128)(2,1)} %value_ref.9, bf16[512,1024]{1,0:T(8,128)(2,1)} %get-tuple-element.12.dout_ref), custom_call_target="tpu_custom_call" | custom-call | flops 1610612736 | bytes 6291456 | tf_op jit(solution)/shard_map/pallas_call | solution.py:148
  76.9 1.1 %all-to-all-done.3 = bf16[8,128,128]{2,1,0:T(8,128)(2,1)S(1)} async-done(((bf16[8,128,128]{2,1,0:T(8,128)(2,1)}), bf16[8,128,128]{2,1,0:T(8,128)(2,1)S(1)}, u32[]{:S(2)}, u32[]{:S(2)}) %all-to-all-start.3) | async-done | bytes 262176 | tf_op jit(solution)/shard_map/all_to_all | solution.py:173
  78.0 0.0 copy-start.1
  78.0 0.7 copy-done.1
  78.7 4.6 %shard_map.84 = (bf16[512,1024]{1,0:T(8,128)(2,1)}, bf16[512,1024]{1,0:T(8,128)(2,1)}) custom-call(bf16[512,1024]{1,0:T(8,128)(2,1)} %key_ref.9, bf16[512,1024]{1,0:T(8,128)(2,1)} %value_ref.9, bf16[512,1024]{1,0:T(8,128)(2,1)} %get-tuple-element.14.key_part, bf16[512,1024]{1,0:T(8,128)(2,1)} %get-tuple-element.15.value_part, bf16[1024,128]{1,0:T(8,128)(2,1)} %bitcast.8), custom_call_target="tpu_custom_call" | custom-call | flops 268435456 | bytes 6553600 | tf_op jit(solution)/shard_map/pallas_call | solution.py:148
Async XLA Ops:
  22.5 12.2 %all-to-all-start.1 = ((bf16[8,128,128]{2,1,0:T(8,128)(2,1)}), bf16[8,128,128]{2,1,0:T(8,128)(2,1)S(1)}, u32[]{:S(2)}, u32[]{:S(2)}) async-start(bf16[8,128,128]{2,1,0:T(8,128)(2,1)} %shard_map.78), calls=%async_computation.1 | async-start | bytes 524288 | tf_op jit(solution)/shard_map/all_to_all | solution.py:173
  34.7 0.7 copy-start
  50.9 12.6 %all-to-all-start.2 = ((bf16[8,128,128]{2,1,0:T(8,128)(2,1)}), bf16[8,128,128]{2,1,0:T(8,128)(2,1)S(1)}, u32[]{:S(2)}, u32[]{:S(2)}) async-start(bf16[8,128,128]{2,1,0:T(8,128)(2,1)} %bitcast.10), calls=%async_computation.2 | async-start | bytes 524288 | tf_op jit(solution)/shard_map/all_to_all | solution.py:173
  63.5 0.7 copy-start.2
  65.9 12.1 %all-to-all-start.3 = ((bf16[8,128,128]{2,1,0:T(8,128)(2,1)}), bf16[8,128,128]{2,1,0:T(8,128)(2,1)S(1)}, u32[]{:S(2)}, u32[]{:S(2)}) async-start(bf16[8,128,128]{2,1,0:T(8,128)(2,1)} %shard_map.83), calls=%async_computation.3 | async-start | bytes 524288 | tf_op jit(solution)/shard_map/all_to_all | solution.py:173
  78.0 0.7 copy-start.1

commit v5 on v4

v5 whole, which is shorter than its diff:
```python
import functools

import jax
import jax.numpy as jnp
from jax import lax
from jax.experimental import pallas as pl
from jax.experimental.pallas import tpu as pltpu
from jax.sharding import PartitionSpec as P

HEAD_DIM = 128
BLOCK = 256
COPY_COLS = 256
EPSILON = 1e-06
MIB = 1 << 20


def mm(a, b):
    return lax.dot_general(a, b, (((1,), (0,)), ((), ())), preferred_element_type=jnp.float32)


def mm_nt(a, b):
    return lax.dot_general(a, b, (((1,), (1,)), ((), ())), preferred_element_type=jnp.float32)


def mm_tn(a, b):
    return lax.dot_general(a, b, (((0,), (0,)), ((), ())), preferred_element_type=jnp.float32)


def pieces_of(ref, size):
    return [slice(at, at + size) for at in range(0, ref.shape[1], size)]


def head_columns(ref):
    return pieces_of(ref, HEAD_DIM)


def masked(scores, row_start, col_start, rows_first):
    rows = row_start + lax.broadcasted_iota(jnp.int32, scores.shape, 0)
    cols = col_start + lax.broadcasted_iota(jnp.int32, scores.shape, 1)
    keep = rows >= cols if rows_first else cols >= rows
    return jnp.where(keep, scores, 0.0).astype(jnp.bfloat16)


def column_copies(source, target, sems):
    copies = []
    for index, cols in enumerate(pieces_of(source, COPY_COLS)):
        copies.append(pltpu.make_async_copy(source.at[:, cols], target.at[:, cols], sems.at[index]))
    return copies


def states_body(key_hbm, value_hbm, key_ref, value_ref, state_ref, key_sems, value_sems):
    key_copies = column_copies(key_hbm, key_ref, key_sems)
    value_copies = column_copies(value_hbm, value_ref, value_sems)
    for key_copy, value_copy in zip(key_copies, value_copies):
        key_copy.start()
        value_copy.start()
    for index, cols in enumerate(pieces_of(key_ref, COPY_COLS)):
        key_copies[index].wait()
        value_copies[index].wait()
        for start in range(cols.start, cols.stop, HEAD_DIM):
            head = slice(start, start + HEAD_DIM)
            state_ref[head, :] = mm_tn(key_ref[:, head], value_ref[:, head]).astype(jnp.bfloat16)


def local_body(query_hbm, grad_hbm, gain_ref, key_ref, value_ref, query_ref, flipped_ref, scaled_ref, local_ref, grad_ref, query_sems, grad_sems):
    rows = query_ref.shape[0]
    query_copies = column_copies(query_hbm, query_ref, query_sems)
    grad_copies = column_copies(grad_hbm, grad_ref, grad_sems)
    for copy in query_copies + grad_copies:
        copy.start()
    for copy in query_copies + grad_copies:
        copy.wait()

    @pl.loop(0, query_ref.shape[1] // HEAD_DIM)
    def _(head):
        cols = pl.ds(pl.multiple_of(head * HEAD_DIM, HEAD_DIM), HEAD_DIM)
        scaled_ref[:, cols] = gain_ref[:, cols] * grad_ref[:, cols].astype(jnp.float32)
        flipped_ref[cols, :] = query_ref[:, cols].T
        for start in range(0, rows, BLOCK):
            end = start + BLOCK
            scores = mm_nt(query_ref[start:end, cols], key_ref[:end, cols])
            weights = masked(scores, start, 0, True)
            local_ref[start:end, cols] = mm(weights, value_ref[:end, cols])


def scan_body(reverse, block_ref, state_ref):
    count = block_ref.shape[0]
    total = jnp.zeros(block_ref.shape[1:], jnp.float32)
    order = range(count - 1, -1, -1) if reverse else range(count)
    for place in order:
        state_ref[place] = total.astype(jnp.bfloat16)
        total = total + block_ref[place].astype(jnp.float32)


def sums_body(query_ref, scaled_ref, local_ref, state_ref, attended_ref, sums_ref):
    for start in range(0, query_ref.shape[0], BLOCK):
        rows = slice(start, start + BLOCK)
        square = jnp.zeros((BLOCK, HEAD_DIM), jnp.float32)
        cross = jnp.zeros((BLOCK, HEAD_DIM), jnp.float32)
        for cols in head_columns(query_ref):
            attended = local_ref[rows, cols] + mm(query_ref[rows, cols], state_ref[cols, :])
            attended_ref[rows, cols] = attended
            square += attended * attended
            cross += scaled_ref[rows, cols] * attended
        sums_ref[0:1, rows] = jnp.sum(square.T, axis=0, keepdims=True)
        sums_ref[1:2, rows] = jnp.sum(cross.T, axis=0, keepdims=True)


def dout_body(width, flipped_ref, scaled_ref, attended_ref, sums_ref, dout_ref, own_ref):
    inverse = 1.0 / jnp.sqrt(sums_ref[0:1, :] / width + EPSILON)
    drop = sums_ref[1:2, :] * (inverse * inverse * inverse) / width
    factors = jnp.concatenate([inverse, drop] + [jnp.zeros_like(drop)] * 6, axis=0).T
    shape = (factors.shape[0], HEAD_DIM)
    inverse = jnp.broadcast_to(factors[:, 0:1], shape)
    drop = jnp.broadcast_to(factors[:, 1:2], shape)
    for cols in head_columns(dout_ref):
        dout = scaled_ref[:, cols] * inverse - attended_ref[:, cols] * drop
        dout = dout.astype(jnp.bfloat16)
        dout_ref[:, cols] = dout
        own_ref[cols, :] = mm(flipped_ref[cols, :], dout).astype(jnp.bfloat16)


def query_body(key_ref, value_ref, dout_ref, state_ref, out_hbm, out_ref, sems):
    rows = dout_ref.shape[0]
    copies = column_copies(out_ref, out_hbm, sems)
    for index, step in enumerate(pieces_of(out_ref, COPY_COLS)):
        for left in range(step.start, step.stop, HEAD_DIM):
            cols = slice(left, left + HEAD_DIM)
            for start in range(0, rows, BLOCK):
                end = start + BLOCK
                dout = dout_ref[start:end, cols]
                dscore = masked(mm_nt(dout, value_ref[:end, cols]), start, 0, True)
                grad = mm(dscore, key_ref[:end, cols]) + mm_nt(dout, state_ref[cols, :])
                out_ref[start:end, cols] = grad.astype(jnp.bfloat16)
        copies[index].start()
    for copy in copies:
        copy.wait()


def inner_body(query_ref, key_ref, value_ref, dout_ref, key_out, value_out):
    rows = dout_ref.shape[0]

    @pl.loop(0, dout_ref.shape[1] // HEAD_DIM)
    def _(head):
        cols = pl.ds(pl.multiple_of(head * HEAD_DIM, HEAD_DIM), HEAD_DIM)
        for start in range(0, rows, BLOCK):
            end = start + BLOCK
            query = query_ref[start:, cols]
            dout = dout_ref[start:, cols]
            dscore = masked(mm_nt(value_ref[start:end, cols], dout), 0, 0, False)
            key_out[start:end, cols] = mm(dscore, query)
            weights = masked(mm_nt(key_ref[start:end, cols], query), 0, 0, False)
            value_out[start:end, cols] = mm(weights, dout)


def final_body(key_ref, value_ref, key_part, value_part, state_ref, key_hbm, value_hbm, key_out, value_out, key_sems, value_sems):
    key_copies = column_copies(key_out, key_hbm, key_sems)
    value_copies = column_copies(value_out, value_hbm, value_sems)
    for index, step in enumerate(pieces_of(key_out, COPY_COLS)):
        for left in range(step.start, step.stop, HEAD_DIM):
            cols = slice(left, left + HEAD_DIM)
            state = state_ref[cols, :]
            key_grad = key_part[:, cols] + mm_nt(value_ref[:, cols], state)
            key_out[:, cols] = key_grad.astype(jnp.bfloat16)
            value_grad = value_part[:, cols] + mm(key_ref[:, cols], state)
            value_out[:, cols] = value_grad.astype(jnp.bfloat16)
        key_copies[index].start()
        value_copies[index].start()
    for copy in key_copies + value_copies:
        copy.wait()


def in_vmem(shape, dtype):
    return pltpu.VMEM(shape, dtype)


def local_call(body, in_args, outs, flops, hbm_args=(), scratch=(), aliases=None):
    args = [pltpu.with_memory_space_constraint(a, pltpu.HBM) for a in hbm_args]
    args += [pltpu.with_memory_space_constraint(a, pltpu.VMEM) for a in in_args]
    specs = [pl.BlockSpec(memory_space=pltpu.HBM)] * len(hbm_args)
    specs += [pl.BlockSpec(memory_space=pltpu.VMEM)] * len(in_args)
    out_specs = []
    for out in outs:
        space = pltpu.HBM if isinstance(out, jax.ShapeDtypeStruct) else pltpu.VMEM
        out_specs.append(pl.BlockSpec(memory_space=space))
    moved = sum(a.size * a.dtype.itemsize for a in args)
    return pl.pallas_call(
        body,
        in_specs=specs,
        out_specs=out_specs,
        out_shape=outs,
        scratch_shapes=scratch,
        input_output_aliases=aliases or {},
        compiler_params=pltpu.CompilerParams(vmem_limit_bytes=16 * MIB),
        cost_estimate=pl.CostEstimate(flops=flops, bytes_accessed=moved, transcendentals=0),
    )(*args)


def scan_blocks(blocks, reverse):
    (states,) = local_call(
        functools.partial(scan_body, reverse),
        [blocks],
        [in_vmem(blocks.shape, blocks.dtype)],
        blocks.size,
    )
    return states


def exchange(pieces, axis):
    return lax.all_to_all(pieces, axis, 0, 0)


def in_pieces(state, axis):
    count = lax.axis_size(axis)
    rows, cols = state.shape
    return state.reshape(count, rows // count, cols)


def shards(queries, keys, values, out_grad, gain):
    rows, width = queries.shape
    total_width = width * lax.axis_size("head")
    bf16, f32 = jnp.bfloat16, jnp.float32
    tokens, state = (rows, width), (width, HEAD_DIM)
    small = 2 * rows * width * HEAD_DIM
    large = 2 * rows * rows * width * 3 // 4
    gain_row = gain.reshape(1, width)
    copy_sems = [pltpu.SemaphoreType.DMA((width // COPY_COLS,))]
    kept, result = in_vmem(tokens, bf16), jax.ShapeDtypeStruct(tokens, bf16)

    key_vm, value_vm, own_kv = local_call(
        states_body,
        [],
        [kept, kept, in_vmem(state, bf16)],
        small,
        [keys, values],
        copy_sems * 2,
    )
    kv_blocks = exchange(in_pieces(own_kv, "seq"), "seq")
    kv_low = exchange(scan_blocks(kv_blocks, False), "seq").reshape(state)
    query_vm, flipped, scaled, local = local_call(
        local_body,
        [gain_row, key_vm, value_vm],
        [kept, in_vmem((width, rows), bf16), in_vmem(tokens, f32), in_vmem(tokens, f32)],
        2 * large,
        [queries, out_grad],
        [pltpu.VMEM(tokens, bf16)] + copy_sems * 2,
    )
    attended, sums = local_call(
        sums_body,
        [query_vm, scaled, local, kv_low],
        [in_vmem(tokens, f32), in_vmem((2, rows), f32)],
        small,
        aliases={2: 0},
    )
    sums = lax.psum(sums, "head")
    dout, own_grad = local_call(
        functools.partial(dout_body, total_width),
        [flipped, scaled, attended, sums],
        [kept, in_vmem(state, bf16)],
        small,
    )
    grad_blocks = exchange(in_pieces(own_grad, "seq"), "seq")
    (query_grad,) = local_call(
        query_body,
        [key_vm, value_vm, dout, kv_low],
        [result],
        2 * large + small,
        scratch=[pltpu.VMEM(tokens, bf16)] + copy_sems,
    )
    grad_blocks, query_grad = lax.optimization_barrier((grad_blocks, query_grad))
    grad_low = exchange(scan_blocks(grad_blocks, True), "seq").reshape(state)
    key_part, value_part = local_call(
        inner_body,
        [query_vm, key_vm, value_vm, dout],
        [in_vmem(tokens, f32)] * 2,
        4 * large,
    )
    key_grad, value_grad = local_call(
        final_body,
        [key_vm, value_vm, key_part, value_part, grad_low],
        [result] * 2,
        2 * small,
        scratch=[pltpu.VMEM(tokens, bf16)] * 2 + copy_sems * 2,
    )
    return query_grad, key_grad, value_grad


def solution(mesh):
    return jax.shard_map(
        shards,
        mesh=mesh,
        in_specs=(
            P("seq", "head"),
            P("seq", "head"),
            P("seq", "head"),
            P("seq", "head"),
            P("head"),
        ),
        out_specs=(P("seq", "head"), P("seq", "head"), P("seq", "head")),
        check_vma=False,
    )
```

time: 84.4 us -> 87.8 us (1.040)
  local copies, waits for them, and re-layouts: 2.1 us -> 21.3 us
  Pallas kernels: 40.4 us -> 24.5 us
  starting transfers between devices: 11.2 us -> 12.9 us
    unnamed x6 -> x36, local copies, waits for them, and re-layouts: 2.1 us -> 21.3 us
    pallas_call x9, Pallas kernels: 40.4 us -> 24.5 us  [local_call(): pl.pallas_call(body, in_specs=specs, out_specs=out_specs, out_shape=outs,...]
    all_to_all x3, starting transfers between devices: 11.2 us -> 12.9 us  [exchange(): return lax.all_to_all(pieces, axis, 0, 0)]
  transfers between devices with their start and end apart: 3 -> 3, of which waited for: 3 -> 1; matrix products, arithmetic and copies ran while one was open for 0% -> 0% of each run, Pallas kernels for 23% -> 19%
where the time goes in v5:
time: 87.8 us; the launch traced here: 87 us
  Pallas kernels  24.5 us (28%)
  blocking collectives  21.9 us (25%)
  local copies, waits for them, and re-layouts  21.3 us (24%)
  starting transfers between devices  12.9 us (15%)
  waiting for transfers between devices  5.7 us (6%)
    pallas_call x9, Pallas kernels, local_call(): pl.pallas_call(body, in_specs=specs, out_specs=out_specs, out_shape=outs,...  24.5 us
    unnamed x36, local copies, waits for them, and re-layouts  21.3 us
    all_to_all x1, blocking collectives, exchange(): return lax.all_to_all(pieces, axis, 0, 0)  16 us
    all_to_all x3, starting transfers between devices, exchange(): return lax.all_to_all(pieces, axis, 0, 0)  12.9 us
    psum x1, blocking collectives, shards(): sums = lax.psum(sums, 'head')  5.92 us
    all_to_all x3, waiting for transfers between devices, exchange(): return lax.all_to_all(pieces, axis, 0, 0)  5.7 us
  transfers between devices with their start and end apart: 3, of which 1 were waited for; matrix products, arithmetic and copies ran while one was open for 0% of the time, Pallas kernels for 19%

profile of v5, /device:TPU:0, one launch (start us, length us, event | category | flops | bytes accessed | tf_op | source)
XLA Modules:
  0.0 87.0 jit_solution(17351784555692034103)
XLA Ops:
  0.6 2.3 %shard_map.76 = (bf16[512,1024]{1,0:T(8,128)(2,1)S(1)}, bf16[512,1024]{1,0:T(8,128)(2,1)S(1)}, bf16[1024,128]{1,0:T(8,128)(2,1)S(1)}) custom-call(bf16[512,1024]{1,0:T(8,128)(2,1)} %key_hbm.1, bf16[512,1024]{1,0:T(8,128)(2,1)} %value_hbm.1), custom_call_target="tpu_custom_call" | custom-call | flops 134217728 | bytes 2097152 | tf_op jit(solution)/shard_map/pallas_call | solution.py:187
  3.0 16.0 %all_to_all.20.block_ref = bf16[8,128,128]{2,1,0:T(8,128)(2,1)S(1)} all-to-all(bf16[8,128,128]{2,1,0:T(8,128)(2,1)S(1)} %bitcast.9), channel_id=1, replica_groups=mesh['seq'=8,'head'=4] {'seq'}, dimensions={0} | all-to-all | bytes 524288 | tf_op jit(solution)/shard_map/all_to_all | solution.py:210
  19.7 3.6 %all-to-all-start.1 = ((bf16[8,128,128]{2,1,0:T(8,128)(2,1)}), bf16[8,128,128]{2,1,0:T(8,128)(2,1)S(1)}, u32[]{:S(2)}, u32[]{:S(2)}) async-start(bf16[8,128,128]{2,1,0:T(8,128)(2,1)} %shard_map.78), calls=%async_computation.1 | async-start | bytes 524288 | tf_op jit(solution)/shard_map/all_to_all | solution.py:210
  23.3 6.4 %shard_map.77 = (bf16[512,1024]{1,0:T(8,128)(2,1)S(1)}, bf16[1024,512]{1,0:T(8,128)(2,1)S(1)}, f32[512,1024]{1,0:T(8,128)S(1)}, f32[512,1024]{1,0:T(8,128)S(1)}) custom-call(bf16[512,1024]{1,0:T(8,128)(2,1)} %query_hbm.1, bf16[512,1024]{1,0:T(8,128)(2,1)} %grad_hbm.1, f32[1,1024]{1,0:T(1,128)S(1)} %bitcast.10, ...), custom_call_target="tpu_custom_call" | custom-call | flops 805306368 | bytes 4198400 | tf_op jit(solution)/shard_map/pallas_call | solution.py:187
  29.7 1.3 %copy-done = f32[512,1024]{1,0:T(8,128)} copy-done((f32[512,1024]{1,0:T(8,128)}, f32[512,1024]{1,0:T(8,128)S(1)}, u32[]{:S(2)}) %copy-start) | copy-done | bytes 2097176
  31.0 1.3 %copy-done.3 = f32[512,1024]{1,0:T(8,128)} copy-done((f32[512,1024]{1,0:T(8,128)}, f32[512,1024]{1,0:T(8,128)S(1)}, u32[]{:S(2)}) %copy-start.3) | copy-done | bytes 2097176
  33.3 2.0 %copy-done.1 = f32[512,1024]{1,0:T(8,128)S(1)} copy-done((f32[512,1024]{1,0:T(8,128)S(1)}, f32[512,1024]{1,0:T(8,128)}, u32[]{:S(2)}) %copy-start.1) | copy-done | bytes 2097176
  35.3 1.6 %copy-done.4 = f32[512,1024]{1,0:T(8,128)S(1)} copy-done((f32[512,1024]{1,0:T(8,128)S(1)}, f32[512,1024]{1,0:T(8,128)}, u32[]{:S(2)}) %copy-start.4) | copy-done | bytes 2097176
  38.0 1.3 %copy-done.5 = f32[512,1024]{1,0:T(8,128)} copy-done((f32[512,1024]{1,0:T(8,128)}, f32[512,1024]{1,0:T(8,128)S(1)}, u32[]{:S(2)}) %copy-start.5) | copy-done | bytes 2097176
  39.3 5.9 %psum.7.sums_ref = f32[2,512]{1,0:T(2,128)S(1)} all-reduce(f32[2,512]{1,0:T(2,128)S(1)} %get-tuple-element.28), channel_id=1, replica_groups=mesh['seq'=8,'head'=4] {'head'}, use_global_device_ids=true, to_apply=%region_0.0 | all-reduce | flops 1024 | bytes 8192 | tf_op jit(solution)/shard_map/psum | solution.py:255
  45.2 1.6 %copy-done.2 = f32[512,1024]{1,0:T(8,128)S(1)} copy-done((f32[512,1024]{1,0:T(8,128)S(1)}, f32[512,1024]{1,0:T(8,128)}, u32[]{:S(2)}) %copy-start.2) | copy-done | bytes 2097176
  46.8 1.6 %copy-done.6 = f32[512,1024]{1,0:T(8,128)S(1)} copy-done((f32[512,1024]{1,0:T(8,128)S(1)}, f32[512,1024]{1,0:T(8,128)}, u32[]{:S(2)}) %copy-start.6) | copy-done | bytes 2097176
  48.4 1.2 %copy-done.15 = bf16[1024,512]{1,0:T(8,128)(2,1)S(1)} copy-done((bf16[1024,512]{1,0:T(8,128)(2,1)S(1)}, bf16[1024,512]{1,0:T(8,128)(2,1)}, u32[]{:S(2)}) %copy-start.15) | copy-done | bytes 1048600
  51.3 5.7 %all-to-all-start.2 = ((bf16[8,128,128]{2,1,0:T(8,128)(2,1)}), bf16[8,128,128]{2,1,0:T(8,128)(2,1)}, u32[]{:S(2)}, u32[]{:S(2)}) async-start(bf16[8,128,128]{2,1,0:T(8,128)(2,1)} %bitcast.8), calls=%async_computation.2 | async-start | bytes 524288 | tf_op jit(solution)/shard_map/all_to_all | solution.py:210
  57.0 3.3 %shard_map.81 = bf16[512,1024]{1,0:T(8,128)(2,1)} custom-call(bf16[512,1024]{1,0:T(8,128)(2,1)S(1)} %get-tuple-element.20.key_ref, bf16[512,1024]{1,0:T(8,128)(2,1)S(1)} %get-tuple-element.21.value_ref, bf16[512,1024]{1,0:T(8,128)(2,1)S(1)} %get-tuple-element.30.dout_ref, bf16[1024,128]{1,0:T(8,128)(2,1)S(1)} %bitcast.6), custom_call_target="tpu_custom_call" | custom-call | flops 939524096 | bytes 3407872 | tf_op jit(solution)/shard_map/pallas_call | solution.py:187
  60.3 5.7 %all-to-all-done.2.block_ref = bf16[8,128,128]{2,1,0:T(8,128)(2,1)} async-done(((bf16[8,128,128]{2,1,0:T(8,128)(2,1)}), bf16[8,128,128]{2,1,0:T(8,128)(2,1)}, u32[]{:S(2)}, u32[]{:S(2)}) %all-to-all-start.2) | async-done | bytes 262176 | tf_op jit(solution)/shard_map/all_to_all | solution.py:210
  67.7 3.6 %all-to-all-start.3 = ((bf16[8,128,128]{2,1,0:T(8,128)(2,1)}), bf16[8,128,128]{2,1,0:T(8,128)(2,1)S(1)}, u32[]{:S(2)}, u32[]{:S(2)}) async-start(bf16[8,128,128]{2,1,0:T(8,128)(2,1)} %copy-done.11), calls=%async_computation.3 | async-start | bytes 524288 | tf_op jit(solution)/shard_map/all_to_all | solution.py:210
  71.3 1.2 %copy-done.13 = bf16[512,1024]{1,0:T(8,128)(2,1)S(1)} copy-done((bf16[512,1024]{1,0:T(8,128)(2,1)S(1)}, bf16[512,1024]{1,0:T(8,128)(2,1)}, u32[]{:S(2)}) %copy-start.13) | copy-done | bytes 1048600
  72.6 6.8 %shard_map.82 = (f32[512,1024]{1,0:T(8,128)S(1)}, f32[512,1024]{1,0:T(8,128)S(1)}) custom-call(bf16[512,1024]{1,0:T(8,128)(2,1)S(1)} %copy-done.13, bf16[512,1024]{1,0:T(8,128)(2,1)S(1)} %get-tuple-element.20.key_ref, bf16[512,1024]{1,0:T(8,128)(2,1)S(1)} %get-tuple-element.21.value_ref, bf16[512,1024]{1,0:T(8,128)(2,1)S(1)} %get-tuple-element.30.dout_ref), custom_call_target="tpu_custom_call" | custom-call | flops 1610612736 | bytes 4194304 | tf_op jit(solution)/shard_map/pallas_call | solution.py:187
  79.4 1.3 %copy-done.7 = f32[512,1024]{1,0:T(8,128)} copy-done((f32[512,1024]{1,0:T(8,128)}, f32[512,1024]{1,0:T(8,128)S(1)}, u32[]{:S(2)}) %copy-start.7) | copy-done | bytes 2097176
  80.7 1.3 %copy-done.9 = f32[512,1024]{1,0:T(8,128)} copy-done((f32[512,1024]{1,0:T(8,128)}, f32[512,1024]{1,0:T(8,128)S(1)}, u32[]{:S(2)}) %copy-start.9) | copy-done | bytes 2097176
  82.0 1.6 %copy-done.8 = f32[512,1024]{1,0:T(8,128)S(1)} copy-done((f32[512,1024]{1,0:T(8,128)S(1)}, f32[512,1024]{1,0:T(8,128)}, u32[]{:S(2)}) %copy-start.8) | copy-done | bytes 2097176
  83.6 1.6 %copy-done.10 = f32[512,1024]{1,0:T(8,128)S(1)} copy-done((f32[512,1024]{1,0:T(8,128)S(1)}, f32[512,1024]{1,0:T(8,128)}, u32[]{:S(2)}) %copy-start.10) | copy-done | bytes 2097176
  85.2 1.8 %shard_map.84 = (bf16[512,1024]{1,0:T(8,128)(2,1)}, bf16[512,1024]{1,0:T(8,128)(2,1)}) custom-call(bf16[512,1024]{1,0:T(8,128)(2,1)S(1)} %get-tuple-element.20.key_ref, bf16[512,1024]{1,0:T(8,128)(2,1)S(1)} %get-tuple-element.21.value_ref, f32[512,1024]{1,0:T(8,128)S(1)} %copy-done.8, f32[512,1024]{1,0:T(8,128)S(1)} %copy-done.10, bf16[1024,128]{1,0:T(8,128)(2,1)S(1)} %bitcast.7), custom_call_target="tpu_custom_call" | custom-call | flops 268435456 | bytes 6553600 | tf_op jit(solution)/shard_map/pallas_call | solution.py:187
  (29 shorter events, 6.2 us)
Async XLA Ops:
  0.6 22.7 %copy-start.17 = (f32[1024]{0:T(1024)S(1)}, f32[1024]{0:T(1024)}, u32[]{:S(2)}) copy-start(f32[1024]{0:T(1024)} %param.9) | copy-start | bytes 12292
  19.7 13.6 %all-to-all-start.1 = ((bf16[8,128,128]{2,1,0:T(8,128)(2,1)}), bf16[8,128,128]{2,1,0:T(8,128)(2,1)S(1)}, u32[]{:S(2)}, u32[]{:S(2)}) async-start(bf16[8,128,128]{2,1,0:T(8,128)(2,1)} %shard_map.78), calls=%async_computation.1 | async-start | bytes 524288 | tf_op jit(solution)/shard_map/all_to_all | solution.py:210
  29.7 1.3 %copy-start = (f32[512,1024]{1,0:T(8,128)}, f32[512,1024]{1,0:T(8,128)S(1)}, u32[]{:S(2)}) copy-start(f32[512,1024]{1,0:T(8,128)S(1)} %get-tuple-element.23.scaled_ref) | copy-start | bytes 6291460
  31.0 1.3 %copy-start.3 = (f32[512,1024]{1,0:T(8,128)}, f32[512,1024]{1,0:T(8,128)S(1)}, u32[]{:S(2)}) copy-start(f32[512,1024]{1,0:T(8,128)S(1)} %get-tuple-element.25.local_ref) | copy-start | bytes 6291460
  32.3 1.0 %copy-start.14 = (bf16[1024,512]{1,0:T(8,128)(2,1)}, bf16[1024,512]{1,0:T(8,128)(2,1)S(1)}, u32[]{:S(2)}) copy-start(bf16[1024,512]{1,0:T(8,128)(2,1)S(1)} %get-tuple-element.22.flipped_ref) | copy-start | bytes 3145732
  33.3 4.7 %copy-start.12 = (bf16[512,1024]{1,0:T(8,128)(2,1)}, bf16[512,1024]{1,0:T(8,128)(2,1)S(1)}, u32[]{:S(2)}) copy-start(bf16[512,1024]{1,0:T(8,128)(2,1)S(1)} %get-tuple-element.24.query_ref) | copy-start | bytes 3145732
  33.3 2.0 %copy-start.1 = (f32[512,1024]{1,0:T(8,128)S(1)}, f32[512,1024]{1,0:T(8,128)}, u32[]{:S(2)}) copy-start(f32[512,1024]{1,0:T(8,128)} %copy-done) | copy-start | bytes 6291460
  35.3 1.6 %copy-start.4 = (f32[512,1024]{1,0:T(8,128)S(1)}, f32[512,1024]{1,0:T(8,128)}, u32[]{:S(2)}) copy-start(f32[512,1024]{1,0:T(8,128)} %copy-done.3) | copy-start | bytes 6291460
  38.0 1.3 %copy-start.5 = (f32[512,1024]{1,0:T(8,128)}, f32[512,1024]{1,0:T(8,128)S(1)}, u32[]{:S(2)}) copy-start(f32[512,1024]{1,0:T(8,128)S(1)} %get-tuple-element.27.attended_ref) | copy-start | bytes 6291460
  45.2 1.6 %copy-start.2 = (f32[512,1024]{1,0:T(8,128)S(1)}, f32[512,1024]{1,0:T(8,128)}, u32[]{:S(2)}) copy-start(f32[512,1024]{1,0:T(8,128)} %copy-done) | copy-start | bytes 6291460
  46.8 1.6 %copy-start.6 = (f32[512,1024]{1,0:T(8,128)S(1)}, f32[512,1024]{1,0:T(8,128)}, u32[]{:S(2)}) copy-start(f32[512,1024]{1,0:T(8,128)} %copy-done.5) | copy-start | bytes 6291460
  48.4 1.2 %copy-start.15 = (bf16[1024,512]{1,0:T(8,128)(2,1)S(1)}, bf16[1024,512]{1,0:T(8,128)(2,1)}, u32[]{:S(2)}) copy-start(bf16[1024,512]{1,0:T(8,128)(2,1)} %copy-done.14) | copy-start | bytes 3145732
  50.6 0.7 copy-start.16
  51.3 14.7 %all-to-all-start.2 = ((bf16[8,128,128]{2,1,0:T(8,128)(2,1)}), bf16[8,128,128]{2,1,0:T(8,128)(2,1)}, u32[]{:S(2)}, u32[]{:S(2)}) async-start(bf16[8,128,128]{2,1,0:T(8,128)(2,1)} %bitcast.8), calls=%async_computation.2 | async-start | bytes 524288 | tf_op jit(solution)/shard_map/all_to_all | solution.py:210
  67.0 0.7 copy-start.11
  67.7 14.3 %all-to-all-start.3 = ((bf16[8,128,128]{2,1,0:T(8,128)(2,1)}), bf16[8,128,128]{2,1,0:T(8,128)(2,1)S(1)}, u32[]{:S(2)}, u32[]{:S(2)}) async-start(bf16[8,128,128]{2,1,0:T(8,128)(2,1)} %copy-done.11), calls=%async_computation.3 | async-start | bytes 524288 | tf_op jit(solution)/shard_map/all_to_all | solution.py:210
  71.3 1.2 %copy-start.13 = (bf16[512,1024]{1,0:T(8,128)(2,1)S(1)}, bf16[512,1024]{1,0:T(8,128)(2,1)}, u32[]{:S(2)}) copy-start(bf16[512,1024]{1,0:T(8,128)(2,1)} %copy-done.12) | copy-start | bytes 3145732
  79.4 1.3 %copy-start.7 = (f32[512,1024]{1,0:T(8,128)}, f32[512,1024]{1,0:T(8,128)S(1)}, u32[]{:S(2)}) copy-start(f32[512,1024]{1,0:T(8,128)S(1)} %get-tuple-element.32.key_part) | copy-start | bytes 6291460
  80.7 1.3 %copy-start.9 = (f32[512,1024]{1,0:T(8,128)}, f32[512,1024]{1,0:T(8,128)S(1)}, u32[]{:S(2)}) copy-start(f32[512,1024]{1,0:T(8,128)S(1)} %get-tuple-element.33.value_part) | copy-start | bytes 6291460
  82.0 1.6 %copy-start.8 = (f32[512,1024]{1,0:T(8,128)S(1)}, f32[512,1024]{1,0:T(8,128)}, u32[]{:S(2)}) copy-start(f32[512,1024]{1,0:T(8,128)} %copy-done.7) | copy-start | bytes 6291460
  83.6 1.6 %copy-start.10 = (f32[512,1024]{1,0:T(8,128)S(1)}, f32[512,1024]{1,0:T(8,128)}, u32[]{:S(2)}) copy-start(f32[512,1024]{1,0:T(8,128)} %copy-done.9) | copy-start | bytes 6291460

commit v6 on v5

v6 whole, which is shorter than its diff:
```python
import functools

import jax
import jax.numpy as jnp
from jax import lax
from jax.experimental import pallas as pl
from jax.experimental.pallas import tpu as pltpu
from jax.sharding import PartitionSpec as P

HEAD_DIM = 128
BLOCK = 256
COPY_COLS = 256
EPSILON = 1e-06
MIB = 1 << 20


def mm(a, b):
    return lax.dot_general(a, b, (((1,), (0,)), ((), ())), preferred_element_type=jnp.float32)


def mm_nt(a, b):
    return lax.dot_general(a, b, (((1,), (1,)), ((), ())), preferred_element_type=jnp.float32)


def mm_tn(a, b):
    return lax.dot_general(a, b, (((0,), (0,)), ((), ())), preferred_element_type=jnp.float32)


def pieces_of(ref, size):
    return [slice(at, at + size) for at in range(0, ref.shape[1], size)]


def masked(scores, row_start, col_start, rows_first):
    rows = row_start + lax.broadcasted_iota(jnp.int32, scores.shape, 0)
    cols = col_start + lax.broadcasted_iota(jnp.int32, scores.shape, 1)
    keep = rows >= cols if rows_first else cols >= rows
    return jnp.where(keep, scores, 0.0).astype(jnp.bfloat16)


def column_copies(source, target, sems):
    copies = []
    for index, cols in enumerate(pieces_of(source, COPY_COLS)):
        copies.append(pltpu.make_async_copy(source.at[:, cols], target.at[:, cols], sems.at[index]))
    return copies


def start_all(*groups):
    for parts in zip(*groups):
        for part in parts:
            part.start()


def wait_all(*groups):
    for group in groups:
        for part in group:
            part.wait()


def whole_copy(source, target, sem):
    return pltpu.make_async_copy(source, target, sem)


def states_body(key_hbm, value_hbm, state_ref, key_ref, value_ref, key_sems, value_sems):
    key_copies = column_copies(key_hbm, key_ref, key_sems)
    value_copies = column_copies(value_hbm, value_ref, value_sems)
    start_all(key_copies, value_copies)
    for index, cols in enumerate(pieces_of(key_ref, COPY_COLS)):
        key_copies[index].wait()
        value_copies[index].wait()
        for start in range(cols.start, cols.stop, HEAD_DIM):
            head = slice(start, start + HEAD_DIM)
            state_ref[head, :] = mm_tn(key_ref[:, head], value_ref[:, head]).astype(jnp.bfloat16)


def local_body(
    query_hbm, key_hbm, value_hbm, grad_hbm,
    flipped_hbm, grad_flipped_hbm, flipped_ref, local_ref,
    query_ref, key_ref, value_ref, grad_ref, rest_ref, grad_flipped_ref, in_sems, out_sems,
):
    rows = query_ref.shape[0]
    sources = (query_hbm, key_hbm, value_hbm, grad_hbm)
    targets = (query_ref, key_ref, value_ref, grad_ref)
    loads = [whole_copy(a, b, in_sems.at[i]) for i, (a, b) in enumerate(zip(sources, targets))]
    start_all(loads)
    wait_all(loads)

    def one(head, target, row):
        cols = pl.ds(pl.multiple_of(head * HEAD_DIM, HEAD_DIM), HEAD_DIM)
        target[pl.ds(pl.multiple_of(row, HEAD_DIM), HEAD_DIM), :] = query_ref[:, cols].T
        grad_flipped_ref[cols, :] = grad_ref[:, cols].T
        value_flipped = value_ref[:, cols].T
        for start in range(0, rows, BLOCK):
            end = start + BLOCK
            scores = mm_nt(query_ref[start:end, cols], key_ref[:end, cols])
            weights = masked(scores, start, 0, True)
            local_ref[cols, start:end] = mm_nt(value_flipped[:, :end], weights)

    kept = flipped_ref.shape[0]

    @pl.loop(0, kept // HEAD_DIM)
    def _(head):
        one(head, flipped_ref, head * HEAD_DIM)

    @pl.loop(kept // HEAD_DIM, query_ref.shape[1] // HEAD_DIM)
    def _(head):
        one(head, rest_ref, head * HEAD_DIM - kept)

    stores = [
        whole_copy(flipped_ref, flipped_hbm.at[:kept, :], out_sems.at[0]),
        whole_copy(rest_ref, flipped_hbm.at[kept:, :], out_sems.at[1]),
        whole_copy(grad_flipped_ref, grad_flipped_hbm, out_sems.at[2]),
    ]
    start_all(stores)
    wait_all(stores)


def scan_body(reverse, block_ref, state_ref):
    count = block_ref.shape[0]
    total = jnp.zeros(block_ref.shape[1:], jnp.float32)
    order = range(count - 1, -1, -1) if reverse else range(count)
    for place in order:
        state_ref[place] = total.astype(jnp.bfloat16)
        total = total + block_ref[place].astype(jnp.float32)


def heads_of(ref):
    return [slice(at, at + HEAD_DIM) for at in range(0, ref.shape[0], HEAD_DIM)]


def scaled_grad(gain_ref, grad_ref, head):
    gain = jnp.broadcast_to(gain_ref[:, head], (HEAD_DIM, HEAD_DIM)).T
    gain = jnp.concatenate([gain] * (grad_ref.shape[1] // HEAD_DIM), axis=1)
    return gain * grad_ref[head, :].astype(jnp.float32)


def fold(values):
    parts = [values[at : at + 8, :] for at in range(0, values.shape[0], 8)]
    while len(parts) > 1:
        parts = [sum(parts[at + 1 : at + 2], parts[at]) for at in range(0, len(parts), 2)]
    return parts[0]


def sums_body(
    flipped_hbm, grad_hbm, gain_ref, flipped_ref, local_ref, state_ref,
    attended_ref, grad_ref, sums_ref, rest_ref, sems,
):
    kept = flipped_ref.shape[0]
    rest = whole_copy(flipped_hbm.at[kept:, :], rest_ref, sems.at[0])
    grad = whole_copy(grad_hbm, grad_ref, sems.at[1])
    rest.start()
    grad.start()
    square = cross = jnp.zeros((8, local_ref.shape[1]), jnp.float32)
    for head in heads_of(local_ref):
        if head.start == kept:
            rest.wait()
        if head.start < kept:
            flipped = flipped_ref[head, :]
        else:
            flipped = rest_ref[head.start - kept : head.stop - kept, :]
        attended = local_ref[head, :] + mm_tn(state_ref[head, :], flipped)
        attended_ref[head, :] = attended
        square += fold(attended * attended)
    grad.wait()
    for head in heads_of(local_ref):
        cross += fold(scaled_grad(gain_ref, grad_ref, head) * attended_ref[head, :])
    sums_ref[0:1, :] = jnp.sum(square, axis=0, keepdims=True)
    sums_ref[1:2, :] = jnp.sum(cross, axis=0, keepdims=True)


def dout_body(
    width, flipped_hbm, gain_ref, grad_ref, attended_ref, sums_ref, dout_ref, own_ref, flipped_ref, sems
):
    half = flipped_ref.shape[0] // 2
    halves = (slice(0, half), slice(half, 2 * half))
    loads = [
        whole_copy(flipped_hbm.at[part, :], flipped_ref.at[part, :], sems.at[index])
        for index, part in enumerate(halves)
    ]
    start_all(loads)
    inverse = 1.0 / jnp.sqrt(sums_ref[0:1, :] / width + EPSILON)
    drop = sums_ref[1:2, :] * (inverse * inverse * inverse) / width
    for head in heads_of(dout_ref):
        dout = scaled_grad(gain_ref, grad_ref, head) * inverse - attended_ref[head, :] * drop
        dout_ref[head, :] = dout.astype(jnp.bfloat16)
    for index, part in enumerate(halves):
        loads[index].wait()
        for start in range(part.start, part.stop, HEAD_DIM):
            head = slice(start, start + HEAD_DIM)
            own_ref[head, :] = mm_nt(flipped_ref[head, :], dout_ref[head, :]).astype(jnp.bfloat16)


def query_body(
    key_hbm, value_hbm, flipped_ref, state_ref, out_hbm, dout_ref, key_ref, value_ref, out_ref, in_sems, sems
):
    rows = dout_ref.shape[0]
    loads = [
        whole_copy(key_hbm, key_ref, in_sems.at[0]),
        whole_copy(value_hbm, value_ref, in_sems.at[1]),
    ]
    start_all(loads)
    for head in heads_of(flipped_ref):
        dout_ref[:, head] = flipped_ref[head, :].T
    wait_all(loads)

    @pl.loop(0, dout_ref.shape[1] // HEAD_DIM)
    def _(head):
        cols = pl.ds(pl.multiple_of(head * HEAD_DIM, HEAD_DIM), HEAD_DIM)
        for start in range(0, rows, BLOCK):
            end = start + BLOCK
            dout = dout_ref[start:end, cols]
            dscore = masked(mm_nt(dout, value_ref[:end, cols]), start, 0, True)
            grad = mm(dscore, key_ref[:end, cols]) + mm_nt(dout, state_ref[cols, :])
            out_ref[start:end, cols] = grad.astype(jnp.bfloat16)

    stores = column_copies(out_ref, out_hbm, sems)
    start_all(stores)
    wait_all(stores)


def inner_body(
    query_hbm, key_hbm, value_hbm, dout_ref, key_out, value_out, kept_ref, query_ref, key_ref, value_ref, sems
):
    rows = dout_ref.shape[0]
    loads = [
        whole_copy(query_hbm, query_ref, sems.at[0]),
        whole_copy(key_hbm, key_ref, sems.at[1]),
        whole_copy(value_hbm, value_ref, sems.at[2]),
        whole_copy(value_hbm.at[:, : kept_ref.shape[1]], kept_ref, sems.at[3]),
    ]
    start_all(loads)
    wait_all(loads)

    @pl.loop(0, dout_ref.shape[1] // HEAD_DIM)
    def _(head):
        cols = pl.ds(pl.multiple_of(head * HEAD_DIM, HEAD_DIM), HEAD_DIM)
        for start in range(0, rows, BLOCK):
            end = start + BLOCK
            query = query_ref[start:, cols]
            dout = dout_ref[start:, cols]
            dscore = masked(mm_nt(value_ref[start:end, cols], dout), 0, 0, False)
            key_out[start:end, cols] = mm(dscore, query).astype(jnp.bfloat16)
            weights = masked(mm_nt(key_ref[start:end, cols], query), 0, 0, False)
            value_out[start:end, cols] = mm(weights, dout).astype(jnp.bfloat16)


def final_body(
    key_hbm, value_hbm, kept_ref, key_part, value_part, state_ref, key_out_hbm, value_out_hbm,
    key_ref, rest_ref, key_out, value_out, key_sems, value_sems, in_sems,
):
    kept = kept_ref.shape[1]
    rest = whole_copy(value_hbm.at[:, kept:], rest_ref, in_sems.at[0])
    keys = column_copies(key_hbm, key_ref, in_sems.at[1:])
    rest.start()
    start_all(keys)
    key_stores = column_copies(key_out, key_out_hbm, key_sems)
    value_stores = column_copies(value_out, value_out_hbm, value_sems)
    for index, step in enumerate(pieces_of(key_out, COPY_COLS)):
        if step.start == kept:
            rest.wait()
        for left in range(step.start, step.stop, HEAD_DIM):
            cols = slice(left, left + HEAD_DIM)
            if left < kept:
                value = kept_ref[:, cols]
            else:
                value = rest_ref[:, left - kept : left - kept + HEAD_DIM]
            grad = key_part[:, cols].astype(jnp.float32) + mm_nt(value, state_ref[cols, :])
            key_out[:, cols] = grad.astype(jnp.bfloat16)
        key_stores[index].start()
    for index, step in enumerate(pieces_of(value_out, COPY_COLS)):
        keys[index].wait()
        for left in range(step.start, step.stop, HEAD_DIM):
            cols = slice(left, left + HEAD_DIM)
            grad = value_part[:, cols].astype(jnp.float32) + mm(key_ref[:, cols], state_ref[cols, :])
            value_out[:, cols] = grad.astype(jnp.bfloat16)
        value_stores[index].start()
    wait_all(key_stores, value_stores)


def local_call(body, in_args, outs, flops, hbm_args=(), scratch=(), aliases=None):
    args = [pltpu.with_memory_space_constraint(a, pltpu.HBM) for a in hbm_args]
    args += [pltpu.with_memory_space_constraint(a, pltpu.VMEM) for a in in_args]
    specs = [pl.BlockSpec(memory_space=pltpu.HBM)] * len(hbm_args)
    specs += [pl.BlockSpec(memory_space=pltpu.VMEM)] * len(in_args)
    out_specs = []
    for out in outs:
        out_specs.append(pl.BlockSpec(memory_space=out.memory_space))
    moved = sum(a.size * a.dtype.itemsize for a in args)
    return pl.pallas_call(
        body,
        in_specs=specs,
        out_specs=out_specs,
        out_shape=outs,
        scratch_shapes=scratch,
        input_output_aliases=aliases or {},
        compiler_params=pltpu.CompilerParams(vmem_limit_bytes=16 * MIB),
        cost_estimate=pl.CostEstimate(flops=flops, bytes_accessed=moved, transcendentals=0),
    )(*args)


def scan_blocks(blocks, reverse):
    (states,) = local_call(
        functools.partial(scan_body, reverse),
        [blocks],
        [pltpu.VMEM(blocks.shape, blocks.dtype)],
        blocks.size,
    )
    return states


def exchange(pieces, axis):
    return lax.all_to_all(pieces, axis, 0, 0)


def in_pieces(state, axis):
    count = lax.axis_size(axis)
    rows, cols = state.shape
    return state.reshape(count, rows // count, cols)


def shards(queries, keys, values, out_grad, gain):
    rows, width = queries.shape
    total_width = width * lax.axis_size("head")
    bf16, f32 = jnp.bfloat16, jnp.float32
    tokens, state = (rows, width), (width, HEAD_DIM)
    small = 2 * rows * width * HEAD_DIM
    large = 2 * rows * rows * width * 3 // 4
    gain_row = gain.reshape(1, width)
    flat = (width, rows)
    dma = pltpu.SemaphoreType.DMA
    chunks = width // COPY_COLS
    kept = width * 3 // 4 // HEAD_DIM * HEAD_DIM
    half = width // 2 // COPY_COLS * COPY_COLS
    vm, hbm = pltpu.VMEM, pltpu.HBM

    (own_kv,) = local_call(
        states_body,
        [],
        [vm(state, bf16)],
        small,
        [keys, values],
        [vm(tokens, bf16)] * 2 + [dma((chunks,))] * 2,
    )
    kv_blocks = exchange(in_pieces(own_kv, "seq"), "seq")
    kv_low = exchange(scan_blocks(kv_blocks, False), "seq").reshape(state)
    flipped, grad_flipped, flipped_vm, local = local_call(
        local_body,
        [],
        [hbm(flat, bf16), hbm(flat, bf16), vm((kept, rows), bf16), vm(flat, f32)],
        2 * large,
        [queries, keys, values, out_grad],
        [vm(tokens, bf16)] * 4
        + [vm((width - kept, rows), bf16), vm(flat, bf16), dma((4,)), dma((3,))],
    )
    attended, grad_vm, sums = local_call(
        sums_body,
        [gain_row, flipped_vm, local, kv_low],
        [vm(flat, f32), vm(flat, bf16), vm((2, rows), f32)],
        small,
        [flipped, grad_flipped],
        [vm((width - kept, rows), bf16), dma((2,))],
        {4: 0},
    )
    sums = lax.psum(sums, "head")
    dout_flipped, own_grad = local_call(
        functools.partial(dout_body, total_width),
        [gain_row, grad_vm, attended, sums],
        [vm(flat, bf16), vm(state, bf16)],
        small,
        [flipped],
        [vm(flat, bf16), dma((2,))],
    )
    grad_blocks = exchange(in_pieces(own_grad, "seq"), "seq")
    query_grad, dout = local_call(
        query_body,
        [dout_flipped, kv_low],
        [hbm(tokens, bf16), vm(tokens, bf16)],
        2 * large + small,
        [keys, values],
        [vm(tokens, bf16)] * 3 + [dma((2,)), dma((chunks,))],
    )
    grad_blocks, query_grad, dout = lax.optimization_barrier((grad_blocks, query_grad, dout))
    grad_low = exchange(scan_blocks(grad_blocks, True), "seq").reshape(state)
    key_part, value_part, value_kept = local_call(
        inner_body,
        [dout],
        [vm(tokens, bf16), vm(tokens, bf16), vm((rows, half), bf16)],
        4 * large,
        [queries, keys, values],
        [vm(tokens, bf16)] * 3 + [dma((4,))],
    )
    key_grad, value_grad = local_call(
        final_body,
        [value_kept, key_part, value_part, grad_low],
        [hbm(tokens, bf16)] * 2,
        2 * small,
        [keys, values],
        [vm(tokens, bf16), vm((rows, width - half), bf16), vm(tokens, bf16), vm(tokens, bf16)]
        + [dma((chunks,))] * 2
        + [dma((chunks + 1,))],
    )
    return query_grad, key_grad, value_grad


def solution(mesh):
    return jax.shard_map(
        shards,
        mesh=mesh,
        in_specs=(
            P("seq", "head"),
            P("seq", "head"),
            P("seq", "head"),
            P("seq", "head"),
            P("head"),
        ),
        out_specs=(P("seq", "head"), P("seq", "head"), P("seq", "head")),
        check_vma=False,
    )
```

time: 87.8 us -> 80.4 us (0.916)
  local copies, waits for them, and re-layouts: 21.3 us -> 7.09 us
  Pallas kernels: 24.5 us -> 34.5 us
  waiting for transfers between devices: 5.7 us -> 0.01 us
  starting transfers between devices: 12.9 us -> 15.3 us
    unnamed x36 -> x16, local copies, waits for them, and re-layouts: 21.3 us -> 7.09 us
    pallas_call x9, Pallas kernels: 24.5 us -> 34.5 us  [local_call(): pl.pallas_call(body, in_specs=specs, out_specs=out_specs, out_shape=outs,...]
    all_to_all x3, waiting for transfers between devices: 5.7 us -> 0.01 us  [exchange(): return lax.all_to_all(pieces, axis, 0, 0)]
    all_to_all x3, starting transfers between devices: 12.9 us -> 15.3 us  [exchange(): return lax.all_to_all(pieces, axis, 0, 0)]
  transfers between devices with their start and end apart: 3 -> 3, of which waited for: 1 -> 0; matrix products, arithmetic and copies ran while one was open for 0% -> 0% of each run, Pallas kernels for 19% -> 30%
where the time goes in v6:
time: 80.4 us; the launch traced here: 79.6 us
  Pallas kernels  34.5 us (43%)
  blocking collectives  22 us (27%)
  starting transfers between devices  15.3 us (19%)
  local copies, waits for them, and re-layouts  7.09 us (9%)
    pallas_call x9, Pallas kernels, local_call(): pl.pallas_call(body, in_specs=specs, out_specs=out_specs, out_shape=outs,...  34.5 us
    all_to_all x1, blocking collectives, exchange(): return lax.all_to_all(pieces, axis, 0, 0)  16 us
    all_to_all x3, starting transfers between devices, exchange(): return lax.all_to_all(pieces, axis, 0, 0)  15.3 us
    unnamed x16, local copies, waits for them, and re-layouts  7.09 us
    psum x1, blocking collectives, shards(): sums = lax.psum(sums, 'head')  5.96 us
  transfers between devices with their start and end apart: 3, of which 0 were waited for; matrix products, arithmetic and copies ran while one was open for 0% of the time, Pallas kernels for 30%

profile of v6, /device:TPU:0, one launch (start us, length us, event | category | flops | bytes accessed | tf_op | source)
XLA Modules:
  0.0 79.6 jit_solution(4978342095127474272)
XLA Ops:
  0.6 2.3 %shard_map.77 = bf16[1024,128]{1,0:T(8,128)(2,1)S(1)} custom-call(bf16[512,1024]{1,0:T(8,128)(2,1)} %key_hbm.9, bf16[512,1024]{1,0:T(8,128)(2,1)} %value_hbm.9), custom_call_target="tpu_custom_call" | custom-call | flops 134217728 | bytes 2097152 | tf_op jit(solution)/shard_map/pallas_call | solution.py:288
  3.0 16.0 %all_to_all.20.block_ref = bf16[8,128,128]{2,1,0:T(8,128)(2,1)S(1)} all-to-all(bf16[8,128,128]{2,1,0:T(8,128)(2,1)S(1)} %bitcast.8), channel_id=1, replica_groups=mesh['seq'=8,'head'=4] {'seq'}, dimensions={0} | all-to-all | bytes 524288 | tf_op jit(solution)/shard_map/all_to_all | solution.py:311
  19.0 0.7 shard_map.78
  19.7 3.6 %all-to-all-start.1 = ((bf16[8,128,128]{2,1,0:T(8,128)(2,1)}), bf16[8,128,128]{2,1,0:T(8,128)(2,1)S(1)}, u32[]{:S(2)}, u32[]{:S(2)}) async-start(bf16[8,128,128]{2,1,0:T(8,128)(2,1)} %shard_map.78), calls=%async_computation.1 | async-start | bytes 524288 | tf_op jit(solution)/shard_map/all_to_all | solution.py:311
  23.3 8.2 %shard_map.76 = (bf16[1024,512]{1,0:T(8,128)(2,1)}, bf16[1024,512]{1,0:T(8,128)(2,1)}, bf16[768,512]{1,0:T(8,128)(2,1)S(1)}, f32[1024,512]{1,0:T(8,128)S(1)}) custom-call(bf16[512,1024]{1,0:T(8,128)(2,1)} %query_hbm.3, bf16[512,1024]{1,0:T(8,128)(2,1)} %key_hbm.9, bf16[512,1024]{1,0:T(8,128)(2,1)} %value_hbm.9, bf16[512,1024]{1,0:T(8,128)(2,1)} %grad_hbm.1), custom_call_target="tpu_custom_call" | custom-call | flops 805306368 | bytes 4194304 | tf_op jit(solution)/shard_map/pallas_call | solution.py:288
  31.5 0.0 copy-start
  31.5 0.9 %copy-done = bf16[768,512]{1,0:T(8,128)(2,1)} copy-done((bf16[768,512]{1,0:T(8,128)(2,1)}, bf16[768,512]{1,0:T(8,128)(2,1)S(1)}, u32[]{:S(2)}) %copy-start) | copy-done | bytes 786456
  32.3 1.1 %copy-done.1 = bf16[768,512]{1,0:T(8,128)(2,1)S(1)} copy-done((bf16[768,512]{1,0:T(8,128)(2,1)S(1)}, bf16[768,512]{1,0:T(8,128)(2,1)}, u32[]{:S(2)}) %copy-start.1) | copy-done | bytes 786456
  33.5 1.7 %shard_map.79 = (f32[1024,512]{1,0:T(8,128)S(1)}, bf16[1024,512]{1,0:T(8,128)(2,1)S(1)}, f32[2,512]{1,0:T(2,128)S(1)}) custom-call(bf16[1024,512]{1,0:T(8,128)(2,1)} %get-tuple-element.22.flipped_hbm, bf16[1024,512]{1,0:T(8,128)(2,1)} %get-tuple-element.23.grad_hbm, f32[1,1024]{1,0:T(1,128)S(1)} %bitcast.10, ...), custom_call_target="tpu_custom_call", output_to_operand_aliasing={{0}: (4, {})} | custom-call | flops 134217728 | bytes 5246976 | tf_op jit(solution)/shard_map/pallas_call | solution.py:288
  35.2 6.0 %psum.7.sums_ref = f32[2,512]{1,0:T(2,128)S(1)} all-reduce(f32[2,512]{1,0:T(2,128)S(1)} %get-tuple-element.28), channel_id=1, replica_groups=mesh['seq'=8,'head'=4] {'head'}, use_global_device_ids=true, to_apply=%region_0.0 | all-reduce | flops 1024 | bytes 8192 | tf_op jit(solution)/shard_map/psum | solution.py:363
  41.1 1.7 %shard_map.80 = (bf16[1024,512]{1,0:T(8,128)(2,1)S(1)}, bf16[1024,128]{1,0:T(8,128)(2,1)S(1)}) custom-call(bf16[1024,512]{1,0:T(8,128)(2,1)} %get-tuple-element.22.flipped_hbm, f32[1,1024]{1,0:T(1,128)S(1)} %bitcast.11, bf16[1024,512]{1,0:T(8,128)(2,1)S(1)} %get-tuple-element.26.grad_ref, f32[1024,512]{1,0:T(8,128)S(1)} %get-tuple-element.27.attended_ref, ...), custom_call_target="tpu_custom_call" | custom-call | flops 134217728 | bytes 4202496 | tf_op jit(solution)/shard_map/pallas_call | solution.py:288
  42.8 0.0 copy-start.2
  42.8 0.7 copy-done.2
  43.5 1.0 %copy-done.4 = bf16[1024,512]{1,0:T(8,128)(2,1)} copy-done((bf16[1024,512]{1,0:T(8,128)(2,1)}, bf16[1024,512]{1,0:T(8,128)(2,1)S(1)}, u32[]{:S(2)}) %copy-start.4) | copy-done | bytes 1048600
  44.5 5.7 %all-to-all-start.2 = ((bf16[8,128,128]{2,1,0:T(8,128)(2,1)}), bf16[8,128,128]{2,1,0:T(8,128)(2,1)S(1)}, u32[]{:S(2)}, u32[]{:S(2)}) async-start(bf16[8,128,128]{2,1,0:T(8,128)(2,1)} %bitcast.9), calls=%async_computation.2 | async-start | bytes 524288 | tf_op jit(solution)/shard_map/all_to_all | solution.py:311
  50.2 1.2 %copy-done.5 = bf16[1024,512]{1,0:T(8,128)(2,1)S(1)} copy-done((bf16[1024,512]{1,0:T(8,128)(2,1)S(1)}, bf16[1024,512]{1,0:T(8,128)(2,1)}, u32[]{:S(2)}) %copy-start.5) | copy-done | bytes 1048600
  51.4 6.9 %shard_map.81 = (bf16[512,1024]{1,0:T(8,128)(2,1)}, bf16[512,1024]{1,0:T(8,128)(2,1)S(1)}) custom-call(bf16[512,1024]{1,0:T(8,128)(2,1)} %key_hbm.9, bf16[512,1024]{1,0:T(8,128)(2,1)} %value_hbm.9, bf16[1024,512]{1,0:T(8,128)(2,1)S(1)} %copy-done.5, bf16[1024,128]{1,0:T(8,128)(2,1)S(1)} %bitcast.6), custom_call_target="tpu_custom_call" | custom-call | flops 939524096 | bytes 3407872 | tf_op jit(solution)/shard_map/pallas_call | solution.py:288
  58.3 0.0 copy-start.6
  58.3 1.0 %copy-done.6 = bf16[512,1024]{1,0:T(8,128)(2,1)} copy-done((bf16[512,1024]{1,0:T(8,128)(2,1)}, bf16[512,1024]{1,0:T(8,128)(2,1)S(1)}, u32[]{:S(2)}) %copy-start.6) | copy-done | bytes 1048600
  59.3 0.7 shard_map.83
  60.0 6.0 %all-to-all-start.3 = ((bf16[8,128,128]{2,1,0:T(8,128)(2,1)}), bf16[8,128,128]{2,1,0:T(8,128)(2,1)S(1)}, u32[]{:S(2)}, u32[]{:S(2)}) async-start(bf16[8,128,128]{2,1,0:T(8,128)(2,1)} %shard_map.83), calls=%async_computation.3 | async-start | bytes 524288 | tf_op jit(solution)/shard_map/all_to_all | solution.py:311
  66.0 1.2 %copy-done.7 = bf16[512,1024]{1,0:T(8,128)(2,1)S(1)} copy-done((bf16[512,1024]{1,0:T(8,128)(2,1)S(1)}, bf16[512,1024]{1,0:T(8,128)(2,1)}, u32[]{:S(2)}) %copy-start.7) | copy-done | bytes 1048600
  67.2 8.9 %shard_map.82 = (bf16[512,1024]{1,0:T(8,128)(2,1)S(1)}, bf16[512,1024]{1,0:T(8,128)(2,1)S(1)}, bf16[512,512]{1,0:T(8,128)(2,1)S(1)}) custom-call(bf16[512,1024]{1,0:T(8,128)(2,1)} %query_hbm.3, bf16[512,1024]{1,0:T(8,128)(2,1)} %key_hbm.9, bf16[512,1024]{1,0:T(8,128)(2,1)} %value_hbm.9, bf16[512,1024]{1,0:T(8,128)(2,1)S(1)} %copy-done.7), custom_call_target="tpu_custom_call" | custom-call | flops 1610612736 | bytes 4194304 | tf_op jit(solution)/shard_map/pallas_call | solution.py:288
  76.2 3.4 %shard_map.84 = (bf16[512,1024]{1,0:T(8,128)(2,1)}, bf16[512,1024]{1,0:T(8,128)(2,1)}) custom-call(bf16[512,1024]{1,0:T(8,128)(2,1)} %key_hbm.9, bf16[512,1024]{1,0:T(8,128)(2,1)} %value_hbm.9, bf16[512,512]{1,0:T(8,128)(2,1)S(1)} %get-tuple-element.35.kept_ref, bf16[512,1024]{1,0:T(8,128)(2,1)S(1)} %get-tuple-element.36.key_part, ...), custom_call_target="tpu_custom_call" | custom-call | flops 268435456 | bytes 4980736 | tf_op jit(solution)/shard_map/pallas_call | solution.py:288
  (9 shorter events, 0.0 us)
Async XLA Ops:
  19.7 12.7 %all-to-all-start.1 = ((bf16[8,128,128]{2,1,0:T(8,128)(2,1)}), bf16[8,128,128]{2,1,0:T(8,128)(2,1)S(1)}, u32[]{:S(2)}, u32[]{:S(2)}) async-start(bf16[8,128,128]{2,1,0:T(8,128)(2,1)} %shard_map.78), calls=%async_computation.1 | async-start | bytes 524288 | tf_op jit(solution)/shard_map/all_to_all | solution.py:311
  23.3 9.1 %copy-start.3 = (f32[1024]{0:T(1024)S(1)}, f32[1024]{0:T(1024)}, u32[]{:S(2)}) copy-start(f32[1024]{0:T(1024)} %param.9) | copy-start | bytes 12292
  31.5 0.9 %copy-start = (bf16[768,512]{1,0:T(8,128)(2,1)}, bf16[768,512]{1,0:T(8,128)(2,1)S(1)}, u32[]{:S(2)}) copy-start(bf16[768,512]{1,0:T(8,128)(2,1)S(1)} %get-tuple-element.24.flipped_ref) | copy-start | bytes 2359300
  32.3 1.1 %copy-start.1 = (bf16[768,512]{1,0:T(8,128)(2,1)S(1)}, bf16[768,512]{1,0:T(8,128)(2,1)}, u32[]{:S(2)}) copy-start(bf16[768,512]{1,0:T(8,128)(2,1)} %copy-done) | copy-start | bytes 2359300
  42.8 0.7 copy-start.2
  43.5 1.0 %copy-start.4 = (bf16[1024,512]{1,0:T(8,128)(2,1)}, bf16[1024,512]{1,0:T(8,128)(2,1)S(1)}, u32[]{:S(2)}) copy-start(bf16[1024,512]{1,0:T(8,128)(2,1)S(1)} %get-tuple-element.30.flipped_ref) | copy-start | bytes 3145732
  44.5 14.8 %all-to-all-start.2 = ((bf16[8,128,128]{2,1,0:T(8,128)(2,1)}), bf16[8,128,128]{2,1,0:T(8,128)(2,1)S(1)}, u32[]{:S(2)}, u32[]{:S(2)}) async-start(bf16[8,128,128]{2,1,0:T(8,128)(2,1)} %bitcast.9), calls=%async_computation.2 | async-start | bytes 524288 | tf_op jit(solution)/shard_map/all_to_all | solution.py:311
  50.2 1.2 %copy-start.5 = (bf16[1024,512]{1,0:T(8,128)(2,1)S(1)}, bf16[1024,512]{1,0:T(8,128)(2,1)}, u32[]{:S(2)}) copy-start(bf16[1024,512]{1,0:T(8,128)(2,1)} %copy-done.4) | copy-start | bytes 3145732
  58.3 1.0 %copy-start.6 = (bf16[512,1024]{1,0:T(8,128)(2,1)}, bf16[512,1024]{1,0:T(8,128)(2,1)S(1)}, u32[]{:S(2)}) copy-start(bf16[512,1024]{1,0:T(8,128)(2,1)S(1)} %get-tuple-element.34.dout_ref) | copy-start | bytes 3145732
  60.0 16.2 %all-to-all-start.3 = ((bf16[8,128,128]{2,1,0:T(8,128)(2,1)}), bf16[8,128,128]{2,1,0:T(8,128)(2,1)S(1)}, u32[]{:S(2)}, u32[]{:S(2)}) async-start(bf16[8,128,128]{2,1,0:T(8,128)(2,1)} %shard_map.83), calls=%async_computation.3 | async-start | bytes 524288 | tf_op jit(solution)/shard_map/all_to_all | solution.py:311
  66.0 1.2 %copy-start.7 = (bf16[512,1024]{1,0:T(8,128)(2,1)S(1)}, bf16[512,1024]{1,0:T(8,128)(2,1)}, u32[]{:S(2)}) copy-start(bf16[512,1024]{1,0:T(8,128)(2,1)} %copy-done.6) | copy-start | bytes 3145732

commit v7 on v6

v7 whole, which is shorter than its diff:
```python
import functools

import jax
import jax.numpy as jnp
from jax import lax
from jax.experimental import pallas as pl
from jax.experimental.pallas import tpu as pltpu
from jax.sharding import PartitionSpec as P

HEAD_DIM = 128
BLOCK = 256
COPY_COLS = 256
EPSILON = 1e-06
MIB = 1 << 20


def mm(a, b):
    return lax.dot_general(a, b, (((1,), (0,)), ((), ())), preferred_element_type=jnp.float32)


def mm_nt(a, b):
    return lax.dot_general(a, b, (((1,), (1,)), ((), ())), preferred_element_type=jnp.float32)


def mm_tn(a, b):
    return lax.dot_general(a, b, (((0,), (0,)), ((), ())), preferred_element_type=jnp.float32)


def pieces_of(ref, size):
    return [slice(at, at + size) for at in range(0, ref.shape[1], size)]


def masked(scores, row_start, col_start, rows_first):
    rows = row_start + lax.broadcasted_iota(jnp.int32, scores.shape, 0)
    cols = col_start + lax.broadcasted_iota(jnp.int32, scores.shape, 1)
    keep = rows >= cols if rows_first else cols >= rows
    return jnp.where(keep, scores, 0.0).astype(jnp.bfloat16)


def column_copies(source, target, sems):
    copies = []
    for index, cols in enumerate(pieces_of(source, COPY_COLS)):
        copies.append(pltpu.make_async_copy(source.at[:, cols], target.at[:, cols], sems.at[index]))
    return copies


def start_all(*groups):
    for parts in zip(*groups):
        for part in parts:
            part.start()


def wait_all(*groups):
    for group in groups:
        for part in group:
            part.wait()


def states_body(key_hbm, value_hbm, state_ref, key_ref, value_ref, key_sems, value_sems):
    key_copies = column_copies(key_hbm, key_ref, key_sems)
    value_copies = column_copies(value_hbm, value_ref, value_sems)
    start_all(key_copies, value_copies)
    for index, cols in enumerate(pieces_of(key_ref, COPY_COLS)):
        key_copies[index].wait()
        value_copies[index].wait()
        for start in range(cols.start, cols.stop, HEAD_DIM):
            head = slice(start, start + HEAD_DIM)
            state_ref[head, :] = mm_tn(key_ref[:, head], value_ref[:, head]).astype(jnp.bfloat16)


def flip_body(query_hbm, grad_hbm, flipped_ref, grad_flipped_ref, query_ref, grad_ref, query_sems, grad_sems):
    loads = (
        (query_ref, flipped_ref, column_copies(query_hbm, query_ref, query_sems)),
        (grad_ref, grad_flipped_ref, column_copies(grad_hbm, grad_ref, grad_sems)),
    )
    start_all(loads[0][2])
    start_all(loads[1][2])
    for source, target, copies in loads:
        for copy, cols in zip(copies, pieces_of(source, COPY_COLS)):
            copy.wait()
            target[cols, :] = source[:, cols].T


def local_body(key_hbm, value_hbm, flipped_ref, local_ref, key_ref, value_ref, key_sems, value_sems):
    rows = key_ref.shape[0]
    key_copies = column_copies(key_hbm, key_ref, key_sems)
    value_copies = column_copies(value_hbm, value_ref, value_sems)
    start_all(key_copies, value_copies)
    for index, step in enumerate(pieces_of(key_ref, COPY_COLS)):
        key_copies[index].wait()
        value_copies[index].wait()
        for left in range(step.start, step.stop, HEAD_DIM):
            cols = slice(left, left + HEAD_DIM)
            for start in range(0, rows, BLOCK):
                end = start + BLOCK
                scores = mm(key_ref[:end, cols], flipped_ref[cols, start:end])
                weights = masked(scores, 0, start, False)
                local = mm_tn(value_ref[:end, cols], weights)
                local_ref[cols, start:end] = local.astype(jnp.bfloat16)


def scan_body(reverse, block_ref, state_ref):
    count = block_ref.shape[0]
    total = jnp.zeros(block_ref.shape[1:], jnp.float32)
    order = range(count - 1, -1, -1) if reverse else range(count)
    for place in order:
        state_ref[place] = total.astype(jnp.bfloat16)
        total = total + block_ref[place].astype(jnp.float32)


def heads_of(ref):
    return [slice(at, at + HEAD_DIM) for at in range(0, ref.shape[0], HEAD_DIM)]


def scaled_grad(gain_ref, grad_ref, head):
    gain = jnp.broadcast_to(gain_ref[:, head], (HEAD_DIM, HEAD_DIM)).T
    gain = jnp.concatenate([gain] * (grad_ref.shape[1] // HEAD_DIM), axis=1)
    return gain * grad_ref[head, :].astype(jnp.float32)


def fold(values):
    parts = [values[at : at + 8, :] for at in range(0, values.shape[0], 8)]
    while len(parts) > 1:
        parts = [sum(parts[at + 1 : at + 2], parts[at]) for at in range(0, len(parts), 2)]
    return parts[0]


def sums_body(gain_ref, flipped_ref, grad_ref, local_ref, state_ref, attended_ref, sums_ref):
    square = cross = jnp.zeros((8, local_ref.shape[1]), jnp.float32)
    for head in heads_of(local_ref):
        attended = mm_tn(state_ref[head, :], flipped_ref[head, :])
        attended = attended + attended_ref[head, :].astype(jnp.float32)
        attended_ref[head, :] = attended.astype(jnp.bfloat16)
        square += fold(attended * attended)
        cross += fold(scaled_grad(gain_ref, grad_ref, head) * attended)
    sums_ref[0:1, :] = jnp.sum(square, axis=0, keepdims=True)
    sums_ref[1:2, :] = jnp.sum(cross, axis=0, keepdims=True)


def dout_body(width, gain_ref, flipped_ref, grad_ref, attended_ref, sums_ref, dout_ref, own_ref):
    inverse = 1.0 / jnp.sqrt(sums_ref[0:1, :] / width + EPSILON)
    drop = sums_ref[1:2, :] * (inverse * inverse * inverse) / width
    for head in heads_of(dout_ref):
        attended = dout_ref[head, :].astype(jnp.float32)
        dout = scaled_grad(gain_ref, grad_ref, head) * inverse - attended * drop
        dout = dout.astype(jnp.bfloat16)
        dout_ref[head, :] = dout
        own_ref[head, :] = mm_nt(flipped_ref[head, :], dout).astype(jnp.bfloat16)


def query_body(
    key_hbm, value_hbm, flipped_ref, state_ref, out_hbm, dout_ref,
    key_ref, value_ref, out_ref, key_sems, value_sems, out_sems,
):
    rows = dout_ref.shape[0]
    key_copies = column_copies(key_hbm, key_ref, key_sems)
    value_copies = column_copies(value_hbm, value_ref, value_sems)
    start_all(key_copies, value_copies)
    for head in heads_of(flipped_ref):
        dout_ref[:, head] = flipped_ref[head, :].T
    stores = column_copies(out_ref, out_hbm, out_sems)
    for index, step in enumerate(pieces_of(out_ref, COPY_COLS)):
        key_copies[index].wait()
        value_copies[index].wait()
        for left in range(step.start, step.stop, HEAD_DIM):
            cols = slice(left, left + HEAD_DIM)
            for start in range(0, rows, BLOCK):
                end = start + BLOCK
                dout = dout_ref[start:end, cols]
                dscore = masked(mm_nt(dout, value_ref[:end, cols]), start, 0, True)
                grad = mm(dscore, key_ref[:end, cols]) + mm_nt(dout, state_ref[cols, :])
                out_ref[start:end, cols] = grad.astype(jnp.bfloat16)
        stores[index].start()
    wait_all(stores)


def inner_body(
    query_hbm, key_hbm, value_hbm, dout_ref, key_out, value_out, value_ref,
    query_ref, key_ref, query_sems, key_sems, value_sems,
):
    rows = value_out.shape[0]
    loads = (
        column_copies(query_hbm, query_ref, query_sems),
        column_copies(key_hbm, key_ref, key_sems),
        column_copies(value_hbm, value_ref, value_sems),
    )
    start_all(*loads)
    for index, step in enumerate(pieces_of(key_out, COPY_COLS)):
        for load in loads:
            load[index].wait()
        for left in range(step.start, step.stop, HEAD_DIM):
            cols = slice(left, left + HEAD_DIM)
            dout_all = value_out[:, cols]
            for start in range(0, rows, BLOCK):
                end = start + BLOCK
                query = query_ref[start:, cols]
                dout = dout_all[start:, :]
                dscore = masked(mm_nt(value_ref[start:end, cols], dout), 0, 0, False)
                key_out[start:end, cols] = mm(dscore, query).astype(jnp.bfloat16)
                weights = masked(mm_nt(key_ref[start:end, cols], query), 0, 0, False)
                value_out[start:end, cols] = mm(weights, dout).astype(jnp.bfloat16)


def final_body(
    key_hbm, value_ref, key_part, value_part, state_ref, key_out_hbm, value_out_hbm,
    key_ref, key_out, value_out, in_sems, key_sems, value_sems,
):
    keys = column_copies(key_hbm, key_ref, in_sems)
    start_all(keys)
    key_stores = column_copies(key_out, key_out_hbm, key_sems)
    value_stores = column_copies(value_out, value_out_hbm, value_sems)
    for index, step in enumerate(pieces_of(key_out, COPY_COLS)):
        for left in range(step.start, step.stop, HEAD_DIM):
            cols = slice(left, left + HEAD_DIM)
            grad = key_part[:, cols].astype(jnp.float32) + mm_nt(value_ref[:, cols], state_ref[cols, :])
            key_out[:, cols] = grad.astype(jnp.bfloat16)
        key_stores[index].start()
    for index, step in enumerate(pieces_of(value_out, COPY_COLS)):
        keys[index].wait()
        for left in range(step.start, step.stop, HEAD_DIM):
            cols = slice(left, left + HEAD_DIM)
            grad = value_part[:, cols].astype(jnp.float32) + mm(key_ref[:, cols], state_ref[cols, :])
            value_out[:, cols] = grad.astype(jnp.bfloat16)
        value_stores[index].start()
    wait_all(key_stores, value_stores)


def local_call(body, in_args, outs, flops, hbm_args=(), scratch=(), aliases=None):
    args = [pltpu.with_memory_space_constraint(a, pltpu.HBM) for a in hbm_args]
    args += [pltpu.with_memory_space_constraint(a, pltpu.VMEM) for a in in_args]
    specs = [pl.BlockSpec(memory_space=pltpu.HBM)] * len(hbm_args)
    specs += [pl.BlockSpec(memory_space=pltpu.VMEM)] * len(in_args)
    out_specs = []
    for out in outs:
        out_specs.append(pl.BlockSpec(memory_space=out.memory_space))
    moved = sum(a.size * a.dtype.itemsize for a in args)
    return pl.pallas_call(
        body,
        in_specs=specs,
        out_specs=out_specs,
        out_shape=outs,
        scratch_shapes=scratch,
        input_output_aliases=aliases or {},
        compiler_params=pltpu.CompilerParams(vmem_limit_bytes=16 * MIB),
        cost_estimate=pl.CostEstimate(flops=flops, bytes_accessed=moved, transcendentals=0),
    )(*args)


def scan_blocks(blocks, reverse):
    (states,) = local_call(
        functools.partial(scan_body, reverse),
        [blocks],
        [pltpu.VMEM(blocks.shape, blocks.dtype)],
        blocks.size,
    )
    return states


def exchange(pieces, axis):
    return lax.all_to_all(pieces, axis, 0, 0)


def in_pieces(state, axis):
    count = lax.axis_size(axis)
    rows, cols = state.shape
    return state.reshape(count, rows // count, cols)


def shards(queries, keys, values, out_grad, gain):
    rows, width = queries.shape
    total_width = width * lax.axis_size("head")
    bf16, f32 = jnp.bfloat16, jnp.float32
    tokens, state = (rows, width), (width, HEAD_DIM)
    small = 2 * rows * width * HEAD_DIM
    large = 2 * rows * rows * width * 3 // 4
    gain_row = gain.reshape(1, width)
    flat = (width, rows)
    chunks = pltpu.SemaphoreType.DMA((width // COPY_COLS,))
    vm, hbm = pltpu.VMEM, pltpu.HBM
    rows_vm, flat_vm, state_vm = vm(tokens, bf16), vm(flat, bf16), vm(state, bf16)

    (own_kv,) = local_call(
        states_body, [], [state_vm], small, [keys, values], [rows_vm] * 2 + [chunks] * 2
    )
    kv_blocks = exchange(in_pieces(own_kv, "seq"), "seq")
    flipped, grad_flipped = local_call(
        flip_body, [], [flat_vm] * 2, large, [queries, out_grad], [rows_vm] * 2 + [chunks] * 2
    )
    kv_blocks, flipped, grad_flipped = lax.optimization_barrier((kv_blocks, flipped, grad_flipped))
    kv_low = exchange(scan_blocks(kv_blocks, False), "seq").reshape(state)
    (local,) = local_call(
        local_body, [flipped], [flat_vm], 2 * large, [keys, values], [rows_vm] * 2 + [chunks] * 2
    )
    attended, sums = local_call(
        sums_body,
        [gain_row, flipped, grad_flipped, local, kv_low],
        [flat_vm, vm((2, rows), f32)],
        small,
        aliases={3: 0},
    )
    sums = lax.psum(sums, "head")
    dout_flipped, own_grad = local_call(
        functools.partial(dout_body, total_width),
        [gain_row, flipped, grad_flipped, attended, sums],
        [flat_vm, state_vm],
        small,
        aliases={3: 0},
    )
    grad_blocks = exchange(in_pieces(own_grad, "seq"), "seq")
    query_grad, dout = local_call(
        query_body,
        [dout_flipped, kv_low],
        [hbm(tokens, bf16), rows_vm],
        2 * large + small,
        [keys, values],
        [rows_vm] * 3 + [chunks] * 3,
    )
    grad_blocks, query_grad, dout = lax.optimization_barrier((grad_blocks, query_grad, dout))
    grad_low = exchange(scan_blocks(grad_blocks, True), "seq").reshape(state)
    key_part, value_part, value_kept = local_call(
        inner_body,
        [dout],
        [rows_vm] * 3,
        4 * large,
        [queries, keys, values],
        [rows_vm] * 2 + [chunks] * 3,
        {3: 1},
    )
    key_grad, value_grad = local_call(
        final_body,
        [value_kept, key_part, value_part, grad_low],
        [hbm(tokens, bf16)] * 2,
        2 * small,
        [keys],
        [rows_vm] * 3 + [chunks] * 3,
    )
    return query_grad, key_grad, value_grad


def solution(mesh):
    return jax.shard_map(
        shards,
        mesh=mesh,
        in_specs=(
            P("seq", "head"),
            P("seq", "head"),
            P("seq", "head"),
            P("seq", "head"),
            P("head"),
        ),
        out_specs=(P("seq", "head"), P("seq", "head"), P("seq", "head")),
        check_vma=False,
    )
```

time: 80.4 us -> 70 us (0.87)
  blocking collectives: 22 us -> 5.67 us
  waiting for transfers between devices: 0.01 us -> 15.7 us
  Pallas kernels: 34.5 us -> 27.8 us
  local copies, waits for them, and re-layouts: 7.09 us -> 0.7 us
  starting transfers between devices: 15.3 us -> 18.5 us
    all_to_all x1 -> x0, blocking collectives: 16 us -> none  [exchange(): return lax.all_to_all(pieces, axis, 0, 0)]
    all_to_all x3 -> x4, waiting for transfers between devices: 0.01 us -> 15.7 us  [exchange(): return lax.all_to_all(pieces, axis, 0, 0)]
    pallas_call x9 -> x10, Pallas kernels: 34.5 us -> 27.8 us  [local_call(): pl.pallas_call(body, in_specs=specs, out_specs=out_specs, out_shape=outs,...]
    unnamed x16 -> x4, local copies, waits for them, and re-layouts: 7.09 us -> 0.7 us
    all_to_all x3 -> x4, starting transfers between devices: 15.3 us -> 18.5 us  [exchange(): return lax.all_to_all(pieces, axis, 0, 0)]
  transfers between devices with their start and end apart: 3 -> 4, of which waited for: 0 -> 4; matrix products, arithmetic and copies ran while one was open for 0% -> 0% of each run, Pallas kernels for 30% -> 27%
where the time goes in v7:
time: 70 us; the launch traced here: 69.3 us
  Pallas kernels  27.8 us (40%)
  starting transfers between devices  18.5 us (26%)
  waiting for transfers between devices  15.7 us (22%)
  blocking collectives  5.67 us (8%)
  between operations  0.87 us (1%)
    pallas_call x10, Pallas kernels, local_call(): pl.pallas_call(body, in_specs=specs, out_specs=out_specs, out_shape=outs,...  27.8 us
    all_to_all x4, starting transfers between devices, exchange(): return lax.all_to_all(pieces, axis, 0, 0)  18.5 us
    all_to_all x4, waiting for transfers between devices, exchange(): return lax.all_to_all(pieces, axis, 0, 0)  15.7 us
    psum x1, blocking collectives, shards(): sums = lax.psum(sums, 'head')  5.67 us
  transfers between devices with their start and end apart: 4, of which 4 were waited for; matrix products, arithmetic and copies ran while one was open for 0% of the time, Pallas kernels for 27%

profile of v7, /device:TPU:0, one launch (start us, length us, event | category | flops | bytes accessed | tf_op | source)
XLA Modules:
  0.0 69.3 jit_solution(80838001542535054)
XLA Ops:
  0.6 3.0 %shard_map.76 = bf16[1024,128]{1,0:T(8,128)(2,1)} custom-call(bf16[512,1024]{1,0:T(8,128)(2,1)} %key_hbm.9, bf16[512,1024]{1,0:T(8,128)(2,1)} %value_hbm.7), custom_call_target="tpu_custom_call" | custom-call | flops 134217728 | bytes 2097152 | tf_op jit(solution)/shard_map/pallas_call | solution.py:237
  3.7 7.3 %all-to-all-start = ((bf16[8,128,128]{2,1,0:T(8,128)(2,1)}), bf16[8,128,128]{2,1,0:T(8,128)(2,1)S(1)}, u32[]{:S(2)}, u32[]{:S(2)}) async-start(bf16[8,128,128]{2,1,0:T(8,128)(2,1)} %bitcast.1), calls=%async_computation | async-start | bytes 524288 | tf_op jit(solution)/shard_map/all_to_all | solution.py:260
  11.0 2.1 %shard_map.77 = (bf16[1024,512]{1,0:T(8,128)(2,1)S(1)}, bf16[1024,512]{1,0:T(8,128)(2,1)S(1)}) custom-call(bf16[512,1024]{1,0:T(8,128)(2,1)} %query_hbm.3, bf16[512,1024]{1,0:T(8,128)(2,1)} %grad_hbm.1), custom_call_target="tpu_custom_call" | custom-call | flops 402653184 | bytes 2097152 | tf_op jit(solution)/shard_map/pallas_call | solution.py:237
  13.1 6.8 %all-to-all-done.block_ref = bf16[8,128,128]{2,1,0:T(8,128)(2,1)S(1)} async-done(((bf16[8,128,128]{2,1,0:T(8,128)(2,1)}), bf16[8,128,128]{2,1,0:T(8,128)(2,1)S(1)}, u32[]{:S(2)}, u32[]{:S(2)}) %all-to-all-start) | async-done | bytes 262176 | tf_op jit(solution)/shard_map/all_to_all | solution.py:260
  19.9 0.7 %shard_map.79 = bf16[8,128,128]{2,1,0:T(8,128)(2,1)} custom-call(bf16[8,128,128]{2,1,0:T(8,128)(2,1)S(1)} %all-to-all-done.block_ref), custom_call_target="tpu_custom_call" | custom-call | flops 131072 | bytes 262144 | tf_op jit(solution)/shard_map/pallas_call | solution.py:237
  20.6 3.6 %all-to-all-start.1 = ((bf16[8,128,128]{2,1,0:T(8,128)(2,1)}), bf16[8,128,128]{2,1,0:T(8,128)(2,1)S(1)}, u32[]{:S(2)}, u32[]{:S(2)}) async-start(bf16[8,128,128]{2,1,0:T(8,128)(2,1)} %shard_map.79), calls=%async_computation.1 | async-start | bytes 524288 | tf_op jit(solution)/shard_map/all_to_all | solution.py:260
  24.2 0.0 copy-start.1
  24.2 4.7 %shard_map.78.local_ref = bf16[1024,512]{1,0:T(8,128)(2,1)S(1)} custom-call(bf16[512,1024]{1,0:T(8,128)(2,1)} %key_hbm.9, bf16[512,1024]{1,0:T(8,128)(2,1)} %value_hbm.7, bf16[1024,512]{1,0:T(8,128)(2,1)S(1)} %get-tuple-element.24.flipped_ref), custom_call_target="tpu_custom_call" | custom-call | flops 805306368 | bytes 3145728 | tf_op jit(solution)/shard_map/pallas_call | solution.py:237
  28.9 3.9 %all-to-all-done.1 = bf16[8,128,128]{2,1,0:T(8,128)(2,1)S(1)} async-done(((bf16[8,128,128]{2,1,0:T(8,128)(2,1)}), bf16[8,128,128]{2,1,0:T(8,128)(2,1)S(1)}, u32[]{:S(2)}, u32[]{:S(2)}) %all-to-all-start.1) | async-done | bytes 262176 | tf_op jit(solution)/shard_map/all_to_all | solution.py:260
  32.8 0.0 copy-done.1
  32.8 0.8 %shard_map.80 = (bf16[1024,512]{1,0:T(8,128)(2,1)S(1)}, f32[2,512]{1,0:T(2,128)S(1)}) custom-call(f32[1,1024]{1,0:T(1,128)S(1)} %bitcast.9, bf16[1024,512]{1,0:T(8,128)(2,1)S(1)} %get-tuple-element.24.flipped_ref, bf16[1024,512]{1,0:T(8,128)(2,1)S(1)} %get-tuple-element.25.grad_ref, ...), custom_call_target="tpu_custom_call", output_to_operand_aliasing={{0}: (3, {})} | custom-call | flops 134217728 | bytes 3411968 | tf_op jit(solution)/shard_map/pallas_call | solution.py:237
  33.6 5.7 %psum.7.sums_ref = f32[2,512]{1,0:T(2,128)S(1)} all-reduce(f32[2,512]{1,0:T(2,128)S(1)} %get-tuple-element.28), channel_id=1, replica_groups=mesh['seq'=8,'head'=4] {'head'}, use_global_device_ids=true, to_apply=%region_0.0 | all-reduce | flops 1024 | bytes 8192 | tf_op jit(solution)/shard_map/psum | solution.py:301
  39.3 0.8 %shard_map.81 = (bf16[1024,512]{1,0:T(8,128)(2,1)S(1)}, bf16[1024,128]{1,0:T(8,128)(2,1)S(1)}) custom-call(f32[1,1024]{1,0:T(1,128)S(1)} %bitcast.10, bf16[1024,512]{1,0:T(8,128)(2,1)S(1)} %get-tuple-element.24.flipped_ref, bf16[1024,512]{1,0:T(8,128)(2,1)S(1)} %get-tuple-element.25.grad_ref, ...), custom_call_target="tpu_custom_call", output_to_operand_aliasing={{0}: (3, {})} | custom-call | flops 134217728 | bytes 3153920 | tf_op jit(solution)/shard_map/pallas_call | solution.py:237
  40.1 0.0 copy-start
  40.1 0.7 %copy-done = bf16[1024,128]{1,0:T(8,128)(2,1)} copy-done((bf16[1024,128]{1,0:T(8,128)(2,1)}, bf16[1024,128]{1,0:T(8,128)(2,1)S(1)}, u32[]{:S(2)}) %copy-start) | copy-done | bytes 262168
  40.8 4.0 %all-to-all-start.2 = ((bf16[8,128,128]{2,1,0:T(8,128)(2,1)}), bf16[8,128,128]{2,1,0:T(8,128)(2,1)S(1)}, u32[]{:S(2)}, u32[]{:S(2)}) async-start(bf16[8,128,128]{2,1,0:T(8,128)(2,1)} %bitcast.8), calls=%async_computation.2 | async-start | bytes 524288 | tf_op jit(solution)/shard_map/all_to_all | solution.py:260
  44.8 5.2 %shard_map.82 = (bf16[512,1024]{1,0:T(8,128)(2,1)}, bf16[512,1024]{1,0:T(8,128)(2,1)S(1)}) custom-call(bf16[512,1024]{1,0:T(8,128)(2,1)} %key_hbm.9, bf16[512,1024]{1,0:T(8,128)(2,1)} %value_hbm.7, bf16[1024,512]{1,0:T(8,128)(2,1)S(1)} %get-tuple-element.30.flipped_ref, bf16[1024,128]{1,0:T(8,128)(2,1)S(1)} %bitcast.7), custom_call_target="tpu_custom_call" | custom-call | flops 939524096 | bytes 3407872 | tf_op jit(solution)/shard_map/pallas_call | solution.py:237
  50.0 3.3 %all-to-all-done.2.block_ref = bf16[8,128,128]{2,1,0:T(8,128)(2,1)S(1)} async-done(((bf16[8,128,128]{2,1,0:T(8,128)(2,1)}), bf16[8,128,128]{2,1,0:T(8,128)(2,1)S(1)}, u32[]{:S(2)}, u32[]{:S(2)}) %all-to-all-start.2) | async-done | bytes 262176 | tf_op jit(solution)/shard_map/all_to_all | solution.py:260
  53.3 0.7 %shard_map.84 = bf16[8,128,128]{2,1,0:T(8,128)(2,1)} custom-call(bf16[8,128,128]{2,1,0:T(8,128)(2,1)S(1)} %all-to-all-done.2.block_ref), custom_call_target="tpu_custom_call" | custom-call | flops 131072 | bytes 262144 | tf_op jit(solution)/shard_map/pallas_call | solution.py:237
  54.1 3.6 %all-to-all-start.3 = ((bf16[8,128,128]{2,1,0:T(8,128)(2,1)}), bf16[8,128,128]{2,1,0:T(8,128)(2,1)S(1)}, u32[]{:S(2)}, u32[]{:S(2)}) async-start(bf16[8,128,128]{2,1,0:T(8,128)(2,1)} %shard_map.84), calls=%async_computation.3 | async-start | bytes 524288 | tf_op jit(solution)/shard_map/all_to_all | solution.py:260
  57.7 6.7 %shard_map.83 = (bf16[512,1024]{1,0:T(8,128)(2,1)S(1)}, bf16[512,1024]{1,0:T(8,128)(2,1)S(1)}, bf16[512,1024]{1,0:T(8,128)(2,1)S(1)}) custom-call(bf16[512,1024]{1,0:T(8,128)(2,1)} %query_hbm.3, bf16[512,1024]{1,0:T(8,128)(2,1)} %key_hbm.9, bf16[512,1024]{1,0:T(8,128)(2,1)} %value_hbm.7, ...), custom_call_target="tpu_custom_call", output_to_operand_aliasing={{1}: (3, {})} | custom-call | flops 1610612736 | bytes 4194304 | tf_op jit(solution)/shard_map/pallas_call | solution.py:237
  64.4 1.7 %all-to-all-done.3 = bf16[8,128,128]{2,1,0:T(8,128)(2,1)S(1)} async-done(((bf16[8,128,128]{2,1,0:T(8,128)(2,1)}), bf16[8,128,128]{2,1,0:T(8,128)(2,1)S(1)}, u32[]{:S(2)}, u32[]{:S(2)}) %all-to-all-start.3) | async-done | bytes 262176 | tf_op jit(solution)/shard_map/all_to_all | solution.py:260
  66.2 2.9 %shard_map.85 = (bf16[512,1024]{1,0:T(8,128)(2,1)}, bf16[512,1024]{1,0:T(8,128)(2,1)}) custom-call(bf16[512,1024]{1,0:T(8,128)(2,1)} %key_hbm.9, bf16[512,1024]{1,0:T(8,128)(2,1)S(1)} %get-tuple-element.35.value_ref, bf16[512,1024]{1,0:T(8,128)(2,1)S(1)} %get-tuple-element.36.key_part, bf16[512,1024]{1,0:T(8,128)(2,1)S(1)} %get-tuple-element.37.value_part, ...), custom_call_target="tpu_custom_call" | custom-call | flops 268435456 | bytes 4456448 | tf_op jit(solution)/shard_map/pallas_call | solution.py:237
Async XLA Ops:
  3.7 16.2 %all-to-all-start = ((bf16[8,128,128]{2,1,0:T(8,128)(2,1)}), bf16[8,128,128]{2,1,0:T(8,128)(2,1)S(1)}, u32[]{:S(2)}, u32[]{:S(2)}) async-start(bf16[8,128,128]{2,1,0:T(8,128)(2,1)} %bitcast.1), calls=%async_computation | async-start | bytes 524288 | tf_op jit(solution)/shard_map/all_to_all | solution.py:260
  20.6 12.2 %all-to-all-start.1 = ((bf16[8,128,128]{2,1,0:T(8,128)(2,1)}), bf16[8,128,128]{2,1,0:T(8,128)(2,1)S(1)}, u32[]{:S(2)}, u32[]{:S(2)}) async-start(bf16[8,128,128]{2,1,0:T(8,128)(2,1)} %shard_map.79), calls=%async_computation.1 | async-start | bytes 524288 | tf_op jit(solution)/shard_map/all_to_all | solution.py:260
  24.2 8.6 %copy-start.1 = (f32[1024]{0:T(1024)S(1)}, f32[1024]{0:T(1024)}, u32[]{:S(2)}) copy-start(f32[1024]{0:T(1024)} %param.9) | copy-start | bytes 12292
  40.1 0.7 %copy-start = (bf16[1024,128]{1,0:T(8,128)(2,1)}, bf16[1024,128]{1,0:T(8,128)(2,1)S(1)}, u32[]{:S(2)}) copy-start(bf16[1024,128]{1,0:T(8,128)(2,1)S(1)} %get-tuple-element.29) | copy-start | bytes 786436
  40.8 12.6 %all-to-all-start.2 = ((bf16[8,128,128]{2,1,0:T(8,128)(2,1)}), bf16[8,128,128]{2,1,0:T(8,128)(2,1)S(1)}, u32[]{:S(2)}, u32[]{:S(2)}) async-start(bf16[8,128,128]{2,1,0:T(8,128)(2,1)} %bitcast.8), calls=%async_computation.2 | async-start | bytes 524288 | tf_op jit(solution)/shard_map/all_to_all | solution.py:260
  54.1 12.1 %all-to-all-start.3 = ((bf16[8,128,128]{2,1,0:T(8,128)(2,1)}), bf16[8,128,128]{2,1,0:T(8,128)(2,1)S(1)}, u32[]{:S(2)}, u32[]{:S(2)}) async-start(bf16[8,128,128]{2,1,0:T(8,128)(2,1)} %shard_map.84), calls=%async_computation.3 | async-start | bytes 524288 | tf_op jit(solution)/shard_map/all_to_all | solution.py:260

commit v8 on v7

--- a/solution.py
+++ b/solution.py
@@ -125,7 +125,11 @@
     return parts[0]
 
 
-def sums_body(gain_ref, flipped_ref, grad_ref, local_ref, state_ref, attended_ref, sums_ref):
+def sums_body(
+    gain_ref, flipped_ref, grad_ref, local_ref, state_ref, attended_ref, sums_ref, state_hbm, sem
+):
+    copy = pltpu.make_async_copy(state_ref, state_hbm, sem.at[0])
+    copy.start()
     square = cross = jnp.zeros((8, local_ref.shape[1]), jnp.float32)
     for head in heads_of(local_ref):
         attended = mm_tn(state_ref[head, :], flipped_ref[head, :])
@@ -133,13 +137,18 @@
         attended_ref[head, :] = attended.astype(jnp.bfloat16)
         square += fold(attended * attended)
         cross += fold(scaled_grad(gain_ref, grad_ref, head) * attended)
-    sums_ref[0:1, :] = jnp.sum(square, axis=0, keepdims=True)
-    sums_ref[1:2, :] = jnp.sum(cross, axis=0, keepdims=True)
+    square = jnp.sum(square, axis=0, keepdims=True)
+    cross = jnp.sum(cross, axis=0, keepdims=True)
+    for group in range(sums_ref.shape[0]):
+        sums_ref[group, 0:1, :] = square
+        sums_ref[group, 1:2, :] = cross
+    copy.wait()
 
 
 def dout_body(width, gain_ref, flipped_ref, grad_ref, attended_ref, sums_ref, dout_ref, own_ref):
-    inverse = 1.0 / jnp.sqrt(sums_ref[0:1, :] / width + EPSILON)
-    drop = sums_ref[1:2, :] * (inverse * inverse * inverse) / width
+    sums = sum(sums_ref[group] for group in range(sums_ref.shape[0]))
+    inverse = 1.0 / jnp.sqrt(sums[0:1, :] / width + EPSILON)
+    drop = sums[1:2, :] * (inverse * inverse * inverse) / width
     for head in heads_of(dout_ref):
         attended = dout_ref[head, :].astype(jnp.float32)
         dout = scaled_grad(gain_ref, grad_ref, head) * inverse - attended * drop
@@ -149,15 +158,18 @@
 
 
 def query_body(
-    key_hbm, value_hbm, flipped_ref, state_ref, out_hbm, dout_ref,
-    key_ref, value_ref, out_ref, key_sems, value_sems, out_sems,
+    key_hbm, value_hbm, state_hbm, flipped_ref, out_hbm, dout_ref,
+    key_ref, value_ref, state_ref, out_ref, key_sems, value_sems, out_sems, state_sem,
 ):
     rows = dout_ref.shape[0]
     key_copies = column_copies(key_hbm, key_ref, key_sems)
     value_copies = column_copies(value_hbm, value_ref, value_sems)
+    state_copy = pltpu.make_async_copy(state_hbm, state_ref, state_sem.at[0])
+    state_copy.start()
     start_all(key_copies, value_copies)
     for head in heads_of(flipped_ref):
         dout_ref[:, head] = flipped_ref[head, :].T
+    state_copy.wait()
     stores = column_copies(out_ref, out_hbm, out_sems)
     for index, step in enumerate(pieces_of(out_ref, COPY_COLS)):
         key_copies[index].wait()
@@ -276,6 +288,7 @@
     gain_row = gain.reshape(1, width)
     flat = (width, rows)
     chunks = pltpu.SemaphoreType.DMA((width // COPY_COLS,))
+    one_sem = pltpu.SemaphoreType.DMA((1,))
     vm, hbm = pltpu.VMEM, pltpu.HBM
     rows_vm, flat_vm, state_vm = vm(tokens, bf16), vm(flat, bf16), vm(state, bf16)
 
@@ -291,14 +304,16 @@
     (local,) = local_call(
         local_body, [flipped], [flat_vm], 2 * large, [keys, values], [rows_vm] * 2 + [chunks] * 2
     )
-    attended, sums = local_call(
+    groups = lax.axis_size("head")
+    attended, sums, kv_copy = local_call(
         sums_body,
         [gain_row, flipped, grad_flipped, local, kv_low],
-        [flat_vm, vm((2, rows), f32)],
+        [flat_vm, vm((groups, 2, rows), f32), hbm(state, bf16)],
         small,
+        scratch=[one_sem],
         aliases={3: 0},
     )
-    sums = lax.psum(sums, "head")
+    sums = exchange(sums, "head")
     dout_flipped, own_grad = local_call(
         functools.partial(dout_body, total_width),
         [gain_row, flipped, grad_flipped, attended, sums],
@@ -309,11 +324,11 @@
     grad_blocks = exchange(in_pieces(own_grad, "seq"), "seq")
     query_grad, dout = local_call(
         query_body,
-        [dout_flipped, kv_low],
+        [dout_flipped],
         [hbm(tokens, bf16), rows_vm],
         2 * large + small,
-        [keys, values],
-        [rows_vm] * 3 + [chunks] * 3,
+        [keys, values, kv_copy],
+        [rows_vm] * 2 + [state_vm, rows_vm] + [chunks] * 3 + [one_sem],
     )
     grad_blocks, query_grad, dout = lax.optimization_barrier((grad_blocks, query_grad, dout))
     grad_low = exchange(scan_blocks(grad_blocks, True), "seq").reshape(state)

time: 70 us -> 70.7 us (1.010)
  Pallas kernels: 27.8 us -> 29 us
  blocking collectives: 5.67 us -> 6.42 us
    all_to_all x0 -> x1, blocking collectives: none -> 6.42 us  [exchange(): return lax.all_to_all(pieces, axis, 0, 0)]
    psum x1 -> x0, blocking collectives: 5.67 us -> none  [shards(): sums = lax.psum(sums, 'head')]
    pallas_call x10, Pallas kernels: 27.8 us -> 29 us  [local_call(): pl.pallas_call(body, in_specs=specs, out_specs=out_specs, out_shape=outs,...]
where the time goes in v8:
time: 70.7 us; the launch traced here: 70 us
  Pallas kernels  29 us (41%)
  starting transfers between devices  18.1 us (26%)
  waiting for transfers between devices  15.7 us (22%)
  blocking collectives  6.42 us (9%)
  between operations  0.85 us (1%)
    pallas_call x10, Pallas kernels, local_call(): pl.pallas_call(body, in_specs=specs, out_specs=out_specs, out_shape=outs,...  29 us
    all_to_all x4, starting transfers between devices, exchange(): return lax.all_to_all(pieces, axis, 0, 0)  18.1 us
    all_to_all x4, waiting for transfers between devices, exchange(): return lax.all_to_all(pieces, axis, 0, 0)  15.7 us
    all_to_all x1, blocking collectives, exchange(): return lax.all_to_all(pieces, axis, 0, 0)  6.42 us
  transfers between devices with their start and end apart: 4, of which 4 were waited for; matrix products, arithmetic and copies ran while one was open for 0% of the time, Pallas kernels for 27%

profile of v8, /device:TPU:0, one launch (start us, length us, event | category | flops | bytes accessed | tf_op | source)
XLA Modules:
  0.0 70.0 jit_solution(1869848443601808846)
XLA Ops:
  0.6 3.0 %shard_map.76 = bf16[1024,128]{1,0:T(8,128)(2,1)} custom-call(bf16[512,1024]{1,0:T(8,128)(2,1)} %key_hbm.9, bf16[512,1024]{1,0:T(8,128)(2,1)} %value_hbm.7), custom_call_target="tpu_custom_call" | custom-call | flops 134217728 | bytes 2097152 | tf_op jit(solution)/shard_map/pallas_call | solution.py:249
  3.7 7.3 %all-to-all-start = ((bf16[8,128,128]{2,1,0:T(8,128)(2,1)}), bf16[8,128,128]{2,1,0:T(8,128)(2,1)S(1)}, u32[]{:S(2)}, u32[]{:S(2)}) async-start(bf16[8,128,128]{2,1,0:T(8,128)(2,1)} %bitcast.1), calls=%async_computation | async-start | bytes 524288 | tf_op jit(solution)/shard_map/all_to_all | solution.py:272
  11.0 2.1 %shard_map.77 = (bf16[1024,512]{1,0:T(8,128)(2,1)S(1)}, bf16[1024,512]{1,0:T(8,128)(2,1)S(1)}) custom-call(bf16[512,1024]{1,0:T(8,128)(2,1)} %query_hbm.3, bf16[512,1024]{1,0:T(8,128)(2,1)} %grad_hbm.1), custom_call_target="tpu_custom_call" | custom-call | flops 402653184 | bytes 2097152 | tf_op jit(solution)/shard_map/pallas_call | solution.py:249
  13.1 6.8 %all-to-all-done.block_ref = bf16[8,128,128]{2,1,0:T(8,128)(2,1)S(1)} async-done(((bf16[8,128,128]{2,1,0:T(8,128)(2,1)}), bf16[8,128,128]{2,1,0:T(8,128)(2,1)S(1)}, u32[]{:S(2)}, u32[]{:S(2)}) %all-to-all-start) | async-done | bytes 262176 | tf_op jit(solution)/shard_map/all_to_all | solution.py:272
  19.9 0.7 %shard_map.79 = bf16[8,128,128]{2,1,0:T(8,128)(2,1)} custom-call(bf16[8,128,128]{2,1,0:T(8,128)(2,1)S(1)} %all-to-all-done.block_ref), custom_call_target="tpu_custom_call" | custom-call | flops 131072 | bytes 262144 | tf_op jit(solution)/shard_map/pallas_call | solution.py:249
  20.6 3.6 %all-to-all-start.1 = ((bf16[8,128,128]{2,1,0:T(8,128)(2,1)}), bf16[8,128,128]{2,1,0:T(8,128)(2,1)S(1)}, u32[]{:S(2)}, u32[]{:S(2)}) async-start(bf16[8,128,128]{2,1,0:T(8,128)(2,1)} %shard_map.79), calls=%async_computation.1 | async-start | bytes 524288 | tf_op jit(solution)/shard_map/all_to_all | solution.py:272
  24.2 0.0 copy-start
  24.2 4.7 %shard_map.78.local_ref = bf16[1024,512]{1,0:T(8,128)(2,1)S(1)} custom-call(bf16[512,1024]{1,0:T(8,128)(2,1)} %key_hbm.9, bf16[512,1024]{1,0:T(8,128)(2,1)} %value_hbm.7, bf16[1024,512]{1,0:T(8,128)(2,1)S(1)} %get-tuple-element.25.flipped_ref), custom_call_target="tpu_custom_call" | custom-call | flops 805306368 | bytes 3145728 | tf_op jit(solution)/shard_map/pallas_call | solution.py:249
  28.9 3.9 %all-to-all-done.1 = bf16[8,128,128]{2,1,0:T(8,128)(2,1)S(1)} async-done(((bf16[8,128,128]{2,1,0:T(8,128)(2,1)}), bf16[8,128,128]{2,1,0:T(8,128)(2,1)S(1)}, u32[]{:S(2)}, u32[]{:S(2)}) %all-to-all-start.1) | async-done | bytes 262176 | tf_op jit(solution)/shard_map/all_to_all | solution.py:272
  32.8 0.0 copy-done
  32.8 0.8 %shard_map.80 = (bf16[1024,512]{1,0:T(8,128)(2,1)S(1)}, f32[4,2,512]{2,1,0:T(2,128)S(1)}, bf16[1024,128]{1,0:T(8,128)(2,1)}) custom-call(f32[1,1024]{1,0:T(1,128)S(1)} %bitcast.7, bf16[1024,512]{1,0:T(8,128)(2,1)S(1)} %get-tuple-element.25.flipped_ref, bf16[1024,512]{1,0:T(8,128)(2,1)S(1)} %get-tuple-element.26.grad_ref, ...), custom_call_target="tpu_custom_call", output_to_operand_aliasing={{0}: (3, {})} | custom-call | flops 134217728 | bytes 3411968 | tf_op jit(solution)/shard_map/pallas_call | solution.py:249
  33.6 6.4 %all_to_all.25.sums_ref = f32[4,2,512]{2,1,0:T(2,128)S(1)} all-to-all(f32[4,2,512]{2,1,0:T(2,128)S(1)} %get-tuple-element.29), channel_id=1, replica_groups=mesh['seq'=8,'head'=4] {'head'}, dimensions={0} | all-to-all | bytes 32768 | tf_op jit(solution)/shard_map/all_to_all | solution.py:272
  40.0 1.5 %shard_map.81 = (bf16[1024,512]{1,0:T(8,128)(2,1)S(1)}, bf16[1024,128]{1,0:T(8,128)(2,1)}) custom-call(f32[1,1024]{1,0:T(1,128)S(1)} %bitcast.8, bf16[1024,512]{1,0:T(8,128)(2,1)S(1)} %get-tuple-element.25.flipped_ref, bf16[1024,512]{1,0:T(8,128)(2,1)S(1)} %get-tuple-element.26.grad_ref, ...), custom_call_target="tpu_custom_call", output_to_operand_aliasing={{0}: (3, {})} | custom-call | flops 134217728 | bytes 3166208 | tf_op jit(solution)/shard_map/pallas_call | solution.py:249
  41.5 3.6 %all-to-all-start.3 = ((bf16[8,128,128]{2,1,0:T(8,128)(2,1)}), bf16[8,128,128]{2,1,0:T(8,128)(2,1)S(1)}, u32[]{:S(2)}, u32[]{:S(2)}) async-start(bf16[8,128,128]{2,1,0:T(8,128)(2,1)} %bitcast.3), calls=%async_computation.3 | async-start | bytes 524288 | tf_op jit(solution)/shard_map/all_to_all | solution.py:272
  45.1 5.7 %shard_map.82 = (bf16[512,1024]{1,0:T(8,128)(2,1)}, bf16[512,1024]{1,0:T(8,128)(2,1)S(1)}) custom-call(bf16[512,1024]{1,0:T(8,128)(2,1)} %key_hbm.9, bf16[512,1024]{1,0:T(8,128)(2,1)} %value_hbm.7, bf16[1024,128]{1,0:T(8,128)(2,1)} %get-tuple-element.31.state_hbm, bf16[1024,512]{1,0:T(8,128)(2,1)S(1)} %get-tuple-element.32.flipped_ref), custom_call_target="tpu_custom_call" | custom-call | flops 939524096 | bytes 3407872 | tf_op jit(solution)/shard_map/pallas_call | solution.py:249
  50.8 3.2 %all-to-all-done.3.block_ref = bf16[8,128,128]{2,1,0:T(8,128)(2,1)S(1)} async-done(((bf16[8,128,128]{2,1,0:T(8,128)(2,1)}), bf16[8,128,128]{2,1,0:T(8,128)(2,1)S(1)}, u32[]{:S(2)}, u32[]{:S(2)}) %all-to-all-start.3) | async-done | bytes 262176 | tf_op jit(solution)/shard_map/all_to_all | solution.py:272
  54.0 0.7 %shard_map.84 = bf16[8,128,128]{2,1,0:T(8,128)(2,1)} custom-call(bf16[8,128,128]{2,1,0:T(8,128)(2,1)S(1)} %all-to-all-done.3.block_ref), custom_call_target="tpu_custom_call" | custom-call | flops 131072 | bytes 262144 | tf_op jit(solution)/shard_map/pallas_call | solution.py:249
  54.8 3.6 %all-to-all-start.4 = ((bf16[8,128,128]{2,1,0:T(8,128)(2,1)}), bf16[8,128,128]{2,1,0:T(8,128)(2,1)S(1)}, u32[]{:S(2)}, u32[]{:S(2)}) async-start(bf16[8,128,128]{2,1,0:T(8,128)(2,1)} %shard_map.84), calls=%async_computation.4 | async-start | bytes 524288 | tf_op jit(solution)/shard_map/all_to_all | solution.py:272
  58.4 6.7 %shard_map.83 = (bf16[512,1024]{1,0:T(8,128)(2,1)S(1)}, bf16[512,1024]{1,0:T(8,128)(2,1)S(1)}, bf16[512,1024]{1,0:T(8,128)(2,1)S(1)}) custom-call(bf16[512,1024]{1,0:T(8,128)(2,1)} %query_hbm.3, bf16[512,1024]{1,0:T(8,128)(2,1)} %key_hbm.9, bf16[512,1024]{1,0:T(8,128)(2,1)} %value_hbm.7, ...), custom_call_target="tpu_custom_call", output_to_operand_aliasing={{1}: (3, {})} | custom-call | flops 1610612736 | bytes 4194304 | tf_op jit(solution)/shard_map/pallas_call | solution.py:249
  65.1 1.8 %all-to-all-done.4 = bf16[8,128,128]{2,1,0:T(8,128)(2,1)S(1)} async-done(((bf16[8,128,128]{2,1,0:T(8,128)(2,1)}), bf16[8,128,128]{2,1,0:T(8,128)(2,1)S(1)}, u32[]{:S(2)}, u32[]{:S(2)}) %all-to-all-start.4) | async-done | bytes 262176 | tf_op jit(solution)/shard_map/all_to_all | solution.py:272
  66.9 2.9 %shard_map.85 = (bf16[512,1024]{1,0:T(8,128)(2,1)}, bf16[512,1024]{1,0:T(8,128)(2,1)}) custom-call(bf16[512,1024]{1,0:T(8,128)(2,1)} %key_hbm.9, bf16[512,1024]{1,0:T(8,128)(2,1)S(1)} %get-tuple-element.37.value_ref, bf16[512,1024]{1,0:T(8,128)(2,1)S(1)} %get-tuple-element.38.key_part, bf16[512,1024]{1,0:T(8,128)(2,1)S(1)} %get-tuple-element.39.value_part, ...), custom_call_target="tpu_custom_call" | custom-call | flops 268435456 | bytes 4456448 | tf_op jit(solution)/shard_map/pallas_call | solution.py:249
Async XLA Ops:
  3.7 16.2 %all-to-all-start = ((bf16[8,128,128]{2,1,0:T(8,128)(2,1)}), bf16[8,128,128]{2,1,0:T(8,128)(2,1)S(1)}, u32[]{:S(2)}, u32[]{:S(2)}) async-start(bf16[8,128,128]{2,1,0:T(8,128)(2,1)} %bitcast.1), calls=%async_computation | async-start | bytes 524288 | tf_op jit(solution)/shard_map/all_to_all | solution.py:272
  20.6 12.2 %all-to-all-start.1 = ((bf16[8,128,128]{2,1,0:T(8,128)(2,1)}), bf16[8,128,128]{2,1,0:T(8,128)(2,1)S(1)}, u32[]{:S(2)}, u32[]{:S(2)}) async-start(bf16[8,128,128]{2,1,0:T(8,128)(2,1)} %shard_map.79), calls=%async_computation.1 | async-start | bytes 524288 | tf_op jit(solution)/shard_map/all_to_all | solution.py:272
  24.2 8.6 %copy-start = (f32[1024]{0:T(1024)S(1)}, f32[1024]{0:T(1024)}, u32[]{:S(2)}) copy-start(f32[1024]{0:T(1024)} %param.9) | copy-start | bytes 12292
  41.5 12.5 %all-to-all-start.3 = ((bf16[8,128,128]{2,1,0:T(8,128)(2,1)}), bf16[8,128,128]{2,1,0:T(8,128)(2,1)S(1)}, u32[]{:S(2)}, u32[]{:S(2)}) async-start(bf16[8,128,128]{2,1,0:T(8,128)(2,1)} %bitcast.3), calls=%async_computation.3 | async-start | bytes 524288 | tf_op jit(solution)/shard_map/all_to_all | solution.py:272
  54.8 12.2 %all-to-all-start.4 = ((bf16[8,128,128]{2,1,0:T(8,128)(2,1)}), bf16[8,128,128]{2,1,0:T(8,128)(2,1)S(1)}, u32[]{:S(2)}, u32[]{:S(2)}) async-start(bf16[8,128,128]{2,1,0:T(8,128)(2,1)} %shard_map.84), calls=%async_computation.4 | async-start | bytes 524288 | tf_op jit(solution)/shard_map/all_to_all | solution.py:272

commit v9 on v8

--- a/solution.py
+++ b/solution.py
@@ -102,10 +102,11 @@
 def scan_body(reverse, block_ref, state_ref):
     count = block_ref.shape[0]
     total = jnp.zeros(block_ref.shape[1:], jnp.float32)
-    order = range(count - 1, -1, -1) if reverse else range(count)
-    for place in order:
-        state_ref[place] = total.astype(jnp.bfloat16)
-        total = total + block_ref[place].astype(jnp.float32)
+    places = places_in_order(count)
+    for place in range(count - 1, -1, -1) if reverse else range(count):
+        rank = places.index(place)
+        state_ref[rank] = total.astype(jnp.bfloat16)
+        total = total + block_ref[rank].astype(jnp.float32)
 
 
 def heads_of(ref):
@@ -139,16 +140,14 @@
         cross += fold(scaled_grad(gain_ref, grad_ref, head) * attended)
     square = jnp.sum(square, axis=0, keepdims=True)
     cross = jnp.sum(cross, axis=0, keepdims=True)
-    for group in range(sums_ref.shape[0]):
-        sums_ref[group, 0:1, :] = square
-        sums_ref[group, 1:2, :] = cross
+    sums_ref[0:1, :] = square
+    sums_ref[1:2, :] = cross
     copy.wait()
 
 
 def dout_body(width, gain_ref, flipped_ref, grad_ref, attended_ref, sums_ref, dout_ref, own_ref):
-    sums = sum(sums_ref[group] for group in range(sums_ref.shape[0]))
-    inverse = 1.0 / jnp.sqrt(sums[0:1, :] / width + EPSILON)
-    drop = sums[1:2, :] * (inverse * inverse * inverse) / width
+    inverse = 1.0 / jnp.sqrt(sums_ref[0:1, :] / width + EPSILON)
+    drop = sums_ref[1:2, :] * (inverse * inverse * inverse) / width
     for head in heads_of(dout_ref):
         attended = dout_ref[head, :].astype(jnp.float32)
         dout = scaled_grad(gain_ref, grad_ref, head) * inverse - attended * drop
@@ -268,8 +267,14 @@
     return states
 
 
+def places_in_order(count):
+    places = list(range(count))
+    return places[count // 4 : count * 3 // 4] + places[: count // 4] + places[count * 3 // 4 :]
+
+
 def exchange(pieces, axis):
-    return lax.all_to_all(pieces, axis, 0, 0)
+    groups = [places_in_order(lax.axis_size(axis))]
+    return lax.all_to_all(pieces, axis, 0, 0, axis_index_groups=groups)
 
 
 def in_pieces(state, axis):
@@ -304,16 +309,15 @@
     (local,) = local_call(
         local_body, [flipped], [flat_vm], 2 * large, [keys, values], [rows_vm] * 2 + [chunks] * 2
     )
-    groups = lax.axis_size("head")
     attended, sums, kv_copy = local_call(
         sums_body,
         [gain_row, flipped, grad_flipped, local, kv_low],
-        [flat_vm, vm((groups, 2, rows), f32), hbm(state, bf16)],
+        [flat_vm, vm((2, rows), f32), hbm(state, bf16)],
         small,
         scratch=[one_sem],
         aliases={3: 0},
     )
-    sums = exchange(sums, "head")
+    sums = lax.psum(sums, "head")
     dout_flipped, own_grad = local_call(
         functools.partial(dout_body, total_width),
         [gain_row, flipped, grad_flipped, attended, sums],

time: 70.7 us -> 66.5 us (0.941)
  waiting for transfers between devices: 15.7 us -> 11.5 us
  blocking collectives: 6.42 us -> 5.67 us
    all_to_all x1 -> x0, blocking collectives: 6.42 us -> none  [exchange(): return lax.all_to_all(pieces, axis, 0, 0)]
    psum x0 -> x1, blocking collectives: none -> 5.67 us  [shards(): sums = lax.psum(sums, 'head')]
    all_to_all x4, waiting for transfers between devices: 15.7 us -> 11.5 us  [exchange(): return lax.all_to_all(pieces, axis, 0, 0, axis_index_groups=groups)]
    all_to_all x4, starting transfers between devices: 18.1 us -> 18.8 us  [exchange(): return lax.all_to_all(pieces, axis, 0, 0, axis_index_groups=groups)]
  transfers between devices with their start and end apart: 4 -> 4, of which waited for: 4 -> 4; matrix products, arithmetic and copies ran while one was open for 0% -> 0% of each run, Pallas kernels for 27% -> 29%
where the time goes in v9:
time: 66.5 us; the launch traced here: 65.8 us
  Pallas kernels  29 us (44%)
  starting transfers between devices  18.8 us (28%)
  waiting for transfers between devices  11.5 us (17%)
  blocking collectives  5.67 us (9%)
  between operations  0.85 us (1%)
    pallas_call x10, Pallas kernels, local_call(): pl.pallas_call(body, in_specs=specs, out_specs=out_specs, out_shape=outs,...  29 us
    all_to_all x4, starting transfers between devices, exchange(): return lax.all_to_all(pieces, axis, 0, 0, axis_index_groups=groups)  18.8 us
    all_to_all x4, waiting for transfers between devices, exchange(): return lax.all_to_all(pieces, axis, 0, 0, axis_index_groups=groups)  11.5 us
    psum x1, blocking collectives, shards(): sums = lax.psum(sums, 'head')  5.67 us
  transfers between devices with their start and end apart: 4, of which 4 were waited for; matrix products, arithmetic and copies ran while one was open for 0% of the time, Pallas kernels for 29%

profile of v9, /device:TPU:0, one launch (start us, length us, event | category | flops | bytes accessed | tf_op | source)
XLA Modules:
  0.0 65.8 jit_solution(13014234186186690219)
XLA Ops:
  0.6 3.0 %shard_map.76 = bf16[1024,128]{1,0:T(8,128)(2,1)} custom-call(bf16[512,1024]{1,0:T(8,128)(2,1)} %key_hbm.9, bf16[512,1024]{1,0:T(8,128)(2,1)} %value_hbm.7), custom_call_target="tpu_custom_call" | custom-call | flops 134217728 | bytes 2097152 | tf_op jit(solution)/shard_map/pallas_call | solution.py:248
  3.7 7.9 %all-to-all-start = ((bf16[8,128,128]{2,1,0:T(8,128)(2,1)}), bf16[8,128,128]{2,1,0:T(8,128)(2,1)S(1)}, u32[]{:S(2)}, u32[]{:S(2)}) async-start(bf16[8,128,128]{2,1,0:T(8,128)(2,1)} %bitcast.1), calls=%async_computation | async-start | bytes 524288 | tf_op jit(solution)/shard_map/all_to_all | solution.py:277
  11.5 2.1 %shard_map.77 = (bf16[1024,512]{1,0:T(8,128)(2,1)S(1)}, bf16[1024,512]{1,0:T(8,128)(2,1)S(1)}) custom-call(bf16[512,1024]{1,0:T(8,128)(2,1)} %query_hbm.3, bf16[512,1024]{1,0:T(8,128)(2,1)} %grad_hbm.1), custom_call_target="tpu_custom_call" | custom-call | flops 402653184 | bytes 2097152 | tf_op jit(solution)/shard_map/pallas_call | solution.py:248
  13.7 6.2 %all-to-all-done.block_ref = bf16[8,128,128]{2,1,0:T(8,128)(2,1)S(1)} async-done(((bf16[8,128,128]{2,1,0:T(8,128)(2,1)}), bf16[8,128,128]{2,1,0:T(8,128)(2,1)S(1)}, u32[]{:S(2)}, u32[]{:S(2)}) %all-to-all-start) | async-done | bytes 262176 | tf_op jit(solution)/shard_map/all_to_all | solution.py:277
  19.8 0.7 %shard_map.79 = bf16[8,128,128]{2,1,0:T(8,128)(2,1)} custom-call(bf16[8,128,128]{2,1,0:T(8,128)(2,1)S(1)} %all-to-all-done.block_ref), custom_call_target="tpu_custom_call" | custom-call | flops 131072 | bytes 262144 | tf_op jit(solution)/shard_map/pallas_call | solution.py:248
  20.6 3.5 %all-to-all-start.1 = ((bf16[8,128,128]{2,1,0:T(8,128)(2,1)}), bf16[8,128,128]{2,1,0:T(8,128)(2,1)S(1)}, u32[]{:S(2)}, u32[]{:S(2)}) async-start(bf16[8,128,128]{2,1,0:T(8,128)(2,1)} %shard_map.79), calls=%async_computation.1 | async-start | bytes 524288 | tf_op jit(solution)/shard_map/all_to_all | solution.py:277
  24.1 0.0 copy-start
  24.1 4.7 %shard_map.78.local_ref = bf16[1024,512]{1,0:T(8,128)(2,1)S(1)} custom-call(bf16[512,1024]{1,0:T(8,128)(2,1)} %key_hbm.9, bf16[512,1024]{1,0:T(8,128)(2,1)} %value_hbm.7, bf16[1024,512]{1,0:T(8,128)(2,1)S(1)} %get-tuple-element.25.flipped_ref), custom_call_target="tpu_custom_call" | custom-call | flops 805306368 | bytes 3145728 | tf_op jit(solution)/shard_map/pallas_call | solution.py:248
  28.8 2.2 %all-to-all-done.1 = bf16[8,128,128]{2,1,0:T(8,128)(2,1)S(1)} async-done(((bf16[8,128,128]{2,1,0:T(8,128)(2,1)}), bf16[8,128,128]{2,1,0:T(8,128)(2,1)S(1)}, u32[]{:S(2)}, u32[]{:S(2)}) %all-to-all-start.1) | async-done | bytes 262176 | tf_op jit(solution)/shard_map/all_to_all | solution.py:277
  31.0 0.0 copy-done
  31.0 0.8 %shard_map.80 = (bf16[1024,512]{1,0:T(8,128)(2,1)S(1)}, f32[2,512]{1,0:T(2,128)S(1)}, bf16[1024,128]{1,0:T(8,128)(2,1)}) custom-call(f32[1,1024]{1,0:T(1,128)S(1)} %bitcast.7, bf16[1024,512]{1,0:T(8,128)(2,1)S(1)} %get-tuple-element.25.flipped_ref, bf16[1024,512]{1,0:T(8,128)(2,1)S(1)} %get-tuple-element.26.grad_ref, ...), custom_call_target="tpu_custom_call", output_to_operand_aliasing={{0}: (3, {})} | custom-call | flops 134217728 | bytes 3411968 | tf_op jit(solution)/shard_map/pallas_call | solution.py:248
  31.9 5.7 %psum.7.sums_ref = f32[2,512]{1,0:T(2,128)S(1)} all-reduce(f32[2,512]{1,0:T(2,128)S(1)} %get-tuple-element.29), channel_id=1, replica_groups=mesh['seq'=8,'head'=4] {'head'}, use_global_device_ids=true, to_apply=%region_0.0 | all-reduce | flops 1024 | bytes 8192 | tf_op jit(solution)/shard_map/psum | solution.py:320
  37.5 1.5 %shard_map.81 = (bf16[1024,512]{1,0:T(8,128)(2,1)S(1)}, bf16[1024,128]{1,0:T(8,128)(2,1)}) custom-call(f32[1,1024]{1,0:T(1,128)S(1)} %bitcast.8, bf16[1024,512]{1,0:T(8,128)(2,1)S(1)} %get-tuple-element.25.flipped_ref, bf16[1024,512]{1,0:T(8,128)(2,1)S(1)} %get-tuple-element.26.grad_ref, ...), custom_call_target="tpu_custom_call", output_to_operand_aliasing={{0}: (3, {})} | custom-call | flops 134217728 | bytes 3153920 | tf_op jit(solution)/shard_map/pallas_call | solution.py:248
  39.0 3.9 %all-to-all-start.2 = ((bf16[8,128,128]{2,1,0:T(8,128)(2,1)}), bf16[8,128,128]{2,1,0:T(8,128)(2,1)S(1)}, u32[]{:S(2)}, u32[]{:S(2)}) async-start(bf16[8,128,128]{2,1,0:T(8,128)(2,1)} %bitcast.3), calls=%async_computation.2 | async-start | bytes 524288 | tf_op jit(solution)/shard_map/all_to_all | solution.py:277
  42.9 5.7 %shard_map.82 = (bf16[512,1024]{1,0:T(8,128)(2,1)}, bf16[512,1024]{1,0:T(8,128)(2,1)S(1)}) custom-call(bf16[512,1024]{1,0:T(8,128)(2,1)} %key_hbm.9, bf16[512,1024]{1,0:T(8,128)(2,1)} %value_hbm.7, bf16[1024,128]{1,0:T(8,128)(2,1)} %get-tuple-element.31.state_hbm, bf16[1024,512]{1,0:T(8,128)(2,1)S(1)} %get-tuple-element.32.flipped_ref), custom_call_target="tpu_custom_call" | custom-call | flops 939524096 | bytes 3407872 | tf_op jit(solution)/shard_map/pallas_call | solution.py:248
  48.6 3.0 %all-to-all-done.2.block_ref = bf16[8,128,128]{2,1,0:T(8,128)(2,1)S(1)} async-done(((bf16[8,128,128]{2,1,0:T(8,128)(2,1)}), bf16[8,128,128]{2,1,0:T(8,128)(2,1)S(1)}, u32[]{:S(2)}, u32[]{:S(2)}) %all-to-all-start.2) | async-done | bytes 262176 | tf_op jit(solution)/shard_map/all_to_all | solution.py:277
  51.5 0.7 %shard_map.84 = bf16[8,128,128]{2,1,0:T(8,128)(2,1)} custom-call(bf16[8,128,128]{2,1,0:T(8,128)(2,1)S(1)} %all-to-all-done.2.block_ref), custom_call_target="tpu_custom_call" | custom-call | flops 131072 | bytes 262144 | tf_op jit(solution)/shard_map/pallas_call | solution.py:248
  52.2 3.5 %all-to-all-start.3 = ((bf16[8,128,128]{2,1,0:T(8,128)(2,1)}), bf16[8,128,128]{2,1,0:T(8,128)(2,1)S(1)}, u32[]{:S(2)}, u32[]{:S(2)}) async-start(bf16[8,128,128]{2,1,0:T(8,128)(2,1)} %shard_map.84), calls=%async_computation.3 | async-start | bytes 524288 | tf_op jit(solution)/shard_map/all_to_all | solution.py:277
  55.8 6.7 %shard_map.83 = (bf16[512,1024]{1,0:T(8,128)(2,1)S(1)}, bf16[512,1024]{1,0:T(8,128)(2,1)S(1)}, bf16[512,1024]{1,0:T(8,128)(2,1)S(1)}) custom-call(bf16[512,1024]{1,0:T(8,128)(2,1)} %query_hbm.3, bf16[512,1024]{1,0:T(8,128)(2,1)} %key_hbm.9, bf16[512,1024]{1,0:T(8,128)(2,1)} %value_hbm.7, ...), custom_call_target="tpu_custom_call", output_to_operand_aliasing={{1}: (3, {})} | custom-call | flops 1610612736 | bytes 4194304 | tf_op jit(solution)/shard_map/pallas_call | solution.py:248
  62.5 0.2 all-to-all-done.3
  62.7 2.9 %shard_map.85 = (bf16[512,1024]{1,0:T(8,128)(2,1)}, bf16[512,1024]{1,0:T(8,128)(2,1)}) custom-call(bf16[512,1024]{1,0:T(8,128)(2,1)} %key_hbm.9, bf16[512,1024]{1,0:T(8,128)(2,1)S(1)} %get-tuple-element.37.value_ref, bf16[512,1024]{1,0:T(8,128)(2,1)S(1)} %get-tuple-element.38.key_part, bf16[512,1024]{1,0:T(8,128)(2,1)S(1)} %get-tuple-element.39.value_part, ...), custom_call_target="tpu_custom_call" | custom-call | flops 268435456 | bytes 4456448 | tf_op jit(solution)/shard_map/pallas_call | solution.py:248
Async XLA Ops:
  3.7 16.2 %all-to-all-start = ((bf16[8,128,128]{2,1,0:T(8,128)(2,1)}), bf16[8,128,128]{2,1,0:T(8,128)(2,1)S(1)}, u32[]{:S(2)}, u32[]{:S(2)}) async-start(bf16[8,128,128]{2,1,0:T(8,128)(2,1)} %bitcast.1), calls=%async_computation | async-start | bytes 524288 | tf_op jit(solution)/shard_map/all_to_all | solution.py:277
  20.6 10.5 %all-to-all-start.1 = ((bf16[8,128,128]{2,1,0:T(8,128)(2,1)}), bf16[8,128,128]{2,1,0:T(8,128)(2,1)S(1)}, u32[]{:S(2)}, u32[]{:S(2)}) async-start(bf16[8,128,128]{2,1,0:T(8,128)(2,1)} %shard_map.79), calls=%async_computation.1 | async-start | bytes 524288 | tf_op jit(solution)/shard_map/all_to_all | solution.py:277
  24.1 6.9 %copy-start = (f32[1024]{0:T(1024)S(1)}, f32[1024]{0:T(1024)}, u32[]{:S(2)}) copy-start(f32[1024]{0:T(1024)} %param.9) | copy-start | bytes 12292
  39.0 12.5 %all-to-all-start.2 = ((bf16[8,128,128]{2,1,0:T(8,128)(2,1)}), bf16[8,128,128]{2,1,0:T(8,128)(2,1)S(1)}, u32[]{:S(2)}, u32[]{:S(2)}) async-start(bf16[8,128,128]{2,1,0:T(8,128)(2,1)} %bitcast.3), calls=%async_computation.2 | async-start | bytes 524288 | tf_op jit(solution)/shard_map/all_to_all | solution.py:277
  52.2 10.5 %all-to-all-start.3 = ((bf16[8,128,128]{2,1,0:T(8,128)(2,1)}), bf16[8,128,128]{2,1,0:T(8,128)(2,1)S(1)}, u32[]{:S(2)}, u32[]{:S(2)}) async-start(bf16[8,128,128]{2,1,0:T(8,128)(2,1)} %shard_map.84), calls=%async_computation.3 | async-start | bytes 524288 | tf_op jit(solution)/shard_map/all_to_all | solution.py:277

commit v10 on v7

--- a/solution.py
+++ b/solution.py
@@ -44,6 +44,14 @@
     return copies
 
 
+def row_copies(source, target, sems):
+    copies = []
+    for index in range(source.shape[0] // COPY_COLS):
+        part = slice(index * COPY_COLS, (index + 1) * COPY_COLS)
+        copies.append(pltpu.make_async_copy(source.at[part, :], target.at[part, :], sems.at[index]))
+    return copies
+
+
 def start_all(*groups):
     for parts in zip(*groups):
         for part in parts:
@@ -56,7 +64,10 @@
             part.wait()
 
 
-def states_body(key_hbm, value_hbm, state_ref, key_ref, value_ref, key_sems, value_sems):
+def states_body(
+    key_hbm, value_hbm, state_hbm, key_ref, value_ref, state_ref, key_sems, value_sems, state_sems
+):
+    stores = row_copies(state_ref, state_hbm, state_sems)
     key_copies = column_copies(key_hbm, key_ref, key_sems)
     value_copies = column_copies(value_hbm, value_ref, value_sems)
     start_all(key_copies, value_copies)
@@ -66,6 +77,8 @@
         for start in range(cols.start, cols.stop, HEAD_DIM):
             head = slice(start, start + HEAD_DIM)
             state_ref[head, :] = mm_tn(key_ref[:, head], value_ref[:, head]).astype(jnp.bfloat16)
+        stores[index].start()
+    wait_all(stores)
 
 
 def flip_body(query_hbm, grad_hbm, flipped_ref, grad_flipped_ref, query_ref, grad_ref, query_sems, grad_sems):
@@ -99,13 +112,18 @@
                 local_ref[cols, start:end] = local.astype(jnp.bfloat16)
 
 
-def scan_body(reverse, block_ref, state_ref):
+def scan_body(reverse, block_ref, state_hbm, state_ref, sems):
     count = block_ref.shape[0]
     total = jnp.zeros(block_ref.shape[1:], jnp.float32)
-    order = range(count - 1, -1, -1) if reverse else range(count)
-    for place in order:
-        state_ref[place] = total.astype(jnp.bfloat16)
-        total = total + block_ref[place].astype(jnp.float32)
+    places = places_in_order(count)
+    stores = []
+    for place in range(count - 1, -1, -1) if reverse else range(count):
+        rank = places.index(place)
+        state_ref[rank] = total.astype(jnp.bfloat16)
+        total = total + block_ref[rank].astype(jnp.float32)
+        stores.append(pltpu.make_async_copy(state_ref.at[rank], state_hbm.at[rank], sems.at[rank]))
+        stores[-1].start()
+    wait_all(stores)
 
 
 def heads_of(ref):
@@ -133,11 +151,16 @@
         attended_ref[head, :] = attended.astype(jnp.bfloat16)
         square += fold(attended * attended)
         cross += fold(scaled_grad(gain_ref, grad_ref, head) * attended)
-    sums_ref[0:1, :] = jnp.sum(square, axis=0, keepdims=True)
-    sums_ref[1:2, :] = jnp.sum(cross, axis=0, keepdims=True)
-
-
-def dout_body(width, gain_ref, flipped_ref, grad_ref, attended_ref, sums_ref, dout_ref, own_ref):
+    square = jnp.sum(square, axis=0, keepdims=True)
+    cross = jnp.sum(cross, axis=0, keepdims=True)
+    sums_ref[0:1, :] = square
+    sums_ref[1:2, :] = cross
+
+
+def dout_body(
+    width, gain_ref, flipped_ref, grad_ref, attended_ref, sums_ref, dout_ref, own_hbm, own_ref, sems
+):
+    stores = row_copies(own_ref, own_hbm, sems)
     inverse = 1.0 / jnp.sqrt(sums_ref[0:1, :] / width + EPSILON)
     drop = sums_ref[1:2, :] * (inverse * inverse * inverse) / width
     for head in heads_of(dout_ref):
@@ -146,6 +169,9 @@
         dout = dout.astype(jnp.bfloat16)
         dout_ref[head, :] = dout
         own_ref[head, :] = mm_nt(flipped_ref[head, :], dout).astype(jnp.bfloat16)
+        if head.stop % COPY_COLS == 0:
+            stores[head.stop // COPY_COLS - 1].start()
+    wait_all(stores)
 
 
 def query_body(
@@ -250,14 +276,26 @@
     (states,) = local_call(
         functools.partial(scan_body, reverse),
         [blocks],
-        [pltpu.VMEM(blocks.shape, blocks.dtype)],
+        [pltpu.HBM(blocks.shape, blocks.dtype)],
         blocks.size,
+        scratch=[
+            pltpu.VMEM(blocks.shape, blocks.dtype),
+            pltpu.SemaphoreType.DMA((blocks.shape[0],)),
+        ],
     )
     return states
 
 
+def places_in_order(count):
+    quarter = count // 4
+    first, second, third, fourth = (list(range(at, at + quarter)) for at in range(0, count, quarter))
+    half = quarter // 2
+    return second + first[:half] + third[:half] + first[half:] + third[half:] + fourth
+
+
 def exchange(pieces, axis):
-    return lax.all_to_all(pieces, axis, 0, 0)
+    groups = [places_in_order(lax.axis_size(axis))]
+    return lax.all_to_all(pieces, axis, 0, 0, axis_index_groups=groups)
 
 
 def in_pieces(state, axis):
@@ -280,7 +318,12 @@
     rows_vm, flat_vm, state_vm = vm(tokens, bf16), vm(flat, bf16), vm(state, bf16)
 
     (own_kv,) = local_call(
-        states_body, [], [state_vm], small, [keys, values], [rows_vm] * 2 + [chunks] * 2
+        states_body,
+        [],
+        [hbm(state, bf16)],
+        small,
+        [keys, values],
+        [rows_vm] * 2 + [state_vm] + [chunks] * 3,
     )
     kv_blocks = exchange(in_pieces(own_kv, "seq"), "seq")
     flipped, grad_flipped = local_call(
@@ -302,8 +345,9 @@
     dout_flipped, own_grad = local_call(
         functools.partial(dout_body, total_width),
         [gain_row, flipped, grad_flipped, attended, sums],
-        [flat_vm, state_vm],
+        [flat_vm, hbm(state, bf16)],
         small,
+        scratch=[state_vm, chunks],
         aliases={3: 0},
     )
     grad_blocks = exchange(in_pieces(own_grad, "seq"), "seq")

time: 70 us -> 65.8 us (0.940)
  waiting for transfers between devices: 15.7 us -> 10.4 us
  starting transfers between devices: 18.5 us -> 19.6 us
    all_to_all x4, waiting for transfers between devices: 15.7 us -> 10.4 us  [exchange(): return lax.all_to_all(pieces, axis, 0, 0, axis_index_groups=groups)]
    all_to_all x4, starting transfers between devices: 18.5 us -> 19.6 us  [exchange(): return lax.all_to_all(pieces, axis, 0, 0, axis_index_groups=groups)]
  transfers between devices with their start and end apart: 4 -> 4, of which waited for: 4 -> 3; matrix products, arithmetic and copies ran while one was open for 0% -> 0% of each run, Pallas kernels for 27% -> 29%
where the time goes in v10:
time: 65.8 us; the launch traced here: 65.1 us
  Pallas kernels  28.5 us (43%)
  starting transfers between devices  19.6 us (30%)
  waiting for transfers between devices  10.4 us (16%)
  blocking collectives  5.67 us (9%)
  between operations  0.87 us (1%)
    pallas_call x10, Pallas kernels, local_call(): pl.pallas_call(body, in_specs=specs, out_specs=out_specs, out_shape=outs,...  28.5 us
    all_to_all x4, starting transfers between devices, exchange(): return lax.all_to_all(pieces, axis, 0, 0, axis_index_groups=groups)  19.6 us
    all_to_all x4, waiting for transfers between devices, exchange(): return lax.all_to_all(pieces, axis, 0, 0, axis_index_groups=groups)  10.4 us
    psum x1, blocking collectives, shards(): sums = lax.psum(sums, 'head')  5.67 us
  transfers between devices with their start and end apart: 4, of which 3 were waited for; matrix products, arithmetic and copies ran while one was open for 0% of the time, Pallas kernels for 29%

profile of v10, /device:TPU:0, one launch (start us, length us, event | category | flops | bytes accessed | tf_op | source)
XLA Modules:
  0.0 65.1 jit_solution(12180135626473173735)
XLA Ops:
  0.6 3.0 %shard_map.76 = bf16[1024,128]{1,0:T(8,128)(2,1)} custom-call(bf16[512,1024]{1,0:T(8,128)(2,1)} %key_hbm.9, bf16[512,1024]{1,0:T(8,128)(2,1)} %value_hbm.7), custom_call_target="tpu_custom_call" | custom-call | flops 134217728 | bytes 2097152 | tf_op jit(solution)/shard_map/pallas_call | solution.py:263
  3.6 7.9 %all-to-all-start = ((bf16[8,128,128]{2,1,0:T(8,128)(2,1)}), bf16[8,128,128]{2,1,0:T(8,128)(2,1)S(1)}, u32[]{:S(2)}, u32[]{:S(2)}) async-start(bf16[8,128,128]{2,1,0:T(8,128)(2,1)} %bitcast.10), calls=%async_computation | async-start | bytes 524288 | tf_op jit(solution)/shard_map/all_to_all | solution.py:298
  11.5 2.1 %shard_map.77 = (bf16[1024,512]{1,0:T(8,128)(2,1)S(1)}, bf16[1024,512]{1,0:T(8,128)(2,1)S(1)}) custom-call(bf16[512,1024]{1,0:T(8,128)(2,1)} %query_hbm.3, bf16[512,1024]{1,0:T(8,128)(2,1)} %grad_hbm.1), custom_call_target="tpu_custom_call" | custom-call | flops 402653184 | bytes 2097152 | tf_op jit(solution)/shard_map/pallas_call | solution.py:263
  13.6 5.8 %all-to-all-done.block_ref = bf16[8,128,128]{2,1,0:T(8,128)(2,1)S(1)} async-done(((bf16[8,128,128]{2,1,0:T(8,128)(2,1)}), bf16[8,128,128]{2,1,0:T(8,128)(2,1)S(1)}, u32[]{:S(2)}, u32[]{:S(2)}) %all-to-all-start) | async-done | bytes 262176 | tf_op jit(solution)/shard_map/all_to_all | solution.py:298
  19.4 0.8 %shard_map.79 = bf16[8,128,128]{2,1,0:T(8,128)(2,1)} custom-call(bf16[8,128,128]{2,1,0:T(8,128)(2,1)S(1)} %all-to-all-done.block_ref), custom_call_target="tpu_custom_call" | custom-call | flops 131072 | bytes 262144 | tf_op jit(solution)/shard_map/pallas_call | solution.py:263
  20.2 3.7 %all-to-all-start.1 = ((bf16[8,128,128]{2,1,0:T(8,128)(2,1)}), bf16[8,128,128]{2,1,0:T(8,128)(2,1)S(1)}, u32[]{:S(2)}, u32[]{:S(2)}) async-start(bf16[8,128,128]{2,1,0:T(8,128)(2,1)} %shard_map.79), calls=%async_computation.1 | async-start | bytes 524288 | tf_op jit(solution)/shard_map/all_to_all | solution.py:298
  23.9 0.0 copy-start
  23.9 4.7 %shard_map.78.local_ref = bf16[1024,512]{1,0:T(8,128)(2,1)S(1)} custom-call(bf16[512,1024]{1,0:T(8,128)(2,1)} %key_hbm.9, bf16[512,1024]{1,0:T(8,128)(2,1)} %value_hbm.7, bf16[1024,512]{1,0:T(8,128)(2,1)S(1)} %get-tuple-element.24.flipped_ref), custom_call_target="tpu_custom_call" | custom-call | flops 805306368 | bytes 3145728 | tf_op jit(solution)/shard_map/pallas_call | solution.py:263
  28.6 1.6 %all-to-all-done.1 = bf16[8,128,128]{2,1,0:T(8,128)(2,1)S(1)} async-done(((bf16[8,128,128]{2,1,0:T(8,128)(2,1)}), bf16[8,128,128]{2,1,0:T(8,128)(2,1)S(1)}, u32[]{:S(2)}, u32[]{:S(2)}) %all-to-all-start.1) | async-done | bytes 262176 | tf_op jit(solution)/shard_map/all_to_all | solution.py:298
  30.1 0.0 copy-done
  30.1 0.8 %shard_map.80 = (bf16[1024,512]{1,0:T(8,128)(2,1)S(1)}, f32[2,512]{1,0:T(2,128)S(1)}) custom-call(f32[1,1024]{1,0:T(1,128)S(1)} %bitcast.8, bf16[1024,512]{1,0:T(8,128)(2,1)S(1)} %get-tuple-element.24.flipped_ref, bf16[1024,512]{1,0:T(8,128)(2,1)S(1)} %get-tuple-element.25.grad_ref, ...), custom_call_target="tpu_custom_call", output_to_operand_aliasing={{0}: (3, {})} | custom-call | flops 134217728 | bytes 3411968 | tf_op jit(solution)/shard_map/pallas_call | solution.py:263
  31.0 5.7 %psum.7.sums_ref = f32[2,512]{1,0:T(2,128)S(1)} all-reduce(f32[2,512]{1,0:T(2,128)S(1)} %get-tuple-element.28), channel_id=1, replica_groups=mesh['seq'=8,'head'=4] {'head'}, use_global_device_ids=true, to_apply=%region_0.0 | all-reduce | flops 1024 | bytes 8192 | tf_op jit(solution)/shard_map/psum | solution.py:344
  36.6 1.5 %shard_map.81 = (bf16[1024,512]{1,0:T(8,128)(2,1)S(1)}, bf16[1024,128]{1,0:T(8,128)(2,1)}) custom-call(f32[1,1024]{1,0:T(1,128)S(1)} %bitcast.9, bf16[1024,512]{1,0:T(8,128)(2,1)S(1)} %get-tuple-element.24.flipped_ref, bf16[1024,512]{1,0:T(8,128)(2,1)S(1)} %get-tuple-element.25.grad_ref, ...), custom_call_target="tpu_custom_call", output_to_operand_aliasing={{0}: (3, {})} | custom-call | flops 134217728 | bytes 3153920 | tf_op jit(solution)/shard_map/pallas_call | solution.py:263
  38.1 4.5 %all-to-all-start.2 = ((bf16[8,128,128]{2,1,0:T(8,128)(2,1)}), bf16[8,128,128]{2,1,0:T(8,128)(2,1)S(1)}, u32[]{:S(2)}, u32[]{:S(2)}) async-start(bf16[8,128,128]{2,1,0:T(8,128)(2,1)} %bitcast.11), calls=%async_computation.2 | async-start | bytes 524288 | tf_op jit(solution)/shard_map/all_to_all | solution.py:298
  42.6 5.2 %shard_map.82 = (bf16[512,1024]{1,0:T(8,128)(2,1)}, bf16[512,1024]{1,0:T(8,128)(2,1)S(1)}) custom-call(bf16[512,1024]{1,0:T(8,128)(2,1)} %key_hbm.9, bf16[512,1024]{1,0:T(8,128)(2,1)} %value_hbm.7, bf16[1024,512]{1,0:T(8,128)(2,1)S(1)} %get-tuple-element.30.flipped_ref, bf16[1024,128]{1,0:T(8,128)(2,1)S(1)} %bitcast.7), custom_call_target="tpu_custom_call" | custom-call | flops 939524096 | bytes 3407872 | tf_op jit(solution)/shard_map/pallas_call | solution.py:263
  47.8 3.0 %all-to-all-done.2.block_ref = bf16[8,128,128]{2,1,0:T(8,128)(2,1)S(1)} async-done(((bf16[8,128,128]{2,1,0:T(8,128)(2,1)}), bf16[8,128,128]{2,1,0:T(8,128)(2,1)S(1)}, u32[]{:S(2)}, u32[]{:S(2)}) %all-to-all-start.2) | async-done | bytes 262176 | tf_op jit(solution)/shard_map/all_to_all | solution.py:298
  50.8 0.8 %shard_map.84 = bf16[8,128,128]{2,1,0:T(8,128)(2,1)} custom-call(bf16[8,128,128]{2,1,0:T(8,128)(2,1)S(1)} %all-to-all-done.2.block_ref), custom_call_target="tpu_custom_call" | custom-call | flops 131072 | bytes 262144 | tf_op jit(solution)/shard_map/pallas_call | solution.py:263
  51.6 3.6 %all-to-all-start.3 = ((bf16[8,128,128]{2,1,0:T(8,128)(2,1)}), bf16[8,128,128]{2,1,0:T(8,128)(2,1)S(1)}, u32[]{:S(2)}, u32[]{:S(2)}) async-start(bf16[8,128,128]{2,1,0:T(8,128)(2,1)} %shard_map.84), calls=%async_computation.3 | async-start | bytes 524288 | tf_op jit(solution)/shard_map/all_to_all | solution.py:298
  55.3 6.7 %shard_map.83 = (bf16[512,1024]{1,0:T(8,128)(2,1)S(1)}, bf16[512,1024]{1,0:T(8,128)(2,1)S(1)}, bf16[512,1024]{1,0:T(8,128)(2,1)S(1)}) custom-call(bf16[512,1024]{1,0:T(8,128)(2,1)} %query_hbm.3, bf16[512,1024]{1,0:T(8,128)(2,1)} %key_hbm.9, bf16[512,1024]{1,0:T(8,128)(2,1)} %value_hbm.7, ...), custom_call_target="tpu_custom_call", output_to_operand_aliasing={{1}: (3, {})} | custom-call | flops 1610612736 | bytes 4194304 | tf_op jit(solution)/shard_map/pallas_call | solution.py:263
  62.0 0.0 all-to-all-done.3
  62.0 2.9 %shard_map.85 = (bf16[512,1024]{1,0:T(8,128)(2,1)}, bf16[512,1024]{1,0:T(8,128)(2,1)}) custom-call(bf16[512,1024]{1,0:T(8,128)(2,1)} %key_hbm.9, bf16[512,1024]{1,0:T(8,128)(2,1)S(1)} %get-tuple-element.35.value_ref, bf16[512,1024]{1,0:T(8,128)(2,1)S(1)} %get-tuple-element.36.key_part, bf16[512,1024]{1,0:T(8,128)(2,1)S(1)} %get-tuple-element.37.value_part, ...), custom_call_target="tpu_custom_call" | custom-call | flops 268435456 | bytes 4456448 | tf_op jit(solution)/shard_map/pallas_call | solution.py:263
Async XLA Ops:
  3.6 15.8 %all-to-all-start = ((bf16[8,128,128]{2,1,0:T(8,128)(2,1)}), bf16[8,128,128]{2,1,0:T(8,128)(2,1)S(1)}, u32[]{:S(2)}, u32[]{:S(2)}) async-start(bf16[8,128,128]{2,1,0:T(8,128)(2,1)} %bitcast.10), calls=%async_computation | async-start | bytes 524288 | tf_op jit(solution)/shard_map/all_to_all | solution.py:298
  20.2 9.9 %all-to-all-start.1 = ((bf16[8,128,128]{2,1,0:T(8,128)(2,1)}), bf16[8,128,128]{2,1,0:T(8,128)(2,1)S(1)}, u32[]{:S(2)}, u32[]{:S(2)}) async-start(bf16[8,128,128]{2,1,0:T(8,128)(2,1)} %shard_map.79), calls=%async_computation.1 | async-start | bytes 524288 | tf_op jit(solution)/shard_map/all_to_all | solution.py:298
  23.9 6.3 %copy-start = (f32[1024]{0:T(1024)S(1)}, f32[1024]{0:T(1024)}, u32[]{:S(2)}) copy-start(f32[1024]{0:T(1024)} %param.9) | copy-start | bytes 12292
  38.1 12.7 %all-to-all-start.2 = ((bf16[8,128,128]{2,1,0:T(8,128)(2,1)}), bf16[8,128,128]{2,1,0:T(8,128)(2,1)S(1)}, u32[]{:S(2)}, u32[]{:S(2)}) async-start(bf16[8,128,128]{2,1,0:T(8,128)(2,1)} %bitcast.11), calls=%async_computation.2 | async-start | bytes 524288 | tf_op jit(solution)/shard_map/all_to_all | solution.py:298
  51.6 10.4 %all-to-all-start.3 = ((bf16[8,128,128]{2,1,0:T(8,128)(2,1)}), bf16[8,128,128]{2,1,0:T(8,128)(2,1)S(1)}, u32[]{:S(2)}, u32[]{:S(2)}) async-start(bf16[8,128,128]{2,1,0:T(8,128)(2,1)} %shard_map.84), calls=%async_computation.3 | async-start | bytes 524288 | tf_op jit(solution)/shard_map/all_to_all | solution.py:298

commit v11 on v10

--- a/solution.py
+++ b/solution.py
@@ -174,14 +174,25 @@
     wait_all(stores)
 
 
+def value_local(query_ref, key_ref, dout, cols, target):
+    rows = key_ref.shape[0]
+    for start in range(0, rows, BLOCK):
+        end = start + BLOCK
+        weights = masked(mm_nt(key_ref[start:end, cols], query_ref[start:, cols]), 0, 0, False)
+        target[start:end, :] = mm(weights, dout[start:, :]).astype(jnp.bfloat16)
+
+
 def query_body(
-    key_hbm, value_hbm, flipped_ref, state_ref, out_hbm, dout_ref,
-    key_ref, value_ref, out_ref, key_sems, value_sems, out_sems,
+    query_hbm, key_hbm, value_hbm, flipped_ref, state_ref, out_hbm, dout_ref, value_out,
+    query_ref, key_ref, value_ref, out_ref, query_sems, key_sems, value_sems, out_sems,
 ):
     rows = dout_ref.shape[0]
+    early = value_out.shape[1]
+    query_copies = column_copies(query_hbm.at[:, :early], query_ref, query_sems)
     key_copies = column_copies(key_hbm, key_ref, key_sems)
     value_copies = column_copies(value_hbm, value_ref, value_sems)
     start_all(key_copies, value_copies)
+    start_all(query_copies)
     for head in heads_of(flipped_ref):
         dout_ref[:, head] = flipped_ref[head, :].T
     stores = column_copies(out_ref, out_hbm, out_sems)
@@ -197,6 +208,9 @@
                 grad = mm(dscore, key_ref[:end, cols]) + mm_nt(dout, state_ref[cols, :])
                 out_ref[start:end, cols] = grad.astype(jnp.bfloat16)
         stores[index].start()
+    wait_all(query_copies)
+    for cols in pieces_of(value_out, HEAD_DIM):
+        value_local(query_ref, key_ref, dout_ref[:, cols], cols, value_out.at[:, cols])
     wait_all(stores)
 
 
@@ -204,31 +218,34 @@
     query_hbm, key_hbm, value_hbm, dout_ref, key_out, value_out, value_ref,
     query_ref, key_ref, query_sems, key_sems, value_sems,
 ):
-    rows = value_out.shape[0]
+    rows, width = key_out.shape
+    early = width - value_out.shape[1]
     loads = (
         column_copies(query_hbm, query_ref, query_sems),
-        column_copies(key_hbm, key_ref, key_sems),
         column_copies(value_hbm, value_ref, value_sems),
-    )
-    start_all(*loads)
+        column_copies(key_hbm.at[:, early:], key_ref, key_sems),
+    )
+    start_all(*loads[:2])
+    start_all(loads[2])
     for index, step in enumerate(pieces_of(key_out, COPY_COLS)):
-        for load in loads:
-            load[index].wait()
+        loads[0][index].wait()
+        loads[1][index].wait()
+        if step.start == early:
+            wait_all(loads[2])
         for left in range(step.start, step.stop, HEAD_DIM):
             cols = slice(left, left + HEAD_DIM)
-            dout_all = value_out[:, cols]
+            dout = key_out[:, cols]
             for start in range(0, rows, BLOCK):
                 end = start + BLOCK
-                query = query_ref[start:, cols]
-                dout = dout_all[start:, :]
-                dscore = masked(mm_nt(value_ref[start:end, cols], dout), 0, 0, False)
-                key_out[start:end, cols] = mm(dscore, query).astype(jnp.bfloat16)
-                weights = masked(mm_nt(key_ref[start:end, cols], query), 0, 0, False)
-                value_out[start:end, cols] = mm(weights, dout).astype(jnp.bfloat16)
+                scores = mm_nt(value_ref[start:end, cols], dout[start:, :])
+                key_out[start:end, cols] = mm(masked(scores, 0, 0, False), query_ref[start:, cols]).astype(jnp.bfloat16)
+            if left >= early:
+                late = slice(left - early, left - early + HEAD_DIM)
+                value_local(query_ref.at[:, early:], key_ref, dout, late, value_out.at[:, late])
 
 
 def final_body(
-    key_hbm, value_ref, key_part, value_part, state_ref, key_out_hbm, value_out_hbm,
+    key_hbm, value_ref, key_part, early_part, late_part, state_ref, key_out_hbm, value_out_hbm,
     key_ref, key_out, value_out, in_sems, key_sems, value_sems,
 ):
     keys = column_copies(key_hbm, key_ref, in_sems)
@@ -245,7 +262,12 @@
         keys[index].wait()
         for left in range(step.start, step.stop, HEAD_DIM):
             cols = slice(left, left + HEAD_DIM)
-            grad = value_part[:, cols].astype(jnp.float32) + mm(key_ref[:, cols], state_ref[cols, :])
+            early = early_part.shape[1]
+            if left < early:
+                part = early_part[:, cols]
+            else:
+                part = late_part[:, left - early : left - early + HEAD_DIM]
+            grad = part.astype(jnp.float32) + mm(key_ref[:, cols], state_ref[cols, :])
             value_out[:, cols] = grad.astype(jnp.bfloat16)
         value_stores[index].start()
     wait_all(key_stores, value_stores)
@@ -289,8 +311,7 @@
 def places_in_order(count):
     quarter = count // 4
     first, second, third, fourth = (list(range(at, at + quarter)) for at in range(0, count, quarter))
-    half = quarter // 2
-    return second + first[:half] + third[:half] + first[half:] + third[half:] + fourth
+    return second + fourth + first[::-1] + third
 
 
 def exchange(pieces, axis):
@@ -351,28 +372,32 @@
         aliases={3: 0},
     )
     grad_blocks = exchange(in_pieces(own_grad, "seq"), "seq")
-    query_grad, dout = local_call(
+    early = width // 2 // COPY_COLS * COPY_COLS
+    early_vm, late_vm = vm((rows, early), bf16), vm((rows, width - early), bf16)
+    query_grad, dout, early_part = local_call(
         query_body,
         [dout_flipped, kv_low],
-        [hbm(tokens, bf16), rows_vm],
+        [hbm(tokens, bf16), rows_vm, early_vm],
         2 * large + small,
-        [keys, values],
-        [rows_vm] * 3 + [chunks] * 3,
-    )
-    grad_blocks, query_grad, dout = lax.optimization_barrier((grad_blocks, query_grad, dout))
+        [queries, keys, values],
+        [early_vm] + [rows_vm] * 3 + [chunks] * 4,
+    )
+    grad_blocks, query_grad, dout, early_part = lax.optimization_barrier(
+        (grad_blocks, query_grad, dout, early_part)
+    )
     grad_low = exchange(scan_blocks(grad_blocks, True), "seq").reshape(state)
-    key_part, value_part, value_kept = local_call(
+    key_part, late_part, value_kept = local_call(
         inner_body,
         [dout],
-        [rows_vm] * 3,
-        4 * large,
+        [rows_vm, late_vm, rows_vm],
+        3 * large,
         [queries, keys, values],
-        [rows_vm] * 2 + [chunks] * 3,
-        {3: 1},
+        [rows_vm, late_vm] + [chunks] * 3,
+        {3: 0},
     )
     key_grad, value_grad = local_call(
         final_body,
-        [value_kept, key_part, value_part, grad_low],
+        [value_kept, key_part, early_part, late_part, grad_low],
         [hbm(tokens, bf16)] * 2,
         2 * small,
         [keys],

time: 65.8 us -> 66.6 us (1.012)
  starting transfers between devices: 19.6 us -> 23.4 us
  waiting for transfers between devices: 10.4 us -> 7.92 us
    all_to_all x4, starting transfers between devices: 19.6 us -> 23.4 us  [exchange(): return lax.all_to_all(pieces, axis, 0, 0, axis_index_groups=groups)]
    all_to_all x4, waiting for transfers between devices: 10.4 us -> 7.92 us  [exchange(): return lax.all_to_all(pieces, axis, 0, 0, axis_index_groups=groups)]
  transfers between devices with their start and end apart: 4 -> 4, of which waited for: 3 -> 4; matrix products, arithmetic and copies ran while one was open for 0% -> 0% of each run, Pallas kernels for 29% -> 28%
where the time goes in v11:
time: 66.6 us; the launch traced here: 65.9 us
  Pallas kernels  28 us (42%)
  starting transfers between devices  23.4 us (35%)
  waiting for transfers between devices  7.92 us (12%)
  blocking collectives  5.67 us (9%)
  between operations  0.87 us (1%)
    pallas_call x10, Pallas kernels, local_call(): pl.pallas_call(body, in_specs=specs, out_specs=out_specs, out_shape=outs,...  28 us
    all_to_all x4, starting transfers between devices, exchange(): return lax.all_to_all(pieces, axis, 0, 0, axis_index_groups=groups)  23.4 us
    all_to_all x4, waiting for transfers between devices, exchange(): return lax.all_to_all(pieces, axis, 0, 0, axis_index_groups=groups)  7.92 us
    psum x1, blocking collectives, shards(): sums = lax.psum(sums, 'head')  5.67 us
  transfers between devices with their start and end apart: 4, of which 4 were waited for; matrix products, arithmetic and copies ran while one was open for 0% of the time, Pallas kernels for 28%

profile of v11, /device:TPU:0, one launch (start us, length us, event | category | flops | bytes accessed | tf_op | source)
XLA Modules:
  0.0 65.9 jit_solution(5720064669720070878)
XLA Ops:
  0.6 3.0 %shard_map.76 = bf16[1024,128]{1,0:T(8,128)(2,1)} custom-call(bf16[512,1024]{1,0:T(8,128)(2,1)} %key_hbm.9, bf16[512,1024]{1,0:T(8,128)(2,1)} %value_hbm.7), custom_call_target="tpu_custom_call" | custom-call | flops 134217728 | bytes 2097152 | tf_op jit(solution)/shard_map/pallas_call | solution.py:285
  3.6 7.9 %all-to-all-start = ((bf16[8,128,128]{2,1,0:T(8,128)(2,1)}), bf16[8,128,128]{2,1,0:T(8,128)(2,1)S(1)}, u32[]{:S(2)}, u32[]{:S(2)}) async-start(bf16[8,128,128]{2,1,0:T(8,128)(2,1)} %bitcast.10), calls=%async_computation | async-start | bytes 524288 | tf_op jit(solution)/shard_map/all_to_all | solution.py:319
  11.5 2.1 %shard_map.77 = (bf16[1024,512]{1,0:T(8,128)(2,1)S(1)}, bf16[1024,512]{1,0:T(8,128)(2,1)S(1)}) custom-call(bf16[512,1024]{1,0:T(8,128)(2,1)} %query_hbm.5, bf16[512,1024]{1,0:T(8,128)(2,1)} %grad_hbm.1), custom_call_target="tpu_custom_call" | custom-call | flops 402653184 | bytes 2097152 | tf_op jit(solution)/shard_map/pallas_call | solution.py:285
  13.6 4.7 %all-to-all-done.block_ref = bf16[8,128,128]{2,1,0:T(8,128)(2,1)S(1)} async-done(((bf16[8,128,128]{2,1,0:T(8,128)(2,1)}), bf16[8,128,128]{2,1,0:T(8,128)(2,1)S(1)}, u32[]{:S(2)}, u32[]{:S(2)}) %all-to-all-start) | async-done | bytes 262176 | tf_op jit(solution)/shard_map/all_to_all | solution.py:319
  18.3 0.8 %shard_map.79 = bf16[8,128,128]{2,1,0:T(8,128)(2,1)} custom-call(bf16[8,128,128]{2,1,0:T(8,128)(2,1)S(1)} %all-to-all-done.block_ref), custom_call_target="tpu_custom_call" | custom-call | flops 131072 | bytes 262144 | tf_op jit(solution)/shard_map/pallas_call | solution.py:285
  19.1 5.4 %all-to-all-start.1 = ((bf16[8,128,128]{2,1,0:T(8,128)(2,1)}), bf16[8,128,128]{2,1,0:T(8,128)(2,1)S(1)}, u32[]{:S(2)}, u32[]{:S(2)}) async-start(bf16[8,128,128]{2,1,0:T(8,128)(2,1)} %shard_map.79), calls=%async_computation.1 | async-start | bytes 524288 | tf_op jit(solution)/shard_map/all_to_all | solution.py:319
  24.5 0.0 copy-start
  24.5 4.7 %shard_map.78.local_ref = bf16[1024,512]{1,0:T(8,128)(2,1)S(1)} custom-call(bf16[512,1024]{1,0:T(8,128)(2,1)} %key_hbm.9, bf16[512,1024]{1,0:T(8,128)(2,1)} %value_hbm.7, bf16[1024,512]{1,0:T(8,128)(2,1)S(1)} %get-tuple-element.26.flipped_ref), custom_call_target="tpu_custom_call" | custom-call | flops 805306368 | bytes 3145728 | tf_op jit(solution)/shard_map/pallas_call | solution.py:285
  29.2 1.5 %all-to-all-done.1 = bf16[8,128,128]{2,1,0:T(8,128)(2,1)S(1)} async-done(((bf16[8,128,128]{2,1,0:T(8,128)(2,1)}), bf16[8,128,128]{2,1,0:T(8,128)(2,1)S(1)}, u32[]{:S(2)}, u32[]{:S(2)}) %all-to-all-start.1) | async-done | bytes 262176 | tf_op jit(solution)/shard_map/all_to_all | solution.py:319
  30.6 0.0 copy-done
  30.6 0.8 %shard_map.80 = (bf16[1024,512]{1,0:T(8,128)(2,1)S(1)}, f32[2,512]{1,0:T(2,128)S(1)}) custom-call(f32[1,1024]{1,0:T(1,128)S(1)} %bitcast.8, bf16[1024,512]{1,0:T(8,128)(2,1)S(1)} %get-tuple-element.26.flipped_ref, bf16[1024,512]{1,0:T(8,128)(2,1)S(1)} %get-tuple-element.27.grad_ref, ...), custom_call_target="tpu_custom_call", output_to_operand_aliasing={{0}: (3, {})} | custom-call | flops 134217728 | bytes 3411968 | tf_op jit(solution)/shard_map/pallas_call | solution.py:285
  31.5 5.7 %psum.7.sums_ref = f32[2,512]{1,0:T(2,128)S(1)} all-reduce(f32[2,512]{1,0:T(2,128)S(1)} %get-tuple-element.30), channel_id=1, replica_groups=mesh['seq'=8,'head'=4] {'head'}, use_global_device_ids=true, to_apply=%region_0.0 | all-reduce | flops 1024 | bytes 8192 | tf_op jit(solution)/shard_map/psum | solution.py:365
  37.1 1.5 %shard_map.81 = (bf16[1024,512]{1,0:T(8,128)(2,1)S(1)}, bf16[1024,128]{1,0:T(8,128)(2,1)}) custom-call(f32[1,1024]{1,0:T(1,128)S(1)} %bitcast.9, bf16[1024,512]{1,0:T(8,128)(2,1)S(1)} %get-tuple-element.26.flipped_ref, bf16[1024,512]{1,0:T(8,128)(2,1)S(1)} %get-tuple-element.27.grad_ref, ...), custom_call_target="tpu_custom_call", output_to_operand_aliasing={{0}: (3, {})} | custom-call | flops 134217728 | bytes 3153920 | tf_op jit(solution)/shard_map/pallas_call | solution.py:285
  38.6 4.7 %all-to-all-start.2 = ((bf16[8,128,128]{2,1,0:T(8,128)(2,1)}), bf16[8,128,128]{2,1,0:T(8,128)(2,1)S(1)}, u32[]{:S(2)}, u32[]{:S(2)}) async-start(bf16[8,128,128]{2,1,0:T(8,128)(2,1)} %bitcast.11), calls=%async_computation.2 | async-start | bytes 524288 | tf_op jit(solution)/shard_map/all_to_all | solution.py:319
  43.3 5.9 %shard_map.82 = (bf16[512,1024]{1,0:T(8,128)(2,1)}, bf16[512,1024]{1,0:T(8,128)(2,1)S(1)}, bf16[512,512]{1,0:T(8,128)(2,1)S(1)}) custom-call(bf16[512,1024]{1,0:T(8,128)(2,1)} %query_hbm.5, bf16[512,1024]{1,0:T(8,128)(2,1)} %key_hbm.9, bf16[512,1024]{1,0:T(8,128)(2,1)} %value_hbm.7, bf16[1024,512]{1,0:T(8,128)(2,1)S(1)} %get-tuple-element.32.flipped_ref, ...), custom_call_target="tpu_custom_call" | custom-call | flops 939524096 | bytes 4456448 | tf_op jit(solution)/shard_map/pallas_call | solution.py:285
  49.2 1.1 %all-to-all-done.2.block_ref = bf16[8,128,128]{2,1,0:T(8,128)(2,1)S(1)} async-done(((bf16[8,128,128]{2,1,0:T(8,128)(2,1)}), bf16[8,128,128]{2,1,0:T(8,128)(2,1)S(1)}, u32[]{:S(2)}, u32[]{:S(2)}) %all-to-all-start.2) | async-done | bytes 262176 | tf_op jit(solution)/shard_map/all_to_all | solution.py:319
  50.3 0.8 %shard_map.84 = bf16[8,128,128]{2,1,0:T(8,128)(2,1)} custom-call(bf16[8,128,128]{2,1,0:T(8,128)(2,1)S(1)} %all-to-all-done.2.block_ref), custom_call_target="tpu_custom_call" | custom-call | flops 131072 | bytes 262144 | tf_op jit(solution)/shard_map/pallas_call | solution.py:285
  51.1 5.5 %all-to-all-start.3 = ((bf16[8,128,128]{2,1,0:T(8,128)(2,1)}), bf16[8,128,128]{2,1,0:T(8,128)(2,1)S(1)}, u32[]{:S(2)}, u32[]{:S(2)}) async-start(bf16[8,128,128]{2,1,0:T(8,128)(2,1)} %shard_map.84), calls=%async_computation.3 | async-start | bytes 524288 | tf_op jit(solution)/shard_map/all_to_all | solution.py:319
  56.6 5.5 %shard_map.83 = (bf16[512,1024]{1,0:T(8,128)(2,1)S(1)}, bf16[512,512]{1,0:T(8,128)(2,1)S(1)}, bf16[512,1024]{1,0:T(8,128)(2,1)S(1)}) custom-call(bf16[512,1024]{1,0:T(8,128)(2,1)} %query_hbm.5, bf16[512,1024]{1,0:T(8,128)(2,1)} %key_hbm.9, bf16[512,1024]{1,0:T(8,128)(2,1)} %value_hbm.7, ...), custom_call_target="tpu_custom_call", output_to_operand_aliasing={{0}: (3, {})} | custom-call | flops 1207959552 | bytes 4194304 | tf_op jit(solution)/shard_map/pallas_call | solution.py:285
  62.1 0.6 all-to-all-done.3
  62.8 2.9 %shard_map.85 = (bf16[512,1024]{1,0:T(8,128)(2,1)}, bf16[512,1024]{1,0:T(8,128)(2,1)}) custom-call(bf16[512,1024]{1,0:T(8,128)(2,1)} %key_hbm.9, bf16[512,1024]{1,0:T(8,128)(2,1)S(1)} %get-tuple-element.38.value_ref, bf16[512,1024]{1,0:T(8,128)(2,1)S(1)} %get-tuple-element.39.key_part, bf16[512,512]{1,0:T(8,128)(2,1)S(1)} %get-tuple-element.40.early_part, ...), custom_call_target="tpu_custom_call" | custom-call | flops 268435456 | bytes 4456448 | tf_op jit(solution)/shard_map/pallas_call | solution.py:285
Async XLA Ops:
  3.6 14.7 %all-to-all-start = ((bf16[8,128,128]{2,1,0:T(8,128)(2,1)}), bf16[8,128,128]{2,1,0:T(8,128)(2,1)S(1)}, u32[]{:S(2)}, u32[]{:S(2)}) async-start(bf16[8,128,128]{2,1,0:T(8,128)(2,1)} %bitcast.10), calls=%async_computation | async-start | bytes 524288 | tf_op jit(solution)/shard_map/all_to_all | solution.py:319
  19.1 11.5 %all-to-all-start.1 = ((bf16[8,128,128]{2,1,0:T(8,128)(2,1)}), bf16[8,128,128]{2,1,0:T(8,128)(2,1)S(1)}, u32[]{:S(2)}, u32[]{:S(2)}) async-start(bf16[8,128,128]{2,1,0:T(8,128)(2,1)} %shard_map.79), calls=%async_computation.1 | async-start | bytes 524288 | tf_op jit(solution)/shard_map/all_to_all | solution.py:319
  24.5 6.1 %copy-start = (f32[1024]{0:T(1024)S(1)}, f32[1024]{0:T(1024)}, u32[]{:S(2)}) copy-start(f32[1024]{0:T(1024)} %param.9) | copy-start | bytes 12292
  38.6 11.7 %all-to-all-start.2 = ((bf16[8,128,128]{2,1,0:T(8,128)(2,1)}), bf16[8,128,128]{2,1,0:T(8,128)(2,1)S(1)}, u32[]{:S(2)}, u32[]{:S(2)}) async-start(bf16[8,128,128]{2,1,0:T(8,128)(2,1)} %bitcast.11), calls=%async_computation.2 | async-start | bytes 524288 | tf_op jit(solution)/shard_map/all_to_all | solution.py:319
  51.1 11.6 %all-to-all-start.3 = ((bf16[8,128,128]{2,1,0:T(8,128)(2,1)}), bf16[8,128,128]{2,1,0:T(8,128)(2,1)S(1)}, u32[]{:S(2)}, u32[]{:S(2)}) async-start(bf16[8,128,128]{2,1,0:T(8,128)(2,1)} %shard_map.84), calls=%async_computation.3 | async-start | bytes 524288 | tf_op jit(solution)/shard_map/all_to_all | solution.py:319

commit v12 on v11

--- a/solution.py
+++ b/solution.py
@@ -53,9 +53,9 @@
 
 
 def start_all(*groups):
-    for parts in zip(*groups):
-        for part in parts:
-            part.start()
+    for index, parts in enumerate(zip(*groups)):
+        for other, part in enumerate(parts):
+            part.start(priority=(index + other) % 2)
 
 
 def wait_all(*groups):
@@ -77,7 +77,7 @@
         for start in range(cols.start, cols.stop, HEAD_DIM):
             head = slice(start, start + HEAD_DIM)
             state_ref[head, :] = mm_tn(key_ref[:, head], value_ref[:, head]).astype(jnp.bfloat16)
-        stores[index].start()
+        stores[index].start(priority=index % 2)
     wait_all(stores)
 
 
@@ -207,7 +207,7 @@
                 dscore = masked(mm_nt(dout, value_ref[:end, cols]), start, 0, True)
                 grad = mm(dscore, key_ref[:end, cols]) + mm_nt(dout, state_ref[cols, :])
                 out_ref[start:end, cols] = grad.astype(jnp.bfloat16)
-        stores[index].start()
+        stores[index].start(priority=index % 2)
     wait_all(query_copies)
     for cols in pieces_of(value_out, HEAD_DIM):
         value_local(query_ref, key_ref, dout_ref[:, cols], cols, value_out.at[:, cols])
@@ -257,7 +257,7 @@
             cols = slice(left, left + HEAD_DIM)
             grad = key_part[:, cols].astype(jnp.float32) + mm_nt(value_ref[:, cols], state_ref[cols, :])
             key_out[:, cols] = grad.astype(jnp.bfloat16)
-        key_stores[index].start()
+        key_stores[index].start(priority=index % 2)
     for index, step in enumerate(pieces_of(value_out, COPY_COLS)):
         keys[index].wait()
         for left in range(step.start, step.stop, HEAD_DIM):
@@ -269,7 +269,7 @@
                 part = late_part[:, left - early : left - early + HEAD_DIM]
             grad = part.astype(jnp.float32) + mm(key_ref[:, cols], state_ref[cols, :])
             value_out[:, cols] = grad.astype(jnp.bfloat16)
-        value_stores[index].start()
+        value_stores[index].start(priority=index % 2)
     wait_all(key_stores, value_stores)
 
 
@@ -311,7 +311,8 @@
 def places_in_order(count):
     quarter = count // 4
     first, second, third, fourth = (list(range(at, at + quarter)) for at in range(0, count, quarter))
-    return second + fourth + first[::-1] + third
+    half = quarter // 2
+    return second + first[:half] + third[:half] + first[half:] + third[half:] + fourth
 
 
 def exchange(pieces, axis):

time: 66.6 us -> 66.5 us (level)
  starting transfers between devices: 23.4 us -> 19.6 us
  waiting for transfers between devices: 7.92 us -> 10.4 us
  Pallas kernels: 28 us -> 29.2 us
    all_to_all x4, starting transfers between devices: 23.4 us -> 19.6 us  [exchange(): return lax.all_to_all(pieces, axis, 0, 0, axis_index_groups=groups)]
    all_to_all x4, waiting for transfers between devices: 7.92 us -> 10.4 us  [exchange(): return lax.all_to_all(pieces, axis, 0, 0, axis_index_groups=groups)]
    pallas_call x10, Pallas kernels: 28 us -> 29.2 us  [local_call(): pl.pallas_call(body, in_specs=specs, out_specs=out_specs, out_shape=outs,...]
  transfers between devices with their start and end apart: 4 -> 4, of which waited for: 4 -> 4; matrix products, arithmetic and copies ran while one was open for 0% -> 0% of each run, Pallas kernels for 28% -> 29%
where the time goes in v12:
time: 66.5 us; the launch traced here: 65.8 us
  Pallas kernels  29.2 us (44%)
  starting transfers between devices  19.6 us (29%)
  waiting for transfers between devices  10.4 us (16%)
  blocking collectives  5.67 us (9%)
  between operations  0.87 us (1%)
    pallas_call x10, Pallas kernels, local_call(): pl.pallas_call(body, in_specs=specs, out_specs=out_specs, out_shape=outs,...  29.2 us
    all_to_all x4, starting transfers between devices, exchange(): return lax.all_to_all(pieces, axis, 0, 0, axis_index_groups=groups)  19.6 us
    all_to_all x4, waiting for transfers between devices, exchange(): return lax.all_to_all(pieces, axis, 0, 0, axis_index_groups=groups)  10.4 us
    psum x1, blocking collectives, shards(): sums = lax.psum(sums, 'head')  5.67 us
  transfers between devices with their start and end apart: 4, of which 4 were waited for; matrix products, arithmetic and copies ran while one was open for 0% of the time, Pallas kernels for 29%

profile of v12, /device:TPU:0, one launch (start us, length us, event | category | flops | bytes accessed | tf_op | source)
XLA Modules:
  0.0 65.8 jit_solution(12342186549015739941)
XLA Ops:
  0.6 3.2 %shard_map.76 = bf16[1024,128]{1,0:T(8,128)(2,1)} custom-call(bf16[512,1024]{1,0:T(8,128)(2,1)} %key_hbm.9, bf16[512,1024]{1,0:T(8,128)(2,1)} %value_hbm.7), custom_call_target="tpu_custom_call" | custom-call | flops 134217728 | bytes 2097152 | tf_op jit(solution)/shard_map/pallas_call | solution.py:285
  3.9 7.9 %all-to-all-start = ((bf16[8,128,128]{2,1,0:T(8,128)(2,1)}), bf16[8,128,128]{2,1,0:T(8,128)(2,1)S(1)}, u32[]{:S(2)}, u32[]{:S(2)}) async-start(bf16[8,128,128]{2,1,0:T(8,128)(2,1)} %bitcast.10), calls=%async_computation | async-start | bytes 524288 | tf_op jit(solution)/shard_map/all_to_all | solution.py:320
  11.7 2.2 %shard_map.77 = (bf16[1024,512]{1,0:T(8,128)(2,1)S(1)}, bf16[1024,512]{1,0:T(8,128)(2,1)S(1)}) custom-call(bf16[512,1024]{1,0:T(8,128)(2,1)} %query_hbm.5, bf16[512,1024]{1,0:T(8,128)(2,1)} %grad_hbm.1), custom_call_target="tpu_custom_call" | custom-call | flops 402653184 | bytes 2097152 | tf_op jit(solution)/shard_map/pallas_call | solution.py:285
  14.0 5.7 %all-to-all-done.block_ref = bf16[8,128,128]{2,1,0:T(8,128)(2,1)S(1)} async-done(((bf16[8,128,128]{2,1,0:T(8,128)(2,1)}), bf16[8,128,128]{2,1,0:T(8,128)(2,1)S(1)}, u32[]{:S(2)}, u32[]{:S(2)}) %all-to-all-start) | async-done | bytes 262176 | tf_op jit(solution)/shard_map/all_to_all | solution.py:320
  19.7 0.8 %shard_map.79 = bf16[8,128,128]{2,1,0:T(8,128)(2,1)} custom-call(bf16[8,128,128]{2,1,0:T(8,128)(2,1)S(1)} %all-to-all-done.block_ref), custom_call_target="tpu_custom_call" | custom-call | flops 131072 | bytes 262144 | tf_op jit(solution)/shard_map/pallas_call | solution.py:285
  20.5 3.7 %all-to-all-start.1 = ((bf16[8,128,128]{2,1,0:T(8,128)(2,1)}), bf16[8,128,128]{2,1,0:T(8,128)(2,1)S(1)}, u32[]{:S(2)}, u32[]{:S(2)}) async-start(bf16[8,128,128]{2,1,0:T(8,128)(2,1)} %shard_map.79), calls=%async_computation.1 | async-start | bytes 524288 | tf_op jit(solution)/shard_map/all_to_all | solution.py:320
  24.1 0.0 copy-start
  24.1 4.9 %shard_map.78.local_ref = bf16[1024,512]{1,0:T(8,128)(2,1)S(1)} custom-call(bf16[512,1024]{1,0:T(8,128)(2,1)} %key_hbm.9, bf16[512,1024]{1,0:T(8,128)(2,1)} %value_hbm.7, bf16[1024,512]{1,0:T(8,128)(2,1)S(1)} %get-tuple-element.26.flipped_ref), custom_call_target="tpu_custom_call" | custom-call | flops 805306368 | bytes 3145728 | tf_op jit(solution)/shard_map/pallas_call | solution.py:285
  29.1 1.3 %all-to-all-done.1 = bf16[8,128,128]{2,1,0:T(8,128)(2,1)S(1)} async-done(((bf16[8,128,128]{2,1,0:T(8,128)(2,1)}), bf16[8,128,128]{2,1,0:T(8,128)(2,1)S(1)}, u32[]{:S(2)}, u32[]{:S(2)}) %all-to-all-start.1) | async-done | bytes 262176 | tf_op jit(solution)/shard_map/all_to_all | solution.py:320
  30.4 0.0 copy-done
  30.4 0.8 %shard_map.80 = (bf16[1024,512]{1,0:T(8,128)(2,1)S(1)}, f32[2,512]{1,0:T(2,128)S(1)}) custom-call(f32[1,1024]{1,0:T(1,128)S(1)} %bitcast.8, bf16[1024,512]{1,0:T(8,128)(2,1)S(1)} %get-tuple-element.26.flipped_ref, bf16[1024,512]{1,0:T(8,128)(2,1)S(1)} %get-tuple-element.27.grad_ref, ...), custom_call_target="tpu_custom_call", output_to_operand_aliasing={{0}: (3, {})} | custom-call | flops 134217728 | bytes 3411968 | tf_op jit(solution)/shard_map/pallas_call | solution.py:285
  31.2 5.7 %psum.7.sums_ref = f32[2,512]{1,0:T(2,128)S(1)} all-reduce(f32[2,512]{1,0:T(2,128)S(1)} %get-tuple-element.30), channel_id=1, replica_groups=mesh['seq'=8,'head'=4] {'head'}, use_global_device_ids=true, to_apply=%region_0.0 | all-reduce | flops 1024 | bytes 8192 | tf_op jit(solution)/shard_map/psum | solution.py:366
  36.9 1.5 %shard_map.81 = (bf16[1024,512]{1,0:T(8,128)(2,1)S(1)}, bf16[1024,128]{1,0:T(8,128)(2,1)}) custom-call(f32[1,1024]{1,0:T(1,128)S(1)} %bitcast.9, bf16[1024,512]{1,0:T(8,128)(2,1)S(1)} %get-tuple-element.26.flipped_ref, bf16[1024,512]{1,0:T(8,128)(2,1)S(1)} %get-tuple-element.27.grad_ref, ...), custom_call_target="tpu_custom_call", output_to_operand_aliasing={{0}: (3, {})} | custom-call | flops 134217728 | bytes 3153920 | tf_op jit(solution)/shard_map/pallas_call | solution.py:285
  38.3 4.5 %all-to-all-start.2 = ((bf16[8,128,128]{2,1,0:T(8,128)(2,1)}), bf16[8,128,128]{2,1,0:T(8,128)(2,1)S(1)}, u32[]{:S(2)}, u32[]{:S(2)}) async-start(bf16[8,128,128]{2,1,0:T(8,128)(2,1)} %bitcast.11), calls=%async_computation.2 | async-start | bytes 524288 | tf_op jit(solution)/shard_map/all_to_all | solution.py:320
  42.8 6.2 %shard_map.82 = (bf16[512,1024]{1,0:T(8,128)(2,1)}, bf16[512,1024]{1,0:T(8,128)(2,1)S(1)}, bf16[512,512]{1,0:T(8,128)(2,1)S(1)}) custom-call(bf16[512,1024]{1,0:T(8,128)(2,1)} %query_hbm.5, bf16[512,1024]{1,0:T(8,128)(2,1)} %key_hbm.9, bf16[512,1024]{1,0:T(8,128)(2,1)} %value_hbm.7, bf16[1024,512]{1,0:T(8,128)(2,1)S(1)} %get-tuple-element.32.flipped_ref, ...), custom_call_target="tpu_custom_call" | custom-call | flops 939524096 | bytes 4456448 | tf_op jit(solution)/shard_map/pallas_call | solution.py:285
  49.0 2.0 %all-to-all-done.2.block_ref = bf16[8,128,128]{2,1,0:T(8,128)(2,1)S(1)} async-done(((bf16[8,128,128]{2,1,0:T(8,128)(2,1)}), bf16[8,128,128]{2,1,0:T(8,128)(2,1)S(1)}, u32[]{:S(2)}, u32[]{:S(2)}) %all-to-all-start.2) | async-done | bytes 262176 | tf_op jit(solution)/shard_map/all_to_all | solution.py:320
  51.1 0.8 %shard_map.84 = bf16[8,128,128]{2,1,0:T(8,128)(2,1)} custom-call(bf16[8,128,128]{2,1,0:T(8,128)(2,1)S(1)} %all-to-all-done.2.block_ref), custom_call_target="tpu_custom_call" | custom-call | flops 131072 | bytes 262144 | tf_op jit(solution)/shard_map/pallas_call | solution.py:285
  51.9 3.6 %all-to-all-start.3 = ((bf16[8,128,128]{2,1,0:T(8,128)(2,1)}), bf16[8,128,128]{2,1,0:T(8,128)(2,1)S(1)}, u32[]{:S(2)}, u32[]{:S(2)}) async-start(bf16[8,128,128]{2,1,0:T(8,128)(2,1)} %shard_map.84), calls=%async_computation.3 | async-start | bytes 524288 | tf_op jit(solution)/shard_map/all_to_all | solution.py:320
  55.5 5.8 %shard_map.83 = (bf16[512,1024]{1,0:T(8,128)(2,1)S(1)}, bf16[512,512]{1,0:T(8,128)(2,1)S(1)}, bf16[512,1024]{1,0:T(8,128)(2,1)S(1)}) custom-call(bf16[512,1024]{1,0:T(8,128)(2,1)} %query_hbm.5, bf16[512,1024]{1,0:T(8,128)(2,1)} %key_hbm.9, bf16[512,1024]{1,0:T(8,128)(2,1)} %value_hbm.7, ...), custom_call_target="tpu_custom_call", output_to_operand_aliasing={{0}: (3, {})} | custom-call | flops 1207959552 | bytes 4194304 | tf_op jit(solution)/shard_map/pallas_call | solution.py:285
  61.4 1.3 %all-to-all-done.3 = bf16[8,128,128]{2,1,0:T(8,128)(2,1)S(1)} async-done(((bf16[8,128,128]{2,1,0:T(8,128)(2,1)}), bf16[8,128,128]{2,1,0:T(8,128)(2,1)S(1)}, u32[]{:S(2)}, u32[]{:S(2)}) %all-to-all-start.3) | async-done | bytes 262176 | tf_op jit(solution)/shard_map/all_to_all | solution.py:320
  62.7 2.9 %shard_map.85 = (bf16[512,1024]{1,0:T(8,128)(2,1)}, bf16[512,1024]{1,0:T(8,128)(2,1)}) custom-call(bf16[512,1024]{1,0:T(8,128)(2,1)} %key_hbm.9, bf16[512,1024]{1,0:T(8,128)(2,1)S(1)} %get-tuple-element.38.value_ref, bf16[512,1024]{1,0:T(8,128)(2,1)S(1)} %get-tuple-element.39.key_part, bf16[512,512]{1,0:T(8,128)(2,1)S(1)} %get-tuple-element.40.early_part, ...), custom_call_target="tpu_custom_call" | custom-call | flops 268435456 | bytes 4456448 | tf_op jit(solution)/shard_map/pallas_call | solution.py:285
Async XLA Ops:
  3.9 15.8 %all-to-all-start = ((bf16[8,128,128]{2,1,0:T(8,128)(2,1)}), bf16[8,128,128]{2,1,0:T(8,128)(2,1)S(1)}, u32[]{:S(2)}, u32[]{:S(2)}) async-start(bf16[8,128,128]{2,1,0:T(8,128)(2,1)} %bitcast.10), calls=%async_computation | async-start | bytes 524288 | tf_op jit(solution)/shard_map/all_to_all | solution.py:320
  20.5 9.9 %all-to-all-start.1 = ((bf16[8,128,128]{2,1,0:T(8,128)(2,1)}), bf16[8,128,128]{2,1,0:T(8,128)(2,1)S(1)}, u32[]{:S(2)}, u32[]{:S(2)}) async-start(bf16[8,128,128]{2,1,0:T(8,128)(2,1)} %shard_map.79), calls=%async_computation.1 | async-start | bytes 524288 | tf_op jit(solution)/shard_map/all_to_all | solution.py:320
  24.1 6.3 %copy-start = (f32[1024]{0:T(1024)S(1)}, f32[1024]{0:T(1024)}, u32[]{:S(2)}) copy-start(f32[1024]{0:T(1024)} %param.9) | copy-start | bytes 12292
  38.3 12.7 %all-to-all-start.2 = ((bf16[8,128,128]{2,1,0:T(8,128)(2,1)}), bf16[8,128,128]{2,1,0:T(8,128)(2,1)S(1)}, u32[]{:S(2)}, u32[]{:S(2)}) async-start(bf16[8,128,128]{2,1,0:T(8,128)(2,1)} %bitcast.11), calls=%async_computation.2 | async-start | bytes 524288 | tf_op jit(solution)/shard_map/all_to_all | solution.py:320
  51.9 10.8 %all-to-all-start.3 = ((bf16[8,128,128]{2,1,0:T(8,128)(2,1)}), bf16[8,128,128]{2,1,0:T(8,128)(2,1)S(1)}, u32[]{:S(2)}, u32[]{:S(2)}) async-start(bf16[8,128,128]{2,1,0:T(8,128)(2,1)} %shard_map.84), calls=%async_computation.3 | async-start | bytes 524288 | tf_op jit(solution)/shard_map/all_to_all | solution.py:320

commit v13 on v11

--- a/solution.py
+++ b/solution.py
@@ -311,7 +311,9 @@
 def places_in_order(count):
     quarter = count // 4
     first, second, third, fourth = (list(range(at, at + quarter)) for at in range(0, count, quarter))
-    return second + fourth + first[::-1] + third
+    half = quarter // 2
+    order = second + first[:half] + third[:half] + first[half:] + third[half:] + fourth
+    return [count - 1 - place for place in order]
 
 
 def exchange(pieces, axis):

time: 66.6 us -> 65.4 us (0.982)
  waiting for transfers between devices: 7.92 us -> 3.41 us
  starting transfers between devices: 23.4 us -> 26.7 us
    all_to_all x4, waiting for transfers between devices: 7.92 us -> 3.41 us  [exchange(): return lax.all_to_all(pieces, axis, 0, 0, axis_index_groups=groups)]
    all_to_all x4, starting transfers between devices: 23.4 us -> 26.7 us  [exchange(): return lax.all_to_all(pieces, axis, 0, 0, axis_index_groups=groups)]
  transfers between devices with their start and end apart: 4 -> 4, of which waited for: 4 -> 1; matrix products, arithmetic and copies ran while one was open for 0% -> 0% of each run, Pallas kernels for 28% -> 28%
where the time goes in v13:
time: 65.4 us; the launch traced here: 64.7 us
  Pallas kernels  28 us (43%)
  starting transfers between devices  26.7 us (41%)
  blocking collectives  5.67 us (9%)
  waiting for transfers between devices  3.41 us (5%)
  between operations  0.9 us (1%)
    pallas_call x10, Pallas kernels, local_call(): pl.pallas_call(body, in_specs=specs, out_specs=out_specs, out_shape=outs,...  28 us
    all_to_all x4, starting transfers between devices, exchange(): return lax.all_to_all(pieces, axis, 0, 0, axis_index_groups=groups)  26.7 us
    psum x1, blocking collectives, shards(): sums = lax.psum(sums, 'head')  5.67 us
    all_to_all x4, waiting for transfers between devices, exchange(): return lax.all_to_all(pieces, axis, 0, 0, axis_index_groups=groups)  3.41 us
  transfers between devices with their start and end apart: 4, of which 1 were waited for; matrix products, arithmetic and copies ran while one was open for 0% of the time, Pallas kernels for 28%

profile of v13, /device:TPU:0, one launch (start us, length us, event | category | flops | bytes accessed | tf_op | source)
XLA Modules:
  0.0 64.7 jit_solution(14662229212829970954)
XLA Ops:
  0.6 3.0 %shard_map.76 = bf16[1024,128]{1,0:T(8,128)(2,1)} custom-call(bf16[512,1024]{1,0:T(8,128)(2,1)} %key_hbm.9, bf16[512,1024]{1,0:T(8,128)(2,1)} %value_hbm.7), custom_call_target="tpu_custom_call" | custom-call | flops 134217728 | bytes 2097152 | tf_op jit(solution)/shard_map/pallas_call | solution.py:285
  3.6 8.4 %all-to-all-start = ((bf16[8,128,128]{2,1,0:T(8,128)(2,1)}), bf16[8,128,128]{2,1,0:T(8,128)(2,1)S(1)}, u32[]{:S(2)}, u32[]{:S(2)}) async-start(bf16[8,128,128]{2,1,0:T(8,128)(2,1)} %bitcast.10), calls=%async_computation | async-start | bytes 524288 | tf_op jit(solution)/shard_map/all_to_all | solution.py:321
  12.0 2.1 %shard_map.77 = (bf16[1024,512]{1,0:T(8,128)(2,1)S(1)}, bf16[1024,512]{1,0:T(8,128)(2,1)S(1)}) custom-call(bf16[512,1024]{1,0:T(8,128)(2,1)} %query_hbm.5, bf16[512,1024]{1,0:T(8,128)(2,1)} %grad_hbm.1), custom_call_target="tpu_custom_call" | custom-call | flops 402653184 | bytes 2097152 | tf_op jit(solution)/shard_map/pallas_call | solution.py:285
  14.1 3.4 %all-to-all-done.block_ref = bf16[8,128,128]{2,1,0:T(8,128)(2,1)S(1)} async-done(((bf16[8,128,128]{2,1,0:T(8,128)(2,1)}), bf16[8,128,128]{2,1,0:T(8,128)(2,1)S(1)}, u32[]{:S(2)}, u32[]{:S(2)}) %all-to-all-start) | async-done | bytes 262176 | tf_op jit(solution)/shard_map/all_to_all | solution.py:321
  17.5 0.8 %shard_map.79 = bf16[8,128,128]{2,1,0:T(8,128)(2,1)} custom-call(bf16[8,128,128]{2,1,0:T(8,128)(2,1)S(1)} %all-to-all-done.block_ref), custom_call_target="tpu_custom_call" | custom-call | flops 131072 | bytes 262144 | tf_op jit(solution)/shard_map/pallas_call | solution.py:285
  18.3 6.3 %all-to-all-start.1 = ((bf16[8,128,128]{2,1,0:T(8,128)(2,1)}), bf16[8,128,128]{2,1,0:T(8,128)(2,1)S(1)}, u32[]{:S(2)}, u32[]{:S(2)}) async-start(bf16[8,128,128]{2,1,0:T(8,128)(2,1)} %shard_map.79), calls=%async_computation.1 | async-start | bytes 524288 | tf_op jit(solution)/shard_map/all_to_all | solution.py:321
  24.6 0.0 copy-start
  24.6 4.7 %shard_map.78.local_ref = bf16[1024,512]{1,0:T(8,128)(2,1)S(1)} custom-call(bf16[512,1024]{1,0:T(8,128)(2,1)} %key_hbm.9, bf16[512,1024]{1,0:T(8,128)(2,1)} %value_hbm.7, bf16[1024,512]{1,0:T(8,128)(2,1)S(1)} %get-tuple-element.26.flipped_ref), custom_call_target="tpu_custom_call" | custom-call | flops 805306368 | bytes 3145728 | tf_op jit(solution)/shard_map/pallas_call | solution.py:285
  29.3 0.0 all-to-all-done.1
  29.3 0.0 copy-done
  29.3 0.8 %shard_map.80 = (bf16[1024,512]{1,0:T(8,128)(2,1)S(1)}, f32[2,512]{1,0:T(2,128)S(1)}) custom-call(f32[1,1024]{1,0:T(1,128)S(1)} %bitcast.8, bf16[1024,512]{1,0:T(8,128)(2,1)S(1)} %get-tuple-element.26.flipped_ref, bf16[1024,512]{1,0:T(8,128)(2,1)S(1)} %get-tuple-element.27.grad_ref, ...), custom_call_target="tpu_custom_call", output_to_operand_aliasing={{0}: (3, {})} | custom-call | flops 134217728 | bytes 3411968 | tf_op jit(solution)/shard_map/pallas_call | solution.py:285
  30.2 5.7 %psum.7.sums_ref = f32[2,512]{1,0:T(2,128)S(1)} all-reduce(f32[2,512]{1,0:T(2,128)S(1)} %get-tuple-element.30), channel_id=1, replica_groups=mesh['seq'=8,'head'=4] {'head'}, use_global_device_ids=true, to_apply=%region_0.0 | all-reduce | flops 1024 | bytes 8192 | tf_op jit(solution)/shard_map/psum | solution.py:367
  35.8 1.5 %shard_map.81 = (bf16[1024,512]{1,0:T(8,128)(2,1)S(1)}, bf16[1024,128]{1,0:T(8,128)(2,1)}) custom-call(f32[1,1024]{1,0:T(1,128)S(1)} %bitcast.9, bf16[1024,512]{1,0:T(8,128)(2,1)S(1)} %get-tuple-element.26.flipped_ref, bf16[1024,512]{1,0:T(8,128)(2,1)S(1)} %get-tuple-element.27.grad_ref, ...), custom_call_target="tpu_custom_call", output_to_operand_aliasing={{0}: (3, {})} | custom-call | flops 134217728 | bytes 3153920 | tf_op jit(solution)/shard_map/pallas_call | solution.py:285
  37.3 6.1 %all-to-all-start.2 = ((bf16[8,128,128]{2,1,0:T(8,128)(2,1)}), bf16[8,128,128]{2,1,0:T(8,128)(2,1)S(1)}, u32[]{:S(2)}, u32[]{:S(2)}) async-start(bf16[8,128,128]{2,1,0:T(8,128)(2,1)} %bitcast.11), calls=%async_computation.2 | async-start | bytes 524288 | tf_op jit(solution)/shard_map/all_to_all | solution.py:321
  43.4 5.9 %shard_map.82 = (bf16[512,1024]{1,0:T(8,128)(2,1)}, bf16[512,1024]{1,0:T(8,128)(2,1)S(1)}, bf16[512,512]{1,0:T(8,128)(2,1)S(1)}) custom-call(bf16[512,1024]{1,0:T(8,128)(2,1)} %query_hbm.5, bf16[512,1024]{1,0:T(8,128)(2,1)} %key_hbm.9, bf16[512,1024]{1,0:T(8,128)(2,1)} %value_hbm.7, bf16[1024,512]{1,0:T(8,128)(2,1)S(1)} %get-tuple-element.32.flipped_ref, ...), custom_call_target="tpu_custom_call" | custom-call | flops 939524096 | bytes 4456448 | tf_op jit(solution)/shard_map/pallas_call | solution.py:285
  49.3 0.0 all-to-all-done.2.block_ref
  49.3 0.8 %shard_map.84 = bf16[8,128,128]{2,1,0:T(8,128)(2,1)} custom-call(bf16[8,128,128]{2,1,0:T(8,128)(2,1)S(1)} %all-to-all-done.2.block_ref), custom_call_target="tpu_custom_call" | custom-call | flops 131072 | bytes 262144 | tf_op jit(solution)/shard_map/pallas_call | solution.py:285
  50.1 6.0 %all-to-all-start.3 = ((bf16[8,128,128]{2,1,0:T(8,128)(2,1)}), bf16[8,128,128]{2,1,0:T(8,128)(2,1)S(1)}, u32[]{:S(2)}, u32[]{:S(2)}) async-start(bf16[8,128,128]{2,1,0:T(8,128)(2,1)} %shard_map.84), calls=%async_computation.3 | async-start | bytes 524288 | tf_op jit(solution)/shard_map/all_to_all | solution.py:321
  56.0 5.5 %shard_map.83 = (bf16[512,1024]{1,0:T(8,128)(2,1)S(1)}, bf16[512,512]{1,0:T(8,128)(2,1)S(1)}, bf16[512,1024]{1,0:T(8,128)(2,1)S(1)}) custom-call(bf16[512,1024]{1,0:T(8,128)(2,1)} %query_hbm.5, bf16[512,1024]{1,0:T(8,128)(2,1)} %key_hbm.9, bf16[512,1024]{1,0:T(8,128)(2,1)} %value_hbm.7, ...), custom_call_target="tpu_custom_call", output_to_operand_aliasing={{0}: (3, {})} | custom-call | flops 1207959552 | bytes 4194304 | tf_op jit(solution)/shard_map/pallas_call | solution.py:285
  61.6 0.0 all-to-all-done.3
  61.6 2.9 %shard_map.85 = (bf16[512,1024]{1,0:T(8,128)(2,1)}, bf16[512,1024]{1,0:T(8,128)(2,1)}) custom-call(bf16[512,1024]{1,0:T(8,128)(2,1)} %key_hbm.9, bf16[512,1024]{1,0:T(8,128)(2,1)S(1)} %get-tuple-element.38.value_ref, bf16[512,1024]{1,0:T(8,128)(2,1)S(1)} %get-tuple-element.39.key_part, bf16[512,512]{1,0:T(8,128)(2,1)S(1)} %get-tuple-element.40.early_part, ...), custom_call_target="tpu_custom_call" | custom-call | flops 268435456 | bytes 4456448 | tf_op jit(solution)/shard_map/pallas_call | solution.py:285
Async XLA Ops:
  3.6 13.9 %all-to-all-start = ((bf16[8,128,128]{2,1,0:T(8,128)(2,1)}), bf16[8,128,128]{2,1,0:T(8,128)(2,1)S(1)}, u32[]{:S(2)}, u32[]{:S(2)}) async-start(bf16[8,128,128]{2,1,0:T(8,128)(2,1)} %bitcast.10), calls=%async_computation | async-start | bytes 524288 | tf_op jit(solution)/shard_map/all_to_all | solution.py:321
  18.3 11.0 %all-to-all-start.1 = ((bf16[8,128,128]{2,1,0:T(8,128)(2,1)}), bf16[8,128,128]{2,1,0:T(8,128)(2,1)S(1)}, u32[]{:S(2)}, u32[]{:S(2)}) async-start(bf16[8,128,128]{2,1,0:T(8,128)(2,1)} %shard_map.79), calls=%async_computation.1 | async-start | bytes 524288 | tf_op jit(solution)/shard_map/all_to_all | solution.py:321
  24.6 4.7 %copy-start = (f32[1024]{0:T(1024)S(1)}, f32[1024]{0:T(1024)}, u32[]{:S(2)}) copy-start(f32[1024]{0:T(1024)} %param.9) | copy-start | bytes 12292
  37.3 12.0 %all-to-all-start.2 = ((bf16[8,128,128]{2,1,0:T(8,128)(2,1)}), bf16[8,128,128]{2,1,0:T(8,128)(2,1)S(1)}, u32[]{:S(2)}, u32[]{:S(2)}) async-start(bf16[8,128,128]{2,1,0:T(8,128)(2,1)} %bitcast.11), calls=%async_computation.2 | async-start | bytes 524288 | tf_op jit(solution)/shard_map/all_to_all | solution.py:321
  50.1 11.5 %all-to-all-start.3 = ((bf16[8,128,128]{2,1,0:T(8,128)(2,1)}), bf16[8,128,128]{2,1,0:T(8,128)(2,1)S(1)}, u32[]{:S(2)}, u32[]{:S(2)}) async-start(bf16[8,128,128]{2,1,0:T(8,128)(2,1)} %shard_map.84), calls=%async_computation.3 | async-start | bytes 524288 | tf_op jit(solution)/shard_map/all_to_all | solution.py:321

commit v14 on v13

--- a/solution.py
+++ b/solution.py
@@ -30,11 +30,17 @@
     return [slice(at, at + size) for at in range(0, ref.shape[1], size)]
 
 
-def masked(scores, row_start, col_start, rows_first):
-    rows = row_start + lax.broadcasted_iota(jnp.int32, scores.shape, 0)
-    cols = col_start + lax.broadcasted_iota(jnp.int32, scores.shape, 1)
+def masked(scores, diagonal, rows_first):
+    shape = (BLOCK, BLOCK)
+    rows = lax.broadcasted_iota(jnp.int32, shape, 0)
+    cols = lax.broadcasted_iota(jnp.int32, shape, 1)
     keep = rows >= cols if rows_first else cols >= rows
-    return jnp.where(keep, scores, 0.0).astype(jnp.bfloat16)
+    inside = slice(diagonal, diagonal + BLOCK)
+    kept = jnp.where(keep, scores[:, inside], 0.0).astype(jnp.bfloat16)
+    before = scores[:, :diagonal].astype(jnp.bfloat16)
+    after = scores[:, inside.stop :].astype(jnp.bfloat16)
+    parts = [part for part in (before, kept, after) if part.shape[1]]
+    return jnp.concatenate(parts, axis=1) if len(parts) > 1 else kept
 
 
 def column_copies(source, target, sems):
@@ -106,8 +112,13 @@
             cols = slice(left, left + HEAD_DIM)
             for start in range(0, rows, BLOCK):
                 end = start + BLOCK
-                scores = mm(key_ref[:end, cols], flipped_ref[cols, start:end])
-                weights = masked(scores, 0, start, False)
+                parts = []
+                for row in range(0, end, BLOCK):
+                    key = key_ref[row : row + BLOCK, cols]
+                    scores = mm(key, flipped_ref[cols, start:end])
+                    below = row == start
+                    parts.append(masked(scores, 0, False) if below else scores.astype(jnp.bfloat16))
+                weights = jnp.concatenate(parts, axis=0) if len(parts) > 1 else parts[0]
                 local = mm_tn(value_ref[:end, cols], weights)
                 local_ref[cols, start:end] = local.astype(jnp.bfloat16)
 
@@ -153,16 +164,18 @@
         cross += fold(scaled_grad(gain_ref, grad_ref, head) * attended)
     square = jnp.sum(square, axis=0, keepdims=True)
     cross = jnp.sum(cross, axis=0, keepdims=True)
-    sums_ref[0:1, :] = square
-    sums_ref[1:2, :] = cross
+    for group in range(sums_ref.shape[0]):
+        sums_ref[group, 0:1, :] = square
+        sums_ref[group, 1:2, :] = cross
 
 
 def dout_body(
     width, gain_ref, flipped_ref, grad_ref, attended_ref, sums_ref, dout_ref, own_hbm, own_ref, sems
 ):
     stores = row_copies(own_ref, own_hbm, sems)
-    inverse = 1.0 / jnp.sqrt(sums_ref[0:1, :] / width + EPSILON)
-    drop = sums_ref[1:2, :] * (inverse * inverse * inverse) / width
+    sums = sum(sums_ref[group] for group in range(sums_ref.shape[0]))
+    inverse = 1.0 / jnp.sqrt(sums[0:1, :] / width + EPSILON)
+    drop = sums[1:2, :] * (inverse * inverse * inverse) / width
     for head in heads_of(dout_ref):
         attended = dout_ref[head, :].astype(jnp.float32)
         dout = scaled_grad(gain_ref, grad_ref, head) * inverse - attended * drop
@@ -178,7 +191,7 @@
     rows = key_ref.shape[0]
     for start in range(0, rows, BLOCK):
         end = start + BLOCK
-        weights = masked(mm_nt(key_ref[start:end, cols], query_ref[start:, cols]), 0, 0, False)
+        weights = masked(mm_nt(key_ref[start:end, cols], query_ref[start:, cols]), 0, False)
         target[start:end, :] = mm(weights, dout[start:, :]).astype(jnp.bfloat16)
 
 
@@ -204,7 +217,7 @@
             for start in range(0, rows, BLOCK):
                 end = start + BLOCK
                 dout = dout_ref[start:end, cols]
-                dscore = masked(mm_nt(dout, value_ref[:end, cols]), start, 0, True)
+                dscore = masked(mm_nt(dout, value_ref[:end, cols]), start, True)
                 grad = mm(dscore, key_ref[:end, cols]) + mm_nt(dout, state_ref[cols, :])
                 out_ref[start:end, cols] = grad.astype(jnp.bfloat16)
         stores[index].start()
@@ -238,7 +251,8 @@
             for start in range(0, rows, BLOCK):
                 end = start + BLOCK
                 scores = mm_nt(value_ref[start:end, cols], dout[start:, :])
-                key_out[start:end, cols] = mm(masked(scores, 0, 0, False), query_ref[start:, cols]).astype(jnp.bfloat16)
+                grad = mm(masked(scores, 0, False), query_ref[start:, cols])
+                key_out[start:end, cols] = grad.astype(jnp.bfloat16)
             if left >= early:
                 late = slice(left - early, left - early + HEAD_DIM)
                 value_local(query_ref.at[:, early:], key_ref, dout, late, value_out.at[:, late])
@@ -316,6 +330,10 @@
     return [count - 1 - place for place in order]
 
 
+def odd_first(count):
+    return list(range(1, count, 2)) + list(range(0, count, 2))
+
+
 def exchange(pieces, axis):
     groups = [places_in_order(lax.axis_size(axis))]
     return lax.all_to_all(pieces, axis, 0, 0, axis_index_groups=groups)
@@ -357,14 +375,15 @@
     (local,) = local_call(
         local_body, [flipped], [flat_vm], 2 * large, [keys, values], [rows_vm] * 2 + [chunks] * 2
     )
+    groups = lax.axis_size("head")
     attended, sums = local_call(
         sums_body,
         [gain_row, flipped, grad_flipped, local, kv_low],
-        [flat_vm, vm((2, rows), f32)],
+        [flat_vm, vm((groups, 2, rows), f32)],
         small,
         aliases={3: 0},
     )
-    sums = lax.psum(sums, "head")
+    sums = lax.all_to_all(sums, "head", 0, 0, axis_index_groups=[odd_first(groups)])
     dout_flipped, own_grad = local_call(
         functools.partial(dout_body, total_width),
         [gain_row, flipped, grad_flipped, attended, sums],
@@ -374,7 +393,7 @@
         aliases={3: 0},
     )
     grad_blocks = exchange(in_pieces(own_grad, "seq"), "seq")
-    early = width // 2 // COPY_COLS * COPY_COLS
+    early = width * 3 // 4 // COPY_COLS * COPY_COLS
     early_vm, late_vm = vm((rows, early), bf16), vm((rows, width - early), bf16)
     query_grad, dout, early_part = local_call(
         query_body,

time: 65.4 us -> 65.3 us (level)
    all_to_all x0 -> x1, blocking collectives: none -> 6.17 us  [shards(): lax.all_to_all(sums, 'head', 0, 0, axis_index_groups=[odd_first(groups)])]
    psum x1 -> x0, blocking collectives: 5.67 us -> none  [shards(): sums = lax.psum(sums, 'head')]
where the time goes in v14:
time: 65.3 us; the launch traced here: 64.6 us
  Pallas kernels  27.9 us (43%)
  starting transfers between devices  26.2 us (40%)
  blocking collectives  6.17 us (9%)
  waiting for transfers between devices  3.46 us (5%)
  between operations  0.88 us (1%)
    pallas_call x10, Pallas kernels, local_call(): pl.pallas_call(body, in_specs=specs, out_specs=out_specs, out_shape=outs,...  27.9 us
    all_to_all x4, starting transfers between devices, exchange(): return lax.all_to_all(pieces, axis, 0, 0, axis_index_groups=groups)  26.2 us
    all_to_all x1, blocking collectives, shards(): lax.all_to_all(sums, 'head', 0, 0, axis_index_groups=[odd_first(groups)])  6.17 us
    all_to_all x4, waiting for transfers between devices, exchange(): return lax.all_to_all(pieces, axis, 0, 0, axis_index_groups=groups)  3.46 us
  transfers between devices with their start and end apart: 4, of which 1 were waited for; matrix products, arithmetic and copies ran while one was open for 0% of the time, Pallas kernels for 28%

profile of v14, /device:TPU:0, one launch (start us, length us, event | category | flops | bytes accessed | tf_op | source)
XLA Modules:
  0.0 64.6 jit_solution(11863399099557597682)
XLA Ops:
  0.6 3.0 %shard_map.76 = bf16[1024,128]{1,0:T(8,128)(2,1)} custom-call(bf16[512,1024]{1,0:T(8,128)(2,1)} %key_hbm.9, bf16[512,1024]{1,0:T(8,128)(2,1)} %value_hbm.7), custom_call_target="tpu_custom_call" | custom-call | flops 134217728 | bytes 2097152 | tf_op jit(solution)/shard_map/pallas_call | solution.py:299
  3.6 8.4 %all-to-all-start = ((bf16[8,128,128]{2,1,0:T(8,128)(2,1)}), bf16[8,128,128]{2,1,0:T(8,128)(2,1)S(1)}, u32[]{:S(2)}, u32[]{:S(2)}) async-start(bf16[8,128,128]{2,1,0:T(8,128)(2,1)} %bitcast.10), calls=%async_computation | async-start | bytes 524288 | tf_op jit(solution)/shard_map/all_to_all | solution.py:339
  12.0 2.1 %shard_map.77 = (bf16[1024,512]{1,0:T(8,128)(2,1)S(1)}, bf16[1024,512]{1,0:T(8,128)(2,1)S(1)}) custom-call(bf16[512,1024]{1,0:T(8,128)(2,1)} %query_hbm.5, bf16[512,1024]{1,0:T(8,128)(2,1)} %grad_hbm.1), custom_call_target="tpu_custom_call" | custom-call | flops 402653184 | bytes 2097152 | tf_op jit(solution)/shard_map/pallas_call | solution.py:299
  14.1 3.4 %all-to-all-done.block_ref = bf16[8,128,128]{2,1,0:T(8,128)(2,1)S(1)} async-done(((bf16[8,128,128]{2,1,0:T(8,128)(2,1)}), bf16[8,128,128]{2,1,0:T(8,128)(2,1)S(1)}, u32[]{:S(2)}, u32[]{:S(2)}) %all-to-all-start) | async-done | bytes 262176 | tf_op jit(solution)/shard_map/all_to_all | solution.py:339
  17.5 0.8 %shard_map.79 = bf16[8,128,128]{2,1,0:T(8,128)(2,1)} custom-call(bf16[8,128,128]{2,1,0:T(8,128)(2,1)S(1)} %all-to-all-done.block_ref), custom_call_target="tpu_custom_call" | custom-call | flops 131072 | bytes 262144 | tf_op jit(solution)/shard_map/pallas_call | solution.py:299
  18.3 6.3 %all-to-all-start.1 = ((bf16[8,128,128]{2,1,0:T(8,128)(2,1)}), bf16[8,128,128]{2,1,0:T(8,128)(2,1)S(1)}, u32[]{:S(2)}, u32[]{:S(2)}) async-start(bf16[8,128,128]{2,1,0:T(8,128)(2,1)} %shard_map.79), calls=%async_computation.1 | async-start | bytes 524288 | tf_op jit(solution)/shard_map/all_to_all | solution.py:339
  24.6 0.0 copy-start
  24.6 4.6 %shard_map.78.local_ref = bf16[1024,512]{1,0:T(8,128)(2,1)S(1)} custom-call(bf16[512,1024]{1,0:T(8,128)(2,1)} %key_hbm.9, bf16[512,1024]{1,0:T(8,128)(2,1)} %value_hbm.7, bf16[1024,512]{1,0:T(8,128)(2,1)S(1)} %get-tuple-element.26.flipped_ref), custom_call_target="tpu_custom_call" | custom-call | flops 805306368 | bytes 3145728 | tf_op jit(solution)/shard_map/pallas_call | solution.py:299
  29.2 0.0 all-to-all-done.1
  29.3 0.0 copy-done
  29.3 0.8 %shard_map.80 = (bf16[1024,512]{1,0:T(8,128)(2,1)S(1)}, f32[4,2,512]{2,1,0:T(2,128)S(1)}) custom-call(f32[1,1024]{1,0:T(1,128)S(1)} %bitcast.8, bf16[1024,512]{1,0:T(8,128)(2,1)S(1)} %get-tuple-element.26.flipped_ref, bf16[1024,512]{1,0:T(8,128)(2,1)S(1)} %get-tuple-element.27.grad_ref, ...), custom_call_target="tpu_custom_call", output_to_operand_aliasing={{0}: (3, {})} | custom-call | flops 134217728 | bytes 3411968 | tf_op jit(solution)/shard_map/pallas_call | solution.py:299
  30.1 6.2 %all_to_all.25.sums_ref = f32[4,2,512]{2,1,0:T(2,128)S(1)} all-to-all(f32[4,2,512]{2,1,0:T(2,128)S(1)} %get-tuple-element.30), channel_id=1, replica_groups={{1,3,0,2},{5,7,4,6},{9,11,8,10},{13,15,12,14},{17,19,16,18},{21,23,20,2..., dimensions={0} | all-to-all | bytes 32768 | tf_op jit(solution)/shard_map/all_to_all | solution.py:386
  36.2 1.5 %shard_map.81 = (bf16[1024,512]{1,0:T(8,128)(2,1)S(1)}, bf16[1024,128]{1,0:T(8,128)(2,1)}) custom-call(f32[1,1024]{1,0:T(1,128)S(1)} %bitcast.9, bf16[1024,512]{1,0:T(8,128)(2,1)S(1)} %get-tuple-element.26.flipped_ref, bf16[1024,512]{1,0:T(8,128)(2,1)S(1)} %get-tuple-element.27.grad_ref, ...), custom_call_target="tpu_custom_call", output_to_operand_aliasing={{0}: (3, {})} | custom-call | flops 134217728 | bytes 3166208 | tf_op jit(solution)/shard_map/pallas_call | solution.py:299
  37.7 6.1 %all-to-all-start.3 = ((bf16[8,128,128]{2,1,0:T(8,128)(2,1)}), bf16[8,128,128]{2,1,0:T(8,128)(2,1)S(1)}, u32[]{:S(2)}, u32[]{:S(2)}) async-start(bf16[8,128,128]{2,1,0:T(8,128)(2,1)} %bitcast.11), calls=%async_computation.3 | async-start | bytes 524288 | tf_op jit(solution)/shard_map/all_to_all | solution.py:339
  43.8 6.4 %shard_map.82 = (bf16[512,1024]{1,0:T(8,128)(2,1)}, bf16[512,1024]{1,0:T(8,128)(2,1)S(1)}, bf16[512,768]{1,0:T(8,128)(2,1)S(1)}) custom-call(bf16[512,1024]{1,0:T(8,128)(2,1)} %query_hbm.5, bf16[512,1024]{1,0:T(8,128)(2,1)} %key_hbm.9, bf16[512,1024]{1,0:T(8,128)(2,1)} %value_hbm.7, bf16[1024,512]{1,0:T(8,128)(2,1)S(1)} %get-tuple-element.32.flipped_ref, ...), custom_call_target="tpu_custom_call" | custom-call | flops 939524096 | bytes 4456448 | tf_op jit(solution)/shard_map/pallas_call | solution.py:299
  50.3 0.0 all-to-all-done.3.block_ref
  50.3 0.8 %shard_map.84 = bf16[8,128,128]{2,1,0:T(8,128)(2,1)} custom-call(bf16[8,128,128]{2,1,0:T(8,128)(2,1)S(1)} %all-to-all-done.3.block_ref), custom_call_target="tpu_custom_call" | custom-call | flops 131072 | bytes 262144 | tf_op jit(solution)/shard_map/pallas_call | solution.py:299
  51.1 5.4 %all-to-all-start.4 = ((bf16[8,128,128]{2,1,0:T(8,128)(2,1)}), bf16[8,128,128]{2,1,0:T(8,128)(2,1)S(1)}, u32[]{:S(2)}, u32[]{:S(2)}) async-start(bf16[8,128,128]{2,1,0:T(8,128)(2,1)} %shard_map.84), calls=%async_computation.4 | async-start | bytes 524288 | tf_op jit(solution)/shard_map/all_to_all | solution.py:339
  56.4 5.0 %shard_map.83 = (bf16[512,1024]{1,0:T(8,128)(2,1)S(1)}, bf16[512,256]{1,0:T(8,128)(2,1)S(1)}, bf16[512,1024]{1,0:T(8,128)(2,1)S(1)}) custom-call(bf16[512,1024]{1,0:T(8,128)(2,1)} %query_hbm.5, bf16[512,1024]{1,0:T(8,128)(2,1)} %key_hbm.9, bf16[512,1024]{1,0:T(8,128)(2,1)} %value_hbm.7, ...), custom_call_target="tpu_custom_call", output_to_operand_aliasing={{0}: (3, {})} | custom-call | flops 1207959552 | bytes 4194304 | tf_op jit(solution)/shard_map/pallas_call | solution.py:299
  61.4 0.0 all-to-all-done.4
  61.5 2.9 %shard_map.85 = (bf16[512,1024]{1,0:T(8,128)(2,1)}, bf16[512,1024]{1,0:T(8,128)(2,1)}) custom-call(bf16[512,1024]{1,0:T(8,128)(2,1)} %key_hbm.9, bf16[512,1024]{1,0:T(8,128)(2,1)S(1)} %get-tuple-element.38.value_ref, bf16[512,1024]{1,0:T(8,128)(2,1)S(1)} %get-tuple-element.39.key_part, bf16[512,768]{1,0:T(8,128)(2,1)S(1)} %get-tuple-element.40.early_part, ...), custom_call_target="tpu_custom_call" | custom-call | flops 268435456 | bytes 4456448 | tf_op jit(solution)/shard_map/pallas_call | solution.py:299
Async XLA Ops:
  3.6 13.9 %all-to-all-start = ((bf16[8,128,128]{2,1,0:T(8,128)(2,1)}), bf16[8,128,128]{2,1,0:T(8,128)(2,1)S(1)}, u32[]{:S(2)}, u32[]{:S(2)}) async-start(bf16[8,128,128]{2,1,0:T(8,128)(2,1)} %bitcast.10), calls=%async_computation | async-start | bytes 524288 | tf_op jit(solution)/shard_map/all_to_all | solution.py:339
  18.3 10.9 %all-to-all-start.1 = ((bf16[8,128,128]{2,1,0:T(8,128)(2,1)}), bf16[8,128,128]{2,1,0:T(8,128)(2,1)S(1)}, u32[]{:S(2)}, u32[]{:S(2)}) async-start(bf16[8,128,128]{2,1,0:T(8,128)(2,1)} %shard_map.79), calls=%async_computation.1 | async-start | bytes 524288 | tf_op jit(solution)/shard_map/all_to_all | solution.py:339
  24.6 4.6 %copy-start = (f32[1024]{0:T(1024)S(1)}, f32[1024]{0:T(1024)}, u32[]{:S(2)}) copy-start(f32[1024]{0:T(1024)} %param.9) | copy-start | bytes 12292
  37.7 12.6 %all-to-all-start.3 = ((bf16[8,128,128]{2,1,0:T(8,128)(2,1)}), bf16[8,128,128]{2,1,0:T(8,128)(2,1)S(1)}, u32[]{:S(2)}, u32[]{:S(2)}) async-start(bf16[8,128,128]{2,1,0:T(8,128)(2,1)} %bitcast.11), calls=%async_computation.3 | async-start | bytes 524288 | tf_op jit(solution)/shard_map/all_to_all | solution.py:339
  51.1 10.4 %all-to-all-start.4 = ((bf16[8,128,128]{2,1,0:T(8,128)(2,1)}), bf16[8,128,128]{2,1,0:T(8,128)(2,1)S(1)}, u32[]{:S(2)}, u32[]{:S(2)}) async-start(bf16[8,128,128]{2,1,0:T(8,128)(2,1)} %shard_map.84), calls=%async_computation.4 | async-start | bytes 524288 | tf_op jit(solution)/shard_map/all_to_all | solution.py:339

commit v15 on v14

--- a/solution.py
+++ b/solution.py
@@ -330,8 +330,8 @@
     return [count - 1 - place for place in order]
 
 
-def odd_first(count):
-    return list(range(1, count, 2)) + list(range(0, count, 2))
+def last_first(count):
+    return list(range(count - 1, -1, -1))
 
 
 def exchange(pieces, axis):
@@ -383,7 +383,7 @@
         small,
         aliases={3: 0},
     )
-    sums = lax.all_to_all(sums, "head", 0, 0, axis_index_groups=[odd_first(groups)])
+    sums = lax.all_to_all(sums, "head", 0, 0, axis_index_groups=[last_first(groups)])
     dout_flipped, own_grad = local_call(
         functools.partial(dout_body, total_width),
         [gain_row, flipped, grad_flipped, attended, sums],

time: 65.3 us -> 64.8 us (level)
  no operation moved by 1% of the time
where the time goes in v15:
time: 64.8 us; the launch traced here: 64.1 us
  Pallas kernels  27.9 us (43%)
  starting transfers between devices  26.2 us (40%)
  blocking collectives  5.67 us (9%)
  waiting for transfers between devices  3.46 us (5%)
  between operations  0.88 us (1%)
    pallas_call x10, Pallas kernels, local_call(): pl.pallas_call(body, in_specs=specs, out_specs=out_specs, out_shape=outs,...  27.9 us
    all_to_all x4, starting transfers between devices, exchange(): return lax.all_to_all(pieces, axis, 0, 0, axis_index_groups=groups)  26.2 us
    all_to_all x1, blocking collectives, shards(): lax.all_to_all(sums, 'head', 0, 0, axis_index_groups=[last_first(groups)])  5.67 us
    all_to_all x4, waiting for transfers between devices, exchange(): return lax.all_to_all(pieces, axis, 0, 0, axis_index_groups=groups)  3.46 us
  transfers between devices with their start and end apart: 4, of which 1 were waited for; matrix products, arithmetic and copies ran while one was open for 0% of the time, Pallas kernels for 28%

profile of v15, /device:TPU:0, one launch (start us, length us, event | category | flops | bytes accessed | tf_op | source)
XLA Modules:
  0.0 64.1 jit_solution(8297013355640888483)
XLA Ops:
  0.6 3.0 %shard_map.76 = bf16[1024,128]{1,0:T(8,128)(2,1)} custom-call(bf16[512,1024]{1,0:T(8,128)(2,1)} %key_hbm.9, bf16[512,1024]{1,0:T(8,128)(2,1)} %value_hbm.7), custom_call_target="tpu_custom_call" | custom-call | flops 134217728 | bytes 2097152 | tf_op jit(solution)/shard_map/pallas_call | solution.py:299
  3.6 8.4 %all-to-all-start = ((bf16[8,128,128]{2,1,0:T(8,128)(2,1)}), bf16[8,128,128]{2,1,0:T(8,128)(2,1)S(1)}, u32[]{:S(2)}, u32[]{:S(2)}) async-start(bf16[8,128,128]{2,1,0:T(8,128)(2,1)} %bitcast.10), calls=%async_computation | async-start | bytes 524288 | tf_op jit(solution)/shard_map/all_to_all | solution.py:339
  12.0 2.1 %shard_map.77 = (bf16[1024,512]{1,0:T(8,128)(2,1)S(1)}, bf16[1024,512]{1,0:T(8,128)(2,1)S(1)}) custom-call(bf16[512,1024]{1,0:T(8,128)(2,1)} %query_hbm.5, bf16[512,1024]{1,0:T(8,128)(2,1)} %grad_hbm.1), custom_call_target="tpu_custom_call" | custom-call | flops 402653184 | bytes 2097152 | tf_op jit(solution)/shard_map/pallas_call | solution.py:299
  14.1 3.4 %all-to-all-done.block_ref = bf16[8,128,128]{2,1,0:T(8,128)(2,1)S(1)} async-done(((bf16[8,128,128]{2,1,0:T(8,128)(2,1)}), bf16[8,128,128]{2,1,0:T(8,128)(2,1)S(1)}, u32[]{:S(2)}, u32[]{:S(2)}) %all-to-all-start) | async-done | bytes 262176 | tf_op jit(solution)/shard_map/all_to_all | solution.py:339
  17.5 0.8 %shard_map.79 = bf16[8,128,128]{2,1,0:T(8,128)(2,1)} custom-call(bf16[8,128,128]{2,1,0:T(8,128)(2,1)S(1)} %all-to-all-done.block_ref), custom_call_target="tpu_custom_call" | custom-call | flops 131072 | bytes 262144 | tf_op jit(solution)/shard_map/pallas_call | solution.py:299
  18.3 6.3 %all-to-all-start.1 = ((bf16[8,128,128]{2,1,0:T(8,128)(2,1)}), bf16[8,128,128]{2,1,0:T(8,128)(2,1)S(1)}, u32[]{:S(2)}, u32[]{:S(2)}) async-start(bf16[8,128,128]{2,1,0:T(8,128)(2,1)} %shard_map.79), calls=%async_computation.1 | async-start | bytes 524288 | tf_op jit(solution)/shard_map/all_to_all | solution.py:339
  24.6 0.0 copy-start
  24.6 4.6 %shard_map.78.local_ref = bf16[1024,512]{1,0:T(8,128)(2,1)S(1)} custom-call(bf16[512,1024]{1,0:T(8,128)(2,1)} %key_hbm.9, bf16[512,1024]{1,0:T(8,128)(2,1)} %value_hbm.7, bf16[1024,512]{1,0:T(8,128)(2,1)S(1)} %get-tuple-element.26.flipped_ref), custom_call_target="tpu_custom_call" | custom-call | flops 805306368 | bytes 3145728 | tf_op jit(solution)/shard_map/pallas_call | solution.py:299
  29.2 0.0 all-to-all-done.1
  29.3 0.0 copy-done
  29.3 0.8 %shard_map.80 = (bf16[1024,512]{1,0:T(8,128)(2,1)S(1)}, f32[4,2,512]{2,1,0:T(2,128)S(1)}) custom-call(f32[1,1024]{1,0:T(1,128)S(1)} %bitcast.8, bf16[1024,512]{1,0:T(8,128)(2,1)S(1)} %get-tuple-element.26.flipped_ref, bf16[1024,512]{1,0:T(8,128)(2,1)S(1)} %get-tuple-element.27.grad_ref, ...), custom_call_target="tpu_custom_call", output_to_operand_aliasing={{0}: (3, {})} | custom-call | flops 134217728 | bytes 3411968 | tf_op jit(solution)/shard_map/pallas_call | solution.py:299
  30.1 5.7 %all_to_all.25.sums_ref = f32[4,2,512]{2,1,0:T(2,128)S(1)} all-to-all(f32[4,2,512]{2,1,0:T(2,128)S(1)} %get-tuple-element.30), channel_id=1, replica_groups={{3,2,1,0},{7,6,5,4},{11,10,9,8},{15,14,13,12},{19,18,17,16},{23,22,21,2..., dimensions={0} | all-to-all | bytes 32768 | tf_op jit(solution)/shard_map/all_to_all | solution.py:386
  35.7 1.5 %shard_map.81 = (bf16[1024,512]{1,0:T(8,128)(2,1)S(1)}, bf16[1024,128]{1,0:T(8,128)(2,1)}) custom-call(f32[1,1024]{1,0:T(1,128)S(1)} %bitcast.9, bf16[1024,512]{1,0:T(8,128)(2,1)S(1)} %get-tuple-element.26.flipped_ref, bf16[1024,512]{1,0:T(8,128)(2,1)S(1)} %get-tuple-element.27.grad_ref, ...), custom_call_target="tpu_custom_call", output_to_operand_aliasing={{0}: (3, {})} | custom-call | flops 134217728 | bytes 3166208 | tf_op jit(solution)/shard_map/pallas_call | solution.py:299
  37.2 6.1 %all-to-all-start.3 = ((bf16[8,128,128]{2,1,0:T(8,128)(2,1)}), bf16[8,128,128]{2,1,0:T(8,128)(2,1)S(1)}, u32[]{:S(2)}, u32[]{:S(2)}) async-start(bf16[8,128,128]{2,1,0:T(8,128)(2,1)} %bitcast.11), calls=%async_computation.3 | async-start | bytes 524288 | tf_op jit(solution)/shard_map/all_to_all | solution.py:339
  43.3 6.4 %shard_map.82 = (bf16[512,1024]{1,0:T(8,128)(2,1)}, bf16[512,1024]{1,0:T(8,128)(2,1)S(1)}, bf16[512,768]{1,0:T(8,128)(2,1)S(1)}) custom-call(bf16[512,1024]{1,0:T(8,128)(2,1)} %query_hbm.5, bf16[512,1024]{1,0:T(8,128)(2,1)} %key_hbm.9, bf16[512,1024]{1,0:T(8,128)(2,1)} %value_hbm.7, bf16[1024,512]{1,0:T(8,128)(2,1)S(1)} %get-tuple-element.32.flipped_ref, ...), custom_call_target="tpu_custom_call" | custom-call | flops 939524096 | bytes 4456448 | tf_op jit(solution)/shard_map/pallas_call | solution.py:299
  49.8 0.0 all-to-all-done.3.block_ref
  49.8 0.8 %shard_map.84 = bf16[8,128,128]{2,1,0:T(8,128)(2,1)} custom-call(bf16[8,128,128]{2,1,0:T(8,128)(2,1)S(1)} %all-to-all-done.3.block_ref), custom_call_target="tpu_custom_call" | custom-call | flops 131072 | bytes 262144 | tf_op jit(solution)/shard_map/pallas_call | solution.py:299
  50.6 5.4 %all-to-all-start.4 = ((bf16[8,128,128]{2,1,0:T(8,128)(2,1)}), bf16[8,128,128]{2,1,0:T(8,128)(2,1)S(1)}, u32[]{:S(2)}, u32[]{:S(2)}) async-start(bf16[8,128,128]{2,1,0:T(8,128)(2,1)} %shard_map.84), calls=%async_computation.4 | async-start | bytes 524288 | tf_op jit(solution)/shard_map/all_to_all | solution.py:339
  56.0 5.0 %shard_map.83 = (bf16[512,1024]{1,0:T(8,128)(2,1)S(1)}, bf16[512,256]{1,0:T(8,128)(2,1)S(1)}, bf16[512,1024]{1,0:T(8,128)(2,1)S(1)}) custom-call(bf16[512,1024]{1,0:T(8,128)(2,1)} %query_hbm.5, bf16[512,1024]{1,0:T(8,128)(2,1)} %key_hbm.9, bf16[512,1024]{1,0:T(8,128)(2,1)} %value_hbm.7, ...), custom_call_target="tpu_custom_call", output_to_operand_aliasing={{0}: (3, {})} | custom-call | flops 1207959552 | bytes 4194304 | tf_op jit(solution)/shard_map/pallas_call | solution.py:299
  60.9 0.0 all-to-all-done.4
  61.0 2.9 %shard_map.85 = (bf16[512,1024]{1,0:T(8,128)(2,1)}, bf16[512,1024]{1,0:T(8,128)(2,1)}) custom-call(bf16[512,1024]{1,0:T(8,128)(2,1)} %key_hbm.9, bf16[512,1024]{1,0:T(8,128)(2,1)S(1)} %get-tuple-element.38.value_ref, bf16[512,1024]{1,0:T(8,128)(2,1)S(1)} %get-tuple-element.39.key_part, bf16[512,768]{1,0:T(8,128)(2,1)S(1)} %get-tuple-element.40.early_part, ...), custom_call_target="tpu_custom_call" | custom-call | flops 268435456 | bytes 4456448 | tf_op jit(solution)/shard_map/pallas_call | solution.py:299
Async XLA Ops:
  3.6 13.9 %all-to-all-start = ((bf16[8,128,128]{2,1,0:T(8,128)(2,1)}), bf16[8,128,128]{2,1,0:T(8,128)(2,1)S(1)}, u32[]{:S(2)}, u32[]{:S(2)}) async-start(bf16[8,128,128]{2,1,0:T(8,128)(2,1)} %bitcast.10), calls=%async_computation | async-start | bytes 524288 | tf_op jit(solution)/shard_map/all_to_all | solution.py:339
  18.3 10.9 %all-to-all-start.1 = ((bf16[8,128,128]{2,1,0:T(8,128)(2,1)}), bf16[8,128,128]{2,1,0:T(8,128)(2,1)S(1)}, u32[]{:S(2)}, u32[]{:S(2)}) async-start(bf16[8,128,128]{2,1,0:T(8,128)(2,1)} %shard_map.79), calls=%async_computation.1 | async-start | bytes 524288 | tf_op jit(solution)/shard_map/all_to_all | solution.py:339
  24.6 4.6 %copy-start = (f32[1024]{0:T(1024)S(1)}, f32[1024]{0:T(1024)}, u32[]{:S(2)}) copy-start(f32[1024]{0:T(1024)} %param.9) | copy-start | bytes 12292
  37.2 12.6 %all-to-all-start.3 = ((bf16[8,128,128]{2,1,0:T(8,128)(2,1)}), bf16[8,128,128]{2,1,0:T(8,128)(2,1)S(1)}, u32[]{:S(2)}, u32[]{:S(2)}) async-start(bf16[8,128,128]{2,1,0:T(8,128)(2,1)} %bitcast.11), calls=%async_computation.3 | async-start | bytes 524288 | tf_op jit(solution)/shard_map/all_to_all | solution.py:339
  50.6 10.4 %all-to-all-start.4 = ((bf16[8,128,128]{2,1,0:T(8,128)(2,1)}), bf16[8,128,128]{2,1,0:T(8,128)(2,1)S(1)}, u32[]{:S(2)}, u32[]{:S(2)}) async-start(bf16[8,128,128]{2,1,0:T(8,128)(2,1)} %shard_map.84), calls=%async_computation.4 | async-start | bytes 524288 | tf_op jit(solution)/shard_map/all_to_all | solution.py:339

commit v16 on v15

--- a/solution.py
+++ b/solution.py
@@ -87,40 +87,81 @@
     wait_all(stores)
 
 
-def flip_body(query_hbm, grad_hbm, flipped_ref, grad_flipped_ref, query_ref, grad_ref, query_sems, grad_sems):
-    loads = (
-        (query_ref, flipped_ref, column_copies(query_hbm, query_ref, query_sems)),
-        (grad_ref, grad_flipped_ref, column_copies(grad_hbm, grad_ref, grad_sems)),
-    )
-    start_all(loads[0][2])
-    start_all(loads[1][2])
-    for source, target, copies in loads:
-        for copy, cols in zip(copies, pieces_of(source, COPY_COLS)):
-            copy.wait()
-            target[cols, :] = source[:, cols].T
-
-
-def local_body(key_hbm, value_hbm, flipped_ref, local_ref, key_ref, value_ref, key_sems, value_sems):
-    rows = key_ref.shape[0]
-    key_copies = column_copies(key_hbm, key_ref, key_sems)
-    value_copies = column_copies(value_hbm, value_ref, value_sems)
-    start_all(key_copies, value_copies)
+def weight_rows(rows):
+    blocks = rows // BLOCK
+    return blocks * (blocks + 1) // 2 * BLOCK
+
+
+def local_part(key_ref, value_ref, own, flipped_ref, head, local_ref, weight_ref, row):
+    for start in range(0, key_ref.shape[0], BLOCK):
+        end = start + BLOCK
+        parts = []
+        for first in range(0, end, BLOCK):
+            scores = mm(key_ref[first : first + BLOCK, own], flipped_ref[head, start:end])
+            part = masked(scores, 0, False) if first == start else scores.astype(jnp.bfloat16)
+            weight_ref[row : row + BLOCK, :] = part
+            parts.append(part)
+            row += BLOCK
+        weights = jnp.concatenate(parts, axis=0) if len(parts) > 1 else parts[0]
+        local = mm_tn(value_ref[:end, own], weights)
+        local_ref[head, start:end] = local.astype(jnp.bfloat16)
+
+
+def local_heads(first, key_ref, value_ref, loads, flipped_ref, local_ref, weight_ref, weight_hbm, sems):
+    size = weight_rows(key_ref.shape[0])
+    stores = []
     for index, step in enumerate(pieces_of(key_ref, COPY_COLS)):
-        key_copies[index].wait()
-        value_copies[index].wait()
+        for load in loads:
+            load[index].wait()
         for left in range(step.start, step.stop, HEAD_DIM):
-            cols = slice(left, left + HEAD_DIM)
-            for start in range(0, rows, BLOCK):
-                end = start + BLOCK
-                parts = []
-                for row in range(0, end, BLOCK):
-                    key = key_ref[row : row + BLOCK, cols]
-                    scores = mm(key, flipped_ref[cols, start:end])
-                    below = row == start
-                    parts.append(masked(scores, 0, False) if below else scores.astype(jnp.bfloat16))
-                weights = jnp.concatenate(parts, axis=0) if len(parts) > 1 else parts[0]
-                local = mm_tn(value_ref[:end, cols], weights)
-                local_ref[cols, start:end] = local.astype(jnp.bfloat16)
+            own = slice(left, left + HEAD_DIM)
+            head = slice(first + left, first + left + HEAD_DIM)
+            number = left // HEAD_DIM
+            part = slice(number * size, (number + 1) * size)
+            local_part(key_ref, value_ref, own, flipped_ref, head, local_ref, weight_ref, part.start)
+            store = pltpu.make_async_copy(weight_ref.at[part, :], weight_hbm.at[part, :], sems.at[number])
+            store.start()
+            stores.append(store)
+    return stores
+
+
+def flip_body(
+    query_hbm, key_hbm, value_hbm, grad_hbm, flipped_ref, grad_flipped_ref, local_ref, weight_hbm,
+    query_ref, key_ref, value_ref, grad_ref, weight_ref,
+    query_sems, key_sems, value_sems, grad_sems, weight_sems,
+):
+    part = slice(0, key_ref.shape[1])
+    query_loads = column_copies(query_hbm, query_ref, query_sems)
+    key_loads = column_copies(key_hbm.at[:, part], key_ref, key_sems)
+    value_loads = column_copies(value_hbm.at[:, part], value_ref, value_sems)
+    grad_loads = column_copies(grad_hbm, grad_ref, grad_sems)
+    start_all(query_loads)
+    start_all(key_loads, value_loads)
+    start_all(grad_loads)
+    for load, cols in zip(query_loads, pieces_of(query_ref, COPY_COLS)):
+        load.wait()
+        flipped_ref[cols, :] = query_ref[:, cols].T
+    stores = local_heads(
+        0, key_ref, value_ref, (key_loads, value_loads), flipped_ref, local_ref, weight_ref, weight_hbm, weight_sems
+    )
+    for load, cols in zip(grad_loads, pieces_of(grad_ref, COPY_COLS)):
+        load.wait()
+        grad_flipped_ref[cols, :] = grad_ref[:, cols].T
+    wait_all(stores)
+
+
+def local_body(
+    key_hbm, value_hbm, flipped_ref, given_ref, local_ref, weight_hbm,
+    key_ref, value_ref, weight_ref, key_sems, value_sems, weight_sems,
+):
+    first = local_ref.shape[0] - key_ref.shape[1]
+    key_loads = column_copies(key_hbm.at[:, first:], key_ref, key_sems)
+    value_loads = column_copies(value_hbm.at[:, first:], value_ref, value_sems)
+    start_all(key_loads, value_loads)
+    stores = local_heads(
+        first, key_ref, value_ref, (key_loads, value_loads), flipped_ref, local_ref, weight_ref, weight_hbm, weight_sems
+    )
+    wait_all(stores)
 
 
 def scan_body(reverse, block_ref, state_hbm, state_ref, sems):
@@ -187,25 +228,34 @@
     wait_all(stores)
 
 
-def value_local(query_ref, key_ref, dout, cols, target):
-    rows = key_ref.shape[0]
-    for start in range(0, rows, BLOCK):
-        end = start + BLOCK
-        weights = masked(mm_nt(key_ref[start:end, cols], query_ref[start:, cols]), 0, False)
-        target[start:end, :] = mm(weights, dout[start:, :]).astype(jnp.bfloat16)
+def value_local(weight_ref, row, dout, target):
+    blocks = dout.shape[0] // BLOCK
+    for own in range(blocks):
+        parts = []
+        for other in range(own, blocks):
+            start = row + (other * (other + 1) // 2 + own) * BLOCK
+            parts.append(weight_ref[start : start + BLOCK, :])
+        weights = jnp.concatenate(parts, axis=1) if len(parts) > 1 else parts[0]
+        at = own * BLOCK
+        target[at : at + BLOCK, :] = mm(weights, dout[at:, :]).astype(jnp.bfloat16)
 
 
 def query_body(
-    query_hbm, key_hbm, value_hbm, flipped_ref, state_ref, out_hbm, dout_ref, value_out,
-    query_ref, key_ref, value_ref, out_ref, query_sems, key_sems, value_sems, out_sems,
+    key_hbm, value_hbm, first_hbm, second_hbm, flipped_ref, state_ref, out_hbm, dout_ref, value_out,
+    key_ref, value_ref, out_ref, weight_ref, key_sems, value_sems, out_sems, weight_sems,
 ):
     rows = dout_ref.shape[0]
-    early = value_out.shape[1]
-    query_copies = column_copies(query_hbm.at[:, :early], query_ref, query_sems)
+    size = weight_rows(rows)
     key_copies = column_copies(key_hbm, key_ref, key_sems)
     value_copies = column_copies(value_hbm, value_ref, value_sems)
+    there = first_hbm.shape[0]
+    rest = weight_ref.shape[0] - there
+    weight_copies = [
+        pltpu.make_async_copy(first_hbm, weight_ref.at[:there, :], weight_sems.at[0]),
+        pltpu.make_async_copy(second_hbm.at[:rest, :], weight_ref.at[there:, :], weight_sems.at[1]),
+    ]
     start_all(key_copies, value_copies)
-    start_all(query_copies)
+    start_all(weight_copies)
     for head in heads_of(flipped_ref):
         dout_ref[:, head] = flipped_ref[head, :].T
     stores = column_copies(out_ref, out_hbm, out_sems)
@@ -221,30 +271,30 @@
                 grad = mm(dscore, key_ref[:end, cols]) + mm_nt(dout, state_ref[cols, :])
                 out_ref[start:end, cols] = grad.astype(jnp.bfloat16)
         stores[index].start()
-    wait_all(query_copies)
-    for cols in pieces_of(value_out, HEAD_DIM):
-        value_local(query_ref, key_ref, dout_ref[:, cols], cols, value_out.at[:, cols])
+    wait_all(weight_copies)
+    for number, cols in enumerate(pieces_of(value_out, HEAD_DIM)):
+        value_local(weight_ref, number * size, dout_ref[:, cols], value_out.at[:, cols])
     wait_all(stores)
 
 
 def inner_body(
-    query_hbm, key_hbm, value_hbm, dout_ref, key_out, value_out, value_ref,
-    query_ref, key_ref, query_sems, key_sems, value_sems,
+    query_hbm, value_hbm, weight_hbm, dout_ref, key_out, value_out, value_ref,
+    query_ref, weight_ref, query_sems, value_sems, weight_sem,
 ):
     rows, width = key_out.shape
+    size = weight_rows(rows)
     early = width - value_out.shape[1]
-    loads = (
-        column_copies(query_hbm, query_ref, query_sems),
-        column_copies(value_hbm, value_ref, value_sems),
-        column_copies(key_hbm.at[:, early:], key_ref, key_sems),
-    )
-    start_all(*loads[:2])
-    start_all(loads[2])
+    query_copies = column_copies(query_hbm, query_ref, query_sems)
+    value_copies = column_copies(value_hbm, value_ref, value_sems)
+    skipped = weight_hbm.shape[0] - weight_ref.shape[0]
+    weight_copy = pltpu.make_async_copy(weight_hbm.at[skipped:, :], weight_ref, weight_sem.at[0])
+    start_all(query_copies, value_copies)
+    weight_copy.start()
     for index, step in enumerate(pieces_of(key_out, COPY_COLS)):
-        loads[0][index].wait()
-        loads[1][index].wait()
+        query_copies[index].wait()
+        value_copies[index].wait()
         if step.start == early:
-            wait_all(loads[2])
+            weight_copy.wait()
         for left in range(step.start, step.stop, HEAD_DIM):
             cols = slice(left, left + HEAD_DIM)
             dout = key_out[:, cols]
@@ -255,7 +305,7 @@
                 key_out[start:end, cols] = grad.astype(jnp.bfloat16)
             if left >= early:
                 late = slice(left - early, left - early + HEAD_DIM)
-                value_local(query_ref.at[:, early:], key_ref, dout, late, value_out.at[:, late])
+                value_local(weight_ref, late.start // HEAD_DIM * size, dout, value_out.at[:, late])
 
 
 def final_body(
@@ -367,13 +417,38 @@
         [rows_vm] * 2 + [state_vm] + [chunks] * 3,
     )
     kv_blocks = exchange(in_pieces(own_kv, "seq"), "seq")
-    flipped, grad_flipped = local_call(
-        flip_body, [], [flat_vm] * 2, large, [queries, out_grad], [rows_vm] * 2 + [chunks] * 2
-    )
-    kv_blocks, flipped, grad_flipped = lax.optimization_barrier((kv_blocks, flipped, grad_flipped))
+    half = width // 2 // COPY_COLS * COPY_COLS
+    early = width * 3 // 4 // COPY_COLS * COPY_COLS
+    dma = pltpu.SemaphoreType.DMA
+
+    def weights_of(cols):
+        return (cols // HEAD_DIM * weight_rows(rows), BLOCK)
+
+    half_vm, half_chunks = vm((rows, half), bf16), dma((half // COPY_COLS,))
+    flipped, grad_flipped, local, first_weights = local_call(
+        flip_body,
+        [],
+        [flat_vm] * 3 + [hbm(weights_of(half), bf16)],
+        2 * large,
+        [queries, keys, values, out_grad],
+        [rows_vm, half_vm, half_vm, rows_vm, vm(weights_of(half), bf16)]
+        + [chunks, half_chunks, half_chunks, chunks, dma((half // HEAD_DIM,))],
+    )
+    kv_blocks, flipped, grad_flipped, local, first_weights = lax.optimization_barrier(
+        (kv_blocks, flipped, grad_flipped, local, first_weights)
+    )
     kv_low = exchange(scan_blocks(kv_blocks, False), "seq").reshape(state)
-    (local,) = local_call(
-        local_body, [flipped], [flat_vm], 2 * large, [keys, values], [rows_vm] * 2 + [chunks] * 2
+    other = width - half
+    other_vm, other_chunks = vm((rows, other), bf16), dma((other // COPY_COLS,))
+    local, second_weights = local_call(
+        local_body,
+        [flipped, local],
+        [flat_vm, hbm(weights_of(other), bf16)],
+        large,
+        [keys, values],
+        [other_vm, other_vm, vm(weights_of(other), bf16)]
+        + [other_chunks, other_chunks, dma((other // HEAD_DIM,))],
+        {3: 0},
     )
     groups = lax.axis_size("head")
     attended, sums = local_call(
@@ -393,15 +468,14 @@
         aliases={3: 0},
     )
     grad_blocks = exchange(in_pieces(own_grad, "seq"), "seq")
-    early = width * 3 // 4 // COPY_COLS * COPY_COLS
     early_vm, late_vm = vm((rows, early), bf16), vm((rows, width - early), bf16)
     query_grad, dout, early_part = local_call(
         query_body,
         [dout_flipped, kv_low],
         [hbm(tokens, bf16), rows_vm, early_vm],
         2 * large + small,
-        [queries, keys, values],
-        [early_vm] + [rows_vm] * 3 + [chunks] * 4,
+        [keys, values, first_weights, second_weights],
+        [rows_vm] * 3 + [vm(weights_of(early), bf16)] + [chunks] * 3 + [dma((2,))],
     )
     grad_blocks, query_grad, dout, early_part = lax.optimization_barrier(
         (grad_blocks, query_grad, dout, early_part)
@@ -412,8 +486,8 @@
         [dout],
         [rows_vm, late_vm, rows_vm],
         3 * large,
-        [queries, keys, values],
-        [rows_vm, late_vm] + [chunks] * 3,
+        [queries, values, second_weights],
+        [rows_vm, vm(weights_of(width - early), bf16)] + [chunks] * 2 + [dma((1,))],
         {3: 0},
     )
     key_grad, value_grad = local_call(

time: 64.8 us -> 64.5 us (level)
  starting transfers between devices: 26.2 us -> 27.1 us
  waiting for transfers between devices: 3.46 us -> 2.6 us
    all_to_all x4, starting transfers between devices: 26.2 us -> 27.1 us  [exchange(): return lax.all_to_all(pieces, axis, 0, 0, axis_index_groups=groups)]
    all_to_all x4, waiting for transfers between devices: 3.46 us -> 2.6 us  [exchange(): return lax.all_to_all(pieces, axis, 0, 0, axis_index_groups=groups)]
  transfers between devices with their start and end apart: 4 -> 4, of which waited for: 1 -> 3; matrix products, arithmetic and copies ran while one was open for 0% -> 0% of each run, Pallas kernels for 28% -> 28%
where the time goes in v16:
time: 64.5 us; the launch traced here: 63.8 us
  Pallas kernels  27.5 us (43%)
  starting transfers between devices  27.1 us (42%)
  blocking collectives  5.67 us (9%)
  waiting for transfers between devices  2.6 us (4%)
  between operations  0.87 us (1%)
    pallas_call x10, Pallas kernels, local_call(): pl.pallas_call(body, in_specs=specs, out_specs=out_specs, out_shape=outs,...  27.5 us
    all_to_all x4, starting transfers between devices, exchange(): return lax.all_to_all(pieces, axis, 0, 0, axis_index_groups=groups)  27.1 us
    all_to_all x1, blocking collectives, shards(): lax.all_to_all(sums, 'head', 0, 0, axis_index_groups=[last_first(groups)])  5.67 us
    all_to_all x4, waiting for transfers between devices, exchange(): return lax.all_to_all(pieces, axis, 0, 0, axis_index_groups=groups)  2.6 us
  transfers between devices with their start and end apart: 4, of which 3 were waited for; matrix products, arithmetic and copies ran while one was open for 0% of the time, Pallas kernels for 28%

profile of v16, /device:TPU:0, one launch (start us, length us, event | category | flops | bytes accessed | tf_op | source)
XLA Modules:
  0.0 63.8 jit_solution(2818726474407933497)
XLA Ops:
  0.6 3.0 %shard_map.76 = bf16[1024,128]{1,0:T(8,128)(2,1)} custom-call(bf16[512,1024]{1,0:T(8,128)(2,1)} %key_hbm.9, bf16[512,1024]{1,0:T(8,128)(2,1)} %value_hbm.9), custom_call_target="tpu_custom_call" | custom-call | flops 134217728 | bytes 2097152 | tf_op jit(solution)/shard_map/pallas_call | solution.py:349
  3.6 8.4 %all-to-all-start = ((bf16[8,128,128]{2,1,0:T(8,128)(2,1)}), bf16[8,128,128]{2,1,0:T(8,128)(2,1)S(1)}, u32[]{:S(2)}, u32[]{:S(2)}) async-start(bf16[8,128,128]{2,1,0:T(8,128)(2,1)} %bitcast.10), calls=%async_computation | async-start | bytes 524288 | tf_op jit(solution)/shard_map/all_to_all | solution.py:389
  12.0 4.2 %shard_map.77 = (bf16[1024,512]{1,0:T(8,128)(2,1)S(1)}, bf16[1024,512]{1,0:T(8,128)(2,1)S(1)}, bf16[1024,512]{1,0:T(8,128)(2,1)S(1)}, bf16[3072,256]{1,0:T(8,128)(2,1)}) custom-call(bf16[512,1024]{1,0:T(8,128)(2,1)} %query_hbm.3, bf16[512,1024]{1,0:T(8,128)(2,1)} %key_hbm.9, bf16[512,1024]{1,0:T(8,128)(2,1)} %value_hbm.9, bf16[512,1024]{1,0:T(8,128)(2,1)} %grad_hbm.1), custom_call_target="tpu_custom_call" | custom-call | flops 805306368 | bytes 4194304 | tf_op jit(solution)/shard_map/pallas_call | solution.py:349
  16.2 1.3 %all-to-all-done.block_ref = bf16[8,128,128]{2,1,0:T(8,128)(2,1)S(1)} async-done(((bf16[8,128,128]{2,1,0:T(8,128)(2,1)}), bf16[8,128,128]{2,1,0:T(8,128)(2,1)S(1)}, u32[]{:S(2)}, u32[]{:S(2)}) %all-to-all-start) | async-done | bytes 262176 | tf_op jit(solution)/shard_map/all_to_all | solution.py:389
  17.5 0.8 %shard_map.79 = bf16[8,128,128]{2,1,0:T(8,128)(2,1)} custom-call(bf16[8,128,128]{2,1,0:T(8,128)(2,1)S(1)} %all-to-all-done.block_ref), custom_call_target="tpu_custom_call" | custom-call | flops 131072 | bytes 262144 | tf_op jit(solution)/shard_map/pallas_call | solution.py:349
  18.3 6.3 %all-to-all-start.1 = ((bf16[8,128,128]{2,1,0:T(8,128)(2,1)}), bf16[8,128,128]{2,1,0:T(8,128)(2,1)S(1)}, u32[]{:S(2)}, u32[]{:S(2)}) async-start(bf16[8,128,128]{2,1,0:T(8,128)(2,1)} %shard_map.79), calls=%async_computation.1 | async-start | bytes 524288 | tf_op jit(solution)/shard_map/all_to_all | solution.py:389
  24.6 0.0 copy-start
  24.6 3.5 %shard_map.78 = (bf16[1024,512]{1,0:T(8,128)(2,1)S(1)}, bf16[3072,256]{1,0:T(8,128)(2,1)}) custom-call(bf16[512,1024]{1,0:T(8,128)(2,1)} %key_hbm.9, bf16[512,1024]{1,0:T(8,128)(2,1)} %value_hbm.9, bf16[1024,512]{1,0:T(8,128)(2,1)S(1)} %get-tuple-element.34.flipped_ref, ...), custom_call_target="tpu_custom_call", output_to_operand_aliasing={{0}: (3, {})} | custom-call | flops 402653184 | bytes 4194304 | tf_op jit(solution)/shard_map/pallas_call | solution.py:349
  28.1 1.1 %all-to-all-done.1 = bf16[8,128,128]{2,1,0:T(8,128)(2,1)S(1)} async-done(((bf16[8,128,128]{2,1,0:T(8,128)(2,1)}), bf16[8,128,128]{2,1,0:T(8,128)(2,1)S(1)}, u32[]{:S(2)}, u32[]{:S(2)}) %all-to-all-start.1) | async-done | bytes 262176 | tf_op jit(solution)/shard_map/all_to_all | solution.py:389
  29.3 0.0 copy-done
  29.3 0.8 %shard_map.80 = (bf16[1024,512]{1,0:T(8,128)(2,1)S(1)}, f32[4,2,512]{2,1,0:T(2,128)S(1)}) custom-call(f32[1,1024]{1,0:T(1,128)S(1)} %bitcast.8, bf16[1024,512]{1,0:T(8,128)(2,1)S(1)} %get-tuple-element.34.flipped_ref, bf16[1024,512]{1,0:T(8,128)(2,1)S(1)} %get-tuple-element.35.grad_ref, ...), custom_call_target="tpu_custom_call", output_to_operand_aliasing={{0}: (3, {})} | custom-call | flops 134217728 | bytes 3411968 | tf_op jit(solution)/shard_map/pallas_call | solution.py:349
  30.1 5.7 %all_to_all.25.sums_ref = f32[4,2,512]{2,1,0:T(2,128)S(1)} all-to-all(f32[4,2,512]{2,1,0:T(2,128)S(1)} %get-tuple-element.40), channel_id=1, replica_groups={{3,2,1,0},{7,6,5,4},{11,10,9,8},{15,14,13,12},{19,18,17,16},{23,22,21,2..., dimensions={0} | all-to-all | bytes 32768 | tf_op jit(solution)/shard_map/all_to_all | solution.py:461
  35.7 1.5 %shard_map.81 = (bf16[1024,512]{1,0:T(8,128)(2,1)S(1)}, bf16[1024,128]{1,0:T(8,128)(2,1)}) custom-call(f32[1,1024]{1,0:T(1,128)S(1)} %bitcast.9, bf16[1024,512]{1,0:T(8,128)(2,1)S(1)} %get-tuple-element.34.flipped_ref, bf16[1024,512]{1,0:T(8,128)(2,1)S(1)} %get-tuple-element.35.grad_ref, ...), custom_call_target="tpu_custom_call", output_to_operand_aliasing={{0}: (3, {})} | custom-call | flops 134217728 | bytes 3166208 | tf_op jit(solution)/shard_map/pallas_call | solution.py:349
  37.2 6.1 %all-to-all-start.3 = ((bf16[8,128,128]{2,1,0:T(8,128)(2,1)}), bf16[8,128,128]{2,1,0:T(8,128)(2,1)S(1)}, u32[]{:S(2)}, u32[]{:S(2)}) async-start(bf16[8,128,128]{2,1,0:T(8,128)(2,1)} %bitcast.11), calls=%async_computation.3 | async-start | bytes 524288 | tf_op jit(solution)/shard_map/all_to_all | solution.py:389
  43.3 5.3 %shard_map.82 = (bf16[512,1024]{1,0:T(8,128)(2,1)}, bf16[512,1024]{1,0:T(8,128)(2,1)S(1)}, bf16[512,768]{1,0:T(8,128)(2,1)S(1)}) custom-call(bf16[512,1024]{1,0:T(8,128)(2,1)} %key_hbm.9, bf16[512,1024]{1,0:T(8,128)(2,1)} %value_hbm.9, bf16[3072,256]{1,0:T(8,128)(2,1)} %get-tuple-element.42.first_hbm, ...), custom_call_target="tpu_custom_call" | custom-call | flops 939524096 | bytes 6553600 | tf_op jit(solution)/shard_map/pallas_call | solution.py:349
  48.7 0.1 all-to-all-done.3.block_ref
  48.8 0.8 %shard_map.84 = bf16[8,128,128]{2,1,0:T(8,128)(2,1)} custom-call(bf16[8,128,128]{2,1,0:T(8,128)(2,1)S(1)} %all-to-all-done.3.block_ref), custom_call_target="tpu_custom_call" | custom-call | flops 131072 | bytes 262144 | tf_op jit(solution)/shard_map/pallas_call | solution.py:349
  49.6 6.3 %all-to-all-start.4 = ((bf16[8,128,128]{2,1,0:T(8,128)(2,1)}), bf16[8,128,128]{2,1,0:T(8,128)(2,1)S(1)}, u32[]{:S(2)}, u32[]{:S(2)}) async-start(bf16[8,128,128]{2,1,0:T(8,128)(2,1)} %shard_map.84), calls=%async_computation.4 | async-start | bytes 524288 | tf_op jit(solution)/shard_map/all_to_all | solution.py:389
  56.0 4.7 %shard_map.83 = (bf16[512,1024]{1,0:T(8,128)(2,1)S(1)}, bf16[512,256]{1,0:T(8,128)(2,1)S(1)}, bf16[512,1024]{1,0:T(8,128)(2,1)S(1)}) custom-call(bf16[512,1024]{1,0:T(8,128)(2,1)} %query_hbm.3, bf16[512,1024]{1,0:T(8,128)(2,1)} %value_hbm.9, bf16[3072,256]{1,0:T(8,128)(2,1)} %get-tuple-element.43.second_hbm.weight_hbm, ...), custom_call_target="tpu_custom_call", output_to_operand_aliasing={{0}: (3, {})} | custom-call | flops 1207959552 | bytes 4718592 | tf_op jit(solution)/shard_map/pallas_call | solution.py:349
  60.7 0.0 all-to-all-done.4
  60.7 2.9 %shard_map.85 = (bf16[512,1024]{1,0:T(8,128)(2,1)}, bf16[512,1024]{1,0:T(8,128)(2,1)}) custom-call(bf16[512,1024]{1,0:T(8,128)(2,1)} %key_hbm.9, bf16[512,1024]{1,0:T(8,128)(2,1)S(1)} %get-tuple-element.50.value_ref, bf16[512,1024]{1,0:T(8,128)(2,1)S(1)} %get-tuple-element.51.key_part, bf16[512,768]{1,0:T(8,128)(2,1)S(1)} %get-tuple-element.52.early_part, ...), custom_call_target="tpu_custom_call" | custom-call | flops 268435456 | bytes 4456448 | tf_op jit(solution)/shard_map/pallas_call | solution.py:349
Async XLA Ops:
  3.6 13.9 %all-to-all-start = ((bf16[8,128,128]{2,1,0:T(8,128)(2,1)}), bf16[8,128,128]{2,1,0:T(8,128)(2,1)S(1)}, u32[]{:S(2)}, u32[]{:S(2)}) async-start(bf16[8,128,128]{2,1,0:T(8,128)(2,1)} %bitcast.10), calls=%async_computation | async-start | bytes 524288 | tf_op jit(solution)/shard_map/all_to_all | solution.py:389
  18.3 10.9 %all-to-all-start.1 = ((bf16[8,128,128]{2,1,0:T(8,128)(2,1)}), bf16[8,128,128]{2,1,0:T(8,128)(2,1)S(1)}, u32[]{:S(2)}, u32[]{:S(2)}) async-start(bf16[8,128,128]{2,1,0:T(8,128)(2,1)} %shard_map.79), calls=%async_computation.1 | async-start | bytes 524288 | tf_op jit(solution)/shard_map/all_to_all | solution.py:389
  24.6 4.6 %copy-start = (f32[1024]{0:T(1024)S(1)}, f32[1024]{0:T(1024)}, u32[]{:S(2)}) copy-start(f32[1024]{0:T(1024)} %param.9) | copy-start | bytes 12292
  37.2 11.6 %all-to-all-start.3 = ((bf16[8,128,128]{2,1,0:T(8,128)(2,1)}), bf16[8,128,128]{2,1,0:T(8,128)(2,1)S(1)}, u32[]{:S(2)}, u32[]{:S(2)}) async-start(bf16[8,128,128]{2,1,0:T(8,128)(2,1)} %bitcast.11), calls=%async_computation.3 | async-start | bytes 524288 | tf_op jit(solution)/shard_map/all_to_all | solution.py:389
  49.6 11.0 %all-to-all-start.4 = ((bf16[8,128,128]{2,1,0:T(8,128)(2,1)}), bf16[8,128,128]{2,1,0:T(8,128)(2,1)S(1)}, u32[]{:S(2)}, u32[]{:S(2)}) async-start(bf16[8,128,128]{2,1,0:T(8,128)(2,1)} %shard_map.84), calls=%async_computation.4 | async-start | bytes 524288 | tf_op jit(solution)/shard_map/all_to_all | solution.py:389

commit v17 on v16

--- a/solution.py
+++ b/solution.py
@@ -9,7 +9,7 @@
 
 HEAD_DIM = 128
 BLOCK = 256
-COPY_COLS = 256
+COPY_COLS = 128
 EPSILON = 1e-06
 MIB = 1 << 20
 

time: 64.5 us -> 67.3 us (1.043)
  Pallas kernels: 27.5 us -> 32.9 us
  waiting for transfers between devices: 2.6 us -> 0.86 us
  starting transfers between devices: 27.1 us -> 26.3 us
    pallas_call x10, Pallas kernels: 27.5 us -> 32.9 us  [local_call(): pl.pallas_call(body, in_specs=specs, out_specs=out_specs, out_shape=outs,...]
    all_to_all x4, waiting for transfers between devices: 2.6 us -> 0.86 us  [exchange(): return lax.all_to_all(pieces, axis, 0, 0, axis_index_groups=groups)]
    all_to_all x4, starting transfers between devices: 27.1 us -> 26.3 us  [exchange(): return lax.all_to_all(pieces, axis, 0, 0, axis_index_groups=groups)]
  transfers between devices with their start and end apart: 4 -> 4, of which waited for: 3 -> 2; matrix products, arithmetic and copies ran while one was open for 0% -> 0% of each run, Pallas kernels for 28% -> 32%
where the time goes in v17:
time: 67.3 us; the launch traced here: 66.6 us
  Pallas kernels  32.9 us (49%)
  starting transfers between devices  26.3 us (39%)
  blocking collectives  5.69 us (8%)
  between operations  0.88 us (1%)
  waiting for transfers between devices  0.86 us (1%)
    pallas_call x10, Pallas kernels, local_call(): pl.pallas_call(body, in_specs=specs, out_specs=out_specs, out_shape=outs,...  32.9 us
    all_to_all x4, starting transfers between devices, exchange(): return lax.all_to_all(pieces, axis, 0, 0, axis_index_groups=groups)  26.3 us
    all_to_all x1, blocking collectives, shards(): lax.all_to_all(sums, 'head', 0, 0, axis_index_groups=[last_first(groups)])  5.69 us
  transfers between devices with their start and end apart: 4, of which 2 were waited for; matrix products, arithmetic and copies ran while one was open for 0% of the time, Pallas kernels for 32%

profile of v17, /device:TPU:0, one launch (start us, length us, event | category | flops | bytes accessed | tf_op | source)
XLA Modules:
  0.0 66.6 jit_solution(9660355244490755085)
XLA Ops:
  0.6 4.0 %shard_map.76 = bf16[1024,128]{1,0:T(8,128)(2,1)} custom-call(bf16[512,1024]{1,0:T(8,128)(2,1)} %key_hbm.9, bf16[512,1024]{1,0:T(8,128)(2,1)} %value_hbm.9), custom_call_target="tpu_custom_call" | custom-call | flops 134217728 | bytes 2097152 | tf_op jit(solution)/shard_map/pallas_call | solution.py:349
  4.6 8.4 %all-to-all-start = ((bf16[8,128,128]{2,1,0:T(8,128)(2,1)}), bf16[8,128,128]{2,1,0:T(8,128)(2,1)S(1)}, u32[]{:S(2)}, u32[]{:S(2)}) async-start(bf16[8,128,128]{2,1,0:T(8,128)(2,1)} %bitcast.10), calls=%async_computation | async-start | bytes 524288 | tf_op jit(solution)/shard_map/all_to_all | solution.py:389
  13.0 5.3 %shard_map.77 = (bf16[1024,512]{1,0:T(8,128)(2,1)S(1)}, bf16[1024,512]{1,0:T(8,128)(2,1)S(1)}, bf16[1024,512]{1,0:T(8,128)(2,1)S(1)}, bf16[3072,256]{1,0:T(8,128)(2,1)}) custom-call(bf16[512,1024]{1,0:T(8,128)(2,1)} %query_hbm.3, bf16[512,1024]{1,0:T(8,128)(2,1)} %key_hbm.9, bf16[512,1024]{1,0:T(8,128)(2,1)} %value_hbm.9, bf16[512,1024]{1,0:T(8,128)(2,1)} %grad_hbm.1), custom_call_target="tpu_custom_call" | custom-call | flops 805306368 | bytes 4194304 | tf_op jit(solution)/shard_map/pallas_call | solution.py:349
  18.2 0.3 all-to-all-done.block_ref
  18.5 0.8 %shard_map.79 = bf16[8,128,128]{2,1,0:T(8,128)(2,1)} custom-call(bf16[8,128,128]{2,1,0:T(8,128)(2,1)S(1)} %all-to-all-done.block_ref), custom_call_target="tpu_custom_call" | custom-call | flops 131072 | bytes 262144 | tf_op jit(solution)/shard_map/pallas_call | solution.py:349
  19.3 6.3 %all-to-all-start.1 = ((bf16[8,128,128]{2,1,0:T(8,128)(2,1)}), bf16[8,128,128]{2,1,0:T(8,128)(2,1)S(1)}, u32[]{:S(2)}, u32[]{:S(2)}) async-start(bf16[8,128,128]{2,1,0:T(8,128)(2,1)} %shard_map.79), calls=%async_computation.1 | async-start | bytes 524288 | tf_op jit(solution)/shard_map/all_to_all | solution.py:389
  25.6 0.0 copy-start
  25.6 4.0 %shard_map.78 = (bf16[1024,512]{1,0:T(8,128)(2,1)S(1)}, bf16[3072,256]{1,0:T(8,128)(2,1)}) custom-call(bf16[512,1024]{1,0:T(8,128)(2,1)} %key_hbm.9, bf16[512,1024]{1,0:T(8,128)(2,1)} %value_hbm.9, bf16[1024,512]{1,0:T(8,128)(2,1)S(1)} %get-tuple-element.34.flipped_ref, ...), custom_call_target="tpu_custom_call", output_to_operand_aliasing={{0}: (3, {})} | custom-call | flops 402653184 | bytes 4194304 | tf_op jit(solution)/shard_map/pallas_call | solution.py:349
  29.6 0.6 all-to-all-done.1
  30.2 0.0 copy-done
  30.2 0.8 %shard_map.80 = (bf16[1024,512]{1,0:T(8,128)(2,1)S(1)}, f32[4,2,512]{2,1,0:T(2,128)S(1)}) custom-call(f32[1,1024]{1,0:T(1,128)S(1)} %bitcast.8, bf16[1024,512]{1,0:T(8,128)(2,1)S(1)} %get-tuple-element.34.flipped_ref, bf16[1024,512]{1,0:T(8,128)(2,1)S(1)} %get-tuple-element.35.grad_ref, ...), custom_call_target="tpu_custom_call", output_to_operand_aliasing={{0}: (3, {})} | custom-call | flops 134217728 | bytes 3411968 | tf_op jit(solution)/shard_map/pallas_call | solution.py:349
  31.0 5.7 %all_to_all.25.sums_ref = f32[4,2,512]{2,1,0:T(2,128)S(1)} all-to-all(f32[4,2,512]{2,1,0:T(2,128)S(1)} %get-tuple-element.40), channel_id=1, replica_groups={{3,2,1,0},{7,6,5,4},{11,10,9,8},{15,14,13,12},{19,18,17,16},{23,22,21,2..., dimensions={0} | all-to-all | bytes 32768 | tf_op jit(solution)/shard_map/all_to_all | solution.py:461
  36.7 1.5 %shard_map.81 = (bf16[1024,512]{1,0:T(8,128)(2,1)S(1)}, bf16[1024,128]{1,0:T(8,128)(2,1)}) custom-call(f32[1,1024]{1,0:T(1,128)S(1)} %bitcast.9, bf16[1024,512]{1,0:T(8,128)(2,1)S(1)} %get-tuple-element.34.flipped_ref, bf16[1024,512]{1,0:T(8,128)(2,1)S(1)} %get-tuple-element.35.grad_ref, ...), custom_call_target="tpu_custom_call", output_to_operand_aliasing={{0}: (3, {})} | custom-call | flops 134217728 | bytes 3166208 | tf_op jit(solution)/shard_map/pallas_call | solution.py:349
  38.2 6.1 %all-to-all-start.3 = ((bf16[8,128,128]{2,1,0:T(8,128)(2,1)}), bf16[8,128,128]{2,1,0:T(8,128)(2,1)S(1)}, u32[]{:S(2)}, u32[]{:S(2)}) async-start(bf16[8,128,128]{2,1,0:T(8,128)(2,1)} %bitcast.11), calls=%async_computation.3 | async-start | bytes 524288 | tf_op jit(solution)/shard_map/all_to_all | solution.py:389
  44.4 6.4 %shard_map.82 = (bf16[512,1024]{1,0:T(8,128)(2,1)}, bf16[512,1024]{1,0:T(8,128)(2,1)S(1)}, bf16[512,768]{1,0:T(8,128)(2,1)S(1)}) custom-call(bf16[512,1024]{1,0:T(8,128)(2,1)} %key_hbm.9, bf16[512,1024]{1,0:T(8,128)(2,1)} %value_hbm.9, bf16[3072,256]{1,0:T(8,128)(2,1)} %get-tuple-element.42.first_hbm, ...), custom_call_target="tpu_custom_call" | custom-call | flops 939524096 | bytes 6553600 | tf_op jit(solution)/shard_map/pallas_call | solution.py:349
  50.7 0.0 all-to-all-done.3.block_ref
  50.7 0.8 %shard_map.84 = bf16[8,128,128]{2,1,0:T(8,128)(2,1)} custom-call(bf16[8,128,128]{2,1,0:T(8,128)(2,1)S(1)} %all-to-all-done.3.block_ref), custom_call_target="tpu_custom_call" | custom-call | flops 131072 | bytes 262144 | tf_op jit(solution)/shard_map/pallas_call | solution.py:349
  51.5 5.4 %all-to-all-start.4 = ((bf16[8,128,128]{2,1,0:T(8,128)(2,1)}), bf16[8,128,128]{2,1,0:T(8,128)(2,1)S(1)}, u32[]{:S(2)}, u32[]{:S(2)}) async-start(bf16[8,128,128]{2,1,0:T(8,128)(2,1)} %shard_map.84), calls=%async_computation.4 | async-start | bytes 524288 | tf_op jit(solution)/shard_map/all_to_all | solution.py:389
  57.0 5.8 %shard_map.83 = (bf16[512,1024]{1,0:T(8,128)(2,1)S(1)}, bf16[512,256]{1,0:T(8,128)(2,1)S(1)}, bf16[512,1024]{1,0:T(8,128)(2,1)S(1)}) custom-call(bf16[512,1024]{1,0:T(8,128)(2,1)} %query_hbm.3, bf16[512,1024]{1,0:T(8,128)(2,1)} %value_hbm.9, bf16[3072,256]{1,0:T(8,128)(2,1)} %get-tuple-element.43.second_hbm.weight_hbm, ...), custom_call_target="tpu_custom_call", output_to_operand_aliasing={{0}: (3, {})} | custom-call | flops 1207959552 | bytes 4718592 | tf_op jit(solution)/shard_map/pallas_call | solution.py:349
  62.8 0.0 all-to-all-done.4
  62.8 3.7 %shard_map.85 = (bf16[512,1024]{1,0:T(8,128)(2,1)}, bf16[512,1024]{1,0:T(8,128)(2,1)}) custom-call(bf16[512,1024]{1,0:T(8,128)(2,1)} %key_hbm.9, bf16[512,1024]{1,0:T(8,128)(2,1)S(1)} %get-tuple-element.50.value_ref, bf16[512,1024]{1,0:T(8,128)(2,1)S(1)} %get-tuple-element.51.key_part, bf16[512,768]{1,0:T(8,128)(2,1)S(1)} %get-tuple-element.52.early_part, ...), custom_call_target="tpu_custom_call" | custom-call | flops 268435456 | bytes 4456448 | tf_op jit(solution)/shard_map/pallas_call | solution.py:349
Async XLA Ops:
  4.6 13.9 %all-to-all-start = ((bf16[8,128,128]{2,1,0:T(8,128)(2,1)}), bf16[8,128,128]{2,1,0:T(8,128)(2,1)S(1)}, u32[]{:S(2)}, u32[]{:S(2)}) async-start(bf16[8,128,128]{2,1,0:T(8,128)(2,1)} %bitcast.10), calls=%async_computation | async-start | bytes 524288 | tf_op jit(solution)/shard_map/all_to_all | solution.py:389
  19.3 10.9 %all-to-all-start.1 = ((bf16[8,128,128]{2,1,0:T(8,128)(2,1)}), bf16[8,128,128]{2,1,0:T(8,128)(2,1)S(1)}, u32[]{:S(2)}, u32[]{:S(2)}) async-start(bf16[8,128,128]{2,1,0:T(8,128)(2,1)} %shard_map.79), calls=%async_computation.1 | async-start | bytes 524288 | tf_op jit(solution)/shard_map/all_to_all | solution.py:389
  25.6 4.6 %copy-start = (f32[1024]{0:T(1024)S(1)}, f32[1024]{0:T(1024)}, u32[]{:S(2)}) copy-start(f32[1024]{0:T(1024)} %param.9) | copy-start | bytes 12292
  38.2 12.5 %all-to-all-start.3 = ((bf16[8,128,128]{2,1,0:T(8,128)(2,1)}), bf16[8,128,128]{2,1,0:T(8,128)(2,1)S(1)}, u32[]{:S(2)}, u32[]{:S(2)}) async-start(bf16[8,128,128]{2,1,0:T(8,128)(2,1)} %bitcast.11), calls=%async_computation.3 | async-start | bytes 524288 | tf_op jit(solution)/shard_map/all_to_all | solution.py:389
  51.5 11.3 %all-to-all-start.4 = ((bf16[8,128,128]{2,1,0:T(8,128)(2,1)}), bf16[8,128,128]{2,1,0:T(8,128)(2,1)S(1)}, u32[]{:S(2)}, u32[]{:S(2)}) async-start(bf16[8,128,128]{2,1,0:T(8,128)(2,1)} %shard_map.84), calls=%async_computation.4 | async-start | bytes 524288 | tf_op jit(solution)/shard_map/all_to_all | solution.py:389

commit v18 on v17

--- a/solution.py
+++ b/solution.py
@@ -9,7 +9,9 @@
 
 HEAD_DIM = 128
 BLOCK = 256
-COPY_COLS = 128
+COPY_COLS = 512
+COPY_ROWS = 128
+STATE_ROWS = 256
 EPSILON = 1e-06
 MIB = 1 << 20
 
@@ -50,10 +52,10 @@
     return copies
 
 
-def row_copies(source, target, sems):
+def row_copies(source, target, size, sems):
     copies = []
-    for index in range(source.shape[0] // COPY_COLS):
-        part = slice(index * COPY_COLS, (index + 1) * COPY_COLS)
+    for index in range(source.shape[0] // size):
+        part = slice(index * size, (index + 1) * size)
         copies.append(pltpu.make_async_copy(source.at[part, :], target.at[part, :], sems.at[index]))
     return copies
 
@@ -71,19 +73,27 @@
 
 
 def states_body(
-    key_hbm, value_hbm, state_hbm, key_ref, value_ref, state_ref, key_sems, value_sems, state_sems
-):
-    stores = row_copies(state_ref, state_hbm, state_sems)
-    key_copies = column_copies(key_hbm, key_ref, key_sems)
-    value_copies = column_copies(value_hbm, value_ref, value_sems)
-    start_all(key_copies, value_copies)
-    for index, cols in enumerate(pieces_of(key_ref, COPY_COLS)):
-        key_copies[index].wait()
-        value_copies[index].wait()
-        for start in range(cols.start, cols.stop, HEAD_DIM):
-            head = slice(start, start + HEAD_DIM)
-            state_ref[head, :] = mm_tn(key_ref[:, head], value_ref[:, head]).astype(jnp.bfloat16)
-        stores[index].start()
+    key_hbm, value_hbm, state_hbm, key_ref, value_ref, total_ref, state_ref,
+    key_sems, value_sems, state_sems,
+):
+    keys = row_copies(key_hbm, key_ref, COPY_ROWS, key_sems)
+    values = row_copies(value_hbm, value_ref, COPY_ROWS, value_sems)
+    stores = row_copies(state_ref, state_hbm, STATE_ROWS, state_sems)
+    start_all(keys, values)
+    for index in range(len(keys)):
+        keys[index].wait()
+        values[index].wait()
+        rows = slice(index * COPY_ROWS, (index + 1) * COPY_ROWS)
+        for head in pieces_of(key_ref, HEAD_DIM):
+            part = mm_tn(key_ref[rows, head], value_ref[rows, head])
+            if index:
+                part = part + total_ref[head, :]
+            if index < len(keys) - 1:
+                total_ref[head, :] = part
+            else:
+                state_ref[head, :] = part.astype(jnp.bfloat16)
+                if head.stop % STATE_ROWS == 0:
+                    stores[head.stop // STATE_ROWS - 1].start()
     wait_all(stores)
 
 
@@ -213,7 +223,7 @@
 def dout_body(
     width, gain_ref, flipped_ref, grad_ref, attended_ref, sums_ref, dout_ref, own_hbm, own_ref, sems
 ):
-    stores = row_copies(own_ref, own_hbm, sems)
+    stores = row_copies(own_ref, own_hbm, STATE_ROWS, sems)
     sums = sum(sums_ref[group] for group in range(sums_ref.shape[0]))
     inverse = 1.0 / jnp.sqrt(sums[0:1, :] / width + EPSILON)
     drop = sums[1:2, :] * (inverse * inverse * inverse) / width
@@ -223,8 +233,8 @@
         dout = dout.astype(jnp.bfloat16)
         dout_ref[head, :] = dout
         own_ref[head, :] = mm_nt(flipped_ref[head, :], dout).astype(jnp.bfloat16)
-        if head.stop % COPY_COLS == 0:
-            stores[head.stop // COPY_COLS - 1].start()
+        if head.stop % STATE_ROWS == 0:
+            stores[head.stop // STATE_ROWS - 1].start()
     wait_all(stores)
 
 
@@ -293,9 +303,9 @@
     for index, step in enumerate(pieces_of(key_out, COPY_COLS)):
         query_copies[index].wait()
         value_copies[index].wait()
-        if step.start == early:
-            weight_copy.wait()
         for left in range(step.start, step.stop, HEAD_DIM):
+            if left == early:
+                weight_copy.wait()
             cols = slice(left, left + HEAD_DIM)
             dout = key_out[:, cols]
             for start in range(0, rows, BLOCK):
@@ -404,7 +414,9 @@
     large = 2 * rows * rows * width * 3 // 4
     gain_row = gain.reshape(1, width)
     flat = (width, rows)
-    chunks = pltpu.SemaphoreType.DMA((width // COPY_COLS,))
+    dma = pltpu.SemaphoreType.DMA
+    chunks, row_chunks = dma((width // COPY_COLS,)), dma((rows // COPY_ROWS,))
+    state_chunks = dma((width // STATE_ROWS,))
     vm, hbm = pltpu.VMEM, pltpu.HBM
     rows_vm, flat_vm, state_vm = vm(tokens, bf16), vm(flat, bf16), vm(state, bf16)
 
@@ -414,13 +426,11 @@
         [hbm(state, bf16)],
         small,
         [keys, values],
-        [rows_vm] * 2 + [state_vm] + [chunks] * 3,
+        [rows_vm] * 2 + [vm(state, f32), state_vm] + [row_chunks] * 2 + [state_chunks],
     )
     kv_blocks = exchange(in_pieces(own_kv, "seq"), "seq")
     half = width // 2 // COPY_COLS * COPY_COLS
-    early = width * 3 // 4 // COPY_COLS * COPY_COLS
-    dma = pltpu.SemaphoreType.DMA
-
+    early = width * 3 // 4 // HEAD_DIM * HEAD_DIM
     def weights_of(cols):
         return (cols // HEAD_DIM * weight_rows(rows), BLOCK)
 
@@ -464,7 +474,7 @@
         [gain_row, flipped, grad_flipped, attended, sums],
         [flat_vm, hbm(state, bf16)],
         small,
-        scratch=[state_vm, chunks],
+        scratch=[state_vm, state_chunks],
         aliases={3: 0},
     )
     grad_blocks = exchange(in_pieces(own_grad, "seq"), "seq")

time: 67.3 us -> 63.4 us (0.942)
  Pallas kernels: 32.9 us -> 25.4 us
  waiting for transfers between devices: 0.86 us -> 3.61 us
  starting transfers between devices: 26.3 us -> 27.2 us
    pallas_call x10, Pallas kernels: 32.9 us -> 25.4 us  [local_call(): pl.pallas_call(body, in_specs=specs, out_specs=out_specs, out_shape=outs,...]
    all_to_all x4, waiting for transfers between devices: 0.86 us -> 3.61 us  [exchange(): return lax.all_to_all(pieces, axis, 0, 0, axis_index_groups=groups)]
    all_to_all x4, starting transfers between devices: 26.3 us -> 27.2 us  [exchange(): return lax.all_to_all(pieces, axis, 0, 0, axis_index_groups=groups)]
  transfers between devices with their start and end apart: 4 -> 4, of which waited for: 2 -> 4; matrix products, arithmetic and copies ran while one was open for 0% -> 0% of each run, Pallas kernels for 32% -> 26%
where the time goes in v18:
time: 63.4 us; the launch traced here: 62.7 us
  starting transfers between devices  27.2 us (43%)
  Pallas kernels  25.4 us (40%)
  blocking collectives  5.67 us (9%)
  waiting for transfers between devices  3.61 us (6%)
  between operations  0.87 us (1%)
    all_to_all x4, starting transfers between devices, exchange(): return lax.all_to_all(pieces, axis, 0, 0, axis_index_groups=groups)  27.2 us
    pallas_call x10, Pallas kernels, local_call(): pl.pallas_call(body, in_specs=specs, out_specs=out_specs, out_shape=outs,...  25.4 us
    all_to_all x1, blocking collectives, shards(): lax.all_to_all(sums, 'head', 0, 0, axis_index_groups=[last_first(groups)])  5.67 us
    all_to_all x4, waiting for transfers between devices, exchange(): return lax.all_to_all(pieces, axis, 0, 0, axis_index_groups=groups)  3.61 us
  transfers between devices with their start and end apart: 4, of which 4 were waited for; matrix products, arithmetic and copies ran while one was open for 0% of the time, Pallas kernels for 26%

profile of v18, /device:TPU:0, one launch (start us, length us, event | category | flops | bytes accessed | tf_op | source)
XLA Modules:
  0.0 62.7 jit_solution(4106917206586852878)
XLA Ops:
  0.6 2.5 %shard_map.76 = bf16[1024,128]{1,0:T(8,128)(2,1)} custom-call(bf16[512,1024]{1,0:T(8,128)(2,1)} %key_hbm.9, bf16[512,1024]{1,0:T(8,128)(2,1)} %value_hbm.9), custom_call_target="tpu_custom_call" | custom-call | flops 134217728 | bytes 2097152 | tf_op jit(solution)/shard_map/pallas_call | solution.py:359
  3.1 8.4 %all-to-all-start = ((bf16[8,128,128]{2,1,0:T(8,128)(2,1)}), bf16[8,128,128]{2,1,0:T(8,128)(2,1)S(1)}, u32[]{:S(2)}, u32[]{:S(2)}) async-start(bf16[8,128,128]{2,1,0:T(8,128)(2,1)} %bitcast.10), calls=%async_computation | async-start | bytes 524288 | tf_op jit(solution)/shard_map/all_to_all | solution.py:399
  11.5 3.8 %shard_map.77 = (bf16[1024,512]{1,0:T(8,128)(2,1)S(1)}, bf16[1024,512]{1,0:T(8,128)(2,1)S(1)}, bf16[1024,512]{1,0:T(8,128)(2,1)S(1)}, bf16[3072,256]{1,0:T(8,128)(2,1)}) custom-call(bf16[512,1024]{1,0:T(8,128)(2,1)} %query_hbm.3, bf16[512,1024]{1,0:T(8,128)(2,1)} %key_hbm.9, bf16[512,1024]{1,0:T(8,128)(2,1)} %value_hbm.9, bf16[512,1024]{1,0:T(8,128)(2,1)} %grad_hbm.1), custom_call_target="tpu_custom_call" | custom-call | flops 805306368 | bytes 4194304 | tf_op jit(solution)/shard_map/pallas_call | solution.py:359
  15.3 1.7 %all-to-all-done.block_ref = bf16[8,128,128]{2,1,0:T(8,128)(2,1)S(1)} async-done(((bf16[8,128,128]{2,1,0:T(8,128)(2,1)}), bf16[8,128,128]{2,1,0:T(8,128)(2,1)S(1)}, u32[]{:S(2)}, u32[]{:S(2)}) %all-to-all-start) | async-done | bytes 262176 | tf_op jit(solution)/shard_map/all_to_all | solution.py:399
  17.0 0.8 %shard_map.79 = bf16[8,128,128]{2,1,0:T(8,128)(2,1)} custom-call(bf16[8,128,128]{2,1,0:T(8,128)(2,1)S(1)} %all-to-all-done.block_ref), custom_call_target="tpu_custom_call" | custom-call | flops 131072 | bytes 262144 | tf_op jit(solution)/shard_map/pallas_call | solution.py:359
  17.8 6.3 %all-to-all-start.1 = ((bf16[8,128,128]{2,1,0:T(8,128)(2,1)}), bf16[8,128,128]{2,1,0:T(8,128)(2,1)S(1)}, u32[]{:S(2)}, u32[]{:S(2)}) async-start(bf16[8,128,128]{2,1,0:T(8,128)(2,1)} %shard_map.79), calls=%async_computation.1 | async-start | bytes 524288 | tf_op jit(solution)/shard_map/all_to_all | solution.py:399
  24.2 0.0 copy-start
  24.2 3.3 %shard_map.78 = (bf16[1024,512]{1,0:T(8,128)(2,1)S(1)}, bf16[3072,256]{1,0:T(8,128)(2,1)}) custom-call(bf16[512,1024]{1,0:T(8,128)(2,1)} %key_hbm.9, bf16[512,1024]{1,0:T(8,128)(2,1)} %value_hbm.9, bf16[1024,512]{1,0:T(8,128)(2,1)S(1)} %get-tuple-element.34.flipped_ref, ...), custom_call_target="tpu_custom_call", output_to_operand_aliasing={{0}: (3, {})} | custom-call | flops 402653184 | bytes 4194304 | tf_op jit(solution)/shard_map/pallas_call | solution.py:359
  27.5 1.3 %all-to-all-done.1 = bf16[8,128,128]{2,1,0:T(8,128)(2,1)S(1)} async-done(((bf16[8,128,128]{2,1,0:T(8,128)(2,1)}), bf16[8,128,128]{2,1,0:T(8,128)(2,1)S(1)}, u32[]{:S(2)}, u32[]{:S(2)}) %all-to-all-start.1) | async-done | bytes 262176 | tf_op jit(solution)/shard_map/all_to_all | solution.py:399
  28.8 0.0 copy-done
  28.8 0.8 %shard_map.80 = (bf16[1024,512]{1,0:T(8,128)(2,1)S(1)}, f32[4,2,512]{2,1,0:T(2,128)S(1)}) custom-call(f32[1,1024]{1,0:T(1,128)S(1)} %bitcast.8, bf16[1024,512]{1,0:T(8,128)(2,1)S(1)} %get-tuple-element.34.flipped_ref, bf16[1024,512]{1,0:T(8,128)(2,1)S(1)} %get-tuple-element.35.grad_ref, ...), custom_call_target="tpu_custom_call", output_to_operand_aliasing={{0}: (3, {})} | custom-call | flops 134217728 | bytes 3411968 | tf_op jit(solution)/shard_map/pallas_call | solution.py:359
  29.6 5.7 %all_to_all.25.sums_ref = f32[4,2,512]{2,1,0:T(2,128)S(1)} all-to-all(f32[4,2,512]{2,1,0:T(2,128)S(1)} %get-tuple-element.40), channel_id=1, replica_groups={{3,2,1,0},{7,6,5,4},{11,10,9,8},{15,14,13,12},{19,18,17,16},{23,22,21,2..., dimensions={0} | all-to-all | bytes 32768 | tf_op jit(solution)/shard_map/all_to_all | solution.py:471
  35.3 1.5 %shard_map.81 = (bf16[1024,512]{1,0:T(8,128)(2,1)S(1)}, bf16[1024,128]{1,0:T(8,128)(2,1)}) custom-call(f32[1,1024]{1,0:T(1,128)S(1)} %bitcast.9, bf16[1024,512]{1,0:T(8,128)(2,1)S(1)} %get-tuple-element.34.flipped_ref, bf16[1024,512]{1,0:T(8,128)(2,1)S(1)} %get-tuple-element.35.grad_ref, ...), custom_call_target="tpu_custom_call", output_to_operand_aliasing={{0}: (3, {})} | custom-call | flops 134217728 | bytes 3166208 | tf_op jit(solution)/shard_map/pallas_call | solution.py:359
  36.7 6.1 %all-to-all-start.3 = ((bf16[8,128,128]{2,1,0:T(8,128)(2,1)}), bf16[8,128,128]{2,1,0:T(8,128)(2,1)S(1)}, u32[]{:S(2)}, u32[]{:S(2)}) async-start(bf16[8,128,128]{2,1,0:T(8,128)(2,1)} %bitcast.11), calls=%async_computation.3 | async-start | bytes 524288 | tf_op jit(solution)/shard_map/all_to_all | solution.py:399
  42.9 4.9 %shard_map.82 = (bf16[512,1024]{1,0:T(8,128)(2,1)}, bf16[512,1024]{1,0:T(8,128)(2,1)S(1)}, bf16[512,768]{1,0:T(8,128)(2,1)S(1)}) custom-call(bf16[512,1024]{1,0:T(8,128)(2,1)} %key_hbm.9, bf16[512,1024]{1,0:T(8,128)(2,1)} %value_hbm.9, bf16[3072,256]{1,0:T(8,128)(2,1)} %get-tuple-element.42.first_hbm, ...), custom_call_target="tpu_custom_call" | custom-call | flops 939524096 | bytes 6553600 | tf_op jit(solution)/shard_map/pallas_call | solution.py:359
  47.8 0.5 all-to-all-done.3.block_ref
  48.4 0.8 %shard_map.84 = bf16[8,128,128]{2,1,0:T(8,128)(2,1)} custom-call(bf16[8,128,128]{2,1,0:T(8,128)(2,1)S(1)} %all-to-all-done.3.block_ref), custom_call_target="tpu_custom_call" | custom-call | flops 131072 | bytes 262144 | tf_op jit(solution)/shard_map/pallas_call | solution.py:359
  49.1 6.3 %all-to-all-start.4 = ((bf16[8,128,128]{2,1,0:T(8,128)(2,1)}), bf16[8,128,128]{2,1,0:T(8,128)(2,1)S(1)}, u32[]{:S(2)}, u32[]{:S(2)}) async-start(bf16[8,128,128]{2,1,0:T(8,128)(2,1)} %shard_map.84), calls=%async_computation.4 | async-start | bytes 524288 | tf_op jit(solution)/shard_map/all_to_all | solution.py:399
  55.5 4.5 %shard_map.83 = (bf16[512,1024]{1,0:T(8,128)(2,1)S(1)}, bf16[512,256]{1,0:T(8,128)(2,1)S(1)}, bf16[512,1024]{1,0:T(8,128)(2,1)S(1)}) custom-call(bf16[512,1024]{1,0:T(8,128)(2,1)} %query_hbm.3, bf16[512,1024]{1,0:T(8,128)(2,1)} %value_hbm.9, bf16[3072,256]{1,0:T(8,128)(2,1)} %get-tuple-element.43.second_hbm.weight_hbm, ...), custom_call_target="tpu_custom_call", output_to_operand_aliasing={{0}: (3, {})} | custom-call | flops 1207959552 | bytes 4718592 | tf_op jit(solution)/shard_map/pallas_call | solution.py:359
  60.0 0.1 all-to-all-done.4
  60.1 2.5 %shard_map.85 = (bf16[512,1024]{1,0:T(8,128)(2,1)}, bf16[512,1024]{1,0:T(8,128)(2,1)}) custom-call(bf16[512,1024]{1,0:T(8,128)(2,1)} %key_hbm.9, bf16[512,1024]{1,0:T(8,128)(2,1)S(1)} %get-tuple-element.50.value_ref, bf16[512,1024]{1,0:T(8,128)(2,1)S(1)} %get-tuple-element.51.key_part, bf16[512,768]{1,0:T(8,128)(2,1)S(1)} %get-tuple-element.52.early_part, ...), custom_call_target="tpu_custom_call" | custom-call | flops 268435456 | bytes 4456448 | tf_op jit(solution)/shard_map/pallas_call | solution.py:359
Async XLA Ops:
  3.1 13.9 %all-to-all-start = ((bf16[8,128,128]{2,1,0:T(8,128)(2,1)}), bf16[8,128,128]{2,1,0:T(8,128)(2,1)S(1)}, u32[]{:S(2)}, u32[]{:S(2)}) async-start(bf16[8,128,128]{2,1,0:T(8,128)(2,1)} %bitcast.10), calls=%async_computation | async-start | bytes 524288 | tf_op jit(solution)/shard_map/all_to_all | solution.py:399
  17.8 10.9 %all-to-all-start.1 = ((bf16[8,128,128]{2,1,0:T(8,128)(2,1)}), bf16[8,128,128]{2,1,0:T(8,128)(2,1)S(1)}, u32[]{:S(2)}, u32[]{:S(2)}) async-start(bf16[8,128,128]{2,1,0:T(8,128)(2,1)} %shard_map.79), calls=%async_computation.1 | async-start | bytes 524288 | tf_op jit(solution)/shard_map/all_to_all | solution.py:399
  24.2 4.6 %copy-start = (f32[1024]{0:T(1024)S(1)}, f32[1024]{0:T(1024)}, u32[]{:S(2)}) copy-start(f32[1024]{0:T(1024)} %param.9) | copy-start | bytes 12292
  36.7 11.6 %all-to-all-start.3 = ((bf16[8,128,128]{2,1,0:T(8,128)(2,1)}), bf16[8,128,128]{2,1,0:T(8,128)(2,1)S(1)}, u32[]{:S(2)}, u32[]{:S(2)}) async-start(bf16[8,128,128]{2,1,0:T(8,128)(2,1)} %bitcast.11), calls=%async_computation.3 | async-start | bytes 524288 | tf_op jit(solution)/shard_map/all_to_all | solution.py:399
  49.1 10.9 %all-to-all-start.4 = ((bf16[8,128,128]{2,1,0:T(8,128)(2,1)}), bf16[8,128,128]{2,1,0:T(8,128)(2,1)S(1)}, u32[]{:S(2)}, u32[]{:S(2)}) async-start(bf16[8,128,128]{2,1,0:T(8,128)(2,1)} %shard_map.84), calls=%async_computation.4 | async-start | bytes 524288 | tf_op jit(solution)/shard_map/all_to_all | solution.py:399

commit v19 on v18

--- a/solution.py
+++ b/solution.py
@@ -322,28 +322,29 @@
     key_hbm, value_ref, key_part, early_part, late_part, state_ref, key_out_hbm, value_out_hbm,
     key_ref, key_out, value_out, in_sems, key_sems, value_sems,
 ):
-    keys = column_copies(key_hbm, key_ref, in_sems)
+    keys = row_copies(key_hbm, key_ref, COPY_ROWS, in_sems)
     start_all(keys)
-    key_stores = column_copies(key_out, key_out_hbm, key_sems)
-    value_stores = column_copies(value_out, value_out_hbm, value_sems)
-    for index, step in enumerate(pieces_of(key_out, COPY_COLS)):
-        for left in range(step.start, step.stop, HEAD_DIM):
-            cols = slice(left, left + HEAD_DIM)
-            grad = key_part[:, cols].astype(jnp.float32) + mm_nt(value_ref[:, cols], state_ref[cols, :])
-            key_out[:, cols] = grad.astype(jnp.bfloat16)
-        key_stores[index].start()
-    for index, step in enumerate(pieces_of(value_out, COPY_COLS)):
+    key_stores = row_copies(key_out, key_out_hbm, COPY_ROWS, key_sems)
+    value_stores = row_copies(value_out, value_out_hbm, COPY_ROWS, value_sems)
+    early = early_part.shape[1]
+    for index, store in enumerate(key_stores):
+        rows = slice(index * COPY_ROWS, (index + 1) * COPY_ROWS)
+        for cols in pieces_of(key_out, HEAD_DIM):
+            part = key_part[rows, cols].astype(jnp.float32)
+            grad = part + mm_nt(value_ref[rows, cols], state_ref[cols, :])
+            key_out[rows, cols] = grad.astype(jnp.bfloat16)
+        store.start()
+    for index, store in enumerate(value_stores):
+        rows = slice(index * COPY_ROWS, (index + 1) * COPY_ROWS)
         keys[index].wait()
-        for left in range(step.start, step.stop, HEAD_DIM):
-            cols = slice(left, left + HEAD_DIM)
-            early = early_part.shape[1]
-            if left < early:
-                part = early_part[:, cols]
+        for cols in pieces_of(value_out, HEAD_DIM):
+            if cols.start < early:
+                part = early_part[rows, cols]
             else:
-                part = late_part[:, left - early : left - early + HEAD_DIM]
-            grad = part.astype(jnp.float32) + mm(key_ref[:, cols], state_ref[cols, :])
-            value_out[:, cols] = grad.astype(jnp.bfloat16)
-        value_stores[index].start()
+                part = late_part[rows, cols.start - early : cols.stop - early]
+            grad = part.astype(jnp.float32) + mm(key_ref[rows, cols], state_ref[cols, :])
+            value_out[rows, cols] = grad.astype(jnp.bfloat16)
+        store.start()
     wait_all(key_stores, value_stores)
 
 
@@ -387,7 +388,7 @@
     first, second, third, fourth = (list(range(at, at + quarter)) for at in range(0, count, quarter))
     half = quarter // 2
     order = second + first[:half] + third[:half] + first[half:] + third[half:] + fourth
-    return [count - 1 - place for place in order]
+    return [(count - 1 - place) ^ 1 for place in order]
 
 
 def last_first(count):
@@ -506,7 +507,7 @@
         [hbm(tokens, bf16)] * 2,
         2 * small,
         [keys],
-        [rows_vm] * 3 + [chunks] * 3,
+        [rows_vm] * 3 + [row_chunks] * 3,
     )
     return query_grad, key_grad, value_grad
 

time: 63.4 us -> 63.8 us (level)
  starting transfers between devices: 27.2 us -> 22.4 us
  waiting for transfers between devices: 3.61 us -> 8.29 us
    all_to_all x4, starting transfers between devices: 27.2 us -> 22.4 us  [exchange(): return lax.all_to_all(pieces, axis, 0, 0, axis_index_groups=groups)]
    all_to_all x4, waiting for transfers between devices: 3.61 us -> 8.29 us  [exchange(): return lax.all_to_all(pieces, axis, 0, 0, axis_index_groups=groups)]
where the time goes in v19:
time: 63.8 us; the launch traced here: 63.1 us
  Pallas kernels  25.8 us (40%)
  starting transfers between devices  22.4 us (35%)
  waiting for transfers between devices  8.29 us (13%)
  blocking collectives  5.68 us (9%)
  between operations  0.87 us (1%)
    pallas_call x10, Pallas kernels, local_call(): pl.pallas_call(body, in_specs=specs, out_specs=out_specs, out_shape=outs,...  25.8 us
    all_to_all x4, starting transfers between devices, exchange(): return lax.all_to_all(pieces, axis, 0, 0, axis_index_groups=groups)  22.4 us
    all_to_all x4, waiting for transfers between devices, exchange(): return lax.all_to_all(pieces, axis, 0, 0, axis_index_groups=groups)  8.29 us
    all_to_all x1, blocking collectives, shards(): lax.all_to_all(sums, 'head', 0, 0, axis_index_groups=[last_first(groups)])  5.68 us
  transfers between devices with their start and end apart: 4, of which 4 were waited for; matrix products, arithmetic and copies ran while one was open for 0% of the time, Pallas kernels for 26%

profile of v19, /device:TPU:0, one launch (start us, length us, event | category | flops | bytes accessed | tf_op | source)
XLA Modules:
  0.0 63.1 jit_solution(8408487564204717781)
XLA Ops:
  0.6 2.5 %shard_map.76 = bf16[1024,128]{1,0:T(8,128)(2,1)} custom-call(bf16[512,1024]{1,0:T(8,128)(2,1)} %key_hbm.9, bf16[512,1024]{1,0:T(8,128)(2,1)} %value_hbm.9), custom_call_target="tpu_custom_call" | custom-call | flops 134217728 | bytes 2097152 | tf_op jit(solution)/shard_map/pallas_call | solution.py:360
  3.1 7.9 %all-to-all-start = ((bf16[8,128,128]{2,1,0:T(8,128)(2,1)}), bf16[8,128,128]{2,1,0:T(8,128)(2,1)S(1)}, u32[]{:S(2)}, u32[]{:S(2)}) async-start(bf16[8,128,128]{2,1,0:T(8,128)(2,1)} %bitcast.10), calls=%async_computation | async-start | bytes 524288 | tf_op jit(solution)/shard_map/all_to_all | solution.py:400
  11.0 3.8 %shard_map.77 = (bf16[1024,512]{1,0:T(8,128)(2,1)S(1)}, bf16[1024,512]{1,0:T(8,128)(2,1)S(1)}, bf16[1024,512]{1,0:T(8,128)(2,1)S(1)}, bf16[3072,256]{1,0:T(8,128)(2,1)}) custom-call(bf16[512,1024]{1,0:T(8,128)(2,1)} %query_hbm.3, bf16[512,1024]{1,0:T(8,128)(2,1)} %key_hbm.9, bf16[512,1024]{1,0:T(8,128)(2,1)} %value_hbm.9, bf16[512,1024]{1,0:T(8,128)(2,1)} %grad_hbm.1), custom_call_target="tpu_custom_call" | custom-call | flops 805306368 | bytes 4194304 | tf_op jit(solution)/shard_map/pallas_call | solution.py:360
  14.8 3.2 %all-to-all-done.block_ref = bf16[8,128,128]{2,1,0:T(8,128)(2,1)S(1)} async-done(((bf16[8,128,128]{2,1,0:T(8,128)(2,1)}), bf16[8,128,128]{2,1,0:T(8,128)(2,1)S(1)}, u32[]{:S(2)}, u32[]{:S(2)}) %all-to-all-start) | async-done | bytes 262176 | tf_op jit(solution)/shard_map/all_to_all | solution.py:400
  18.0 0.8 %shard_map.79 = bf16[8,128,128]{2,1,0:T(8,128)(2,1)} custom-call(bf16[8,128,128]{2,1,0:T(8,128)(2,1)S(1)} %all-to-all-done.block_ref), custom_call_target="tpu_custom_call" | custom-call | flops 131072 | bytes 262144 | tf_op jit(solution)/shard_map/pallas_call | solution.py:360
  18.8 4.6 %all-to-all-start.1 = ((bf16[8,128,128]{2,1,0:T(8,128)(2,1)}), bf16[8,128,128]{2,1,0:T(8,128)(2,1)S(1)}, u32[]{:S(2)}, u32[]{:S(2)}) async-start(bf16[8,128,128]{2,1,0:T(8,128)(2,1)} %shard_map.79), calls=%async_computation.1 | async-start | bytes 524288 | tf_op jit(solution)/shard_map/all_to_all | solution.py:400
  23.4 0.0 copy-start
  23.4 3.3 %shard_map.78 = (bf16[1024,512]{1,0:T(8,128)(2,1)S(1)}, bf16[3072,256]{1,0:T(8,128)(2,1)}) custom-call(bf16[512,1024]{1,0:T(8,128)(2,1)} %key_hbm.9, bf16[512,1024]{1,0:T(8,128)(2,1)} %value_hbm.9, bf16[1024,512]{1,0:T(8,128)(2,1)S(1)} %get-tuple-element.34.flipped_ref, ...), custom_call_target="tpu_custom_call", output_to_operand_aliasing={{0}: (3, {})} | custom-call | flops 402653184 | bytes 4194304 | tf_op jit(solution)/shard_map/pallas_call | solution.py:360
  26.7 2.0 %all-to-all-done.1 = bf16[8,128,128]{2,1,0:T(8,128)(2,1)S(1)} async-done(((bf16[8,128,128]{2,1,0:T(8,128)(2,1)}), bf16[8,128,128]{2,1,0:T(8,128)(2,1)S(1)}, u32[]{:S(2)}, u32[]{:S(2)}) %all-to-all-start.1) | async-done | bytes 262176 | tf_op jit(solution)/shard_map/all_to_all | solution.py:400
  28.7 0.0 copy-done
  28.7 0.8 %shard_map.80 = (bf16[1024,512]{1,0:T(8,128)(2,1)S(1)}, f32[4,2,512]{2,1,0:T(2,128)S(1)}) custom-call(f32[1,1024]{1,0:T(1,128)S(1)} %bitcast.8, bf16[1024,512]{1,0:T(8,128)(2,1)S(1)} %get-tuple-element.34.flipped_ref, bf16[1024,512]{1,0:T(8,128)(2,1)S(1)} %get-tuple-element.35.grad_ref, ...), custom_call_target="tpu_custom_call", output_to_operand_aliasing={{0}: (3, {})} | custom-call | flops 134217728 | bytes 3411968 | tf_op jit(solution)/shard_map/pallas_call | solution.py:360
  29.5 5.7 %all_to_all.25.sums_ref = f32[4,2,512]{2,1,0:T(2,128)S(1)} all-to-all(f32[4,2,512]{2,1,0:T(2,128)S(1)} %get-tuple-element.40), channel_id=1, replica_groups={{3,2,1,0},{7,6,5,4},{11,10,9,8},{15,14,13,12},{19,18,17,16},{23,22,21,2..., dimensions={0} | all-to-all | bytes 32768 | tf_op jit(solution)/shard_map/all_to_all | solution.py:472
  35.2 1.5 %shard_map.81 = (bf16[1024,512]{1,0:T(8,128)(2,1)S(1)}, bf16[1024,128]{1,0:T(8,128)(2,1)}) custom-call(f32[1,1024]{1,0:T(1,128)S(1)} %bitcast.9, bf16[1024,512]{1,0:T(8,128)(2,1)S(1)} %get-tuple-element.34.flipped_ref, bf16[1024,512]{1,0:T(8,128)(2,1)S(1)} %get-tuple-element.35.grad_ref, ...), custom_call_target="tpu_custom_call", output_to_operand_aliasing={{0}: (3, {})} | custom-call | flops 134217728 | bytes 3166208 | tf_op jit(solution)/shard_map/pallas_call | solution.py:360
  36.7 5.4 %all-to-all-start.3 = ((bf16[8,128,128]{2,1,0:T(8,128)(2,1)}), bf16[8,128,128]{2,1,0:T(8,128)(2,1)S(1)}, u32[]{:S(2)}, u32[]{:S(2)}) async-start(bf16[8,128,128]{2,1,0:T(8,128)(2,1)} %bitcast.11), calls=%async_computation.3 | async-start | bytes 524288 | tf_op jit(solution)/shard_map/all_to_all | solution.py:400
  42.1 4.9 %shard_map.82 = (bf16[512,1024]{1,0:T(8,128)(2,1)}, bf16[512,1024]{1,0:T(8,128)(2,1)S(1)}, bf16[512,768]{1,0:T(8,128)(2,1)S(1)}) custom-call(bf16[512,1024]{1,0:T(8,128)(2,1)} %key_hbm.9, bf16[512,1024]{1,0:T(8,128)(2,1)} %value_hbm.9, bf16[3072,256]{1,0:T(8,128)(2,1)} %get-tuple-element.42.first_hbm, ...), custom_call_target="tpu_custom_call" | custom-call | flops 939524096 | bytes 6553600 | tf_op jit(solution)/shard_map/pallas_call | solution.py:360
  47.1 2.3 %all-to-all-done.3.block_ref = bf16[8,128,128]{2,1,0:T(8,128)(2,1)S(1)} async-done(((bf16[8,128,128]{2,1,0:T(8,128)(2,1)}), bf16[8,128,128]{2,1,0:T(8,128)(2,1)S(1)}, u32[]{:S(2)}, u32[]{:S(2)}) %all-to-all-start.3) | async-done | bytes 262176 | tf_op jit(solution)/shard_map/all_to_all | solution.py:400
  49.4 0.8 %shard_map.84 = bf16[8,128,128]{2,1,0:T(8,128)(2,1)} custom-call(bf16[8,128,128]{2,1,0:T(8,128)(2,1)S(1)} %all-to-all-done.3.block_ref), custom_call_target="tpu_custom_call" | custom-call | flops 131072 | bytes 262144 | tf_op jit(solution)/shard_map/pallas_call | solution.py:360
  50.1 4.6 %all-to-all-start.4 = ((bf16[8,128,128]{2,1,0:T(8,128)(2,1)}), bf16[8,128,128]{2,1,0:T(8,128)(2,1)S(1)}, u32[]{:S(2)}, u32[]{:S(2)}) async-start(bf16[8,128,128]{2,1,0:T(8,128)(2,1)} %shard_map.84), calls=%async_computation.4 | async-start | bytes 524288 | tf_op jit(solution)/shard_map/all_to_all | solution.py:400
  54.7 4.5 %shard_map.83 = (bf16[512,1024]{1,0:T(8,128)(2,1)S(1)}, bf16[512,256]{1,0:T(8,128)(2,1)S(1)}, bf16[512,1024]{1,0:T(8,128)(2,1)S(1)}) custom-call(bf16[512,1024]{1,0:T(8,128)(2,1)} %query_hbm.3, bf16[512,1024]{1,0:T(8,128)(2,1)} %value_hbm.9, bf16[3072,256]{1,0:T(8,128)(2,1)} %get-tuple-element.43.second_hbm.weight_hbm, ...), custom_call_target="tpu_custom_call", output_to_operand_aliasing={{0}: (3, {})} | custom-call | flops 1207959552 | bytes 4718592 | tf_op jit(solution)/shard_map/pallas_call | solution.py:360
  59.2 0.8 %all-to-all-done.4 = bf16[8,128,128]{2,1,0:T(8,128)(2,1)S(1)} async-done(((bf16[8,128,128]{2,1,0:T(8,128)(2,1)}), bf16[8,128,128]{2,1,0:T(8,128)(2,1)S(1)}, u32[]{:S(2)}, u32[]{:S(2)}) %all-to-all-start.4) | async-done | bytes 262176 | tf_op jit(solution)/shard_map/all_to_all | solution.py:400
  60.0 2.9 %shard_map.85 = (bf16[512,1024]{1,0:T(8,128)(2,1)}, bf16[512,1024]{1,0:T(8,128)(2,1)}) custom-call(bf16[512,1024]{1,0:T(8,128)(2,1)} %key_hbm.9, bf16[512,1024]{1,0:T(8,128)(2,1)S(1)} %get-tuple-element.50.value_ref, bf16[512,1024]{1,0:T(8,128)(2,1)S(1)} %get-tuple-element.51.key_part, bf16[512,768]{1,0:T(8,128)(2,1)S(1)} %get-tuple-element.52.early_part, ...), custom_call_target="tpu_custom_call" | custom-call | flops 268435456 | bytes 4456448 | tf_op jit(solution)/shard_map/pallas_call | solution.py:360
Async XLA Ops:
  3.1 14.9 %all-to-all-start = ((bf16[8,128,128]{2,1,0:T(8,128)(2,1)}), bf16[8,128,128]{2,1,0:T(8,128)(2,1)S(1)}, u32[]{:S(2)}, u32[]{:S(2)}) async-start(bf16[8,128,128]{2,1,0:T(8,128)(2,1)} %bitcast.10), calls=%async_computation | async-start | bytes 524288 | tf_op jit(solution)/shard_map/all_to_all | solution.py:400
  18.8 9.9 %all-to-all-start.1 = ((bf16[8,128,128]{2,1,0:T(8,128)(2,1)}), bf16[8,128,128]{2,1,0:T(8,128)(2,1)S(1)}, u32[]{:S(2)}, u32[]{:S(2)}) async-start(bf16[8,128,128]{2,1,0:T(8,128)(2,1)} %shard_map.79), calls=%async_computation.1 | async-start | bytes 524288 | tf_op jit(solution)/shard_map/all_to_all | solution.py:400
  23.4 5.3 %copy-start = (f32[1024]{0:T(1024)S(1)}, f32[1024]{0:T(1024)}, u32[]{:S(2)}) copy-start(f32[1024]{0:T(1024)} %param.9) | copy-start | bytes 12292
  36.7 12.7 %all-to-all-start.3 = ((bf16[8,128,128]{2,1,0:T(8,128)(2,1)}), bf16[8,128,128]{2,1,0:T(8,128)(2,1)S(1)}, u32[]{:S(2)}, u32[]{:S(2)}) async-start(bf16[8,128,128]{2,1,0:T(8,128)(2,1)} %bitcast.11), calls=%async_computation.3 | async-start | bytes 524288 | tf_op jit(solution)/shard_map/all_to_all | solution.py:400
  50.1 9.9 %all-to-all-start.4 = ((bf16[8,128,128]{2,1,0:T(8,128)(2,1)}), bf16[8,128,128]{2,1,0:T(8,128)(2,1)S(1)}, u32[]{:S(2)}, u32[]{:S(2)}) async-start(bf16[8,128,128]{2,1,0:T(8,128)(2,1)} %shard_map.84), calls=%async_computation.4 | async-start | bytes 524288 | tf_op jit(solution)/shard_map/all_to_all | solution.py:400

commit v20 on v18

--- a/solution.py
+++ b/solution.py
@@ -177,12 +177,12 @@
 def scan_body(reverse, block_ref, state_hbm, state_ref, sems):
     count = block_ref.shape[0]
     total = jnp.zeros(block_ref.shape[1:], jnp.float32)
-    places = places_in_order(count)
+    owners, back = owner_order(count), return_order(count)
     stores = []
     for place in range(count - 1, -1, -1) if reverse else range(count):
-        rank = places.index(place)
+        rank = back.index(place)
         state_ref[rank] = total.astype(jnp.bfloat16)
-        total = total + block_ref[rank].astype(jnp.float32)
+        total = total + block_ref[owners.index(place)].astype(jnp.float32)
         stores.append(pltpu.make_async_copy(state_ref.at[rank], state_hbm.at[rank], sems.at[rank]))
         stores[-1].start()
     wait_all(stores)
@@ -205,10 +205,10 @@
     return parts[0]
 
 
-def sums_body(gain_ref, flipped_ref, grad_ref, local_ref, state_ref, attended_ref, sums_ref):
+def sums_body(table, gain_ref, flipped_ref, grad_ref, local_ref, state_ref, attended_ref, sums_ref):
     square = cross = jnp.zeros((8, local_ref.shape[1]), jnp.float32)
     for head in heads_of(local_ref):
-        attended = mm_tn(state_ref[head, :], flipped_ref[head, :])
+        attended = mm_tn(state_of(state_ref, head, table), flipped_ref[head, :])
         attended = attended + attended_ref[head, :].astype(jnp.float32)
         attended_ref[head, :] = attended.astype(jnp.bfloat16)
         square += fold(attended * attended)
@@ -251,7 +251,7 @@
 
 
 def query_body(
-    key_hbm, value_hbm, first_hbm, second_hbm, flipped_ref, state_ref, out_hbm, dout_ref, value_out,
+    table, key_hbm, value_hbm, first_hbm, second_hbm, flipped_ref, state_ref, out_hbm, dout_ref, value_out,
     key_ref, value_ref, out_ref, weight_ref, key_sems, value_sems, out_sems, weight_sems,
 ):
     rows = dout_ref.shape[0]
@@ -274,11 +274,12 @@
         value_copies[index].wait()
         for left in range(step.start, step.stop, HEAD_DIM):
             cols = slice(left, left + HEAD_DIM)
+            state = state_of(state_ref, cols, table)
             for start in range(0, rows, BLOCK):
                 end = start + BLOCK
                 dout = dout_ref[start:end, cols]
                 dscore = masked(mm_nt(dout, value_ref[:end, cols]), start, True)
-                grad = mm(dscore, key_ref[:end, cols]) + mm_nt(dout, state_ref[cols, :])
+                grad = mm(dscore, key_ref[:end, cols]) + mm_nt(dout, state)
                 out_ref[start:end, cols] = grad.astype(jnp.bfloat16)
         stores[index].start()
     wait_all(weight_copies)
@@ -319,7 +320,7 @@
 
 
 def final_body(
-    key_hbm, value_ref, key_part, early_part, late_part, state_ref, key_out_hbm, value_out_hbm,
+    table, key_hbm, value_ref, key_part, early_part, late_part, state_ref, key_out_hbm, value_out_hbm,
     key_ref, key_out, value_out, in_sems, key_sems, value_sems,
 ):
     keys = column_copies(key_hbm, key_ref, in_sems)
@@ -329,7 +330,7 @@
     for index, step in enumerate(pieces_of(key_out, COPY_COLS)):
         for left in range(step.start, step.stop, HEAD_DIM):
             cols = slice(left, left + HEAD_DIM)
-            grad = key_part[:, cols].astype(jnp.float32) + mm_nt(value_ref[:, cols], state_ref[cols, :])
+            grad = key_part[:, cols].astype(jnp.float32) + mm_nt(value_ref[:, cols], state_of(state_ref, cols, table))
             key_out[:, cols] = grad.astype(jnp.bfloat16)
         key_stores[index].start()
     for index, step in enumerate(pieces_of(value_out, COPY_COLS)):
@@ -341,7 +342,7 @@
                 part = early_part[:, cols]
             else:
                 part = late_part[:, left - early : left - early + HEAD_DIM]
-            grad = part.astype(jnp.float32) + mm(key_ref[:, cols], state_ref[cols, :])
+            grad = part.astype(jnp.float32) + mm(key_ref[:, cols], state_of(state_ref, cols, table))
             value_out[:, cols] = grad.astype(jnp.bfloat16)
         value_stores[index].start()
     wait_all(key_stores, value_stores)
@@ -382,7 +383,7 @@
     return states
 
 
-def places_in_order(count):
+def owner_order(count):
     quarter = count // 4
     first, second, third, fourth = (list(range(at, at + quarter)) for at in range(0, count, quarter))
     half = quarter // 2
@@ -390,13 +391,30 @@
     return [count - 1 - place for place in order]
 
 
+def return_order(count):
+    return [place ^ 1 for place in owner_order(count)]
+
+
+def piece_table(count):
+    back = return_order(count)
+    return [back.index(place) for place in owner_order(count)]
+
+
+def state_of(state_ref, head, table):
+    size = state_ref.shape[0] // len(table)
+    if size >= HEAD_DIM:
+        at = table[head.start // size] * size + head.start % size
+        return state_ref[at : at + HEAD_DIM, :]
+    pieces = table[head.start // size : head.stop // size]
+    return jnp.concatenate([state_ref[at * size : (at + 1) * size, :] for at in pieces], axis=0)
+
+
 def last_first(count):
     return list(range(count - 1, -1, -1))
 
 
-def exchange(pieces, axis):
-    groups = [places_in_order(lax.axis_size(axis))]
-    return lax.all_to_all(pieces, axis, 0, 0, axis_index_groups=groups)
+def exchange(pieces, axis, order):
+    return lax.all_to_all(pieces, axis, 0, 0, axis_index_groups=[order(lax.axis_size(axis))])
 
 
 def in_pieces(state, axis):
@@ -413,6 +431,7 @@
     small = 2 * rows * width * HEAD_DIM
     large = 2 * rows * rows * width * 3 // 4
     gain_row = gain.reshape(1, width)
+    table = piece_table(lax.axis_size("seq"))
     flat = (width, rows)
     dma = pltpu.SemaphoreType.DMA
     chunks, row_chunks = dma((width // COPY_COLS,)), dma((rows // COPY_ROWS,))
@@ -428,7 +447,7 @@
         [keys, values],
         [rows_vm] * 2 + [vm(state, f32), state_vm] + [row_chunks] * 2 + [state_chunks],
     )
-    kv_blocks = exchange(in_pieces(own_kv, "seq"), "seq")
+    kv_blocks = exchange(in_pieces(own_kv, "seq"), "seq", owner_order)
     half = width // 2 // COPY_COLS * COPY_COLS
     early = width * 3 // 4 // HEAD_DIM * HEAD_DIM
     def weights_of(cols):
@@ -447,7 +466,7 @@
     kv_blocks, flipped, grad_flipped, local, first_weights = lax.optimization_barrier(
         (kv_blocks, flipped, grad_flipped, local, first_weights)
     )
-    kv_low = exchange(scan_blocks(kv_blocks, False), "seq").reshape(state)
+    kv_low = exchange(scan_blocks(kv_blocks, False), "seq", return_order).reshape(state)
     other = width - half
     other_vm, other_chunks = vm((rows, other), bf16), dma((other // COPY_COLS,))
     local, second_weights = local_call(
@@ -462,7 +481,7 @@
     )
     groups = lax.axis_size("head")
     attended, sums = local_call(
-        sums_body,
+        functools.partial(sums_body, table),
         [gain_row, flipped, grad_flipped, local, kv_low],
         [flat_vm, vm((groups, 2, rows), f32)],
         small,
@@ -477,10 +496,10 @@
         scratch=[state_vm, state_chunks],
         aliases={3: 0},
     )
-    grad_blocks = exchange(in_pieces(own_grad, "seq"), "seq")
+    grad_blocks = exchange(in_pieces(own_grad, "seq"), "seq", owner_order)
     early_vm, late_vm = vm((rows, early), bf16), vm((rows, width - early), bf16)
     query_grad, dout, early_part = local_call(
-        query_body,
+        functools.partial(query_body, table),
         [dout_flipped, kv_low],
         [hbm(tokens, bf16), rows_vm, early_vm],
         2 * large + small,
@@ -490,7 +509,7 @@
     grad_blocks, query_grad, dout, early_part = lax.optimization_barrier(
         (grad_blocks, query_grad, dout, early_part)
     )
-    grad_low = exchange(scan_blocks(grad_blocks, True), "seq").reshape(state)
+    grad_low = exchange(scan_blocks(grad_blocks, True), "seq", return_order).reshape(state)
     key_part, late_part, value_kept = local_call(
         inner_body,
         [dout],
@@ -501,7 +520,7 @@
         {3: 0},
     )
     key_grad, value_grad = local_call(
-        final_body,
+        functools.partial(final_body, table),
         [value_kept, key_part, early_part, late_part, grad_low],
         [hbm(tokens, bf16)] * 2,
         2 * small,

time: 63.4 us -> 63.6 us (level)
  waiting for transfers between devices: 3.61 us -> 4.98 us
  starting transfers between devices: 27.2 us -> 26 us
    all_to_all x4, waiting for transfers between devices: 3.61 us -> 4.98 us  [exchange(): lax.all_to_all(pieces, axis, 0, 0, axis_index_groups=[order(lax.axis_size...]
    all_to_all x4, starting transfers between devices: 27.2 us -> 26 us  [exchange(): lax.all_to_all(pieces, axis, 0, 0, axis_index_groups=[order(lax.axis_size...]
where the time goes in v20:
time: 63.6 us; the launch traced here: 62.9 us
  starting transfers between devices  26 us (41%)
  Pallas kernels  25.4 us (40%)
  blocking collectives  5.67 us (9%)
  waiting for transfers between devices  4.98 us (8%)
  between operations  0.87 us (1%)
    all_to_all x4, starting transfers between devices, exchange(): lax.all_to_all(pieces, axis, 0, 0, axis_index_groups=[order(lax.axis_size...  26 us
    pallas_call x10, Pallas kernels, local_call(): pl.pallas_call(body, in_specs=specs, out_specs=out_specs, out_shape=outs,...  25.4 us
    all_to_all x1, blocking collectives, shards(): lax.all_to_all(sums, 'head', 0, 0, axis_index_groups=[last_first(groups)])  5.67 us
    all_to_all x4, waiting for transfers between devices, exchange(): lax.all_to_all(pieces, axis, 0, 0, axis_index_groups=[order(lax.axis_size...  4.98 us
  transfers between devices with their start and end apart: 4, of which 4 were waited for; matrix products, arithmetic and copies ran while one was open for 0% of the time, Pallas kernels for 26%

profile of v20, /device:TPU:0, one launch (start us, length us, event | category | flops | bytes accessed | tf_op | source)
XLA Modules:
  0.0 62.9 jit_solution(4764318846072564698)
XLA Ops:
  0.6 2.5 %shard_map.76 = bf16[1024,128]{1,0:T(8,128)(2,1)} custom-call(bf16[512,1024]{1,0:T(8,128)(2,1)} %key_hbm.9, bf16[512,1024]{1,0:T(8,128)(2,1)} %value_hbm.9), custom_call_target="tpu_custom_call" | custom-call | flops 134217728 | bytes 2097152 | tf_op jit(solution)/shard_map/pallas_call | solution.py:360
  3.1 8.4 %all-to-all-start = ((bf16[8,128,128]{2,1,0:T(8,128)(2,1)}), bf16[8,128,128]{2,1,0:T(8,128)(2,1)S(1)}, u32[]{:S(2)}, u32[]{:S(2)}) async-start(bf16[8,128,128]{2,1,0:T(8,128)(2,1)} %bitcast.10), calls=%async_computation | async-start | bytes 524288 | tf_op jit(solution)/shard_map/all_to_all | solution.py:417
  11.5 3.8 %shard_map.77 = (bf16[1024,512]{1,0:T(8,128)(2,1)S(1)}, bf16[1024,512]{1,0:T(8,128)(2,1)S(1)}, bf16[1024,512]{1,0:T(8,128)(2,1)S(1)}, bf16[3072,256]{1,0:T(8,128)(2,1)}) custom-call(bf16[512,1024]{1,0:T(8,128)(2,1)} %query_hbm.3, bf16[512,1024]{1,0:T(8,128)(2,1)} %key_hbm.9, bf16[512,1024]{1,0:T(8,128)(2,1)} %value_hbm.9, bf16[512,1024]{1,0:T(8,128)(2,1)} %grad_hbm.1), custom_call_target="tpu_custom_call" | custom-call | flops 805306368 | bytes 4194304 | tf_op jit(solution)/shard_map/pallas_call | solution.py:360
  15.3 1.7 %all-to-all-done.block_ref = bf16[8,128,128]{2,1,0:T(8,128)(2,1)S(1)} async-done(((bf16[8,128,128]{2,1,0:T(8,128)(2,1)}), bf16[8,128,128]{2,1,0:T(8,128)(2,1)S(1)}, u32[]{:S(2)}, u32[]{:S(2)}) %all-to-all-start) | async-done | bytes 262176 | tf_op jit(solution)/shard_map/all_to_all | solution.py:417
  17.0 0.8 %shard_map.79 = bf16[8,128,128]{2,1,0:T(8,128)(2,1)} custom-call(bf16[8,128,128]{2,1,0:T(8,128)(2,1)S(1)} %all-to-all-done.block_ref), custom_call_target="tpu_custom_call" | custom-call | flops 131072 | bytes 262144 | tf_op jit(solution)/shard_map/pallas_call | solution.py:360
  17.8 6.1 %all-to-all-start.1 = ((bf16[8,128,128]{2,1,0:T(8,128)(2,1)}), bf16[8,128,128]{2,1,0:T(8,128)(2,1)S(1)}, u32[]{:S(2)}, u32[]{:S(2)}) async-start(bf16[8,128,128]{2,1,0:T(8,128)(2,1)} %shard_map.79), calls=%async_computation.1 | async-start | bytes 524288 | tf_op jit(solution)/shard_map/all_to_all | solution.py:417
  23.9 0.0 copy-start
  23.9 3.3 %shard_map.78 = (bf16[1024,512]{1,0:T(8,128)(2,1)S(1)}, bf16[3072,256]{1,0:T(8,128)(2,1)}) custom-call(bf16[512,1024]{1,0:T(8,128)(2,1)} %key_hbm.9, bf16[512,1024]{1,0:T(8,128)(2,1)} %value_hbm.9, bf16[1024,512]{1,0:T(8,128)(2,1)S(1)} %get-tuple-element.34.flipped_ref, ...), custom_call_target="tpu_custom_call", output_to_operand_aliasing={{0}: (3, {})} | custom-call | flops 402653184 | bytes 4194304 | tf_op jit(solution)/shard_map/pallas_call | solution.py:360
  27.2 1.9 %all-to-all-done.1 = bf16[8,128,128]{2,1,0:T(8,128)(2,1)S(1)} async-done(((bf16[8,128,128]{2,1,0:T(8,128)(2,1)}), bf16[8,128,128]{2,1,0:T(8,128)(2,1)S(1)}, u32[]{:S(2)}, u32[]{:S(2)}) %all-to-all-start.1) | async-done | bytes 262176 | tf_op jit(solution)/shard_map/all_to_all | solution.py:417
  29.2 0.0 copy-done
  29.2 0.8 %shard_map.80 = (bf16[1024,512]{1,0:T(8,128)(2,1)S(1)}, f32[4,2,512]{2,1,0:T(2,128)S(1)}) custom-call(f32[1,1024]{1,0:T(1,128)S(1)} %bitcast.8, bf16[1024,512]{1,0:T(8,128)(2,1)S(1)} %get-tuple-element.34.flipped_ref, bf16[1024,512]{1,0:T(8,128)(2,1)S(1)} %get-tuple-element.35.grad_ref, ...), custom_call_target="tpu_custom_call", output_to_operand_aliasing={{0}: (3, {})} | custom-call | flops 134217728 | bytes 3411968 | tf_op jit(solution)/shard_map/pallas_call | solution.py:360
  30.0 5.7 %all_to_all.25.sums_ref = f32[4,2,512]{2,1,0:T(2,128)S(1)} all-to-all(f32[4,2,512]{2,1,0:T(2,128)S(1)} %get-tuple-element.40), channel_id=1, replica_groups={{3,2,1,0},{7,6,5,4},{11,10,9,8},{15,14,13,12},{19,18,17,16},{23,22,21,2..., dimensions={0} | all-to-all | bytes 32768 | tf_op jit(solution)/shard_map/all_to_all | solution.py:490
  35.7 1.5 %shard_map.81 = (bf16[1024,512]{1,0:T(8,128)(2,1)S(1)}, bf16[1024,128]{1,0:T(8,128)(2,1)}) custom-call(f32[1,1024]{1,0:T(1,128)S(1)} %bitcast.9, bf16[1024,512]{1,0:T(8,128)(2,1)S(1)} %get-tuple-element.34.flipped_ref, bf16[1024,512]{1,0:T(8,128)(2,1)S(1)} %get-tuple-element.35.grad_ref, ...), custom_call_target="tpu_custom_call", output_to_operand_aliasing={{0}: (3, {})} | custom-call | flops 134217728 | bytes 3166208 | tf_op jit(solution)/shard_map/pallas_call | solution.py:360
  37.1 5.6 %all-to-all-start.3 = ((bf16[8,128,128]{2,1,0:T(8,128)(2,1)}), bf16[8,128,128]{2,1,0:T(8,128)(2,1)S(1)}, u32[]{:S(2)}, u32[]{:S(2)}) async-start(bf16[8,128,128]{2,1,0:T(8,128)(2,1)} %bitcast.11), calls=%async_computation.3 | async-start | bytes 524288 | tf_op jit(solution)/shard_map/all_to_all | solution.py:417
  42.7 4.9 %shard_map.82 = (bf16[512,1024]{1,0:T(8,128)(2,1)}, bf16[512,1024]{1,0:T(8,128)(2,1)S(1)}, bf16[512,768]{1,0:T(8,128)(2,1)S(1)}) custom-call(bf16[512,1024]{1,0:T(8,128)(2,1)} %key_hbm.9, bf16[512,1024]{1,0:T(8,128)(2,1)} %value_hbm.9, bf16[3072,256]{1,0:T(8,128)(2,1)} %get-tuple-element.42.first_hbm, ...), custom_call_target="tpu_custom_call" | custom-call | flops 939524096 | bytes 6553600 | tf_op jit(solution)/shard_map/pallas_call | solution.py:360
  47.6 0.5 all-to-all-done.3.block_ref
  48.2 0.8 %shard_map.84 = bf16[8,128,128]{2,1,0:T(8,128)(2,1)} custom-call(bf16[8,128,128]{2,1,0:T(8,128)(2,1)S(1)} %all-to-all-done.3.block_ref), custom_call_target="tpu_custom_call" | custom-call | flops 131072 | bytes 262144 | tf_op jit(solution)/shard_map/pallas_call | solution.py:360
  49.0 6.1 %all-to-all-start.4 = ((bf16[8,128,128]{2,1,0:T(8,128)(2,1)}), bf16[8,128,128]{2,1,0:T(8,128)(2,1)S(1)}, u32[]{:S(2)}, u32[]{:S(2)}) async-start(bf16[8,128,128]{2,1,0:T(8,128)(2,1)} %shard_map.84), calls=%async_computation.4 | async-start | bytes 524288 | tf_op jit(solution)/shard_map/all_to_all | solution.py:417
  55.0 4.5 %shard_map.83 = (bf16[512,1024]{1,0:T(8,128)(2,1)S(1)}, bf16[512,256]{1,0:T(8,128)(2,1)S(1)}, bf16[512,1024]{1,0:T(8,128)(2,1)S(1)}) custom-call(bf16[512,1024]{1,0:T(8,128)(2,1)} %query_hbm.3, bf16[512,1024]{1,0:T(8,128)(2,1)} %value_hbm.9, bf16[3072,256]{1,0:T(8,128)(2,1)} %get-tuple-element.43.second_hbm.weight_hbm, ...), custom_call_target="tpu_custom_call", output_to_operand_aliasing={{0}: (3, {})} | custom-call | flops 1207959552 | bytes 4718592 | tf_op jit(solution)/shard_map/pallas_call | solution.py:360
  59.5 0.8 %all-to-all-done.4 = bf16[8,128,128]{2,1,0:T(8,128)(2,1)S(1)} async-done(((bf16[8,128,128]{2,1,0:T(8,128)(2,1)}), bf16[8,128,128]{2,1,0:T(8,128)(2,1)S(1)}, u32[]{:S(2)}, u32[]{:S(2)}) %all-to-all-start.4) | async-done | bytes 262176 | tf_op jit(solution)/shard_map/all_to_all | solution.py:417
  60.3 2.5 %shard_map.85 = (bf16[512,1024]{1,0:T(8,128)(2,1)}, bf16[512,1024]{1,0:T(8,128)(2,1)}) custom-call(bf16[512,1024]{1,0:T(8,128)(2,1)} %key_hbm.9, bf16[512,1024]{1,0:T(8,128)(2,1)S(1)} %get-tuple-element.50.value_ref, bf16[512,1024]{1,0:T(8,128)(2,1)S(1)} %get-tuple-element.51.key_part, bf16[512,768]{1,0:T(8,128)(2,1)S(1)} %get-tuple-element.52.early_part, ...), custom_call_target="tpu_custom_call" | custom-call | flops 268435456 | bytes 4456448 | tf_op jit(solution)/shard_map/pallas_call | solution.py:360
Async XLA Ops:
  3.1 13.9 %all-to-all-start = ((bf16[8,128,128]{2,1,0:T(8,128)(2,1)}), bf16[8,128,128]{2,1,0:T(8,128)(2,1)S(1)}, u32[]{:S(2)}, u32[]{:S(2)}) async-start(bf16[8,128,128]{2,1,0:T(8,128)(2,1)} %bitcast.10), calls=%async_computation | async-start | bytes 524288 | tf_op jit(solution)/shard_map/all_to_all | solution.py:417
  17.8 11.3 %all-to-all-start.1 = ((bf16[8,128,128]{2,1,0:T(8,128)(2,1)}), bf16[8,128,128]{2,1,0:T(8,128)(2,1)S(1)}, u32[]{:S(2)}, u32[]{:S(2)}) async-start(bf16[8,128,128]{2,1,0:T(8,128)(2,1)} %shard_map.79), calls=%async_computation.1 | async-start | bytes 524288 | tf_op jit(solution)/shard_map/all_to_all | solution.py:417
  23.9 5.3 %copy-start = (f32[1024]{0:T(1024)S(1)}, f32[1024]{0:T(1024)}, u32[]{:S(2)}) copy-start(f32[1024]{0:T(1024)} %param.9) | copy-start | bytes 12292
  37.1 11.0 %all-to-all-start.3 = ((bf16[8,128,128]{2,1,0:T(8,128)(2,1)}), bf16[8,128,128]{2,1,0:T(8,128)(2,1)S(1)}, u32[]{:S(2)}, u32[]{:S(2)}) async-start(bf16[8,128,128]{2,1,0:T(8,128)(2,1)} %bitcast.11), calls=%async_computation.3 | async-start | bytes 524288 | tf_op jit(solution)/shard_map/all_to_all | solution.py:417
  49.0 11.3 %all-to-all-start.4 = ((bf16[8,128,128]{2,1,0:T(8,128)(2,1)}), bf16[8,128,128]{2,1,0:T(8,128)(2,1)S(1)}, u32[]{:S(2)}, u32[]{:S(2)}) async-start(bf16[8,128,128]{2,1,0:T(8,128)(2,1)} %shard_map.84), calls=%async_computation.4 | async-start | bytes 524288 | tf_op jit(solution)/shard_map/all_to_all | solution.py:417

commit v21 on v18

--- a/solution.py
+++ b/solution.py
@@ -220,10 +220,35 @@
         sums_ref[group, 1:2, :] = cross
 
 
+def query_part(dout, key_ref, value_ref, own, state, out_ref):
+    for start in range(0, dout.shape[0], BLOCK):
+        end = start + BLOCK
+        block = dout[start:end, :]
+        dscore = masked(mm_nt(block, value_ref[:end, own]), start, True)
+        grad = mm(dscore, key_ref[:end, own]) + mm_nt(block, state)
+        out_ref[start:end, own] = grad.astype(jnp.bfloat16)
+
+
+def on_odd_place():
+    return lax.axis_index("head") % 2 == 1
+
+
 def dout_body(
-    width, gain_ref, flipped_ref, grad_ref, attended_ref, sums_ref, dout_ref, own_hbm, own_ref, sems
-):
-    stores = row_copies(own_ref, own_hbm, STATE_ROWS, sems)
+    width, key_hbm, value_hbm, gain_ref, flipped_ref, grad_ref, attended_ref, sums_ref, state_ref,
+    dout_ref, own_hbm, out_hbm, own_ref, key_ref, value_ref, out_ref, own_sems, sems,
+):
+    odd = on_odd_place()
+    part = slice(0, key_ref.shape[1])
+    stores = row_copies(own_ref, own_hbm, STATE_ROWS, own_sems)
+    key_copy = pltpu.make_async_copy(key_hbm.at[:, part], key_ref, sems.at[0])
+    value_copy = pltpu.make_async_copy(value_hbm.at[:, part], value_ref, sems.at[1])
+    out_copy = pltpu.make_async_copy(out_ref, out_hbm.at[:, part], sems.at[2])
+
+    @pl.when(odd)
+    def _():
+        key_copy.start()
+        value_copy.start()
+
     sums = sum(sums_ref[group] for group in range(sums_ref.shape[0]))
     inverse = 1.0 / jnp.sqrt(sums[0:1, :] / width + EPSILON)
     drop = sums[1:2, :] * (inverse * inverse * inverse) / width
@@ -235,6 +260,16 @@
         own_ref[head, :] = mm_nt(flipped_ref[head, :], dout).astype(jnp.bfloat16)
         if head.stop % STATE_ROWS == 0:
             stores[head.stop // STATE_ROWS - 1].start()
+
+    @pl.when(odd)
+    def _():
+        key_copy.wait()
+        value_copy.wait()
+        for own in pieces_of(key_ref, HEAD_DIM):
+            query_part(dout_ref[own, :].T, key_ref, value_ref, own, state_ref[own, :], out_ref)
+        out_copy.start()
+        out_copy.wait()
+
     wait_all(stores)
 
 
@@ -251,11 +286,12 @@
 
 
 def query_body(
-    key_hbm, value_hbm, first_hbm, second_hbm, flipped_ref, state_ref, out_hbm, dout_ref, value_out,
+    key_hbm, value_hbm, first_hbm, second_hbm, given_hbm, flipped_ref, state_ref,
+    out_hbm, dout_ref, value_out,
     key_ref, value_ref, out_ref, weight_ref, key_sems, value_sems, out_sems, weight_sems,
 ):
-    rows = dout_ref.shape[0]
-    size = weight_rows(rows)
+    even = jnp.logical_not(on_odd_place())
+    size = weight_rows(dout_ref.shape[0])
     key_copies = column_copies(key_hbm, key_ref, key_sems)
     value_copies = column_copies(value_hbm, value_ref, value_sems)
     there = first_hbm.shape[0]
@@ -264,27 +300,36 @@
         pltpu.make_async_copy(first_hbm, weight_ref.at[:there, :], weight_sems.at[0]),
         pltpu.make_async_copy(second_hbm.at[:rest, :], weight_ref.at[there:, :], weight_sems.at[1]),
     ]
-    start_all(key_copies, value_copies)
+
+    @pl.when(even)
+    def _():
+        key_copies[0].start()
+        value_copies[0].start()
+
+    start_all(key_copies[1:], value_copies[1:])
     start_all(weight_copies)
     for head in heads_of(flipped_ref):
         dout_ref[:, head] = flipped_ref[head, :].T
     stores = column_copies(out_ref, out_hbm, out_sems)
-    for index, step in enumerate(pieces_of(out_ref, COPY_COLS)):
+
+    def one(index, step):
         key_copies[index].wait()
         value_copies[index].wait()
         for left in range(step.start, step.stop, HEAD_DIM):
             cols = slice(left, left + HEAD_DIM)
-            for start in range(0, rows, BLOCK):
-                end = start + BLOCK
-                dout = dout_ref[start:end, cols]
-                dscore = masked(mm_nt(dout, value_ref[:end, cols]), start, True)
-                grad = mm(dscore, key_ref[:end, cols]) + mm_nt(dout, state_ref[cols, :])
-                out_ref[start:end, cols] = grad.astype(jnp.bfloat16)
+            query_part(dout_ref[:, cols], key_ref, value_ref, cols, state_ref[cols, :], out_ref)
         stores[index].start()
+
+    for index, step in enumerate(pieces_of(out_ref, COPY_COLS)):
+        if index:
+            one(index, step)
+        else:
+            pl.when(even)(functools.partial(one, index, step))
     wait_all(weight_copies)
     for number, cols in enumerate(pieces_of(value_out, HEAD_DIM)):
         value_local(weight_ref, number * size, dout_ref[:, cols], value_out.at[:, cols])
-    wait_all(stores)
+    pl.when(even)(stores[0].wait)
+    wait_all(stores[1:])
 
 
 def inner_body(
@@ -387,7 +432,7 @@
     first, second, third, fourth = (list(range(at, at + quarter)) for at in range(0, count, quarter))
     half = quarter // 2
     order = second + first[:half] + third[:half] + first[half:] + third[half:] + fourth
-    return [count - 1 - place for place in order]
+    return [(count - 1 - place) ^ 1 for place in order]
 
 
 def last_first(count):
@@ -469,13 +514,15 @@
         aliases={3: 0},
     )
     sums = lax.all_to_all(sums, "head", 0, 0, axis_index_groups=[last_first(groups)])
-    dout_flipped, own_grad = local_call(
+    part_vm = vm((rows, COPY_COLS), bf16)
+    dout_flipped, own_grad, query_grad = local_call(
         functools.partial(dout_body, total_width),
-        [gain_row, flipped, grad_flipped, attended, sums],
-        [flat_vm, hbm(state, bf16)],
-        small,
-        scratch=[state_vm, state_chunks],
-        aliases={3: 0},
+        [gain_row, flipped, grad_flipped, attended, sums, kv_low],
+        [flat_vm, hbm(state, bf16), hbm(tokens, bf16)],
+        2 * small,
+        [keys, values],
+        [state_vm] + [part_vm] * 3 + [state_chunks, dma((3,))],
+        {5: 0},
     )
     grad_blocks = exchange(in_pieces(own_grad, "seq"), "seq")
     early_vm, late_vm = vm((rows, early), bf16), vm((rows, width - early), bf16)
@@ -484,8 +531,9 @@
         [dout_flipped, kv_low],
         [hbm(tokens, bf16), rows_vm, early_vm],
         2 * large + small,
-        [keys, values, first_weights, second_weights],
+        [keys, values, first_weights, second_weights, query_grad],
         [rows_vm] * 3 + [vm(weights_of(early), bf16)] + [chunks] * 3 + [dma((2,))],
+        {4: 0},
     )
     grad_blocks, query_grad, dout, early_part = lax.optimization_barrier(
         (grad_blocks, query_grad, dout, early_part)

time: 63.4 us -> 64.9 us (1.024)
  the two profiles are of different devices: /device:TPU:0 before, /device:TPU:1 now
where the time goes in v21:
time: 64.9 us; the launch traced here: 64.2 us
  Pallas kernels  27.2 us (42%)
  starting transfers between devices  20.8 us (32%)
  blocking collectives  8.84 us (14%)
  waiting for transfers between devices  6.56 us (10%)
  between operations  0.87 us (1%)
    pallas_call x10, Pallas kernels, local_call(): pl.pallas_call(body, in_specs=specs, out_specs=out_specs, out_shape=outs,...  27.2 us
    all_to_all x4, starting transfers between devices, exchange(): return lax.all_to_all(pieces, axis, 0, 0, axis_index_groups=groups)  20.8 us
    all_to_all x1, blocking collectives, shards(): lax.all_to_all(sums, 'head', 0, 0, axis_index_groups=[last_first(groups)])  8.84 us
    all_to_all x4, waiting for transfers between devices, exchange(): return lax.all_to_all(pieces, axis, 0, 0, axis_index_groups=groups)  6.56 us
  transfers between devices with their start and end apart: 4, of which 4 were waited for; matrix products, arithmetic and copies ran while one was open for 0% of the time, Pallas kernels for 24%

profile of v21, /device:TPU:1, one launch (start us, length us, event | category | flops | bytes accessed | tf_op | source)
XLA Modules:
  0.0 64.2 jit_solution(12909707999325388929)
XLA Ops:
  0.6 2.5 %shard_map.76 = bf16[1024,128]{1,0:T(8,128)(2,1)} custom-call(bf16[512,1024]{1,0:T(8,128)(2,1)} %key_hbm.11, bf16[512,1024]{1,0:T(8,128)(2,1)} %value_hbm.11), custom_call_target="tpu_custom_call" | custom-call | flops 134217728 | bytes 2097152 | tf_op jit(solution)/shard_map/pallas_call | solution.py:404
  3.1 6.7 %all-to-all-start = ((bf16[8,128,128]{2,1,0:T(8,128)(2,1)}), bf16[8,128,128]{2,1,0:T(8,128)(2,1)S(1)}, u32[]{:S(2)}, u32[]{:S(2)}) async-start(bf16[8,128,128]{2,1,0:T(8,128)(2,1)} %bitcast.11), calls=%async_computation | async-start | bytes 524288 | tf_op jit(solution)/shard_map/all_to_all | solution.py:444
  9.8 3.8 %shard_map.77 = (bf16[1024,512]{1,0:T(8,128)(2,1)S(1)}, bf16[1024,512]{1,0:T(8,128)(2,1)S(1)}, bf16[1024,512]{1,0:T(8,128)(2,1)S(1)}, bf16[3072,256]{1,0:T(8,128)(2,1)}) custom-call(bf16[512,1024]{1,0:T(8,128)(2,1)} %query_hbm.3, bf16[512,1024]{1,0:T(8,128)(2,1)} %key_hbm.11, bf16[512,1024]{1,0:T(8,128)(2,1)} %value_hbm.11, bf16[512,1024]{1,0:T(8,128)(2,1)} %grad_hbm.1), custom_call_target="tpu_custom_call" | custom-call | flops 805306368 | bytes 4194304 | tf_op jit(solution)/shard_map/pallas_call | solution.py:404
  13.6 1.2 %all-to-all-done.block_ref = bf16[8,128,128]{2,1,0:T(8,128)(2,1)S(1)} async-done(((bf16[8,128,128]{2,1,0:T(8,128)(2,1)}), bf16[8,128,128]{2,1,0:T(8,128)(2,1)S(1)}, u32[]{:S(2)}, u32[]{:S(2)}) %all-to-all-start) | async-done | bytes 262176 | tf_op jit(solution)/shard_map/all_to_all | solution.py:444
  14.9 0.8 %shard_map.79 = bf16[8,128,128]{2,1,0:T(8,128)(2,1)} custom-call(bf16[8,128,128]{2,1,0:T(8,128)(2,1)S(1)} %all-to-all-done.block_ref), custom_call_target="tpu_custom_call" | custom-call | flops 131072 | bytes 262144 | tf_op jit(solution)/shard_map/pallas_call | solution.py:404
  15.7 4.7 %all-to-all-start.1 = ((bf16[8,128,128]{2,1,0:T(8,128)(2,1)}), bf16[8,128,128]{2,1,0:T(8,128)(2,1)S(1)}, u32[]{:S(2)}, u32[]{:S(2)}) async-start(bf16[8,128,128]{2,1,0:T(8,128)(2,1)} %shard_map.79), calls=%async_computation.1 | async-start | bytes 524288 | tf_op jit(solution)/shard_map/all_to_all | solution.py:444
  20.4 0.0 copy-start
  20.4 3.3 %shard_map.78 = (bf16[1024,512]{1,0:T(8,128)(2,1)S(1)}, bf16[3072,256]{1,0:T(8,128)(2,1)}) custom-call(bf16[512,1024]{1,0:T(8,128)(2,1)} %key_hbm.11, bf16[512,1024]{1,0:T(8,128)(2,1)} %value_hbm.11, bf16[1024,512]{1,0:T(8,128)(2,1)S(1)} %get-tuple-element.35.flipped_ref, ...), custom_call_target="tpu_custom_call", output_to_operand_aliasing={{0}: (3, {})} | custom-call | flops 402653184 | bytes 4194304 | tf_op jit(solution)/shard_map/pallas_call | solution.py:404
  23.8 1.1 %all-to-all-done.1 = bf16[8,128,128]{2,1,0:T(8,128)(2,1)S(1)} async-done(((bf16[8,128,128]{2,1,0:T(8,128)(2,1)}), bf16[8,128,128]{2,1,0:T(8,128)(2,1)S(1)}, u32[]{:S(2)}, u32[]{:S(2)}) %all-to-all-start.1) | async-done | bytes 262176 | tf_op jit(solution)/shard_map/all_to_all | solution.py:444
  24.9 0.0 copy-done
  24.9 0.8 %shard_map.80 = (bf16[1024,512]{1,0:T(8,128)(2,1)S(1)}, f32[4,2,512]{2,1,0:T(2,128)S(1)}) custom-call(f32[1,1024]{1,0:T(1,128)S(1)} %bitcast.9, bf16[1024,512]{1,0:T(8,128)(2,1)S(1)} %get-tuple-element.35.flipped_ref, bf16[1024,512]{1,0:T(8,128)(2,1)S(1)} %get-tuple-element.36.grad_ref, ...), custom_call_target="tpu_custom_call", output_to_operand_aliasing={{0}: (3, {})} | custom-call | flops 134217728 | bytes 3411968 | tf_op jit(solution)/shard_map/pallas_call | solution.py:404
  25.7 8.8 %all_to_all.25.sums_ref = f32[4,2,512]{2,1,0:T(2,128)S(1)} all-to-all(f32[4,2,512]{2,1,0:T(2,128)S(1)} %get-tuple-element.41), channel_id=1, replica_groups={{3,2,1,0},{7,6,5,4},{11,10,9,8},{15,14,13,12},{19,18,17,16},{23,22,21,2..., dimensions={0} | all-to-all | bytes 32768 | tf_op jit(solution)/shard_map/all_to_all | solution.py:516
  34.5 4.2 %shard_map.81 = (bf16[1024,512]{1,0:T(8,128)(2,1)S(1)}, bf16[1024,128]{1,0:T(8,128)(2,1)}, bf16[512,1024]{1,0:T(8,128)(2,1)}) custom-call(bf16[512,1024]{1,0:T(8,128)(2,1)} %key_hbm.11, bf16[512,1024]{1,0:T(8,128)(2,1)} %value_hbm.11, f32[1,1024]{1,0:T(1,128)S(1)} %bitcast.10, ...), custom_call_target="tpu_custom_call", output_to_operand_aliasing={{0}: (5, {})} | custom-call | flops 268435456 | bytes 5525504 | tf_op jit(solution)/shard_map/pallas_call | solution.py:404
  38.7 5.2 %all-to-all-start.3 = ((bf16[8,128,128]{2,1,0:T(8,128)(2,1)}), bf16[8,128,128]{2,1,0:T(8,128)(2,1)S(1)}, u32[]{:S(2)}, u32[]{:S(2)}) async-start(bf16[8,128,128]{2,1,0:T(8,128)(2,1)} %bitcast.12), calls=%async_computation.3 | async-start | bytes 524288 | tf_op jit(solution)/shard_map/all_to_all | solution.py:444
  43.9 4.0 %shard_map.82 = (bf16[512,1024]{1,0:T(8,128)(2,1)}, bf16[512,1024]{1,0:T(8,128)(2,1)S(1)}, bf16[512,768]{1,0:T(8,128)(2,1)S(1)}) custom-call(bf16[512,1024]{1,0:T(8,128)(2,1)} %key_hbm.11, bf16[512,1024]{1,0:T(8,128)(2,1)} %value_hbm.11, bf16[3072,256]{1,0:T(8,128)(2,1)} %get-tuple-element.43.first_hbm, ...), custom_call_target="tpu_custom_call", output_to_operand_aliasing={{0}: (4, {})} | custom-call | flops 939524096 | bytes 7602176 | tf_op jit(solution)/shard_map/pallas_call | solution.py:404
  47.9 2.1 %all-to-all-done.3.block_ref = bf16[8,128,128]{2,1,0:T(8,128)(2,1)S(1)} async-done(((bf16[8,128,128]{2,1,0:T(8,128)(2,1)}), bf16[8,128,128]{2,1,0:T(8,128)(2,1)S(1)}, u32[]{:S(2)}, u32[]{:S(2)}) %all-to-all-start.3) | async-done | bytes 262176 | tf_op jit(solution)/shard_map/all_to_all | solution.py:444
  49.9 0.8 %shard_map.84 = bf16[8,128,128]{2,1,0:T(8,128)(2,1)} custom-call(bf16[8,128,128]{2,1,0:T(8,128)(2,1)S(1)} %all-to-all-done.3.block_ref), custom_call_target="tpu_custom_call" | custom-call | flops 131072 | bytes 262144 | tf_op jit(solution)/shard_map/pallas_call | solution.py:404
  50.7 4.2 %all-to-all-start.4 = ((bf16[8,128,128]{2,1,0:T(8,128)(2,1)}), bf16[8,128,128]{2,1,0:T(8,128)(2,1)S(1)}, u32[]{:S(2)}, u32[]{:S(2)}) async-start(bf16[8,128,128]{2,1,0:T(8,128)(2,1)} %shard_map.84), calls=%async_computation.4 | async-start | bytes 524288 | tf_op jit(solution)/shard_map/all_to_all | solution.py:444
  54.9 4.5 %shard_map.83 = (bf16[512,1024]{1,0:T(8,128)(2,1)S(1)}, bf16[512,256]{1,0:T(8,128)(2,1)S(1)}, bf16[512,1024]{1,0:T(8,128)(2,1)S(1)}) custom-call(bf16[512,1024]{1,0:T(8,128)(2,1)} %query_hbm.3, bf16[512,1024]{1,0:T(8,128)(2,1)} %value_hbm.11, bf16[3072,256]{1,0:T(8,128)(2,1)} %get-tuple-element.44.second_hbm.weight_hbm, ...), custom_call_target="tpu_custom_call", output_to_operand_aliasing={{0}: (3, {})} | custom-call | flops 1207959552 | bytes 4718592 | tf_op jit(solution)/shard_map/pallas_call | solution.py:404
  59.5 2.2 %all-to-all-done.4 = bf16[8,128,128]{2,1,0:T(8,128)(2,1)S(1)} async-done(((bf16[8,128,128]{2,1,0:T(8,128)(2,1)}), bf16[8,128,128]{2,1,0:T(8,128)(2,1)S(1)}, u32[]{:S(2)}, u32[]{:S(2)}) %all-to-all-start.4) | async-done | bytes 262176 | tf_op jit(solution)/shard_map/all_to_all | solution.py:444
  61.6 2.5 %shard_map.85 = (bf16[512,1024]{1,0:T(8,128)(2,1)}, bf16[512,1024]{1,0:T(8,128)(2,1)}) custom-call(bf16[512,1024]{1,0:T(8,128)(2,1)} %key_hbm.11, bf16[512,1024]{1,0:T(8,128)(2,1)S(1)} %get-tuple-element.52.value_ref, bf16[512,1024]{1,0:T(8,128)(2,1)S(1)} %get-tuple-element.53.key_part, bf16[512,768]{1,0:T(8,128)(2,1)S(1)} %get-tuple-element.54.early_part, ...), custom_call_target="tpu_custom_call" | custom-call | flops 268435456 | bytes 4456448 | tf_op jit(solution)/shard_map/pallas_call | solution.py:404
Async XLA Ops:
  3.1 11.8 %all-to-all-start = ((bf16[8,128,128]{2,1,0:T(8,128)(2,1)}), bf16[8,128,128]{2,1,0:T(8,128)(2,1)S(1)}, u32[]{:S(2)}, u32[]{:S(2)}) async-start(bf16[8,128,128]{2,1,0:T(8,128)(2,1)} %bitcast.11), calls=%async_computation | async-start | bytes 524288 | tf_op jit(solution)/shard_map/all_to_all | solution.py:444
  15.7 9.2 %all-to-all-start.1 = ((bf16[8,128,128]{2,1,0:T(8,128)(2,1)}), bf16[8,128,128]{2,1,0:T(8,128)(2,1)S(1)}, u32[]{:S(2)}, u32[]{:S(2)}) async-start(bf16[8,128,128]{2,1,0:T(8,128)(2,1)} %shard_map.79), calls=%async_computation.1 | async-start | bytes 524288 | tf_op jit(solution)/shard_map/all_to_all | solution.py:444
  20.4 4.5 %copy-start = (f32[1024]{0:T(1024)S(1)}, f32[1024]{0:T(1024)}, u32[]{:S(2)}) copy-start(f32[1024]{0:T(1024)} %param.9) | copy-start | bytes 12292
  38.7 11.2 %all-to-all-start.3 = ((bf16[8,128,128]{2,1,0:T(8,128)(2,1)}), bf16[8,128,128]{2,1,0:T(8,128)(2,1)S(1)}, u32[]{:S(2)}, u32[]{:S(2)}) async-start(bf16[8,128,128]{2,1,0:T(8,128)(2,1)} %bitcast.12), calls=%async_computation.3 | async-start | bytes 524288 | tf_op jit(solution)/shard_map/all_to_all | solution.py:444
  50.7 10.9 %all-to-all-start.4 = ((bf16[8,128,128]{2,1,0:T(8,128)(2,1)}), bf16[8,128,128]{2,1,0:T(8,128)(2,1)S(1)}, u32[]{:S(2)}, u32[]{:S(2)}) async-start(bf16[8,128,128]{2,1,0:T(8,128)(2,1)} %shard_map.84), calls=%async_computation.4 | async-start | bytes 524288 | tf_op jit(solution)/shard_map/all_to_all | solution.py:444

commit v22 on v18

--- a/solution.py
+++ b/solution.py
@@ -174,7 +174,11 @@
     wait_all(stores)
 
 
-def scan_body(reverse, block_ref, state_hbm, state_ref, sems):
+def on_odd_place():
+    return lax.axis_index("head") % 2 == 1
+
+
+def scan_ranks(reverse, block_ref, state_hbm, state_ref, sems):
     count = block_ref.shape[0]
     total = jnp.zeros(block_ref.shape[1:], jnp.float32)
     places = places_in_order(count)
@@ -186,6 +190,18 @@
         stores.append(pltpu.make_async_copy(state_ref.at[rank], state_hbm.at[rank], sems.at[rank]))
         stores[-1].start()
     wait_all(stores)
+
+
+def scan_body(reverse, block_ref, state_hbm, state_ref, sems):
+    odd = on_odd_place()
+
+    @pl.when(odd)
+    def _():
+        scan_ranks(not reverse, block_ref, state_hbm, state_ref, sems)
+
+    @pl.when(jnp.logical_not(odd))
+    def _():
+        scan_ranks(reverse, block_ref, state_hbm, state_ref, sems)
 
 
 def heads_of(ref):
@@ -394,9 +410,15 @@
     return list(range(count - 1, -1, -1))
 
 
-def exchange(pieces, axis):
-    groups = [places_in_order(lax.axis_size(axis))]
-    return lax.all_to_all(pieces, axis, 0, 0, axis_index_groups=groups)
+def exchange(pieces):
+    count, heads = lax.axis_size("seq"), lax.axis_size("head")
+    groups = []
+    for head in range(heads):
+        places = places_in_order(count)
+        if head % 2:
+            places = [count - 1 - place for place in places]
+        groups.append([place * heads + head for place in places])
+    return lax.all_to_all(pieces, ("seq", "head"), 0, 0, axis_index_groups=groups)
 
 
 def in_pieces(state, axis):
@@ -428,7 +450,7 @@
         [keys, values],
         [rows_vm] * 2 + [vm(state, f32), state_vm] + [row_chunks] * 2 + [state_chunks],
     )
-    kv_blocks = exchange(in_pieces(own_kv, "seq"), "seq")
+    kv_blocks = exchange(in_pieces(own_kv, "seq"))
     half = width // 2 // COPY_COLS * COPY_COLS
     early = width * 3 // 4 // HEAD_DIM * HEAD_DIM
     def weights_of(cols):
@@ -447,7 +469,7 @@
     kv_blocks, flipped, grad_flipped, local, first_weights = lax.optimization_barrier(
         (kv_blocks, flipped, grad_flipped, local, first_weights)
     )
-    kv_low = exchange(scan_blocks(kv_blocks, False), "seq").reshape(state)
+    kv_low = exchange(scan_blocks(kv_blocks, False)).reshape(state)
     other = width - half
     other_vm, other_chunks = vm((rows, other), bf16), dma((other // COPY_COLS,))
     local, second_weights = local_call(
@@ -477,7 +499,7 @@
         scratch=[state_vm, state_chunks],
         aliases={3: 0},
     )
-    grad_blocks = exchange(in_pieces(own_grad, "seq"), "seq")
+    grad_blocks = exchange(in_pieces(own_grad, "seq"))
     early_vm, late_vm = vm((rows, early), bf16), vm((rows, width - early), bf16)
     query_grad, dout, early_part = local_call(
         query_body,
@@ -490,7 +512,7 @@
     grad_blocks, query_grad, dout, early_part = lax.optimization_barrier(
         (grad_blocks, query_grad, dout, early_part)
     )
-    grad_low = exchange(scan_blocks(grad_blocks, True), "seq").reshape(state)
+    grad_low = exchange(scan_blocks(grad_blocks, True)).reshape(state)
     key_part, late_part, value_kept = local_call(
         inner_body,
         [dout],

time: 63.4 us -> 66 us (1.041)
  waiting for transfers between devices: 3.61 us -> 6.89 us
  starting transfers between devices: 27.2 us -> 26.4 us
    all_to_all x4, waiting for transfers between devices: 3.61 us -> 6.89 us  [exchange(): lax.all_to_all(pieces, ('seq', 'head'), 0, 0, axis_index_groups=groups)]
    all_to_all x4, starting transfers between devices: 27.2 us -> 26.4 us  [exchange(): lax.all_to_all(pieces, ('seq', 'head'), 0, 0, axis_index_groups=groups)]
  transfers between devices with their start and end apart: 4 -> 4, of which waited for: 4 -> 4; matrix products, arithmetic and copies ran while one was open for 0% -> 0% of each run, Pallas kernels for 26% -> 25%
where the time goes in v22:
time: 66 us; the launch traced here: 65.3 us
  starting transfers between devices  26.4 us (40%)
  Pallas kernels  25.4 us (38%)
  waiting for transfers between devices  6.89 us (10%)
  blocking collectives  5.68 us (9%)
  between operations  0.87 us (1%)
    all_to_all x4, starting transfers between devices, exchange(): lax.all_to_all(pieces, ('seq', 'head'), 0, 0, axis_index_groups=groups)  26.4 us
    pallas_call x10, Pallas kernels, local_call(): pl.pallas_call(body, in_specs=specs, out_specs=out_specs, out_shape=outs,...  25.4 us
    all_to_all x4, waiting for transfers between devices, exchange(): lax.all_to_all(pieces, ('seq', 'head'), 0, 0, axis_index_groups=groups)  6.89 us
    all_to_all x1, blocking collectives, shards(): lax.all_to_all(sums, 'head', 0, 0, axis_index_groups=[last_first(groups)])  5.68 us
  transfers between devices with their start and end apart: 4, of which 4 were waited for; matrix products, arithmetic and copies ran while one was open for 0% of the time, Pallas kernels for 25%

profile of v22, /device:TPU:0, one launch (start us, length us, event | category | flops | bytes accessed | tf_op | source)
XLA Modules:
  0.0 65.3 jit_solution(15641514383374835963)
XLA Ops:
  0.6 2.5 %shard_map.76 = bf16[1024,128]{1,0:T(8,128)(2,1)} custom-call(bf16[512,1024]{1,0:T(8,128)(2,1)} %key_hbm.9, bf16[512,1024]{1,0:T(8,128)(2,1)} %value_hbm.9), custom_call_target="tpu_custom_call" | custom-call | flops 134217728 | bytes 2097152 | tf_op jit(solution)/shard_map/pallas_call | solution.py:375
  3.1 8.4 %all-to-all-start = ((bf16[8,128,128]{2,1,0:T(8,128)(2,1)}), bf16[8,128,128]{2,1,0:T(8,128)(2,1)S(1)}, u32[]{:S(2)}, u32[]{:S(2)}) async-start(bf16[8,128,128]{2,1,0:T(8,128)(2,1)} %bitcast.10), calls=%async_computation | async-start | bytes 524288 | tf_op jit(solution)/shard_map/all_to_all | solution.py:421
  11.5 3.8 %shard_map.77 = (bf16[1024,512]{1,0:T(8,128)(2,1)S(1)}, bf16[1024,512]{1,0:T(8,128)(2,1)S(1)}, bf16[1024,512]{1,0:T(8,128)(2,1)S(1)}, bf16[3072,256]{1,0:T(8,128)(2,1)}) custom-call(bf16[512,1024]{1,0:T(8,128)(2,1)} %query_hbm.3, bf16[512,1024]{1,0:T(8,128)(2,1)} %key_hbm.9, bf16[512,1024]{1,0:T(8,128)(2,1)} %value_hbm.9, bf16[512,1024]{1,0:T(8,128)(2,1)} %grad_hbm.1), custom_call_target="tpu_custom_call" | custom-call | flops 805306368 | bytes 4194304 | tf_op jit(solution)/shard_map/pallas_call | solution.py:375
  15.3 2.2 %all-to-all-done.block_ref = bf16[8,128,128]{2,1,0:T(8,128)(2,1)S(1)} async-done(((bf16[8,128,128]{2,1,0:T(8,128)(2,1)}), bf16[8,128,128]{2,1,0:T(8,128)(2,1)S(1)}, u32[]{:S(2)}, u32[]{:S(2)}) %all-to-all-start) | async-done | bytes 262176 | tf_op jit(solution)/shard_map/all_to_all | solution.py:421
  17.5 0.8 %shard_map.79 = bf16[8,128,128]{2,1,0:T(8,128)(2,1)} custom-call(bf16[8,128,128]{2,1,0:T(8,128)(2,1)S(1)} %all-to-all-done.block_ref), custom_call_target="tpu_custom_call" | custom-call | flops 131072 | bytes 262144 | tf_op jit(solution)/shard_map/pallas_call | solution.py:375
  18.3 6.0 %all-to-all-start.1 = ((bf16[8,128,128]{2,1,0:T(8,128)(2,1)}), bf16[8,128,128]{2,1,0:T(8,128)(2,1)S(1)}, u32[]{:S(2)}, u32[]{:S(2)}) async-start(bf16[8,128,128]{2,1,0:T(8,128)(2,1)} %shard_map.79), calls=%async_computation.1 | async-start | bytes 524288 | tf_op jit(solution)/shard_map/all_to_all | solution.py:421
  24.3 0.0 copy-start
  24.3 3.3 %shard_map.78 = (bf16[1024,512]{1,0:T(8,128)(2,1)S(1)}, bf16[3072,256]{1,0:T(8,128)(2,1)}) custom-call(bf16[512,1024]{1,0:T(8,128)(2,1)} %key_hbm.9, bf16[512,1024]{1,0:T(8,128)(2,1)} %value_hbm.9, bf16[1024,512]{1,0:T(8,128)(2,1)S(1)} %get-tuple-element.34.flipped_ref, ...), custom_call_target="tpu_custom_call", output_to_operand_aliasing={{0}: (3, {})} | custom-call | flops 402653184 | bytes 4194304 | tf_op jit(solution)/shard_map/pallas_call | solution.py:375
  27.6 2.4 %all-to-all-done.1 = bf16[8,128,128]{2,1,0:T(8,128)(2,1)S(1)} async-done(((bf16[8,128,128]{2,1,0:T(8,128)(2,1)}), bf16[8,128,128]{2,1,0:T(8,128)(2,1)S(1)}, u32[]{:S(2)}, u32[]{:S(2)}) %all-to-all-start.1) | async-done | bytes 262176 | tf_op jit(solution)/shard_map/all_to_all | solution.py:421
  30.1 0.0 copy-done
  30.1 0.8 %shard_map.80 = (bf16[1024,512]{1,0:T(8,128)(2,1)S(1)}, f32[4,2,512]{2,1,0:T(2,128)S(1)}) custom-call(f32[1,1024]{1,0:T(1,128)S(1)} %bitcast.8, bf16[1024,512]{1,0:T(8,128)(2,1)S(1)} %get-tuple-element.34.flipped_ref, bf16[1024,512]{1,0:T(8,128)(2,1)S(1)} %get-tuple-element.35.grad_ref, ...), custom_call_target="tpu_custom_call", output_to_operand_aliasing={{0}: (3, {})} | custom-call | flops 134217728 | bytes 3411968 | tf_op jit(solution)/shard_map/pallas_call | solution.py:375
  30.9 5.7 %all_to_all.25.sums_ref = f32[4,2,512]{2,1,0:T(2,128)S(1)} all-to-all(f32[4,2,512]{2,1,0:T(2,128)S(1)} %get-tuple-element.40), channel_id=1, replica_groups={{3,2,1,0},{7,6,5,4},{11,10,9,8},{15,14,13,12},{19,18,17,16},{23,22,21,2..., dimensions={0} | all-to-all | bytes 32768 | tf_op jit(solution)/shard_map/all_to_all | solution.py:493
  36.6 1.5 %shard_map.81 = (bf16[1024,512]{1,0:T(8,128)(2,1)S(1)}, bf16[1024,128]{1,0:T(8,128)(2,1)}) custom-call(f32[1,1024]{1,0:T(1,128)S(1)} %bitcast.9, bf16[1024,512]{1,0:T(8,128)(2,1)S(1)} %get-tuple-element.34.flipped_ref, bf16[1024,512]{1,0:T(8,128)(2,1)S(1)} %get-tuple-element.35.grad_ref, ...), custom_call_target="tpu_custom_call", output_to_operand_aliasing={{0}: (3, {})} | custom-call | flops 134217728 | bytes 3166208 | tf_op jit(solution)/shard_map/pallas_call | solution.py:375
  38.1 5.4 %all-to-all-start.3 = ((bf16[8,128,128]{2,1,0:T(8,128)(2,1)}), bf16[8,128,128]{2,1,0:T(8,128)(2,1)S(1)}, u32[]{:S(2)}, u32[]{:S(2)}) async-start(bf16[8,128,128]{2,1,0:T(8,128)(2,1)} %bitcast.11), calls=%async_computation.3 | async-start | bytes 524288 | tf_op jit(solution)/shard_map/all_to_all | solution.py:421
  43.5 4.9 %shard_map.82 = (bf16[512,1024]{1,0:T(8,128)(2,1)}, bf16[512,1024]{1,0:T(8,128)(2,1)S(1)}, bf16[512,768]{1,0:T(8,128)(2,1)S(1)}) custom-call(bf16[512,1024]{1,0:T(8,128)(2,1)} %key_hbm.9, bf16[512,1024]{1,0:T(8,128)(2,1)} %value_hbm.9, bf16[3072,256]{1,0:T(8,128)(2,1)} %get-tuple-element.42.first_hbm, ...), custom_call_target="tpu_custom_call" | custom-call | flops 939524096 | bytes 6553600 | tf_op jit(solution)/shard_map/pallas_call | solution.py:375
  48.4 0.8 %all-to-all-done.3.block_ref = bf16[8,128,128]{2,1,0:T(8,128)(2,1)S(1)} async-done(((bf16[8,128,128]{2,1,0:T(8,128)(2,1)}), bf16[8,128,128]{2,1,0:T(8,128)(2,1)S(1)}, u32[]{:S(2)}, u32[]{:S(2)}) %all-to-all-start.3) | async-done | bytes 262176 | tf_op jit(solution)/shard_map/all_to_all | solution.py:421
  49.2 0.8 %shard_map.84 = bf16[8,128,128]{2,1,0:T(8,128)(2,1)} custom-call(bf16[8,128,128]{2,1,0:T(8,128)(2,1)S(1)} %all-to-all-done.3.block_ref), custom_call_target="tpu_custom_call" | custom-call | flops 131072 | bytes 262144 | tf_op jit(solution)/shard_map/pallas_call | solution.py:375
  50.0 6.6 %all-to-all-start.4 = ((bf16[8,128,128]{2,1,0:T(8,128)(2,1)}), bf16[8,128,128]{2,1,0:T(8,128)(2,1)S(1)}, u32[]{:S(2)}, u32[]{:S(2)}) async-start(bf16[8,128,128]{2,1,0:T(8,128)(2,1)} %shard_map.84), calls=%async_computation.4 | async-start | bytes 524288 | tf_op jit(solution)/shard_map/all_to_all | solution.py:421
  56.7 4.5 %shard_map.83 = (bf16[512,1024]{1,0:T(8,128)(2,1)S(1)}, bf16[512,256]{1,0:T(8,128)(2,1)S(1)}, bf16[512,1024]{1,0:T(8,128)(2,1)S(1)}) custom-call(bf16[512,1024]{1,0:T(8,128)(2,1)} %query_hbm.3, bf16[512,1024]{1,0:T(8,128)(2,1)} %value_hbm.9, bf16[3072,256]{1,0:T(8,128)(2,1)} %get-tuple-element.43.second_hbm.weight_hbm, ...), custom_call_target="tpu_custom_call", output_to_operand_aliasing={{0}: (3, {})} | custom-call | flops 1207959552 | bytes 4718592 | tf_op jit(solution)/shard_map/pallas_call | solution.py:375
  61.2 1.5 %all-to-all-done.4 = bf16[8,128,128]{2,1,0:T(8,128)(2,1)S(1)} async-done(((bf16[8,128,128]{2,1,0:T(8,128)(2,1)}), bf16[8,128,128]{2,1,0:T(8,128)(2,1)S(1)}, u32[]{:S(2)}, u32[]{:S(2)}) %all-to-all-start.4) | async-done | bytes 262176 | tf_op jit(solution)/shard_map/all_to_all | solution.py:421
  62.6 2.5 %shard_map.85 = (bf16[512,1024]{1,0:T(8,128)(2,1)}, bf16[512,1024]{1,0:T(8,128)(2,1)}) custom-call(bf16[512,1024]{1,0:T(8,128)(2,1)} %key_hbm.9, bf16[512,1024]{1,0:T(8,128)(2,1)S(1)} %get-tuple-element.50.value_ref, bf16[512,1024]{1,0:T(8,128)(2,1)S(1)} %get-tuple-element.51.key_part, bf16[512,768]{1,0:T(8,128)(2,1)S(1)} %get-tuple-element.52.early_part, ...), custom_call_target="tpu_custom_call" | custom-call | flops 268435456 | bytes 4456448 | tf_op jit(solution)/shard_map/pallas_call | solution.py:375
Async XLA Ops:
  3.1 14.3 %all-to-all-start = ((bf16[8,128,128]{2,1,0:T(8,128)(2,1)}), bf16[8,128,128]{2,1,0:T(8,128)(2,1)S(1)}, u32[]{:S(2)}, u32[]{:S(2)}) async-start(bf16[8,128,128]{2,1,0:T(8,128)(2,1)} %bitcast.10), calls=%async_computation | async-start | bytes 524288 | tf_op jit(solution)/shard_map/all_to_all | solution.py:421
  18.3 11.8 %all-to-all-start.1 = ((bf16[8,128,128]{2,1,0:T(8,128)(2,1)}), bf16[8,128,128]{2,1,0:T(8,128)(2,1)S(1)}, u32[]{:S(2)}, u32[]{:S(2)}) async-start(bf16[8,128,128]{2,1,0:T(8,128)(2,1)} %shard_map.79), calls=%async_computation.1 | async-start | bytes 524288 | tf_op jit(solution)/shard_map/all_to_all | solution.py:421
  24.3 5.8 %copy-start = (f32[1024]{0:T(1024)S(1)}, f32[1024]{0:T(1024)}, u32[]{:S(2)}) copy-start(f32[1024]{0:T(1024)} %param.9) | copy-start | bytes 12292
  38.1 11.2 %all-to-all-start.3 = ((bf16[8,128,128]{2,1,0:T(8,128)(2,1)}), bf16[8,128,128]{2,1,0:T(8,128)(2,1)S(1)}, u32[]{:S(2)}, u32[]{:S(2)}) async-start(bf16[8,128,128]{2,1,0:T(8,128)(2,1)} %bitcast.11), calls=%async_computation.3 | async-start | bytes 524288 | tf_op jit(solution)/shard_map/all_to_all | solution.py:421
  50.0 12.6 %all-to-all-start.4 = ((bf16[8,128,128]{2,1,0:T(8,128)(2,1)}), bf16[8,128,128]{2,1,0:T(8,128)(2,1)S(1)}, u32[]{:S(2)}, u32[]{:S(2)}) async-start(bf16[8,128,128]{2,1,0:T(8,128)(2,1)} %shard_map.84), calls=%async_computation.4 | async-start | bytes 524288 | tf_op jit(solution)/shard_map/all_to_all | solution.py:421

commit v23 on v18

--- a/solution.py
+++ b/solution.py
@@ -177,7 +177,7 @@
 def scan_body(reverse, block_ref, state_hbm, state_ref, sems):
     count = block_ref.shape[0]
     total = jnp.zeros(block_ref.shape[1:], jnp.float32)
-    places = places_in_order(count)
+    places = places_in_order(count, 0 if reverse else 1)
     stores = []
     for place in range(count - 1, -1, -1) if reverse else range(count):
         rank = places.index(place)
@@ -322,8 +322,8 @@
     key_hbm, value_ref, key_part, early_part, late_part, state_ref, key_out_hbm, value_out_hbm,
     key_ref, key_out, value_out, in_sems, key_sems, value_sems,
 ):
-    keys = column_copies(key_hbm, key_ref, in_sems)
-    start_all(keys)
+    key_copy = pltpu.make_async_copy(key_hbm, key_ref, in_sems.at[0])
+    key_copy.start()
     key_stores = column_copies(key_out, key_out_hbm, key_sems)
     value_stores = column_copies(value_out, value_out_hbm, value_sems)
     for index, step in enumerate(pieces_of(key_out, COPY_COLS)):
@@ -332,8 +332,8 @@
             grad = key_part[:, cols].astype(jnp.float32) + mm_nt(value_ref[:, cols], state_ref[cols, :])
             key_out[:, cols] = grad.astype(jnp.bfloat16)
         key_stores[index].start()
+    key_copy.wait()
     for index, step in enumerate(pieces_of(value_out, COPY_COLS)):
-        keys[index].wait()
         for left in range(step.start, step.stop, HEAD_DIM):
             cols = slice(left, left + HEAD_DIM)
             early = early_part.shape[1]
@@ -382,20 +382,20 @@
     return states
 
 
-def places_in_order(count):
+def places_in_order(count, flip):
     quarter = count // 4
     first, second, third, fourth = (list(range(at, at + quarter)) for at in range(0, count, quarter))
     half = quarter // 2
     order = second + first[:half] + third[:half] + first[half:] + third[half:] + fourth
-    return [count - 1 - place for place in order]
+    return [(count - 1 - place) ^ flip for place in order]
 
 
 def last_first(count):
     return list(range(count - 1, -1, -1))
 
 
-def exchange(pieces, axis):
-    groups = [places_in_order(lax.axis_size(axis))]
+def exchange(pieces, axis, flip):
+    groups = [places_in_order(lax.axis_size(axis), flip)]
     return lax.all_to_all(pieces, axis, 0, 0, axis_index_groups=groups)
 
 
@@ -428,7 +428,7 @@
         [keys, values],
         [rows_vm] * 2 + [vm(state, f32), state_vm] + [row_chunks] * 2 + [state_chunks],
     )
-    kv_blocks = exchange(in_pieces(own_kv, "seq"), "seq")
+    kv_blocks = exchange(in_pieces(own_kv, "seq"), "seq", 1)
     half = width // 2 // COPY_COLS * COPY_COLS
     early = width * 3 // 4 // HEAD_DIM * HEAD_DIM
     def weights_of(cols):
@@ -447,7 +447,7 @@
     kv_blocks, flipped, grad_flipped, local, first_weights = lax.optimization_barrier(
         (kv_blocks, flipped, grad_flipped, local, first_weights)
     )
-    kv_low = exchange(scan_blocks(kv_blocks, False), "seq").reshape(state)
+    kv_low = exchange(scan_blocks(kv_blocks, False), "seq", 1).reshape(state)
     other = width - half
     other_vm, other_chunks = vm((rows, other), bf16), dma((other // COPY_COLS,))
     local, second_weights = local_call(
@@ -477,7 +477,7 @@
         scratch=[state_vm, state_chunks],
         aliases={3: 0},
     )
-    grad_blocks = exchange(in_pieces(own_grad, "seq"), "seq")
+    grad_blocks = exchange(in_pieces(own_grad, "seq"), "seq", 0)
     early_vm, late_vm = vm((rows, early), bf16), vm((rows, width - early), bf16)
     query_grad, dout, early_part = local_call(
         query_body,
@@ -490,7 +490,7 @@
     grad_blocks, query_grad, dout, early_part = lax.optimization_barrier(
         (grad_blocks, query_grad, dout, early_part)
     )
-    grad_low = exchange(scan_blocks(grad_blocks, True), "seq").reshape(state)
+    grad_low = exchange(scan_blocks(grad_blocks, True), "seq", 0).reshape(state)
     key_part, late_part, value_kept = local_call(
         inner_body,
         [dout],
@@ -506,7 +506,7 @@
         [hbm(tokens, bf16)] * 2,
         2 * small,
         [keys],
-        [rows_vm] * 3 + [chunks] * 3,
+        [rows_vm] * 3 + [dma((1,))] + [chunks] * 2,
     )
     return query_grad, key_grad, value_grad
 

time: 63.4 us -> 62.8 us (level)
  starting transfers between devices: 27.2 us -> 24.3 us
  waiting for transfers between devices: 3.61 us -> 5.83 us
    all_to_all x4, starting transfers between devices: 27.2 us -> 24.3 us  [exchange(): return lax.all_to_all(pieces, axis, 0, 0, axis_index_groups=groups)]
    all_to_all x4, waiting for transfers between devices: 3.61 us -> 5.83 us  [exchange(): return lax.all_to_all(pieces, axis, 0, 0, axis_index_groups=groups)]
  transfers between devices with their start and end apart: 4 -> 4, of which waited for: 4 -> 4; matrix products, arithmetic and copies ran while one was open for 0% -> 0% of each run, Pallas kernels for 26% -> 27%
where the time goes in v23:
time: 62.8 us; the launch traced here: 62.1 us
  Pallas kernels  25.4 us (40%)
  starting transfers between devices  24.3 us (39%)
  waiting for transfers between devices  5.83 us (9%)
  blocking collectives  5.68 us (9%)
  between operations  0.87 us (1%)
    pallas_call x10, Pallas kernels, local_call(): pl.pallas_call(body, in_specs=specs, out_specs=out_specs, out_shape=outs,...  25.4 us
    all_to_all x4, starting transfers between devices, exchange(): return lax.all_to_all(pieces, axis, 0, 0, axis_index_groups=groups)  24.3 us
    all_to_all x4, waiting for transfers between devices, exchange(): return lax.all_to_all(pieces, axis, 0, 0, axis_index_groups=groups)  5.83 us
    all_to_all x1, blocking collectives, shards(): lax.all_to_all(sums, 'head', 0, 0, axis_index_groups=[last_first(groups)])  5.68 us
  transfers between devices with their start and end apart: 4, of which 4 were waited for; matrix products, arithmetic and copies ran while one was open for 0% of the time, Pallas kernels for 27%

profile of v23, /device:TPU:0, one launch (start us, length us, event | category | flops | bytes accessed | tf_op | source)
XLA Modules:
  0.0 62.1 jit_solution(502960492210565955)
XLA Ops:
  0.6 2.5 %shard_map.76 = bf16[1024,128]{1,0:T(8,128)(2,1)} custom-call(bf16[512,1024]{1,0:T(8,128)(2,1)} %key_hbm.9, bf16[512,1024]{1,0:T(8,128)(2,1)} %value_hbm.9), custom_call_target="tpu_custom_call" | custom-call | flops 134217728 | bytes 2097152 | tf_op jit(solution)/shard_map/pallas_call | solution.py:359
  3.1 7.9 %all-to-all-start = ((bf16[8,128,128]{2,1,0:T(8,128)(2,1)}), bf16[8,128,128]{2,1,0:T(8,128)(2,1)S(1)}, u32[]{:S(2)}, u32[]{:S(2)}) async-start(bf16[8,128,128]{2,1,0:T(8,128)(2,1)} %bitcast.10), calls=%async_computation | async-start | bytes 524288 | tf_op jit(solution)/shard_map/all_to_all | solution.py:399
  11.0 3.8 %shard_map.77 = (bf16[1024,512]{1,0:T(8,128)(2,1)S(1)}, bf16[1024,512]{1,0:T(8,128)(2,1)S(1)}, bf16[1024,512]{1,0:T(8,128)(2,1)S(1)}, bf16[3072,256]{1,0:T(8,128)(2,1)}) custom-call(bf16[512,1024]{1,0:T(8,128)(2,1)} %query_hbm.3, bf16[512,1024]{1,0:T(8,128)(2,1)} %key_hbm.9, bf16[512,1024]{1,0:T(8,128)(2,1)} %value_hbm.9, bf16[512,1024]{1,0:T(8,128)(2,1)} %grad_hbm.1), custom_call_target="tpu_custom_call" | custom-call | flops 805306368 | bytes 4194304 | tf_op jit(solution)/shard_map/pallas_call | solution.py:359
  14.8 3.2 %all-to-all-done.block_ref = bf16[8,128,128]{2,1,0:T(8,128)(2,1)S(1)} async-done(((bf16[8,128,128]{2,1,0:T(8,128)(2,1)}), bf16[8,128,128]{2,1,0:T(8,128)(2,1)S(1)}, u32[]{:S(2)}, u32[]{:S(2)}) %all-to-all-start) | async-done | bytes 262176 | tf_op jit(solution)/shard_map/all_to_all | solution.py:399
  18.0 0.8 %shard_map.79 = bf16[8,128,128]{2,1,0:T(8,128)(2,1)} custom-call(bf16[8,128,128]{2,1,0:T(8,128)(2,1)S(1)} %all-to-all-done.block_ref), custom_call_target="tpu_custom_call" | custom-call | flops 131072 | bytes 262144 | tf_op jit(solution)/shard_map/pallas_call | solution.py:359
  18.8 4.6 %all-to-all-start.1 = ((bf16[8,128,128]{2,1,0:T(8,128)(2,1)}), bf16[8,128,128]{2,1,0:T(8,128)(2,1)S(1)}, u32[]{:S(2)}, u32[]{:S(2)}) async-start(bf16[8,128,128]{2,1,0:T(8,128)(2,1)} %shard_map.79), calls=%async_computation.1 | async-start | bytes 524288 | tf_op jit(solution)/shard_map/all_to_all | solution.py:399
  23.4 0.0 copy-start
  23.4 3.3 %shard_map.78 = (bf16[1024,512]{1,0:T(8,128)(2,1)S(1)}, bf16[3072,256]{1,0:T(8,128)(2,1)}) custom-call(bf16[512,1024]{1,0:T(8,128)(2,1)} %key_hbm.9, bf16[512,1024]{1,0:T(8,128)(2,1)} %value_hbm.9, bf16[1024,512]{1,0:T(8,128)(2,1)S(1)} %get-tuple-element.34.flipped_ref, ...), custom_call_target="tpu_custom_call", output_to_operand_aliasing={{0}: (3, {})} | custom-call | flops 402653184 | bytes 4194304 | tf_op jit(solution)/shard_map/pallas_call | solution.py:359
  26.7 2.0 %all-to-all-done.1 = bf16[8,128,128]{2,1,0:T(8,128)(2,1)S(1)} async-done(((bf16[8,128,128]{2,1,0:T(8,128)(2,1)}), bf16[8,128,128]{2,1,0:T(8,128)(2,1)S(1)}, u32[]{:S(2)}, u32[]{:S(2)}) %all-to-all-start.1) | async-done | bytes 262176 | tf_op jit(solution)/shard_map/all_to_all | solution.py:399
  28.7 0.0 copy-done
  28.7 0.8 %shard_map.80 = (bf16[1024,512]{1,0:T(8,128)(2,1)S(1)}, f32[4,2,512]{2,1,0:T(2,128)S(1)}) custom-call(f32[1,1024]{1,0:T(1,128)S(1)} %bitcast.8, bf16[1024,512]{1,0:T(8,128)(2,1)S(1)} %get-tuple-element.34.flipped_ref, bf16[1024,512]{1,0:T(8,128)(2,1)S(1)} %get-tuple-element.35.grad_ref, ...), custom_call_target="tpu_custom_call", output_to_operand_aliasing={{0}: (3, {})} | custom-call | flops 134217728 | bytes 3411968 | tf_op jit(solution)/shard_map/pallas_call | solution.py:359
  29.5 5.7 %all_to_all.25.sums_ref = f32[4,2,512]{2,1,0:T(2,128)S(1)} all-to-all(f32[4,2,512]{2,1,0:T(2,128)S(1)} %get-tuple-element.40), channel_id=1, replica_groups={{3,2,1,0},{7,6,5,4},{11,10,9,8},{15,14,13,12},{19,18,17,16},{23,22,21,2..., dimensions={0} | all-to-all | bytes 32768 | tf_op jit(solution)/shard_map/all_to_all | solution.py:471
  35.2 1.5 %shard_map.81 = (bf16[1024,512]{1,0:T(8,128)(2,1)S(1)}, bf16[1024,128]{1,0:T(8,128)(2,1)}) custom-call(f32[1,1024]{1,0:T(1,128)S(1)} %bitcast.9, bf16[1024,512]{1,0:T(8,128)(2,1)S(1)} %get-tuple-element.34.flipped_ref, bf16[1024,512]{1,0:T(8,128)(2,1)S(1)} %get-tuple-element.35.grad_ref, ...), custom_call_target="tpu_custom_call", output_to_operand_aliasing={{0}: (3, {})} | custom-call | flops 134217728 | bytes 3166208 | tf_op jit(solution)/shard_map/pallas_call | solution.py:359
  36.7 5.5 %all-to-all-start.3 = ((bf16[8,128,128]{2,1,0:T(8,128)(2,1)}), bf16[8,128,128]{2,1,0:T(8,128)(2,1)S(1)}, u32[]{:S(2)}, u32[]{:S(2)}) async-start(bf16[8,128,128]{2,1,0:T(8,128)(2,1)} %bitcast.11), calls=%async_computation.3 | async-start | bytes 524288 | tf_op jit(solution)/shard_map/all_to_all | solution.py:399
  42.2 4.9 %shard_map.82 = (bf16[512,1024]{1,0:T(8,128)(2,1)}, bf16[512,1024]{1,0:T(8,128)(2,1)S(1)}, bf16[512,768]{1,0:T(8,128)(2,1)S(1)}) custom-call(bf16[512,1024]{1,0:T(8,128)(2,1)} %key_hbm.9, bf16[512,1024]{1,0:T(8,128)(2,1)} %value_hbm.9, bf16[3072,256]{1,0:T(8,128)(2,1)} %get-tuple-element.42.first_hbm, ...), custom_call_target="tpu_custom_call" | custom-call | flops 939524096 | bytes 6553600 | tf_op jit(solution)/shard_map/pallas_call | solution.py:359
  47.2 0.5 all-to-all-done.3.block_ref
  47.7 0.8 %shard_map.84 = bf16[8,128,128]{2,1,0:T(8,128)(2,1)} custom-call(bf16[8,128,128]{2,1,0:T(8,128)(2,1)S(1)} %all-to-all-done.3.block_ref), custom_call_target="tpu_custom_call" | custom-call | flops 131072 | bytes 262144 | tf_op jit(solution)/shard_map/pallas_call | solution.py:359
  48.5 6.3 %all-to-all-start.4 = ((bf16[8,128,128]{2,1,0:T(8,128)(2,1)}), bf16[8,128,128]{2,1,0:T(8,128)(2,1)S(1)}, u32[]{:S(2)}, u32[]{:S(2)}) async-start(bf16[8,128,128]{2,1,0:T(8,128)(2,1)} %shard_map.84), calls=%async_computation.4 | async-start | bytes 524288 | tf_op jit(solution)/shard_map/all_to_all | solution.py:399
  54.8 4.5 %shard_map.83 = (bf16[512,1024]{1,0:T(8,128)(2,1)S(1)}, bf16[512,256]{1,0:T(8,128)(2,1)S(1)}, bf16[512,1024]{1,0:T(8,128)(2,1)S(1)}) custom-call(bf16[512,1024]{1,0:T(8,128)(2,1)} %query_hbm.3, bf16[512,1024]{1,0:T(8,128)(2,1)} %value_hbm.9, bf16[3072,256]{1,0:T(8,128)(2,1)} %get-tuple-element.43.second_hbm.weight_hbm, ...), custom_call_target="tpu_custom_call", output_to_operand_aliasing={{0}: (3, {})} | custom-call | flops 1207959552 | bytes 4718592 | tf_op jit(solution)/shard_map/pallas_call | solution.py:359
  59.3 0.1 all-to-all-done.4
  59.4 2.5 %shard_map.85 = (bf16[512,1024]{1,0:T(8,128)(2,1)}, bf16[512,1024]{1,0:T(8,128)(2,1)}) custom-call(bf16[512,1024]{1,0:T(8,128)(2,1)} %key_hbm.9, bf16[512,1024]{1,0:T(8,128)(2,1)S(1)} %get-tuple-element.50.value_ref, bf16[512,1024]{1,0:T(8,128)(2,1)S(1)} %get-tuple-element.51.key_part, bf16[512,768]{1,0:T(8,128)(2,1)S(1)} %get-tuple-element.52.early_part, ...), custom_call_target="tpu_custom_call" | custom-call | flops 268435456 | bytes 4456448 | tf_op jit(solution)/shard_map/pallas_call | solution.py:359
Async XLA Ops:
  3.1 14.9 %all-to-all-start = ((bf16[8,128,128]{2,1,0:T(8,128)(2,1)}), bf16[8,128,128]{2,1,0:T(8,128)(2,1)S(1)}, u32[]{:S(2)}, u32[]{:S(2)}) async-start(bf16[8,128,128]{2,1,0:T(8,128)(2,1)} %bitcast.10), calls=%async_computation | async-start | bytes 524288 | tf_op jit(solution)/shard_map/all_to_all | solution.py:399
  18.8 9.9 %all-to-all-start.1 = ((bf16[8,128,128]{2,1,0:T(8,128)(2,1)}), bf16[8,128,128]{2,1,0:T(8,128)(2,1)S(1)}, u32[]{:S(2)}, u32[]{:S(2)}) async-start(bf16[8,128,128]{2,1,0:T(8,128)(2,1)} %shard_map.79), calls=%async_computation.1 | async-start | bytes 524288 | tf_op jit(solution)/shard_map/all_to_all | solution.py:399
  23.4 5.3 %copy-start = (f32[1024]{0:T(1024)S(1)}, f32[1024]{0:T(1024)}, u32[]{:S(2)}) copy-start(f32[1024]{0:T(1024)} %param.9) | copy-start | bytes 12292
  36.7 11.0 %all-to-all-start.3 = ((bf16[8,128,128]{2,1,0:T(8,128)(2,1)}), bf16[8,128,128]{2,1,0:T(8,128)(2,1)S(1)}, u32[]{:S(2)}, u32[]{:S(2)}) async-start(bf16[8,128,128]{2,1,0:T(8,128)(2,1)} %bitcast.11), calls=%async_computation.3 | async-start | bytes 524288 | tf_op jit(solution)/shard_map/all_to_all | solution.py:399
  48.5 10.9 %all-to-all-start.4 = ((bf16[8,128,128]{2,1,0:T(8,128)(2,1)}), bf16[8,128,128]{2,1,0:T(8,128)(2,1)S(1)}, u32[]{:S(2)}, u32[]{:S(2)}) async-start(bf16[8,128,128]{2,1,0:T(8,128)(2,1)} %shard_map.84), calls=%async_computation.4 | async-start | bytes 524288 | tf_op jit(solution)/shard_map/all_to_all | solution.py:399

commit v24 on v23

--- a/solution.py
+++ b/solution.py
@@ -215,16 +215,14 @@
         cross += fold(scaled_grad(gain_ref, grad_ref, head) * attended)
     square = jnp.sum(square, axis=0, keepdims=True)
     cross = jnp.sum(cross, axis=0, keepdims=True)
-    for group in range(sums_ref.shape[0]):
-        sums_ref[group, 0:1, :] = square
-        sums_ref[group, 1:2, :] = cross
-
-
-def dout_body(
-    width, gain_ref, flipped_ref, grad_ref, attended_ref, sums_ref, dout_ref, own_hbm, own_ref, sems
-):
+    sums_ref[0:1, :] = square
+    sums_ref[1:2, :] = cross
+
+
+def dout_body(width, groups, gain_ref, flipped_ref, grad_ref, attended_ref, *refs):
+    dout_ref, own_hbm, own_ref, sems = refs[groups:]
     stores = row_copies(own_ref, own_hbm, STATE_ROWS, sems)
-    sums = sum(sums_ref[group] for group in range(sums_ref.shape[0]))
+    sums = sum(ref[...] for ref in refs[:groups])
     inverse = 1.0 / jnp.sqrt(sums[0:1, :] / width + EPSILON)
     drop = sums[1:2, :] * (inverse * inverse * inverse) / width
     for head in heads_of(dout_ref):
@@ -390,8 +388,13 @@
     return [(count - 1 - place) ^ flip for place in order]
 
 
-def last_first(count):
-    return list(range(count - 1, -1, -1))
+def from_all(part, axis):
+    count = lax.axis_size(axis)
+    parts = [part]
+    for shift in range(1, count):
+        pairs = [(place, (place + shift) % count) for place in range(count)]
+        parts.append(lax.ppermute(part, axis, pairs))
+    return parts
 
 
 def exchange(pieces, axis, flip):
@@ -464,14 +467,14 @@
     attended, sums = local_call(
         sums_body,
         [gain_row, flipped, grad_flipped, local, kv_low],
-        [flat_vm, vm((groups, 2, rows), f32)],
+        [flat_vm, vm((2, rows), f32)],
         small,
         aliases={3: 0},
     )
-    sums = lax.all_to_all(sums, "head", 0, 0, axis_index_groups=[last_first(groups)])
+    sums = from_all(sums, "head")
     dout_flipped, own_grad = local_call(
-        functools.partial(dout_body, total_width),
-        [gain_row, flipped, grad_flipped, attended, sums],
+        functools.partial(dout_body, total_width, groups),
+        [gain_row, flipped, grad_flipped, attended] + sums,
         [flat_vm, hbm(state, bf16)],
         small,
         scratch=[state_vm, state_chunks],

time: 62.8 us -> 60.6 us (0.965)
  blocking collectives: 5.68 us -> 0 us
  waiting for transfers between devices: 5.83 us -> 8.16 us
  starting transfers between devices: 24.3 us -> 25.5 us
    all_to_all x1 -> x0, blocking collectives: 5.68 us -> none  [shards(): lax.all_to_all(sums, 'head', 0, 0, axis_index_groups=[last_first(groups)])]
    ppermute x0 -> x3, waiting for transfers between devices: none -> 2.87 us  [from_all(): parts.append(lax.ppermute(part, axis, pairs))]
    ppermute x0 -> x3, starting transfers between devices: none -> 1.78 us  [from_all(): parts.append(lax.ppermute(part, axis, pairs))]
  transfers between devices with their start and end apart: 4 -> 7, of which waited for: 4 -> 5; matrix products, arithmetic and copies ran while one was open for 0% -> 0% of each run, Pallas kernels for 27% -> 28%
where the time goes in v24:
time: 60.6 us; the launch traced here: 59.9 us
  starting transfers between devices  25.5 us (42%)
  Pallas kernels  25.4 us (42%)
  waiting for transfers between devices  8.16 us (13%)
  between operations  0.88 us (1%)
    pallas_call x10, Pallas kernels, local_call(): pl.pallas_call(body, in_specs=specs, out_specs=out_specs, out_shape=outs,...  25.4 us
    all_to_all x4, starting transfers between devices, exchange(): return lax.all_to_all(pieces, axis, 0, 0, axis_index_groups=groups)  23.7 us
    all_to_all x4, waiting for transfers between devices, exchange(): return lax.all_to_all(pieces, axis, 0, 0, axis_index_groups=groups)  5.3 us
    ppermute x3, waiting for transfers between devices, from_all(): parts.append(lax.ppermute(part, axis, pairs))  2.87 us
    ppermute x3, starting transfers between devices, from_all(): parts.append(lax.ppermute(part, axis, pairs))  1.78 us
  transfers between devices with their start and end apart: 7, of which 5 were waited for; matrix products, arithmetic and copies ran while one was open for 0% of the time, Pallas kernels for 28%

profile of v24, /device:TPU:0, one launch (start us, length us, event | category | flops | bytes accessed | tf_op | source)
XLA Modules:
  0.0 59.9 jit_solution(12570013152139700632)
XLA Ops:
  0.6 2.5 %shard_map.76 = bf16[1024,128]{1,0:T(8,128)(2,1)} custom-call(bf16[512,1024]{1,0:T(8,128)(2,1)} %key_hbm.9, bf16[512,1024]{1,0:T(8,128)(2,1)} %value_hbm.9), custom_call_target="tpu_custom_call" | custom-call | flops 134217728 | bytes 2097152 | tf_op jit(solution)/shard_map/pallas_call | solution.py:357
  3.1 7.9 %all-to-all-start = ((bf16[8,128,128]{2,1,0:T(8,128)(2,1)}), bf16[8,128,128]{2,1,0:T(8,128)(2,1)S(1)}, u32[]{:S(2)}, u32[]{:S(2)}) async-start(bf16[8,128,128]{2,1,0:T(8,128)(2,1)} %bitcast.10), calls=%async_computation | async-start | bytes 524288 | tf_op jit(solution)/shard_map/all_to_all | solution.py:402
  11.0 3.8 %shard_map.77 = (bf16[1024,512]{1,0:T(8,128)(2,1)S(1)}, bf16[1024,512]{1,0:T(8,128)(2,1)S(1)}, bf16[1024,512]{1,0:T(8,128)(2,1)S(1)}, bf16[3072,256]{1,0:T(8,128)(2,1)}) custom-call(bf16[512,1024]{1,0:T(8,128)(2,1)} %query_hbm.3, bf16[512,1024]{1,0:T(8,128)(2,1)} %key_hbm.9, bf16[512,1024]{1,0:T(8,128)(2,1)} %value_hbm.9, bf16[512,1024]{1,0:T(8,128)(2,1)} %grad_hbm.1), custom_call_target="tpu_custom_call" | custom-call | flops 805306368 | bytes 4194304 | tf_op jit(solution)/shard_map/pallas_call | solution.py:357
  14.8 3.2 %all-to-all-done.block_ref = bf16[8,128,128]{2,1,0:T(8,128)(2,1)S(1)} async-done(((bf16[8,128,128]{2,1,0:T(8,128)(2,1)}), bf16[8,128,128]{2,1,0:T(8,128)(2,1)S(1)}, u32[]{:S(2)}, u32[]{:S(2)}) %all-to-all-start) | async-done | bytes 262176 | tf_op jit(solution)/shard_map/all_to_all | solution.py:402
  18.0 0.8 %shard_map.79 = bf16[8,128,128]{2,1,0:T(8,128)(2,1)} custom-call(bf16[8,128,128]{2,1,0:T(8,128)(2,1)S(1)} %all-to-all-done.block_ref), custom_call_target="tpu_custom_call" | custom-call | flops 131072 | bytes 262144 | tf_op jit(solution)/shard_map/pallas_call | solution.py:357
  18.8 4.6 %all-to-all-start.1 = ((bf16[8,128,128]{2,1,0:T(8,128)(2,1)}), bf16[8,128,128]{2,1,0:T(8,128)(2,1)S(1)}, u32[]{:S(2)}, u32[]{:S(2)}) async-start(bf16[8,128,128]{2,1,0:T(8,128)(2,1)} %shard_map.79), calls=%async_computation.1 | async-start | bytes 524288 | tf_op jit(solution)/shard_map/all_to_all | solution.py:402
  23.4 3.3 %shard_map.78 = (bf16[1024,512]{1,0:T(8,128)(2,1)S(1)}, bf16[3072,256]{1,0:T(8,128)(2,1)}) custom-call(bf16[512,1024]{1,0:T(8,128)(2,1)} %key_hbm.9, bf16[512,1024]{1,0:T(8,128)(2,1)} %value_hbm.9, bf16[1024,512]{1,0:T(8,128)(2,1)S(1)} %get-tuple-element.34.flipped_ref, ...), custom_call_target="tpu_custom_call", output_to_operand_aliasing={{0}: (3, {})} | custom-call | flops 402653184 | bytes 4194304 | tf_op jit(solution)/shard_map/pallas_call | solution.py:357
  26.7 2.0 %all-to-all-done.1 = bf16[8,128,128]{2,1,0:T(8,128)(2,1)S(1)} async-done(((bf16[8,128,128]{2,1,0:T(8,128)(2,1)}), bf16[8,128,128]{2,1,0:T(8,128)(2,1)S(1)}, u32[]{:S(2)}, u32[]{:S(2)}) %all-to-all-start.1) | async-done | bytes 262176 | tf_op jit(solution)/shard_map/all_to_all | solution.py:402
  28.7 0.8 %shard_map.80 = (bf16[1024,512]{1,0:T(8,128)(2,1)S(1)}, f32[2,512]{1,0:T(2,128)S(1)}) custom-call(f32[1,1024]{1,0:T(1,128)S(1)} %bitcast.8, bf16[1024,512]{1,0:T(8,128)(2,1)S(1)} %get-tuple-element.34.flipped_ref, bf16[1024,512]{1,0:T(8,128)(2,1)S(1)} %get-tuple-element.35.grad_ref, ...), custom_call_target="tpu_custom_call", output_to_operand_aliasing={{0}: (3, {})} | custom-call | flops 134217728 | bytes 3411968 | tf_op jit(solution)/shard_map/pallas_call | solution.py:357
  29.5 0.1 collective-permute-start.2
  29.6 1.6 %collective-permute-start.1 = (f32[2,512]{1,0:T(2,128)S(1)}, f32[2,512]{1,0:T(2,128)S(1)}, u32[]{:S(2)}, u32[]{:S(2)}) collective-permute-start(f32[2,512]{1,0:T(2,128)S(1)} %get-tuple-element.40.refs_0_), channel_id=1, source_target_pairs={{0,2},{1,3},{2,0},{3,1},{4,6},{5,7},{6,4},{7,5},{8,10},{9,11},{10,... | collective-permute-start | bytes 12296 | tf_op jit(solution)/shard_map/ppermute | solution.py:396
  31.1 0.2 collective-permute-start
  31.3 0.0 collective-permute-done.2.refs_3_
  31.3 1.9 %collective-permute-done.1.refs_2_ = f32[2,512]{1,0:T(2,128)S(1)} collective-permute-done((f32[2,512]{1,0:T(2,128)S(1)}, f32[2,512]{1,0:T(2,128)S(1)}, u32[]{:S(2)}, u32[]{:S(2)}) %collective-permute-start.1) | collective-permute-done | bytes 4128 | tf_op jit(solution)/shard_map/ppermute | solution.py:396
  33.3 0.9 %collective-permute-done.refs_1_ = f32[2,512]{1,0:T(2,128)S(1)} collective-permute-done((f32[2,512]{1,0:T(2,128)S(1)}, f32[2,512]{1,0:T(2,128)S(1)}, u32[]{:S(2)}, u32[]{:S(2)}) %collective-permute-start) | collective-permute-done | bytes 4128 | tf_op jit(solution)/shard_map/ppermute | solution.py:396
  34.2 1.5 %shard_map.81 = (bf16[1024,512]{1,0:T(8,128)(2,1)S(1)}, bf16[1024,128]{1,0:T(8,128)(2,1)}) custom-call(f32[1,1024]{1,0:T(1,128)S(1)} %bitcast.9, bf16[1024,512]{1,0:T(8,128)(2,1)S(1)} %get-tuple-element.34.flipped_ref, bf16[1024,512]{1,0:T(8,128)(2,1)S(1)} %get-tuple-element.35.grad_ref, ...), custom_call_target="tpu_custom_call", output_to_operand_aliasing={{0}: (3, {})} | custom-call | flops 134217728 | bytes 3166208 | tf_op jit(solution)/shard_map/pallas_call | solution.py:357
  35.6 5.5 %all-to-all-start.2 = ((bf16[8,128,128]{2,1,0:T(8,128)(2,1)}), bf16[8,128,128]{2,1,0:T(8,128)(2,1)S(1)}, u32[]{:S(2)}, u32[]{:S(2)}) async-start(bf16[8,128,128]{2,1,0:T(8,128)(2,1)} %bitcast.11), calls=%async_computation.2 | async-start | bytes 524288 | tf_op jit(solution)/shard_map/all_to_all | solution.py:402
  41.2 4.9 %shard_map.82 = (bf16[512,1024]{1,0:T(8,128)(2,1)}, bf16[512,1024]{1,0:T(8,128)(2,1)S(1)}, bf16[512,768]{1,0:T(8,128)(2,1)S(1)}) custom-call(bf16[512,1024]{1,0:T(8,128)(2,1)} %key_hbm.9, bf16[512,1024]{1,0:T(8,128)(2,1)} %value_hbm.9, bf16[3072,256]{1,0:T(8,128)(2,1)} %get-tuple-element.42.first_hbm, ...), custom_call_target="tpu_custom_call" | custom-call | flops 939524096 | bytes 6553600 | tf_op jit(solution)/shard_map/pallas_call | solution.py:357
  46.1 0.0 all-to-all-done.2.block_ref
  46.1 0.8 %shard_map.84 = bf16[8,128,128]{2,1,0:T(8,128)(2,1)} custom-call(bf16[8,128,128]{2,1,0:T(8,128)(2,1)S(1)} %all-to-all-done.2.block_ref), custom_call_target="tpu_custom_call" | custom-call | flops 131072 | bytes 262144 | tf_op jit(solution)/shard_map/pallas_call | solution.py:357
  46.9 5.7 %all-to-all-start.3 = ((bf16[8,128,128]{2,1,0:T(8,128)(2,1)}), bf16[8,128,128]{2,1,0:T(8,128)(2,1)S(1)}, u32[]{:S(2)}, u32[]{:S(2)}) async-start(bf16[8,128,128]{2,1,0:T(8,128)(2,1)} %shard_map.84), calls=%async_computation.3 | async-start | bytes 524288 | tf_op jit(solution)/shard_map/all_to_all | solution.py:402
  52.7 4.5 %shard_map.83 = (bf16[512,1024]{1,0:T(8,128)(2,1)S(1)}, bf16[512,256]{1,0:T(8,128)(2,1)S(1)}, bf16[512,1024]{1,0:T(8,128)(2,1)S(1)}) custom-call(bf16[512,1024]{1,0:T(8,128)(2,1)} %query_hbm.3, bf16[512,1024]{1,0:T(8,128)(2,1)} %value_hbm.9, bf16[3072,256]{1,0:T(8,128)(2,1)} %get-tuple-element.43.second_hbm.weight_hbm, ...), custom_call_target="tpu_custom_call", output_to_operand_aliasing={{0}: (3, {})} | custom-call | flops 1207959552 | bytes 4718592 | tf_op jit(solution)/shard_map/pallas_call | solution.py:357
  57.2 0.1 all-to-all-done.3
  57.2 2.5 %shard_map.85 = (bf16[512,1024]{1,0:T(8,128)(2,1)}, bf16[512,1024]{1,0:T(8,128)(2,1)}) custom-call(bf16[512,1024]{1,0:T(8,128)(2,1)} %key_hbm.9, bf16[512,1024]{1,0:T(8,128)(2,1)S(1)} %get-tuple-element.50.value_ref, bf16[512,1024]{1,0:T(8,128)(2,1)S(1)} %get-tuple-element.51.key_part, bf16[512,768]{1,0:T(8,128)(2,1)S(1)} %get-tuple-element.52.early_part, ...), custom_call_target="tpu_custom_call" | custom-call | flops 268435456 | bytes 4456448 | tf_op jit(solution)/shard_map/pallas_call | solution.py:357
  (2 shorter events, 0.0 us)
Async XLA Ops:
  3.1 14.9 %all-to-all-start = ((bf16[8,128,128]{2,1,0:T(8,128)(2,1)}), bf16[8,128,128]{2,1,0:T(8,128)(2,1)S(1)}, u32[]{:S(2)}, u32[]{:S(2)}) async-start(bf16[8,128,128]{2,1,0:T(8,128)(2,1)} %bitcast.10), calls=%async_computation | async-start | bytes 524288 | tf_op jit(solution)/shard_map/all_to_all | solution.py:402
  18.8 9.9 %all-to-all-start.1 = ((bf16[8,128,128]{2,1,0:T(8,128)(2,1)}), bf16[8,128,128]{2,1,0:T(8,128)(2,1)S(1)}, u32[]{:S(2)}, u32[]{:S(2)}) async-start(bf16[8,128,128]{2,1,0:T(8,128)(2,1)} %shard_map.79), calls=%async_computation.1 | async-start | bytes 524288 | tf_op jit(solution)/shard_map/all_to_all | solution.py:402
  23.4 5.3 %copy-start = (f32[1024]{0:T(1024)S(1)}, f32[1024]{0:T(1024)}, u32[]{:S(2)}) copy-start(f32[1024]{0:T(1024)} %param.9) | copy-start | bytes 12292
  29.5 1.8 %collective-permute-start.2 = (f32[2,512]{1,0:T(2,128)S(1)}, f32[2,512]{1,0:T(2,128)S(1)}, u32[]{:S(2)}, u32[]{:S(2)}) collective-permute-start(f32[2,512]{1,0:T(2,128)S(1)} %get-tuple-element.40.refs_0_), channel_id=1, source_target_pairs={{0,3},{1,0},{2,1},{3,2},{4,7},{5,4},{6,5},{7,6},{8,11},{9,8},{10,9... | collective-permute-start | bytes 12296 | tf_op jit(solution)/shard_map/ppermute | solution.py:396
  29.6 3.7 %collective-permute-start.1 = (f32[2,512]{1,0:T(2,128)S(1)}, f32[2,512]{1,0:T(2,128)S(1)}, u32[]{:S(2)}, u32[]{:S(2)}) collective-permute-start(f32[2,512]{1,0:T(2,128)S(1)} %get-tuple-element.40.refs_0_), channel_id=1, source_target_pairs={{0,2},{1,3},{2,0},{3,1},{4,6},{5,7},{6,4},{7,5},{8,10},{9,11},{10,... | collective-permute-start | bytes 12296 | tf_op jit(solution)/shard_map/ppermute | solution.py:396
  31.1 3.0 %collective-permute-start = (f32[2,512]{1,0:T(2,128)S(1)}, f32[2,512]{1,0:T(2,128)S(1)}, u32[]{:S(2)}, u32[]{:S(2)}) collective-permute-start(f32[2,512]{1,0:T(2,128)S(1)} %get-tuple-element.40.refs_0_), channel_id=1, source_target_pairs={{0,1},{1,2},{2,3},{3,0},{4,5},{5,6},{6,7},{7,4},{8,9},{9,10},{10,1... | collective-permute-start | bytes 12296 | tf_op jit(solution)/shard_map/ppermute | solution.py:396
  35.6 10.5 %all-to-all-start.2 = ((bf16[8,128,128]{2,1,0:T(8,128)(2,1)}), bf16[8,128,128]{2,1,0:T(8,128)(2,1)S(1)}, u32[]{:S(2)}, u32[]{:S(2)}) async-start(bf16[8,128,128]{2,1,0:T(8,128)(2,1)} %bitcast.11), calls=%async_computation.2 | async-start | bytes 524288 | tf_op jit(solution)/shard_map/all_to_all | solution.py:402
  46.9 10.3 %all-to-all-start.3 = ((bf16[8,128,128]{2,1,0:T(8,128)(2,1)}), bf16[8,128,128]{2,1,0:T(8,128)(2,1)S(1)}, u32[]{:S(2)}, u32[]{:S(2)}) async-start(bf16[8,128,128]{2,1,0:T(8,128)(2,1)} %shard_map.84), calls=%async_computation.3 | async-start | bytes 524288 | tf_op jit(solution)/shard_map/all_to_all | solution.py:402

commit v25 on v24

--- a/solution.py
+++ b/solution.py
@@ -391,8 +391,9 @@
 def from_all(part, axis):
     count = lax.axis_size(axis)
     parts = [part]
+    paired = count & (count - 1) == 0
     for shift in range(1, count):
-        pairs = [(place, (place + shift) % count) for place in range(count)]
+        pairs = [(place, place ^ shift if paired else (place + shift) % count) for place in range(count)]
         parts.append(lax.ppermute(part, axis, pairs))
     return parts
 

time: 60.6 us -> 61.4 us (1.013)
  starting transfers between devices: 25.5 us -> 26.4 us
    ppermute x3, waiting for transfers between devices: 2.87 us -> 1.83 us  [from_all(): parts.append(lax.ppermute(part, axis, pairs))]
    all_to_all x4, waiting for transfers between devices: 5.3 us -> 6.3 us  [exchange(): return lax.all_to_all(pieces, axis, 0, 0, axis_index_groups=groups)]
    all_to_all x4, starting transfers between devices: 23.7 us -> 24.4 us  [exchange(): return lax.all_to_all(pieces, axis, 0, 0, axis_index_groups=groups)]
  transfers between devices with their start and end apart: 7 -> 7, of which waited for: 5 -> 6; matrix products, arithmetic and copies ran while one was open for 0% -> 0% of each run, Pallas kernels for 28% -> 27%
where the time goes in v25:
time: 61.4 us; the launch traced here: 60.8 us
  starting transfers between devices  26.4 us (43%)
  Pallas kernels  25.4 us (41%)
  waiting for transfers between devices  8.12 us (13%)
  between operations  0.88 us (1%)
    pallas_call x10, Pallas kernels, local_call(): pl.pallas_call(body, in_specs=specs, out_specs=out_specs, out_shape=outs,...  25.4 us
    all_to_all x4, starting transfers between devices, exchange(): return lax.all_to_all(pieces, axis, 0, 0, axis_index_groups=groups)  24.4 us
    all_to_all x4, waiting for transfers between devices, exchange(): return lax.all_to_all(pieces, axis, 0, 0, axis_index_groups=groups)  6.3 us
    ppermute x3, starting transfers between devices, from_all(): parts.append(lax.ppermute(part, axis, pairs))  1.92 us
    ppermute x3, waiting for transfers between devices, from_all(): parts.append(lax.ppermute(part, axis, pairs))  1.83 us
  transfers between devices with their start and end apart: 7, of which 6 were waited for; matrix products, arithmetic and copies ran while one was open for 0% of the time, Pallas kernels for 27%

profile of v25, /device:TPU:0, one launch (start us, length us, event | category | flops | bytes accessed | tf_op | source)
XLA Modules:
  0.0 60.8 jit_solution(17500431253131703847)
XLA Ops:
  0.6 2.5 %shard_map.76 = bf16[1024,128]{1,0:T(8,128)(2,1)} custom-call(bf16[512,1024]{1,0:T(8,128)(2,1)} %key_hbm.9, bf16[512,1024]{1,0:T(8,128)(2,1)} %value_hbm.9), custom_call_target="tpu_custom_call" | custom-call | flops 134217728 | bytes 2097152 | tf_op jit(solution)/shard_map/pallas_call | solution.py:357
  3.1 7.9 %all-to-all-start = ((bf16[8,128,128]{2,1,0:T(8,128)(2,1)}), bf16[8,128,128]{2,1,0:T(8,128)(2,1)S(1)}, u32[]{:S(2)}, u32[]{:S(2)}) async-start(bf16[8,128,128]{2,1,0:T(8,128)(2,1)} %bitcast.10), calls=%async_computation | async-start | bytes 524288 | tf_op jit(solution)/shard_map/all_to_all | solution.py:403
  11.0 3.8 %shard_map.77 = (bf16[1024,512]{1,0:T(8,128)(2,1)S(1)}, bf16[1024,512]{1,0:T(8,128)(2,1)S(1)}, bf16[1024,512]{1,0:T(8,128)(2,1)S(1)}, bf16[3072,256]{1,0:T(8,128)(2,1)}) custom-call(bf16[512,1024]{1,0:T(8,128)(2,1)} %query_hbm.3, bf16[512,1024]{1,0:T(8,128)(2,1)} %key_hbm.9, bf16[512,1024]{1,0:T(8,128)(2,1)} %value_hbm.9, bf16[512,1024]{1,0:T(8,128)(2,1)} %grad_hbm.1), custom_call_target="tpu_custom_call" | custom-call | flops 805306368 | bytes 4194304 | tf_op jit(solution)/shard_map/pallas_call | solution.py:357
  14.8 3.2 %all-to-all-done.block_ref = bf16[8,128,128]{2,1,0:T(8,128)(2,1)S(1)} async-done(((bf16[8,128,128]{2,1,0:T(8,128)(2,1)}), bf16[8,128,128]{2,1,0:T(8,128)(2,1)S(1)}, u32[]{:S(2)}, u32[]{:S(2)}) %all-to-all-start) | async-done | bytes 262176 | tf_op jit(solution)/shard_map/all_to_all | solution.py:403
  18.0 0.8 %shard_map.79 = bf16[8,128,128]{2,1,0:T(8,128)(2,1)} custom-call(bf16[8,128,128]{2,1,0:T(8,128)(2,1)S(1)} %all-to-all-done.block_ref), custom_call_target="tpu_custom_call" | custom-call | flops 131072 | bytes 262144 | tf_op jit(solution)/shard_map/pallas_call | solution.py:357
  18.8 4.6 %all-to-all-start.1 = ((bf16[8,128,128]{2,1,0:T(8,128)(2,1)}), bf16[8,128,128]{2,1,0:T(8,128)(2,1)S(1)}, u32[]{:S(2)}, u32[]{:S(2)}) async-start(bf16[8,128,128]{2,1,0:T(8,128)(2,1)} %shard_map.79), calls=%async_computation.1 | async-start | bytes 524288 | tf_op jit(solution)/shard_map/all_to_all | solution.py:403
  23.4 3.3 %shard_map.78 = (bf16[1024,512]{1,0:T(8,128)(2,1)S(1)}, bf16[3072,256]{1,0:T(8,128)(2,1)}) custom-call(bf16[512,1024]{1,0:T(8,128)(2,1)} %key_hbm.9, bf16[512,1024]{1,0:T(8,128)(2,1)} %value_hbm.9, bf16[1024,512]{1,0:T(8,128)(2,1)S(1)} %get-tuple-element.34.flipped_ref, ...), custom_call_target="tpu_custom_call", output_to_operand_aliasing={{0}: (3, {})} | custom-call | flops 402653184 | bytes 4194304 | tf_op jit(solution)/shard_map/pallas_call | solution.py:357
  26.7 2.0 %all-to-all-done.1 = bf16[8,128,128]{2,1,0:T(8,128)(2,1)S(1)} async-done(((bf16[8,128,128]{2,1,0:T(8,128)(2,1)}), bf16[8,128,128]{2,1,0:T(8,128)(2,1)S(1)}, u32[]{:S(2)}, u32[]{:S(2)}) %all-to-all-start.1) | async-done | bytes 262176 | tf_op jit(solution)/shard_map/all_to_all | solution.py:403
  28.7 0.8 %shard_map.80 = (bf16[1024,512]{1,0:T(8,128)(2,1)S(1)}, f32[2,512]{1,0:T(2,128)S(1)}) custom-call(f32[1,1024]{1,0:T(1,128)S(1)} %bitcast.8, bf16[1024,512]{1,0:T(8,128)(2,1)S(1)} %get-tuple-element.34.flipped_ref, bf16[1024,512]{1,0:T(8,128)(2,1)S(1)} %get-tuple-element.35.grad_ref, ...), custom_call_target="tpu_custom_call", output_to_operand_aliasing={{0}: (3, {})} | custom-call | flops 134217728 | bytes 3411968 | tf_op jit(solution)/shard_map/pallas_call | solution.py:357
  29.5 0.1 collective-permute-start.2
  29.6 1.6 %collective-permute-start.1 = (f32[2,512]{1,0:T(2,128)S(1)}, f32[2,512]{1,0:T(2,128)S(1)}, u32[]{:S(2)}, u32[]{:S(2)}) collective-permute-start(f32[2,512]{1,0:T(2,128)S(1)} %get-tuple-element.40.refs_0_), channel_id=1, source_target_pairs={{0,2},{1,3},{2,0},{3,1},{4,6},{5,7},{6,4},{7,5},{8,10},{9,11},{10,... | collective-permute-start | bytes 12296 | tf_op jit(solution)/shard_map/ppermute | solution.py:397
  31.2 0.3 collective-permute-start
  31.4 1.2 %collective-permute-done.2.refs_3_ = f32[2,512]{1,0:T(2,128)S(1)} collective-permute-done((f32[2,512]{1,0:T(2,128)S(1)}, f32[2,512]{1,0:T(2,128)S(1)}, u32[]{:S(2)}, u32[]{:S(2)}) %collective-permute-start.2) | collective-permute-done | bytes 4128 | tf_op jit(solution)/shard_map/ppermute | solution.py:397
  32.6 0.7 %collective-permute-done.1.refs_2_ = f32[2,512]{1,0:T(2,128)S(1)} collective-permute-done((f32[2,512]{1,0:T(2,128)S(1)}, f32[2,512]{1,0:T(2,128)S(1)}, u32[]{:S(2)}, u32[]{:S(2)}) %collective-permute-start.1) | collective-permute-done | bytes 4128 | tf_op jit(solution)/shard_map/ppermute | solution.py:397
  33.3 0.0 collective-permute-done.refs_1_
  33.3 1.5 %shard_map.81 = (bf16[1024,512]{1,0:T(8,128)(2,1)S(1)}, bf16[1024,128]{1,0:T(8,128)(2,1)}) custom-call(f32[1,1024]{1,0:T(1,128)S(1)} %bitcast.9, bf16[1024,512]{1,0:T(8,128)(2,1)S(1)} %get-tuple-element.34.flipped_ref, bf16[1024,512]{1,0:T(8,128)(2,1)S(1)} %get-tuple-element.35.grad_ref, ...), custom_call_target="tpu_custom_call", output_to_operand_aliasing={{0}: (3, {})} | custom-call | flops 134217728 | bytes 3166208 | tf_op jit(solution)/shard_map/pallas_call | solution.py:357
  34.7 5.6 %all-to-all-start.2 = ((bf16[8,128,128]{2,1,0:T(8,128)(2,1)}), bf16[8,128,128]{2,1,0:T(8,128)(2,1)S(1)}, u32[]{:S(2)}, u32[]{:S(2)}) async-start(bf16[8,128,128]{2,1,0:T(8,128)(2,1)} %bitcast.11), calls=%async_computation.2 | async-start | bytes 524288 | tf_op jit(solution)/shard_map/all_to_all | solution.py:403
  40.3 4.9 %shard_map.82 = (bf16[512,1024]{1,0:T(8,128)(2,1)}, bf16[512,1024]{1,0:T(8,128)(2,1)S(1)}, bf16[512,768]{1,0:T(8,128)(2,1)S(1)}) custom-call(bf16[512,1024]{1,0:T(8,128)(2,1)} %key_hbm.9, bf16[512,1024]{1,0:T(8,128)(2,1)} %value_hbm.9, bf16[3072,256]{1,0:T(8,128)(2,1)} %get-tuple-element.42.first_hbm, ...), custom_call_target="tpu_custom_call" | custom-call | flops 939524096 | bytes 6553600 | tf_op jit(solution)/shard_map/pallas_call | solution.py:357
  45.3 1.0 %all-to-all-done.2.block_ref = bf16[8,128,128]{2,1,0:T(8,128)(2,1)S(1)} async-done(((bf16[8,128,128]{2,1,0:T(8,128)(2,1)}), bf16[8,128,128]{2,1,0:T(8,128)(2,1)S(1)}, u32[]{:S(2)}, u32[]{:S(2)}) %all-to-all-start.2) | async-done | bytes 262176 | tf_op jit(solution)/shard_map/all_to_all | solution.py:403
  46.2 0.8 %shard_map.84 = bf16[8,128,128]{2,1,0:T(8,128)(2,1)} custom-call(bf16[8,128,128]{2,1,0:T(8,128)(2,1)S(1)} %all-to-all-done.2.block_ref), custom_call_target="tpu_custom_call" | custom-call | flops 131072 | bytes 262144 | tf_op jit(solution)/shard_map/pallas_call | solution.py:357
  47.0 6.5 %all-to-all-start.3 = ((bf16[8,128,128]{2,1,0:T(8,128)(2,1)}), bf16[8,128,128]{2,1,0:T(8,128)(2,1)S(1)}, u32[]{:S(2)}, u32[]{:S(2)}) async-start(bf16[8,128,128]{2,1,0:T(8,128)(2,1)} %shard_map.84), calls=%async_computation.3 | async-start | bytes 524288 | tf_op jit(solution)/shard_map/all_to_all | solution.py:403
  53.5 4.5 %shard_map.83 = (bf16[512,1024]{1,0:T(8,128)(2,1)S(1)}, bf16[512,256]{1,0:T(8,128)(2,1)S(1)}, bf16[512,1024]{1,0:T(8,128)(2,1)S(1)}) custom-call(bf16[512,1024]{1,0:T(8,128)(2,1)} %query_hbm.3, bf16[512,1024]{1,0:T(8,128)(2,1)} %value_hbm.9, bf16[3072,256]{1,0:T(8,128)(2,1)} %get-tuple-element.43.second_hbm.weight_hbm, ...), custom_call_target="tpu_custom_call", output_to_operand_aliasing={{0}: (3, {})} | custom-call | flops 1207959552 | bytes 4718592 | tf_op jit(solution)/shard_map/pallas_call | solution.py:357
  58.0 0.1 all-to-all-done.3
  58.1 2.5 %shard_map.85 = (bf16[512,1024]{1,0:T(8,128)(2,1)}, bf16[512,1024]{1,0:T(8,128)(2,1)}) custom-call(bf16[512,1024]{1,0:T(8,128)(2,1)} %key_hbm.9, bf16[512,1024]{1,0:T(8,128)(2,1)S(1)} %get-tuple-element.50.value_ref, bf16[512,1024]{1,0:T(8,128)(2,1)S(1)} %get-tuple-element.51.key_part, bf16[512,768]{1,0:T(8,128)(2,1)S(1)} %get-tuple-element.52.early_part, ...), custom_call_target="tpu_custom_call" | custom-call | flops 268435456 | bytes 4456448 | tf_op jit(solution)/shard_map/pallas_call | solution.py:357
  (2 shorter events, 0.0 us)
Async XLA Ops:
  3.1 14.9 %all-to-all-start = ((bf16[8,128,128]{2,1,0:T(8,128)(2,1)}), bf16[8,128,128]{2,1,0:T(8,128)(2,1)S(1)}, u32[]{:S(2)}, u32[]{:S(2)}) async-start(bf16[8,128,128]{2,1,0:T(8,128)(2,1)} %bitcast.10), calls=%async_computation | async-start | bytes 524288 | tf_op jit(solution)/shard_map/all_to_all | solution.py:403
  18.8 9.9 %all-to-all-start.1 = ((bf16[8,128,128]{2,1,0:T(8,128)(2,1)}), bf16[8,128,128]{2,1,0:T(8,128)(2,1)S(1)}, u32[]{:S(2)}, u32[]{:S(2)}) async-start(bf16[8,128,128]{2,1,0:T(8,128)(2,1)} %shard_map.79), calls=%async_computation.1 | async-start | bytes 524288 | tf_op jit(solution)/shard_map/all_to_all | solution.py:403
  23.4 5.3 %copy-start = (f32[1024]{0:T(1024)S(1)}, f32[1024]{0:T(1024)}, u32[]{:S(2)}) copy-start(f32[1024]{0:T(1024)} %param.9) | copy-start | bytes 12292
  29.5 3.1 %collective-permute-start.2 = (f32[2,512]{1,0:T(2,128)S(1)}, f32[2,512]{1,0:T(2,128)S(1)}, u32[]{:S(2)}, u32[]{:S(2)}) collective-permute-start(f32[2,512]{1,0:T(2,128)S(1)} %get-tuple-element.40.refs_0_), channel_id=1, source_target_pairs={{0,3},{1,2},{2,1},{3,0},{4,7},{5,6},{6,5},{7,4},{8,11},{9,10},{10,... | collective-permute-start | bytes 12296 | tf_op jit(solution)/shard_map/ppermute | solution.py:397
  29.6 3.7 %collective-permute-start.1 = (f32[2,512]{1,0:T(2,128)S(1)}, f32[2,512]{1,0:T(2,128)S(1)}, u32[]{:S(2)}, u32[]{:S(2)}) collective-permute-start(f32[2,512]{1,0:T(2,128)S(1)} %get-tuple-element.40.refs_0_), channel_id=1, source_target_pairs={{0,2},{1,3},{2,0},{3,1},{4,6},{5,7},{6,4},{7,5},{8,10},{9,11},{10,... | collective-permute-start | bytes 12296 | tf_op jit(solution)/shard_map/ppermute | solution.py:397
  31.2 2.1 %collective-permute-start = (f32[2,512]{1,0:T(2,128)S(1)}, f32[2,512]{1,0:T(2,128)S(1)}, u32[]{:S(2)}, u32[]{:S(2)}) collective-permute-start(f32[2,512]{1,0:T(2,128)S(1)} %get-tuple-element.40.refs_0_), channel_id=1, source_target_pairs={{0,1},{1,0},{2,3},{3,2},{4,5},{5,4},{6,7},{7,6},{8,9},{9,8},{10,11... | collective-permute-start | bytes 12296 | tf_op jit(solution)/shard_map/ppermute | solution.py:397
  34.7 11.5 %all-to-all-start.2 = ((bf16[8,128,128]{2,1,0:T(8,128)(2,1)}), bf16[8,128,128]{2,1,0:T(8,128)(2,1)S(1)}, u32[]{:S(2)}, u32[]{:S(2)}) async-start(bf16[8,128,128]{2,1,0:T(8,128)(2,1)} %bitcast.11), calls=%async_computation.2 | async-start | bytes 524288 | tf_op jit(solution)/shard_map/all_to_all | solution.py:403
  47.0 11.1 %all-to-all-start.3 = ((bf16[8,128,128]{2,1,0:T(8,128)(2,1)}), bf16[8,128,128]{2,1,0:T(8,128)(2,1)S(1)}, u32[]{:S(2)}, u32[]{:S(2)}) async-start(bf16[8,128,128]{2,1,0:T(8,128)(2,1)} %shard_map.84), calls=%async_computation.3 | async-start | bytes 524288 | tf_op jit(solution)/shard_map/all_to_all | solution.py:403

commit v26 on v25

--- a/solution.py
+++ b/solution.py
@@ -392,7 +392,7 @@
     count = lax.axis_size(axis)
     parts = [part]
     paired = count & (count - 1) == 0
-    for shift in range(1, count):
+    for shift in sorted(range(1, count), key=lambda shift: shift % 2):
         pairs = [(place, place ^ shift if paired else (place + shift) % count) for place in range(count)]
         parts.append(lax.ppermute(part, axis, pairs))
     return parts

time: 61.4 us -> 61.4 us (level)
    ppermute x3, waiting for transfers between devices: 1.83 us -> 3.07 us  [from_all(): parts.append(lax.ppermute(part, axis, pairs))]
    all_to_all x4, waiting for transfers between devices: 6.3 us -> 5.32 us  [exchange(): return lax.all_to_all(pieces, axis, 0, 0, axis_index_groups=groups)]
  transfers between devices with their start and end apart: 7 -> 7, of which waited for: 6 -> 5; matrix products, arithmetic and copies ran while one was open for 0% -> 0% of each run, Pallas kernels for 27% -> 27%
where the time goes in v26:
time: 61.4 us; the launch traced here: 60.8 us
  starting transfers between devices  26.1 us (43%)
  Pallas kernels  25.4 us (41%)
  waiting for transfers between devices  8.39 us (14%)
  between operations  0.88 us (1%)
    pallas_call x10, Pallas kernels, local_call(): pl.pallas_call(body, in_specs=specs, out_specs=out_specs, out_shape=outs,...  25.4 us
    all_to_all x4, starting transfers between devices, exchange(): return lax.all_to_all(pieces, axis, 0, 0, axis_index_groups=groups)  23.9 us
    all_to_all x4, waiting for transfers between devices, exchange(): return lax.all_to_all(pieces, axis, 0, 0, axis_index_groups=groups)  5.32 us
    ppermute x3, waiting for transfers between devices, from_all(): parts.append(lax.ppermute(part, axis, pairs))  3.07 us
    ppermute x3, starting transfers between devices, from_all(): parts.append(lax.ppermute(part, axis, pairs))  2.2 us
  transfers between devices with their start and end apart: 7, of which 5 were waited for; matrix products, arithmetic and copies ran while one was open for 0% of the time, Pallas kernels for 27%

profile of v26, /device:TPU:0, one launch (start us, length us, event | category | flops | bytes accessed | tf_op | source)
XLA Modules:
  0.0 60.8 jit_solution(8957432188494367538)
XLA Ops:
  0.6 2.5 %shard_map.76 = bf16[1024,128]{1,0:T(8,128)(2,1)} custom-call(bf16[512,1024]{1,0:T(8,128)(2,1)} %key_hbm.9, bf16[512,1024]{1,0:T(8,128)(2,1)} %value_hbm.9), custom_call_target="tpu_custom_call" | custom-call | flops 134217728 | bytes 2097152 | tf_op jit(solution)/shard_map/pallas_call | solution.py:357
  3.1 7.9 %all-to-all-start = ((bf16[8,128,128]{2,1,0:T(8,128)(2,1)}), bf16[8,128,128]{2,1,0:T(8,128)(2,1)S(1)}, u32[]{:S(2)}, u32[]{:S(2)}) async-start(bf16[8,128,128]{2,1,0:T(8,128)(2,1)} %bitcast.10), calls=%async_computation | async-start | bytes 524288 | tf_op jit(solution)/shard_map/all_to_all | solution.py:403
  11.0 3.8 %shard_map.77 = (bf16[1024,512]{1,0:T(8,128)(2,1)S(1)}, bf16[1024,512]{1,0:T(8,128)(2,1)S(1)}, bf16[1024,512]{1,0:T(8,128)(2,1)S(1)}, bf16[3072,256]{1,0:T(8,128)(2,1)}) custom-call(bf16[512,1024]{1,0:T(8,128)(2,1)} %query_hbm.3, bf16[512,1024]{1,0:T(8,128)(2,1)} %key_hbm.9, bf16[512,1024]{1,0:T(8,128)(2,1)} %value_hbm.9, bf16[512,1024]{1,0:T(8,128)(2,1)} %grad_hbm.1), custom_call_target="tpu_custom_call" | custom-call | flops 805306368 | bytes 4194304 | tf_op jit(solution)/shard_map/pallas_call | solution.py:357
  14.8 3.2 %all-to-all-done.block_ref = bf16[8,128,128]{2,1,0:T(8,128)(2,1)S(1)} async-done(((bf16[8,128,128]{2,1,0:T(8,128)(2,1)}), bf16[8,128,128]{2,1,0:T(8,128)(2,1)S(1)}, u32[]{:S(2)}, u32[]{:S(2)}) %all-to-all-start) | async-done | bytes 262176 | tf_op jit(solution)/shard_map/all_to_all | solution.py:403
  18.0 0.8 %shard_map.79 = bf16[8,128,128]{2,1,0:T(8,128)(2,1)} custom-call(bf16[8,128,128]{2,1,0:T(8,128)(2,1)S(1)} %all-to-all-done.block_ref), custom_call_target="tpu_custom_call" | custom-call | flops 131072 | bytes 262144 | tf_op jit(solution)/shard_map/pallas_call | solution.py:357
  18.8 4.6 %all-to-all-start.1 = ((bf16[8,128,128]{2,1,0:T(8,128)(2,1)}), bf16[8,128,128]{2,1,0:T(8,128)(2,1)S(1)}, u32[]{:S(2)}, u32[]{:S(2)}) async-start(bf16[8,128,128]{2,1,0:T(8,128)(2,1)} %shard_map.79), calls=%async_computation.1 | async-start | bytes 524288 | tf_op jit(solution)/shard_map/all_to_all | solution.py:403
  23.4 3.3 %shard_map.78 = (bf16[1024,512]{1,0:T(8,128)(2,1)S(1)}, bf16[3072,256]{1,0:T(8,128)(2,1)}) custom-call(bf16[512,1024]{1,0:T(8,128)(2,1)} %key_hbm.9, bf16[512,1024]{1,0:T(8,128)(2,1)} %value_hbm.9, bf16[1024,512]{1,0:T(8,128)(2,1)S(1)} %get-tuple-element.34.flipped_ref, ...), custom_call_target="tpu_custom_call", output_to_operand_aliasing={{0}: (3, {})} | custom-call | flops 402653184 | bytes 4194304 | tf_op jit(solution)/shard_map/pallas_call | solution.py:357
  26.7 2.0 %all-to-all-done.1 = bf16[8,128,128]{2,1,0:T(8,128)(2,1)S(1)} async-done(((bf16[8,128,128]{2,1,0:T(8,128)(2,1)}), bf16[8,128,128]{2,1,0:T(8,128)(2,1)S(1)}, u32[]{:S(2)}, u32[]{:S(2)}) %all-to-all-start.1) | async-done | bytes 262176 | tf_op jit(solution)/shard_map/all_to_all | solution.py:403
  28.7 0.8 %shard_map.80 = (bf16[1024,512]{1,0:T(8,128)(2,1)S(1)}, f32[2,512]{1,0:T(2,128)S(1)}) custom-call(f32[1,1024]{1,0:T(1,128)S(1)} %bitcast.8, bf16[1024,512]{1,0:T(8,128)(2,1)S(1)} %get-tuple-element.34.flipped_ref, bf16[1024,512]{1,0:T(8,128)(2,1)S(1)} %get-tuple-element.35.grad_ref, ...), custom_call_target="tpu_custom_call", output_to_operand_aliasing={{0}: (3, {})} | custom-call | flops 134217728 | bytes 3411968 | tf_op jit(solution)/shard_map/pallas_call | solution.py:357
  29.5 0.1 collective-permute-start.2
  29.6 1.6 %collective-permute-start.1 = (f32[2,512]{1,0:T(2,128)S(1)}, f32[2,512]{1,0:T(2,128)S(1)}, u32[]{:S(2)}, u32[]{:S(2)}) collective-permute-start(f32[2,512]{1,0:T(2,128)S(1)} %get-tuple-element.40.refs_0_), channel_id=1, source_target_pairs={{0,1},{1,0},{2,3},{3,2},{4,5},{5,4},{6,7},{7,6},{8,9},{9,8},{10,11... | collective-permute-start | bytes 12296 | tf_op jit(solution)/shard_map/ppermute | solution.py:397
  31.2 0.5 collective-permute-start
  31.7 0.9 %collective-permute-done.2.refs_3_ = f32[2,512]{1,0:T(2,128)S(1)} collective-permute-done((f32[2,512]{1,0:T(2,128)S(1)}, f32[2,512]{1,0:T(2,128)S(1)}, u32[]{:S(2)}, u32[]{:S(2)}) %collective-permute-start.2) | collective-permute-done | bytes 4128 | tf_op jit(solution)/shard_map/ppermute | solution.py:397
  32.6 0.0 collective-permute-done.1.refs_2_
  32.6 2.2 %collective-permute-done.refs_1_ = f32[2,512]{1,0:T(2,128)S(1)} collective-permute-done((f32[2,512]{1,0:T(2,128)S(1)}, f32[2,512]{1,0:T(2,128)S(1)}, u32[]{:S(2)}, u32[]{:S(2)}) %collective-permute-start) | collective-permute-done | bytes 4128 | tf_op jit(solution)/shard_map/ppermute | solution.py:397
  34.8 1.5 %shard_map.81 = (bf16[1024,512]{1,0:T(8,128)(2,1)S(1)}, bf16[1024,128]{1,0:T(8,128)(2,1)}) custom-call(f32[1,1024]{1,0:T(1,128)S(1)} %bitcast.9, bf16[1024,512]{1,0:T(8,128)(2,1)S(1)} %get-tuple-element.34.flipped_ref, bf16[1024,512]{1,0:T(8,128)(2,1)S(1)} %get-tuple-element.35.grad_ref, ...), custom_call_target="tpu_custom_call", output_to_operand_aliasing={{0}: (3, {})} | custom-call | flops 134217728 | bytes 3166208 | tf_op jit(solution)/shard_map/pallas_call | solution.py:357
  36.3 5.5 %all-to-all-start.2 = ((bf16[8,128,128]{2,1,0:T(8,128)(2,1)}), bf16[8,128,128]{2,1,0:T(8,128)(2,1)S(1)}, u32[]{:S(2)}, u32[]{:S(2)}) async-start(bf16[8,128,128]{2,1,0:T(8,128)(2,1)} %bitcast.11), calls=%async_computation.2 | async-start | bytes 524288 | tf_op jit(solution)/shard_map/all_to_all | solution.py:403
  41.8 4.9 %shard_map.82 = (bf16[512,1024]{1,0:T(8,128)(2,1)}, bf16[512,1024]{1,0:T(8,128)(2,1)S(1)}, bf16[512,768]{1,0:T(8,128)(2,1)S(1)}) custom-call(bf16[512,1024]{1,0:T(8,128)(2,1)} %key_hbm.9, bf16[512,1024]{1,0:T(8,128)(2,1)} %value_hbm.9, bf16[3072,256]{1,0:T(8,128)(2,1)} %get-tuple-element.42.first_hbm, ...), custom_call_target="tpu_custom_call" | custom-call | flops 939524096 | bytes 6553600 | tf_op jit(solution)/shard_map/pallas_call | solution.py:357
  46.8 0.0 all-to-all-done.2.block_ref
  46.8 0.8 %shard_map.84 = bf16[8,128,128]{2,1,0:T(8,128)(2,1)} custom-call(bf16[8,128,128]{2,1,0:T(8,128)(2,1)S(1)} %all-to-all-done.2.block_ref), custom_call_target="tpu_custom_call" | custom-call | flops 131072 | bytes 262144 | tf_op jit(solution)/shard_map/pallas_call | solution.py:357
  47.6 5.9 %all-to-all-start.3 = ((bf16[8,128,128]{2,1,0:T(8,128)(2,1)}), bf16[8,128,128]{2,1,0:T(8,128)(2,1)S(1)}, u32[]{:S(2)}, u32[]{:S(2)}) async-start(bf16[8,128,128]{2,1,0:T(8,128)(2,1)} %shard_map.84), calls=%async_computation.3 | async-start | bytes 524288 | tf_op jit(solution)/shard_map/all_to_all | solution.py:403
  53.5 4.5 %shard_map.83 = (bf16[512,1024]{1,0:T(8,128)(2,1)S(1)}, bf16[512,256]{1,0:T(8,128)(2,1)S(1)}, bf16[512,1024]{1,0:T(8,128)(2,1)S(1)}) custom-call(bf16[512,1024]{1,0:T(8,128)(2,1)} %query_hbm.3, bf16[512,1024]{1,0:T(8,128)(2,1)} %value_hbm.9, bf16[3072,256]{1,0:T(8,128)(2,1)} %get-tuple-element.43.second_hbm.weight_hbm, ...), custom_call_target="tpu_custom_call", output_to_operand_aliasing={{0}: (3, {})} | custom-call | flops 1207959552 | bytes 4718592 | tf_op jit(solution)/shard_map/pallas_call | solution.py:357
  58.0 0.1 all-to-all-done.3
  58.1 2.5 %shard_map.85 = (bf16[512,1024]{1,0:T(8,128)(2,1)}, bf16[512,1024]{1,0:T(8,128)(2,1)}) custom-call(bf16[512,1024]{1,0:T(8,128)(2,1)} %key_hbm.9, bf16[512,1024]{1,0:T(8,128)(2,1)S(1)} %get-tuple-element.50.value_ref, bf16[512,1024]{1,0:T(8,128)(2,1)S(1)} %get-tuple-element.51.key_part, bf16[512,768]{1,0:T(8,128)(2,1)S(1)} %get-tuple-element.52.early_part, ...), custom_call_target="tpu_custom_call" | custom-call | flops 268435456 | bytes 4456448 | tf_op jit(solution)/shard_map/pallas_call | solution.py:357
  (2 shorter events, 0.0 us)
Async XLA Ops:
  3.1 14.9 %all-to-all-start = ((bf16[8,128,128]{2,1,0:T(8,128)(2,1)}), bf16[8,128,128]{2,1,0:T(8,128)(2,1)S(1)}, u32[]{:S(2)}, u32[]{:S(2)}) async-start(bf16[8,128,128]{2,1,0:T(8,128)(2,1)} %bitcast.10), calls=%async_computation | async-start | bytes 524288 | tf_op jit(solution)/shard_map/all_to_all | solution.py:403
  18.8 9.9 %all-to-all-start.1 = ((bf16[8,128,128]{2,1,0:T(8,128)(2,1)}), bf16[8,128,128]{2,1,0:T(8,128)(2,1)S(1)}, u32[]{:S(2)}, u32[]{:S(2)}) async-start(bf16[8,128,128]{2,1,0:T(8,128)(2,1)} %shard_map.79), calls=%async_computation.1 | async-start | bytes 524288 | tf_op jit(solution)/shard_map/all_to_all | solution.py:403
  23.4 5.3 %copy-start = (f32[1024]{0:T(1024)S(1)}, f32[1024]{0:T(1024)}, u32[]{:S(2)}) copy-start(f32[1024]{0:T(1024)} %param.9) | copy-start | bytes 12292
  29.5 3.1 %collective-permute-start.2 = (f32[2,512]{1,0:T(2,128)S(1)}, f32[2,512]{1,0:T(2,128)S(1)}, u32[]{:S(2)}, u32[]{:S(2)}) collective-permute-start(f32[2,512]{1,0:T(2,128)S(1)} %get-tuple-element.40.refs_0_), channel_id=1, source_target_pairs={{0,3},{1,2},{2,1},{3,0},{4,7},{5,6},{6,5},{7,4},{8,11},{9,10},{10,... | collective-permute-start | bytes 12296 | tf_op jit(solution)/shard_map/ppermute | solution.py:397
  29.6 3.0 %collective-permute-start.1 = (f32[2,512]{1,0:T(2,128)S(1)}, f32[2,512]{1,0:T(2,128)S(1)}, u32[]{:S(2)}, u32[]{:S(2)}) collective-permute-start(f32[2,512]{1,0:T(2,128)S(1)} %get-tuple-element.40.refs_0_), channel_id=1, source_target_pairs={{0,1},{1,0},{2,3},{3,2},{4,5},{5,4},{6,7},{7,6},{8,9},{9,8},{10,11... | collective-permute-start | bytes 12296 | tf_op jit(solution)/shard_map/ppermute | solution.py:397
  31.2 3.6 %collective-permute-start = (f32[2,512]{1,0:T(2,128)S(1)}, f32[2,512]{1,0:T(2,128)S(1)}, u32[]{:S(2)}, u32[]{:S(2)}) collective-permute-start(f32[2,512]{1,0:T(2,128)S(1)} %get-tuple-element.40.refs_0_), channel_id=1, source_target_pairs={{0,2},{1,3},{2,0},{3,1},{4,6},{5,7},{6,4},{7,5},{8,10},{9,11},{10,... | collective-permute-start | bytes 12296 | tf_op jit(solution)/shard_map/ppermute | solution.py:397
  36.3 10.5 %all-to-all-start.2 = ((bf16[8,128,128]{2,1,0:T(8,128)(2,1)}), bf16[8,128,128]{2,1,0:T(8,128)(2,1)S(1)}, u32[]{:S(2)}, u32[]{:S(2)}) async-start(bf16[8,128,128]{2,1,0:T(8,128)(2,1)} %bitcast.11), calls=%async_computation.2 | async-start | bytes 524288 | tf_op jit(solution)/shard_map/all_to_all | solution.py:403
  47.6 10.5 %all-to-all-start.3 = ((bf16[8,128,128]{2,1,0:T(8,128)(2,1)}), bf16[8,128,128]{2,1,0:T(8,128)(2,1)S(1)}, u32[]{:S(2)}, u32[]{:S(2)}) async-start(bf16[8,128,128]{2,1,0:T(8,128)(2,1)} %shard_map.84), calls=%async_computation.3 | async-start | bytes 524288 | tf_op jit(solution)/shard_map/all_to_all | solution.py:403

commit v27 on v24

--- a/solution.py
+++ b/solution.py
@@ -391,7 +391,7 @@
 def from_all(part, axis):
     count = lax.axis_size(axis)
     parts = [part]
-    for shift in range(1, count):
+    for shift in range(count - 1, 0, -1):
         pairs = [(place, (place + shift) % count) for place in range(count)]
         parts.append(lax.ppermute(part, axis, pairs))
     return parts

time: 60.6 us -> 63 us (1.040)
  starting transfers between devices: 25.5 us -> 27.7 us
    all_to_all x4, waiting for transfers between devices: 5.3 us -> 7 us  [exchange(): return lax.all_to_all(pieces, axis, 0, 0, axis_index_groups=groups)]
    ppermute x3, waiting for transfers between devices: 2.87 us -> 1.33 us  [from_all(): parts.append(lax.ppermute(part, axis, pairs))]
    ppermute x3, starting transfers between devices: 1.78 us -> 3 us  [from_all(): parts.append(lax.ppermute(part, axis, pairs))]
    all_to_all x4, starting transfers between devices: 23.7 us -> 24.7 us  [exchange(): return lax.all_to_all(pieces, axis, 0, 0, axis_index_groups=groups)]
  transfers between devices with their start and end apart: 7 -> 7, of which waited for: 5 -> 7; matrix products, arithmetic and copies ran while one was open for 0% -> 0% of each run, Pallas kernels for 28% -> 27%
where the time goes in v27:
time: 63 us; the launch traced here: 62.3 us
  starting transfers between devices  27.7 us (44%)
  Pallas kernels  25.4 us (40%)
  waiting for transfers between devices  8.32 us (13%)
  between operations  0.88 us (1%)
    pallas_call x10, Pallas kernels, local_call(): pl.pallas_call(body, in_specs=specs, out_specs=out_specs, out_shape=outs,...  25.4 us
    all_to_all x4, starting transfers between devices, exchange(): return lax.all_to_all(pieces, axis, 0, 0, axis_index_groups=groups)  24.7 us
    all_to_all x4, waiting for transfers between devices, exchange(): return lax.all_to_all(pieces, axis, 0, 0, axis_index_groups=groups)  7 us
    ppermute x3, starting transfers between devices, from_all(): parts.append(lax.ppermute(part, axis, pairs))  3 us
    ppermute x3, waiting for transfers between devices, from_all(): parts.append(lax.ppermute(part, axis, pairs))  1.33 us
  transfers between devices with their start and end apart: 7, of which 7 were waited for; matrix products, arithmetic and copies ran while one was open for 0% of the time, Pallas kernels for 27%

profile of v27, /device:TPU:0, one launch (start us, length us, event | category | flops | bytes accessed | tf_op | source)
XLA Modules:
  0.0 62.3 jit_solution(6106734083347089491)
XLA Ops:
  0.6 2.5 %shard_map.76 = bf16[1024,128]{1,0:T(8,128)(2,1)} custom-call(bf16[512,1024]{1,0:T(8,128)(2,1)} %key_hbm.9, bf16[512,1024]{1,0:T(8,128)(2,1)} %value_hbm.9), custom_call_target="tpu_custom_call" | custom-call | flops 134217728 | bytes 2097152 | tf_op jit(solution)/shard_map/pallas_call | solution.py:357
  3.1 7.9 %all-to-all-start = ((bf16[8,128,128]{2,1,0:T(8,128)(2,1)}), bf16[8,128,128]{2,1,0:T(8,128)(2,1)S(1)}, u32[]{:S(2)}, u32[]{:S(2)}) async-start(bf16[8,128,128]{2,1,0:T(8,128)(2,1)} %bitcast.10), calls=%async_computation | async-start | bytes 524288 | tf_op jit(solution)/shard_map/all_to_all | solution.py:402
  11.0 3.8 %shard_map.77 = (bf16[1024,512]{1,0:T(8,128)(2,1)S(1)}, bf16[1024,512]{1,0:T(8,128)(2,1)S(1)}, bf16[1024,512]{1,0:T(8,128)(2,1)S(1)}, bf16[3072,256]{1,0:T(8,128)(2,1)}) custom-call(bf16[512,1024]{1,0:T(8,128)(2,1)} %query_hbm.3, bf16[512,1024]{1,0:T(8,128)(2,1)} %key_hbm.9, bf16[512,1024]{1,0:T(8,128)(2,1)} %value_hbm.9, bf16[512,1024]{1,0:T(8,128)(2,1)} %grad_hbm.1), custom_call_target="tpu_custom_call" | custom-call | flops 805306368 | bytes 4194304 | tf_op jit(solution)/shard_map/pallas_call | solution.py:357
  14.8 3.2 %all-to-all-done.block_ref = bf16[8,128,128]{2,1,0:T(8,128)(2,1)S(1)} async-done(((bf16[8,128,128]{2,1,0:T(8,128)(2,1)}), bf16[8,128,128]{2,1,0:T(8,128)(2,1)S(1)}, u32[]{:S(2)}, u32[]{:S(2)}) %all-to-all-start) | async-done | bytes 262176 | tf_op jit(solution)/shard_map/all_to_all | solution.py:402
  18.0 0.8 %shard_map.79 = bf16[8,128,128]{2,1,0:T(8,128)(2,1)} custom-call(bf16[8,128,128]{2,1,0:T(8,128)(2,1)S(1)} %all-to-all-done.block_ref), custom_call_target="tpu_custom_call" | custom-call | flops 131072 | bytes 262144 | tf_op jit(solution)/shard_map/pallas_call | solution.py:357
  18.8 4.6 %all-to-all-start.1 = ((bf16[8,128,128]{2,1,0:T(8,128)(2,1)}), bf16[8,128,128]{2,1,0:T(8,128)(2,1)S(1)}, u32[]{:S(2)}, u32[]{:S(2)}) async-start(bf16[8,128,128]{2,1,0:T(8,128)(2,1)} %shard_map.79), calls=%async_computation.1 | async-start | bytes 524288 | tf_op jit(solution)/shard_map/all_to_all | solution.py:402
  23.4 3.3 %shard_map.78 = (bf16[1024,512]{1,0:T(8,128)(2,1)S(1)}, bf16[3072,256]{1,0:T(8,128)(2,1)}) custom-call(bf16[512,1024]{1,0:T(8,128)(2,1)} %key_hbm.9, bf16[512,1024]{1,0:T(8,128)(2,1)} %value_hbm.9, bf16[1024,512]{1,0:T(8,128)(2,1)S(1)} %get-tuple-element.34.flipped_ref, ...), custom_call_target="tpu_custom_call", output_to_operand_aliasing={{0}: (3, {})} | custom-call | flops 402653184 | bytes 4194304 | tf_op jit(solution)/shard_map/pallas_call | solution.py:357
  26.7 2.0 %all-to-all-done.1 = bf16[8,128,128]{2,1,0:T(8,128)(2,1)S(1)} async-done(((bf16[8,128,128]{2,1,0:T(8,128)(2,1)}), bf16[8,128,128]{2,1,0:T(8,128)(2,1)S(1)}, u32[]{:S(2)}, u32[]{:S(2)}) %all-to-all-start.1) | async-done | bytes 262176 | tf_op jit(solution)/shard_map/all_to_all | solution.py:402
  28.7 0.8 %shard_map.80 = (bf16[1024,512]{1,0:T(8,128)(2,1)S(1)}, f32[2,512]{1,0:T(2,128)S(1)}) custom-call(f32[1,1024]{1,0:T(1,128)S(1)} %bitcast.8, bf16[1024,512]{1,0:T(8,128)(2,1)S(1)} %get-tuple-element.34.flipped_ref, bf16[1024,512]{1,0:T(8,128)(2,1)S(1)} %get-tuple-element.35.grad_ref, ...), custom_call_target="tpu_custom_call", output_to_operand_aliasing={{0}: (3, {})} | custom-call | flops 134217728 | bytes 3411968 | tf_op jit(solution)/shard_map/pallas_call | solution.py:357
  29.5 0.1 collective-permute-start.2
  29.6 1.6 %collective-permute-start.1 = (f32[2,512]{1,0:T(2,128)S(1)}, f32[2,512]{1,0:T(2,128)S(1)}, u32[]{:S(2)}, u32[]{:S(2)}) collective-permute-start(f32[2,512]{1,0:T(2,128)S(1)} %get-tuple-element.40.refs_0_), channel_id=1, source_target_pairs={{0,2},{1,3},{2,0},{3,1},{4,6},{5,7},{6,4},{7,5},{8,10},{9,11},{10,... | collective-permute-start | bytes 12296 | tf_op jit(solution)/shard_map/ppermute | solution.py:396
  31.1 1.4 %collective-permute-start = (f32[2,512]{1,0:T(2,128)S(1)}, f32[2,512]{1,0:T(2,128)S(1)}, u32[]{:S(2)}, u32[]{:S(2)}) collective-permute-start(f32[2,512]{1,0:T(2,128)S(1)} %get-tuple-element.40.refs_0_), channel_id=1, source_target_pairs={{0,3},{1,0},{2,1},{3,2},{4,7},{5,4},{6,5},{7,6},{8,11},{9,8},{10,9... | collective-permute-start | bytes 12296 | tf_op jit(solution)/shard_map/ppermute | solution.py:396
  32.5 0.1 collective-permute-done.2.refs_3_
  32.6 0.7 %collective-permute-done.1.refs_2_ = f32[2,512]{1,0:T(2,128)S(1)} collective-permute-done((f32[2,512]{1,0:T(2,128)S(1)}, f32[2,512]{1,0:T(2,128)S(1)}, u32[]{:S(2)}, u32[]{:S(2)}) %collective-permute-start.1) | collective-permute-done | bytes 4128 | tf_op jit(solution)/shard_map/ppermute | solution.py:396
  33.3 0.6 collective-permute-done.refs_1_
  33.9 1.5 %shard_map.81 = (bf16[1024,512]{1,0:T(8,128)(2,1)S(1)}, bf16[1024,128]{1,0:T(8,128)(2,1)}) custom-call(f32[1,1024]{1,0:T(1,128)S(1)} %bitcast.9, bf16[1024,512]{1,0:T(8,128)(2,1)S(1)} %get-tuple-element.34.flipped_ref, bf16[1024,512]{1,0:T(8,128)(2,1)S(1)} %get-tuple-element.35.grad_ref, ...), custom_call_target="tpu_custom_call", output_to_operand_aliasing={{0}: (3, {})} | custom-call | flops 134217728 | bytes 3166208 | tf_op jit(solution)/shard_map/pallas_call | solution.py:357
  35.3 5.5 %all-to-all-start.2 = ((bf16[8,128,128]{2,1,0:T(8,128)(2,1)}), bf16[8,128,128]{2,1,0:T(8,128)(2,1)S(1)}, u32[]{:S(2)}, u32[]{:S(2)}) async-start(bf16[8,128,128]{2,1,0:T(8,128)(2,1)} %bitcast.11), calls=%async_computation.2 | async-start | bytes 524288 | tf_op jit(solution)/shard_map/all_to_all | solution.py:402
  40.9 4.9 %shard_map.82 = (bf16[512,1024]{1,0:T(8,128)(2,1)}, bf16[512,1024]{1,0:T(8,128)(2,1)S(1)}, bf16[512,768]{1,0:T(8,128)(2,1)S(1)}) custom-call(bf16[512,1024]{1,0:T(8,128)(2,1)} %key_hbm.9, bf16[512,1024]{1,0:T(8,128)(2,1)} %value_hbm.9, bf16[3072,256]{1,0:T(8,128)(2,1)} %get-tuple-element.42.first_hbm, ...), custom_call_target="tpu_custom_call" | custom-call | flops 939524096 | bytes 6553600 | tf_op jit(solution)/shard_map/pallas_call | solution.py:357
  45.8 0.9 %all-to-all-done.2.block_ref = bf16[8,128,128]{2,1,0:T(8,128)(2,1)S(1)} async-done(((bf16[8,128,128]{2,1,0:T(8,128)(2,1)}), bf16[8,128,128]{2,1,0:T(8,128)(2,1)S(1)}, u32[]{:S(2)}, u32[]{:S(2)}) %all-to-all-start.2) | async-done | bytes 262176 | tf_op jit(solution)/shard_map/all_to_all | solution.py:402
  46.8 0.8 %shard_map.84 = bf16[8,128,128]{2,1,0:T(8,128)(2,1)} custom-call(bf16[8,128,128]{2,1,0:T(8,128)(2,1)S(1)} %all-to-all-done.2.block_ref), custom_call_target="tpu_custom_call" | custom-call | flops 131072 | bytes 262144 | tf_op jit(solution)/shard_map/pallas_call | solution.py:357
  47.5 6.8 %all-to-all-start.3 = ((bf16[8,128,128]{2,1,0:T(8,128)(2,1)}), bf16[8,128,128]{2,1,0:T(8,128)(2,1)S(1)}, u32[]{:S(2)}, u32[]{:S(2)}) async-start(bf16[8,128,128]{2,1,0:T(8,128)(2,1)} %shard_map.84), calls=%async_computation.3 | async-start | bytes 524288 | tf_op jit(solution)/shard_map/all_to_all | solution.py:402
  54.3 4.5 %shard_map.83 = (bf16[512,1024]{1,0:T(8,128)(2,1)S(1)}, bf16[512,256]{1,0:T(8,128)(2,1)S(1)}, bf16[512,1024]{1,0:T(8,128)(2,1)S(1)}) custom-call(bf16[512,1024]{1,0:T(8,128)(2,1)} %query_hbm.3, bf16[512,1024]{1,0:T(8,128)(2,1)} %value_hbm.9, bf16[3072,256]{1,0:T(8,128)(2,1)} %get-tuple-element.43.second_hbm.weight_hbm, ...), custom_call_target="tpu_custom_call", output_to_operand_aliasing={{0}: (3, {})} | custom-call | flops 1207959552 | bytes 4718592 | tf_op jit(solution)/shard_map/pallas_call | solution.py:357
  58.8 0.8 %all-to-all-done.3 = bf16[8,128,128]{2,1,0:T(8,128)(2,1)S(1)} async-done(((bf16[8,128,128]{2,1,0:T(8,128)(2,1)}), bf16[8,128,128]{2,1,0:T(8,128)(2,1)S(1)}, u32[]{:S(2)}, u32[]{:S(2)}) %all-to-all-start.3) | async-done | bytes 262176 | tf_op jit(solution)/shard_map/all_to_all | solution.py:402
  59.7 2.5 %shard_map.85 = (bf16[512,1024]{1,0:T(8,128)(2,1)}, bf16[512,1024]{1,0:T(8,128)(2,1)}) custom-call(bf16[512,1024]{1,0:T(8,128)(2,1)} %key_hbm.9, bf16[512,1024]{1,0:T(8,128)(2,1)S(1)} %get-tuple-element.50.value_ref, bf16[512,1024]{1,0:T(8,128)(2,1)S(1)} %get-tuple-element.51.key_part, bf16[512,768]{1,0:T(8,128)(2,1)S(1)} %get-tuple-element.52.early_part, ...), custom_call_target="tpu_custom_call" | custom-call | flops 268435456 | bytes 4456448 | tf_op jit(solution)/shard_map/pallas_call | solution.py:357
  (2 shorter events, 0.0 us)
Async XLA Ops:
  3.1 14.9 %all-to-all-start = ((bf16[8,128,128]{2,1,0:T(8,128)(2,1)}), bf16[8,128,128]{2,1,0:T(8,128)(2,1)S(1)}, u32[]{:S(2)}, u32[]{:S(2)}) async-start(bf16[8,128,128]{2,1,0:T(8,128)(2,1)} %bitcast.10), calls=%async_computation | async-start | bytes 524288 | tf_op jit(solution)/shard_map/all_to_all | solution.py:402
  18.8 9.9 %all-to-all-start.1 = ((bf16[8,128,128]{2,1,0:T(8,128)(2,1)}), bf16[8,128,128]{2,1,0:T(8,128)(2,1)S(1)}, u32[]{:S(2)}, u32[]{:S(2)}) async-start(bf16[8,128,128]{2,1,0:T(8,128)(2,1)} %shard_map.79), calls=%async_computation.1 | async-start | bytes 524288 | tf_op jit(solution)/shard_map/all_to_all | solution.py:402
  23.4 5.3 %copy-start = (f32[1024]{0:T(1024)S(1)}, f32[1024]{0:T(1024)}, u32[]{:S(2)}) copy-start(f32[1024]{0:T(1024)} %param.9) | copy-start | bytes 12292
  29.5 3.1 %collective-permute-start.2 = (f32[2,512]{1,0:T(2,128)S(1)}, f32[2,512]{1,0:T(2,128)S(1)}, u32[]{:S(2)}, u32[]{:S(2)}) collective-permute-start(f32[2,512]{1,0:T(2,128)S(1)} %get-tuple-element.40.refs_0_), channel_id=1, source_target_pairs={{0,1},{1,2},{2,3},{3,0},{4,5},{5,6},{6,7},{7,4},{8,9},{9,10},{10,1... | collective-permute-start | bytes 12296 | tf_op jit(solution)/shard_map/ppermute | solution.py:396
  29.6 3.7 %collective-permute-start.1 = (f32[2,512]{1,0:T(2,128)S(1)}, f32[2,512]{1,0:T(2,128)S(1)}, u32[]{:S(2)}, u32[]{:S(2)}) collective-permute-start(f32[2,512]{1,0:T(2,128)S(1)} %get-tuple-element.40.refs_0_), channel_id=1, source_target_pairs={{0,2},{1,3},{2,0},{3,1},{4,6},{5,7},{6,4},{7,5},{8,10},{9,11},{10,... | collective-permute-start | bytes 12296 | tf_op jit(solution)/shard_map/ppermute | solution.py:396
  31.1 2.7 %collective-permute-start = (f32[2,512]{1,0:T(2,128)S(1)}, f32[2,512]{1,0:T(2,128)S(1)}, u32[]{:S(2)}, u32[]{:S(2)}) collective-permute-start(f32[2,512]{1,0:T(2,128)S(1)} %get-tuple-element.40.refs_0_), channel_id=1, source_target_pairs={{0,3},{1,0},{2,1},{3,2},{4,7},{5,4},{6,5},{7,6},{8,11},{9,8},{10,9... | collective-permute-start | bytes 12296 | tf_op jit(solution)/shard_map/ppermute | solution.py:396
  35.3 11.4 %all-to-all-start.2 = ((bf16[8,128,128]{2,1,0:T(8,128)(2,1)}), bf16[8,128,128]{2,1,0:T(8,128)(2,1)S(1)}, u32[]{:S(2)}, u32[]{:S(2)}) async-start(bf16[8,128,128]{2,1,0:T(8,128)(2,1)} %bitcast.11), calls=%async_computation.2 | async-start | bytes 524288 | tf_op jit(solution)/shard_map/all_to_all | solution.py:402
  47.5 12.1 %all-to-all-start.3 = ((bf16[8,128,128]{2,1,0:T(8,128)(2,1)}), bf16[8,128,128]{2,1,0:T(8,128)(2,1)S(1)}, u32[]{:S(2)}, u32[]{:S(2)}) async-start(bf16[8,128,128]{2,1,0:T(8,128)(2,1)} %shard_map.84), calls=%async_computation.3 | async-start | bytes 524288 | tf_op jit(solution)/shard_map/all_to_all | solution.py:402
